TPU v7x, 32 devices: a whole 2x2x4 slice. The times are simulated.
32 devices in a mesh: seq: 16 (over z, x, core), dp: 2 (over y).
Axes of the slice: x: 2, y: 2, z: 4, core: 2. Of those that a mesh axis runs over, the one named last changes fastest.
Arguments:
- queries: bfloat16 [2, 2048, 2048], P('dp', 'seq'), may hold values from -18 to 18
- key_vectors: bfloat16 [2, 2048, 2048], P('dp', 'seq'), may hold values from -18 to 18
- value_vectors: bfloat16 [2, 2048, 2048], P('dp', 'seq'), may hold values from -6 to 6
- cotangent: bfloat16 [2, 2048, 2048], P('dp', 'seq'), may hold values from -6 to 6
- compress_kernel: bfloat16 [512, 128], replicated, may hold values from -0.25 to 0.25
- memory_reach: int32 [2, 16], P('dp', 'seq'), may hold values from 1 to 4, as said below
Outputs:
- attended: bfloat16 [2, 2048, 2048], P('dp', 'seq')
- grad_queries: bfloat16 [2, 2048, 2048], P('dp', 'seq')
- grad_keys: bfloat16 [2, 2048, 2048], P('dp', 'seq')
- grad_values: bfloat16 [2, 2048, 2048], P('dp', 'seq')
- grad_kernel: float32 [512, 128], P('seq')
Inputs may be any that keep to these rules, and one draw needn't show every extreme that they name: `memory_reach`: some segment reads 4 earlier segments and some reads 1.
All inputs are finite; a program needn't handle non-finite values.
Results may differ from a plain program's by a relative error of at most 0.0076.
Values may be sent and summed in bfloat16 or wider, within the bound.
No kernel may reach another device: no remote copies, remote signals or barrier semaphores. Data moves between devices by JAX's collectives and lax.ppermute only.
A program may use at most 64 MiB of HBM per device.

v0:
```python
import jax
import jax.numpy as jnp
from jax import lax
from jax.sharding import PartitionSpec as P

H = 16
E = 128


def shifted(value, axis, steps):
    count = lax.axis_size(axis)
    initial, last = (max(0, -steps), min(count, count - steps))
    return lax.ppermute(value, axis, [(source, source + steps) for source in range(initial, last)])


def attend_block(query_rows, key_rows, value_rows, grad_rows, memory_keys, memory_values, visible):
    segment_len = query_rows.shape[0]
    slot_rows = segment_len // 4
    span_len = 2 * segment_len
    score_scale = E ** (-0.5)
    query_heads = query_rows.reshape(segment_len, H, E)
    grad_heads = grad_rows.reshape(segment_len, H, E)
    key_heads = jnp.concatenate([memory_keys, key_rows], 0).reshape(span_len, H, E)
    value_heads = jnp.concatenate([memory_values, value_rows], 0).reshape(span_len, H, E)
    columns = jnp.arange(span_len, dtype=jnp.int32)
    row_ids = jnp.arange(segment_len, dtype=jnp.int32)
    slot_of = jnp.minimum(columns // slot_rows, 3)
    memory_open = jnp.any(
        (slot_of[:, None] == jnp.arange(4, dtype=jnp.int32)[None, :]) & visible[None, :], axis=1
    )
    allowed = jnp.where(
        columns[None, :] < segment_len,
        memory_open[None, :],
        columns[None, :] - segment_len <= row_ids[:, None],
    )
    scores = (
        jnp.einsum("shd,lhd->hsl", query_heads, key_heads, preferred_element_type=jnp.float32)
        * score_scale
    )
    scores = jnp.where(allowed[None], scores, -1e30)
    highest = jnp.max(scores, axis=2, keepdims=True)
    raised = jnp.where(allowed[None], jnp.exp(scores - highest), 0.0)
    weights = raised / jnp.sum(raised, axis=2, keepdims=True)
    weights_low = weights.astype(jnp.bfloat16)
    attended = jnp.einsum(
        "hsl,lhd->shd", weights_low, value_heads, preferred_element_type=jnp.float32
    )
    grad_weights = jnp.einsum(
        "shd,lhd->hsl", grad_heads, value_heads, preferred_element_type=jnp.float32
    )
    row_delta = jnp.sum(weights * grad_weights, axis=2, keepdims=True)
    grad_scores = (weights * (grad_weights - row_delta) * score_scale).astype(jnp.bfloat16)
    grad_query = jnp.einsum(
        "hsl,lhd->shd", grad_scores, key_heads, preferred_element_type=jnp.float32
    )
    grad_key_list = jnp.einsum(
        "hsl,shd->lhd", grad_scores, query_heads, preferred_element_type=jnp.float32
    ).reshape(span_len, H * E)
    grad_value_list = jnp.einsum(
        "hsl,shd->lhd", weights_low, grad_heads, preferred_element_type=jnp.float32
    ).reshape(span_len, H * E)
    return (
        attended.reshape(segment_len, H * E).astype(jnp.bfloat16),
        grad_query.reshape(segment_len, H * E).astype(jnp.bfloat16),
        grad_key_list[segment_len:],
        grad_value_list[segment_len:],
        grad_key_list[:segment_len],
        grad_value_list[:segment_len],
    )


def local(queries, key_vectors, value_vectors, cotangent, compress_kernel, memory_reach):
    query_rows = queries[0]
    key_rows = key_vectors[0]
    value_rows = value_vectors[0]
    grad_rows = cotangent[0]
    segment_len = query_rows.shape[0]
    slot_rows = segment_len // 4
    kernel = compress_kernel.reshape(4, E, E)
    key_blocks = key_rows.reshape(slot_rows, 4, H, E)
    value_blocks = value_rows.reshape(slot_rows, 4, H, E)
    packed_keys = (
        jnp.einsum("mthe,tef->mhf", key_blocks, kernel, preferred_element_type=jnp.float32)
        .astype(jnp.bfloat16)
        .reshape(slot_rows, H * E)
    )
    packed_values = (
        jnp.einsum("mthe,tef->mhf", value_blocks, kernel, preferred_element_type=jnp.float32)
        .astype(jnp.bfloat16)
        .reshape(slot_rows, H * E)
    )
    received = []
    for offset in range(1, 5):
        received.append(shifted((packed_keys, packed_values), "seq", offset))
    memory_keys = jnp.concatenate([shifted_pair[0] for shifted_pair in received], 0)
    memory_values = jnp.concatenate([shifted_pair[1] for shifted_pair in received], 0)
    position = lax.axis_index("seq")
    slot_ids = jnp.arange(1, 5, dtype=jnp.int32)
    visible = (slot_ids <= memory_reach[0, 0]) & (position - slot_ids >= 0)
    attended, grad_query, local_keys, local_values, memory_grad_keys, memory_grad_values = (
        attend_block(
            query_rows, key_rows, value_rows, grad_rows, memory_keys, memory_values, visible
        )
    )
    slot_keys = memory_grad_keys.reshape(4, slot_rows, H * E)
    slot_values = memory_grad_values.reshape(4, slot_rows, H * E)
    summed_keys = jnp.zeros((slot_rows, H * E), jnp.float32)
    summed_values = jnp.zeros((slot_rows, H * E), jnp.float32)
    for offset in range(1, 5):
        arrived = shifted((slot_keys[offset - 1], slot_values[offset - 1]), "seq", -offset)
        summed_keys = summed_keys + arrived[0]
        summed_values = summed_values + arrived[1]
    packed_grad_keys = summed_keys.astype(jnp.bfloat16).reshape(slot_rows, H, E)
    packed_grad_values = summed_values.astype(jnp.bfloat16).reshape(slot_rows, H, E)
    back_keys = jnp.einsum(
        "mhf,tef->mthe", packed_grad_keys, kernel, preferred_element_type=jnp.float32
    ).reshape(segment_len, H * E)
    back_values = jnp.einsum(
        "mhf,tef->mthe", packed_grad_values, kernel, preferred_element_type=jnp.float32
    ).reshape(segment_len, H * E)
    key_grad = (local_keys + back_keys).astype(jnp.bfloat16)
    value_grad = (local_values + back_values).astype(jnp.bfloat16)
    kernel_terms = (
        jnp.einsum(
            "mthe,mhf->tef", key_blocks, packed_grad_keys, preferred_element_type=jnp.float32
        )
        + jnp.einsum(
            "mthe,mhf->tef", value_blocks, packed_grad_values, preferred_element_type=jnp.float32
        )
    ).reshape(4 * E, E)
    partial_sum = lax.psum_scatter(kernel_terms, "seq", scatter_dimension=0, tiled=True)
    grad_kernel = lax.psum(partial_sum, "dp")
    return (attended[None], grad_query[None], key_grad[None], value_grad[None], grad_kernel)


def solution(mesh):
    return jax.shard_map(
        local,
        mesh=mesh,
        in_specs=(
            P("dp", "seq", None),
            P("dp", "seq", None),
            P("dp", "seq", None),
            P("dp", "seq", None),
            P(),
            P("dp", "seq"),
        ),
        out_specs=(
            P("dp", "seq", None),
            P("dp", "seq", None),
            P("dp", "seq", None),
            P("dp", "seq", None),
            P("seq", None),
        ),
        check_vma=False,
    )
```

profile of v0, /device:TPU:0, one launch (start us, length us, event | category | flops | bytes accessed | tf_op | source)
XLA Modules:
  0.0 212.4 jit_solution(7734019243496852412)
XLA Ops:
  9.5 4.9 %collective-permute-start.3 = (bf16[32,2048]{1,0:T(8,128)(2,1)}, bf16[32,2048]{1,0:T(8,128)(2,1)S(1)}, u32[]{:S(2)}, u32[]{:S(2)}) collective-permute-start(bf16[32,2048]{1,0:T(8,128)(2,1)} %bitcast.202), channel_id=1, source_target_pairs={{0,8},{2,10},{4,12},{6,14},{8,16},{10,18},{12,20},{14,22},{16,24},... | collective-permute-start | bytes 393224 | tf_op jit(solution)/shard_map/ppermute | solution.py:13
  14.4 2.6 %collective-permute-start.2 = (bf16[32,2048]{1,0:T(8,128)(2,1)}, bf16[32,2048]{1,0:T(8,128)(2,1)S(1)}, u32[]{:S(2)}, u32[]{:S(2)}) collective-permute-start(bf16[32,2048]{1,0:T(8,128)(2,1)} %bitcast.202), channel_id=1, source_target_pairs={{0,6},{2,8},{4,10},{6,12},{8,14},{10,16},{12,18},{14,20},{16,22},{... | collective-permute-start | bytes 393224 | tf_op jit(solution)/shard_map/ppermute | solution.py:13
  17.0 4.1 %collective-permute-start.1 = (bf16[32,2048]{1,0:T(8,128)(2,1)}, bf16[32,2048]{1,0:T(8,128)(2,1)}, u32[]{:S(2)}, u32[]{:S(2)}) collective-permute-start(bf16[32,2048]{1,0:T(8,128)(2,1)} %bitcast.202), channel_id=1, source_target_pairs={{0,4},{2,6},{4,8},{6,10},{8,12},{10,14},{12,16},{14,18},{16,20},{1... | collective-permute-start | bytes 393224 | tf_op jit(solution)/shard_map/ppermute | solution.py:13
  21.1 3.3 %collective-permute-start = (bf16[32,2048]{1,0:T(8,128)(2,1)}, bf16[32,2048]{1,0:T(8,128)(2,1)}, u32[]{:S(2)}, u32[]{:S(2)}) collective-permute-start(bf16[32,2048]{1,0:T(8,128)(2,1)} %bitcast.202), channel_id=1, source_target_pairs={{0,2},{2,4},{4,6},{6,8},{8,10},{10,12},{12,14},{14,16},{16,18},{18... | collective-permute-start | bytes 393224 | tf_op jit(solution)/shard_map/ppermute | solution.py:13
  25.4 2.2 %collective-permute-start.4 = (bf16[32,2048]{1,0:T(8,128)(2,1)}, bf16[32,2048]{1,0:T(8,128)(2,1)}, u32[]{:S(2)}, u32[]{:S(2)}) collective-permute-start(bf16[32,2048]{1,0:T(8,128)(2,1)} %bitcast.201), channel_id=1, source_target_pairs={{0,2},{2,4},{4,6},{6,8},{8,10},{10,12},{12,14},{14,16},{16,18},{18... | collective-permute-start | bytes 393224 | tf_op jit(solution)/shard_map/ppermute | solution.py:13
  32.6 2.8 %collective-permute-start.5 = (bf16[32,2048]{1,0:T(8,128)(2,1)}, bf16[32,2048]{1,0:T(8,128)(2,1)S(1)}, u32[]{:S(2)}, u32[]{:S(2)}) collective-permute-start(bf16[32,2048]{1,0:T(8,128)(2,1)} %bitcast.201), channel_id=1, source_target_pairs={{0,4},{2,6},{4,8},{6,10},{8,12},{10,14},{12,16},{14,18},{16,20},{1... | collective-permute-start | bytes 393224 | tf_op jit(solution)/shard_map/ppermute | solution.py:13
  36.4 3.0 %collective-permute-done.5 = bf16[32,2048]{1,0:T(8,128)(2,1)S(1)} collective-permute-done((bf16[32,2048]{1,0:T(8,128)(2,1)}, bf16[32,2048]{1,0:T(8,128)(2,1)S(1)}, u32[]{:S(2)}, u32[]{:S(2)}) %collective-permute-start.5) | collective-permute-done | bytes 131104 | tf_op jit(solution)/shard_map/ppermute | solution.py:13
  39.3 3.7 %collective-permute-start.6 = (bf16[32,2048]{1,0:T(8,128)(2,1)}, bf16[32,2048]{1,0:T(8,128)(2,1)S(1)}, u32[]{:S(2)}, u32[]{:S(2)}) collective-permute-start(bf16[32,2048]{1,0:T(8,128)(2,1)} %bitcast.201), channel_id=1, source_target_pairs={{0,6},{2,8},{4,10},{6,12},{8,14},{10,16},{12,18},{14,20},{16,22},{... | collective-permute-start | bytes 393224 | tf_op jit(solution)/shard_map/ppermute | solution.py:13
  43.1 2.8 %collective-permute-done.6 = bf16[32,2048]{1,0:T(8,128)(2,1)S(1)} collective-permute-done((bf16[32,2048]{1,0:T(8,128)(2,1)}, bf16[32,2048]{1,0:T(8,128)(2,1)S(1)}, u32[]{:S(2)}, u32[]{:S(2)}) %collective-permute-start.6) | collective-permute-done | bytes 131104 | tf_op jit(solution)/shard_map/ppermute | solution.py:13
  45.9 4.4 %collective-permute-start.7 = (bf16[32,2048]{1,0:T(8,128)(2,1)}, bf16[32,2048]{1,0:T(8,128)(2,1)S(1)}, u32[]{:S(2)}, u32[]{:S(2)}) collective-permute-start(bf16[32,2048]{1,0:T(8,128)(2,1)} %bitcast.201), channel_id=1, source_target_pairs={{0,8},{2,10},{4,12},{6,14},{8,16},{10,18},{12,20},{14,22},{16,24},... | collective-permute-start | bytes 393224 | tf_op jit(solution)/shard_map/ppermute | solution.py:13
  50.4 3.8 %collective-permute-done.7 = bf16[32,2048]{1,0:T(8,128)(2,1)S(1)} collective-permute-done((bf16[32,2048]{1,0:T(8,128)(2,1)}, bf16[32,2048]{1,0:T(8,128)(2,1)S(1)}, u32[]{:S(2)}, u32[]{:S(2)}) %collective-permute-start.7) | collective-permute-done | bytes 131104 | tf_op jit(solution)/shard_map/ppermute | solution.py:13
  60.6 2.8 %concatenate.33 = bf16[256,16,128]{0,2,1:T(8,128)(2,1)S(1)} concatenate(bf16[32,16,128]{0,2,1:T(8,128)(2,1)S(1)} %bitcast.212, bf16[32,16,128]{0,2,1:T(8,128)(2,1)S(1)} %bitcast.213, bf16[32,16,128]{0,2,1:T(8,128)(2,1)} %bitcast.214, bf16[32,16,128]{0,2,1:T(8,128)(2,1)} %bitcast.215, bf16[128,16,128]{0,2,1:T(8,128)(2,1)} %bitcast.218), dimensions={0} | concatenate | bytes 2097152 | tf_op jit(solution)/shard_map/concatenate | solution.py:24
  63.4 2.9 %fusion.18 = f32[16,256,128]{2,1,0:T(8,128)} fusion(bf16[256,16,128]{0,2,1:T(8,128)(2,1)S(1)} %concatenate.33, bf16[128,16,128]{2,1,0:T(8,128)(2,1)} %bitcast.216), kind=kOutput, calls=%fused_computation.35 | convolution fusion | flops 134217728 | bytes 3670016 | tf_op jit(solution)/shard_map/shd,lhd->hsl/dot_general | solution.py:48
  66.3 3.5 %fusion.45 = (f32[16,128]{1,0:T(8,128)S(1)}, f32[16,128,256]{1,2,0:T(8,128)}) fusion(pred[128,256]{0,1:T(8,128)(4,1)S(1)} %copy-done.10, bf16[256,16,128]{2,0,1:T(8,128)(2,1)} %constant_dynamic-update-slice_fusion, bf16[128,16,128]{2,1,0:T(8,128)(2,1)S(1)} %bitcast.230), kind=kOutput, calls=%fused_computation.90 | convolution fusion | flops 136839424 | bytes 3710976 | tf_op jit(solution)/shard_map/sub | solution.py:42
  69.8 3.0 %convolution_convert_fusion.1 = bf16[16,128,128]{2,1,0:T(8,128)(2,1)} fusion(bf16[256,16,128]{0,2,1:T(8,128)(2,1)S(1)} %concatenate.33, f32[16,128,256]{1,2,0:T(8,128)} %get-tuple-element.29, f32[16,128]{1,0:T(8,128)S(1)} %get-tuple-element.28), kind=kOutput, calls=%fused_computation.15 | convolution fusion | flops 135528448 | bytes 3678208 | tf_op jit(solution)/shard_map/hsl,lhd->shd/dot_general | solution.py:45
  73.3 6.5 %convolution_bitcast_fusion.1 = f32[256,16,128]{2,0,1:T(8,128)} fusion(f32[16,256,128]{2,1,0:T(8,128)} %fusion.18, bf16[128,16,128]{2,1,0:T(8,128)(2,1)} %bitcast.229, f32[16,128,256]{1,2,0:T(8,128)} %get-tuple-element.29, f32[16,128]{1,0:T(8,128)S(1)} %get-tuple-element.28), kind=kOutput, calls=%fused_computation.11 | convolution fusion | flops 137890048 | bytes 6823936 | tf_op jit(solution)/shard_map/hsl,shd->lhd/dot_general | solution.py:56
  87.9 5.6 %convolution_convert_fusion = bf16[16,128,128]{2,1,0:T(8,128)(2,1)} fusion(bf16[256,16,128]{2,0,1:T(8,128)(2,1)} %constant_dynamic-update-slice_fusion, f32[16,256,128]{2,1,0:T(8,128)} %fusion.18, f32[16,128,256]{1,2,0:T(8,128)} %get-tuple-element.29, f32[16,128]{1,0:T(8,128)S(1)} %get-tuple-element.28), kind=kOutput, calls=%fused_computation.14 | convolution fusion | flops 138152192 | bytes 5775360 | tf_op jit(solution)/shard_map/hsl,lhd->shd/dot_general | solution.py:53
  93.5 2.1 %copy.102 = bf16[1,128,2048]{2,1,0:T(8,128)(2,1)} copy(bf16[1,128,2048]{1,2,0:T(8,128)(2,1)} %bitcast.231) | data formatting | bytes 1048576
  95.6 2.0 copy.103
  115.0 2.6 %copy.99 = f32[1,128,2048]{1,2,0:T(8,128)} copy(f32[1,128,2048]{2,1,0:T(8,128)} %reshape.229) | data formatting | bytes 2097152 | tf_op jit(solution)/shard_map/reshape | solution.py:120
  117.6 2.1 fusion.9
  122.2 8.2 %collective-permute-done.11 = f32[32,2048]{1,0:T(8,128)} collective-permute-done((f32[32,2048]{1,0:T(8,128)}, f32[32,2048]{1,0:T(8,128)}, u32[]{:S(2)}, u32[]{:S(2)}) %collective-permute-start.11) | collective-permute-done | bytes 262176 | tf_op jit(solution)/shard_map/ppermute | solution.py:13
  136.9 59.2 %reduce-scatter.2.cloned.1.call-done = f32[32,128]{1,0:T(8,128)} async-done(((f32[512,128]{1,0:T(8,128)}), f32[32,128]{1,0:T(8,128)}) %reduce-scatter.2.cloned.1.call-update) | async-done | bytes 16400 | tf_op jit(solution)/shard_map/reduce_scatter | solution.py:131
  196.1 9.4 %psum.7 = f32[32,128]{1,0:T(8,128)} all-reduce(f32[32,128]{1,0:T(8,128)} %reduce-scatter.2.cloned.1.call-done), channel_id=1, replica_groups=mesh['seq'=16,'dp'=2] {'dp'}, use_global_device_ids=true, to_apply=%region_5.6 | all-reduce | flops 4096 | bytes 32768 | tf_op jit(solution)/shard_map/psum | solution.py:132
  (104 shorter events, 49.6 us)
Async XLA Ops:
  7.2 17.1 %copy-start.5 = (bf16[1,128,2048]{2,1,0:T(8,128)(2,1)S(1)}, bf16[1,128,2048]{2,1,0:T(8,128)(2,1)}, u32[]{:S(2)}) copy-start(bf16[1,128,2048]{2,1,0:T(8,128)(2,1)} %param.7) | copy-start | bytes 1572868
  7.2 188.9 %reduce-scatter.2.cloned.1.call-start = ((), (), s32[]{:S(2)}) async-start(), calls=%async_computation.1 | async-start | bytes 278528 | tf_op jit(solution)/shard_map/reduce_scatter | solution.py:131
  8.5 19.5 %copy-start.6 = (bf16[1,128,2048]{2,1,0:T(8,128)(2,1)S(1)}, bf16[1,128,2048]{2,1,0:T(8,128)(2,1)}, u32[]{:S(2)}) copy-start(bf16[1,128,2048]{2,1,0:T(8,128)(2,1)} %param.8) | copy-start | bytes 1572868
  9.5 50.1 %collective-permute-start.3 = (bf16[32,2048]{1,0:T(8,128)(2,1)}, bf16[32,2048]{1,0:T(8,128)(2,1)S(1)}, u32[]{:S(2)}, u32[]{:S(2)}) collective-permute-start(bf16[32,2048]{1,0:T(8,128)(2,1)} %bitcast.202), channel_id=1, source_target_pairs={{0,8},{2,10},{4,12},{6,14},{8,16},{10,18},{12,20},{14,22},{16,24},... | collective-permute-start | bytes 393224 | tf_op jit(solution)/shard_map/ppermute | solution.py:13
  14.4 43.3 %collective-permute-start.2 = (bf16[32,2048]{1,0:T(8,128)(2,1)}, bf16[32,2048]{1,0:T(8,128)(2,1)S(1)}, u32[]{:S(2)}, u32[]{:S(2)}) collective-permute-start(bf16[32,2048]{1,0:T(8,128)(2,1)} %bitcast.202), channel_id=1, source_target_pairs={{0,6},{2,8},{4,10},{6,12},{8,14},{10,16},{12,18},{14,20},{16,22},{... | collective-permute-start | bytes 393224 | tf_op jit(solution)/shard_map/ppermute | solution.py:13
  17.0 39.5 %collective-permute-start.1 = (bf16[32,2048]{1,0:T(8,128)(2,1)}, bf16[32,2048]{1,0:T(8,128)(2,1)}, u32[]{:S(2)}, u32[]{:S(2)}) collective-permute-start(bf16[32,2048]{1,0:T(8,128)(2,1)} %bitcast.202), channel_id=1, source_target_pairs={{0,4},{2,6},{4,8},{6,10},{8,12},{10,14},{12,16},{14,18},{16,20},{1... | collective-permute-start | bytes 393224 | tf_op jit(solution)/shard_map/ppermute | solution.py:13
  21.1 34.2 %collective-permute-start = (bf16[32,2048]{1,0:T(8,128)(2,1)}, bf16[32,2048]{1,0:T(8,128)(2,1)}, u32[]{:S(2)}, u32[]{:S(2)}) collective-permute-start(bf16[32,2048]{1,0:T(8,128)(2,1)} %bitcast.202), channel_id=1, source_target_pairs={{0,2},{2,4},{4,6},{6,8},{8,10},{10,12},{12,14},{14,16},{16,18},{18... | collective-permute-start | bytes 393224 | tf_op jit(solution)/shard_map/ppermute | solution.py:13
  24.3 5.3 %copy-start.7 = (bf16[1,128,2048]{2,1,0:T(8,128)(2,1)S(1)}, bf16[1,128,2048]{2,1,0:T(8,128)(2,1)}, u32[]{:S(2)}) copy-start(bf16[1,128,2048]{2,1,0:T(8,128)(2,1)} %param.6) | copy-start | bytes 1572868
  25.4 7.2 %collective-permute-start.4 = (bf16[32,2048]{1,0:T(8,128)(2,1)}, bf16[32,2048]{1,0:T(8,128)(2,1)}, u32[]{:S(2)}, u32[]{:S(2)}) collective-permute-start(bf16[32,2048]{1,0:T(8,128)(2,1)} %bitcast.201), channel_id=1, source_target_pairs={{0,2},{2,4},{4,6},{6,8},{8,10},{10,12},{12,14},{14,16},{16,18},{18... | collective-permute-start | bytes 393224 | tf_op jit(solution)/shard_map/ppermute | solution.py:13
  32.6 6.7 %collective-permute-start.5 = (bf16[32,2048]{1,0:T(8,128)(2,1)}, bf16[32,2048]{1,0:T(8,128)(2,1)S(1)}, u32[]{:S(2)}, u32[]{:S(2)}) collective-permute-start(bf16[32,2048]{1,0:T(8,128)(2,1)} %bitcast.201), channel_id=1, source_target_pairs={{0,4},{2,6},{4,8},{6,10},{8,12},{10,14},{12,16},{14,18},{16,20},{1... | collective-permute-start | bytes 393224 | tf_op jit(solution)/shard_map/ppermute | solution.py:13
  39.3 6.6 %collective-permute-start.6 = (bf16[32,2048]{1,0:T(8,128)(2,1)}, bf16[32,2048]{1,0:T(8,128)(2,1)S(1)}, u32[]{:S(2)}, u32[]{:S(2)}) collective-permute-start(bf16[32,2048]{1,0:T(8,128)(2,1)} %bitcast.201), channel_id=1, source_target_pairs={{0,6},{2,8},{4,10},{6,12},{8,14},{10,16},{12,18},{14,20},{16,22},{... | collective-permute-start | bytes 393224 | tf_op jit(solution)/shard_map/ppermute | solution.py:13
  45.9 8.3 %collective-permute-start.7 = (bf16[32,2048]{1,0:T(8,128)(2,1)}, bf16[32,2048]{1,0:T(8,128)(2,1)S(1)}, u32[]{:S(2)}, u32[]{:S(2)}) collective-permute-start(bf16[32,2048]{1,0:T(8,128)(2,1)} %bitcast.201), channel_id=1, source_target_pairs={{0,8},{2,10},{4,12},{6,14},{8,16},{10,18},{12,20},{14,22},{16,24},... | collective-permute-start | bytes 393224 | tf_op jit(solution)/shard_map/ppermute | solution.py:13
  69.8 3.0 %copy-start.3 = (bf16[16,8,16,128]{3,2,1,0:T(8,128)(2,1)S(1)}, bf16[16,8,16,128]{3,2,1,0:T(8,128)(2,1)}, u32[]{:S(2)}) copy-start(bf16[16,8,16,128]{3,2,1,0:T(8,128)(2,1)} %copy.133) | copy-start | bytes 1572868
  69.8 3.0 %copy-start.12 = (f32[16,128,256]{1,2,0:T(8,128)S(1)}, f32[16,128,256]{1,2,0:T(8,128)}, u32[]{:S(2)}) copy-start(f32[16,128,256]{1,2,0:T(8,128)} %get-tuple-element.29) | copy-start | bytes 6291460
  73.3 20.2 %copy-start.2 = (f32[256,16,128]{2,0,1:T(8,128)}, f32[256,16,128]{2,0,1:T(8,128)S(1)}, u32[]{:S(2)}) copy-start(f32[256,16,128]{2,0,1:T(8,128)S(1)} %convolution_bitcast_fusion) | copy-start | bytes 6291460
  82.7 25.4 %collective-permute-start.12 = (f32[32,2048]{1,0:T(8,128)}, f32[32,2048]{1,0:T(8,128)}, u32[]{:S(2)}, u32[]{:S(2)}) collective-permute-start(f32[32,2048]{1,0:T(8,128)} %bitcast.196), channel_id=1, source_target_pairs={{2,0},{4,2},{6,4},{8,6},{10,8},{12,10},{14,12},{16,14},{18,16},{20... | collective-permute-start | bytes 786440 | tf_op jit(solution)/shard_map/ppermute | solution.py:13
  84.0 25.4 %collective-permute-start.14 = (f32[32,2048]{1,0:T(8,128)}, f32[32,2048]{1,0:T(8,128)}, u32[]{:S(2)}, u32[]{:S(2)}) collective-permute-start(f32[32,2048]{1,0:T(8,128)} %bitcast.194), channel_id=1, source_target_pairs={{6,0},{8,2},{10,4},{12,6},{14,8},{16,10},{18,12},{20,14},{22,16},{... | collective-permute-start | bytes 786440 | tf_op jit(solution)/shard_map/ppermute | solution.py:13
  85.3 25.5 %collective-permute-start.15 = (f32[32,2048]{1,0:T(8,128)}, f32[32,2048]{1,0:T(8,128)}, u32[]{:S(2)}, u32[]{:S(2)}) collective-permute-start(f32[32,2048]{1,0:T(8,128)} %bitcast.193), channel_id=1, source_target_pairs={{8,0},{10,2},{12,4},{14,6},{16,8},{18,10},{20,12},{22,14},{24,16},... | collective-permute-start | bytes 786440 | tf_op jit(solution)/shard_map/ppermute | solution.py:13
  86.6 25.6 %collective-permute-start.13 = (f32[32,2048]{1,0:T(8,128)}, f32[32,2048]{1,0:T(8,128)}, u32[]{:S(2)}, u32[]{:S(2)}) collective-permute-start(f32[32,2048]{1,0:T(8,128)} %bitcast.195), channel_id=1, source_target_pairs={{4,0},{6,2},{8,4},{10,6},{12,8},{14,10},{16,12},{18,14},{20,16},{2... | collective-permute-start | bytes 786440 | tf_op jit(solution)/shard_map/ppermute | solution.py:13
  93.5 4.2 %slice-start = ((f32[256,16,128]{2,0,1:T(8,128)}), f32[128,16,128]{2,0,1:T(8,128)S(1)}, s32[]{:S(2)}) async-start(f32[256,16,128]{2,0,1:T(8,128)} %copy-done.2), calls=%async_computation.2 | async-start | bytes 2097152 | tf_op jit(solution)/shard_map/slice | solution.py:66
  106.9 15.3 %collective-permute-start.8 = (f32[32,2048]{1,0:T(8,128)}, f32[32,2048]{1,0:T(8,128)}, u32[]{:S(2)}, u32[]{:S(2)}) collective-permute-start(f32[32,2048]{1,0:T(8,128)} %bitcast.200), channel_id=1, source_target_pairs={{2,0},{4,2},{6,4},{8,6},{10,8},{12,10},{14,12},{16,14},{18,16},{20... | collective-permute-start | bytes 786440 | tf_op jit(solution)/shard_map/ppermute | solution.py:13
  108.2 14.0 %collective-permute-start.10 = (f32[32,2048]{1,0:T(8,128)}, f32[32,2048]{1,0:T(8,128)}, u32[]{:S(2)}, u32[]{:S(2)}) collective-permute-start(f32[32,2048]{1,0:T(8,128)} %bitcast.198), channel_id=1, source_target_pairs={{6,0},{8,2},{10,4},{12,6},{14,8},{16,10},{18,12},{20,14},{22,16},{... | collective-permute-start | bytes 786440 | tf_op jit(solution)/shard_map/ppermute | solution.py:13
  109.5 20.9 %collective-permute-start.11 = (f32[32,2048]{1,0:T(8,128)}, f32[32,2048]{1,0:T(8,128)}, u32[]{:S(2)}, u32[]{:S(2)}) collective-permute-start(f32[32,2048]{1,0:T(8,128)} %bitcast.197), channel_id=1, source_target_pairs={{8,0},{10,2},{12,4},{14,6},{16,8},{18,10},{20,12},{22,14},{24,16},... | collective-permute-start | bytes 786440 | tf_op jit(solution)/shard_map/ppermute | solution.py:13
  110.8 19.6 %collective-permute-start.9 = (f32[32,2048]{1,0:T(8,128)}, f32[32,2048]{1,0:T(8,128)}, u32[]{:S(2)}, u32[]{:S(2)}) collective-permute-start(f32[32,2048]{1,0:T(8,128)} %bitcast.235), channel_id=1, source_target_pairs={{4,0},{6,2},{8,4},{10,6},{12,8},{14,10},{16,12},{18,14},{20,16},{2... | collective-permute-start | bytes 786440 | tf_op jit(solution)/shard_map/ppermute | solution.py:13
  (7 other events, 15.3 us)
Sparse Core Ops, SparseCore 0:
  133.2 62.8 reduce-scatter.1
where the time goes:
time: 213 us; the launch traced here: 212 us
  waiting for transfers between devices  77.1 us (36%)
  local copies, waits for them, and re-layouts  42.1 us (20%)
  starting transfers between devices  38.6 us (18%)
  matrix products  24.5 us (12%)
  between operations  15.1 us (7%)
  blocking collectives  9.4 us (4%)
  other arithmetic  5.59 us (3%)
    reduce_scatter x1, waiting for transfers between devices, local(): lax.psum_scatter(kernel_terms, 'seq', scatter_dimension=0, tiled=True)  59.2 us
    ppermute x16, starting transfers between devices, shifted(): lax.ppermute(value, axis, [(source, source + steps) for source in range(i...  38.5 us
    ppermute x16, waiting for transfers between devices, shifted(): lax.ppermute(value, axis, [(source, source + steps) for source in range(i...  17.8 us
    unnamed x46, local copies, waits for them, and re-layouts  16.6 us
    psum x1, blocking collectives, local(): grad_kernel = lax.psum(partial_sum, 'dp')  9.4 us
    dot_general x1, matrix products, attend_block(): jnp.einsum('hsl,shd->lhd', grad_scores, query_heads, preferred_element_ty...  6.49 us
    dot_general x1, matrix products, attend_block(): jnp.einsum('hsl,lhd->shd', grad_scores, key_heads, preferred_element_type...  5.57 us
    squeeze x4, local copies, waits for them, and re-layouts, local(): slot_keys[offset - 1]  4.77 us
  transfers between devices with their start and end apart: 17, of which 5 were waited for; matrix products, arithmetic and copies ran while one was open for 20% of the time, Pallas kernels for 0%

commit v1 on v0

v1 whole, which is shorter than its diff:
```python
import functools

import jax
import jax.numpy as jnp
from jax import lax
from jax.experimental import pallas as pl
from jax.experimental.pallas import tpu as pltpu
from jax.sharding import PartitionSpec as P

F32 = jnp.float32
BF16 = jnp.bfloat16
TAPS = 4
SLOTS = 4
MASKED = -1e30
VMEM_BYTES = 40 * 2**20


def nt(a, b):
    return lax.dot_general(a, b, (((1,), (1,)), ((), ())), preferred_element_type=F32)


def nn(a, b):
    return lax.dot_general(a, b, (((1,), (0,)), ((), ())), preferred_element_type=F32)


def tn(a, b):
    return lax.dot_general(a, b, (((0,), (0,)), ((), ())), preferred_element_type=F32)


def tap_major(seg, inverse=False):
    slot = seg // TAPS
    spot = lax.broadcasted_iota(jnp.int32, (seg, seg), 1 if inverse else 0)
    token = lax.broadcasted_iota(jnp.int32, (seg, seg), 0 if inverse else 1)
    return (token == TAPS * (spot % slot) + spot // slot).astype(BF16)


def pack_kernel(k_ref, v_ref, w_ref, kp_ref, vp_ref, packed_ref):
    seg, width = k_ref.shape
    feat = w_ref.shape[1]
    slot = seg // TAPS
    order = tap_major(seg)
    rows = []
    for src, dst in ((k_ref, kp_ref), (v_ref, vp_ref)):
        sorted_rows = nn(order, src[...]).astype(BF16)
        dst[...] = sorted_rows
        for h in range(width // feat):
            part = sorted_rows[:, h * feat : (h + 1) * feat]
            rows.append(
                jnp.concatenate([part[t * slot : (t + 1) * slot] for t in range(TAPS)], 1)
            )
    packed = nn(jnp.concatenate(rows, 0), w_ref[...]).astype(BF16)
    packed_ref[...] = packed.reshape(packed_ref.shape)


def own_kernel(q_ref, g_ref, kp_ref, vp_ref, stat_ref, kt_ref, vt_ref):
    seg, width = q_ref.shape
    heads = stat_ref.shape[1]
    feat = width // heads
    slot = seg // TAPS
    scale = feat**-0.5
    spot = lax.broadcasted_iota(jnp.int32, (seg, seg), 0)
    query = lax.broadcasted_iota(jnp.int32, (seg, seg), 1)
    allowed = TAPS * (spot % slot) + spot // slot <= query
    for h in range(heads):
        cols = slice(h * feat, (h + 1) * feat)
        scores = jnp.where(allowed, nt(kp_ref[:, cols], q_ref[:, cols]) * scale, MASKED)
        top = jnp.max(scores, axis=0, keepdims=True)
        raised = jnp.exp(scores - top)
        grad_weights = nt(vp_ref[:, cols], g_ref[:, cols])
        stat_ref[0, h] = top
        stat_ref[1, h] = jnp.sum(raised, axis=0, keepdims=True)
        stat_ref[2, h] = jnp.sum(raised * grad_weights, axis=0, keepdims=True)
    for src, dst in ((kp_ref, kt_ref), (vp_ref, vt_ref)):
        for t in range(TAPS):
            stacked = jnp.concatenate(
                [
                    src[t * slot : (t + 1) * slot, h * feat : (h + 1) * feat]
                    for h in range(heads)
                ],
                0,
            )
            dst[t * feat : (t + 1) * feat, :] = stacked.T


def memory_kernel(
    place_ref, q_ref, g_ref, stat_ref, near_ref, r2_ref, r2s_ref, r4_ref, r4s_ref,
    swap_ref, t2_ref, t4_ref, w_ref, gs_ref, fin_ref,
):
    seg, width = q_ref.shape
    heads = stat_ref.shape[1]
    feat = width // heads
    slot = seg // TAPS
    scale = feat**-0.5
    position, reach = place_ref[0], place_ref[1]
    even = position % 2 == 0
    slot_of = lax.broadcasted_iota(jnp.int32, (SLOTS * slot, seg), 0) // slot + 1
    allowed = slot_of <= jnp.minimum(reach, position)
    for h in range(heads):
        cols = slice(h * feat, (h + 1) * feat)
        memory = []
        for kv in range(2):
            far = r2s_ref[kv, h]
            memory.append(
                jnp.concatenate(
                    [
                        jnp.where(even, far, near_ref[kv, h]),
                        r2_ref[kv, h],
                        jnp.where(even, r4s_ref[kv, h], far),
                        r4_ref[kv, h],
                    ],
                    0,
                )
            )
        q, g = q_ref[:, cols], g_ref[:, cols]
        scores = jnp.where(allowed, nt(memory[0], q) * scale, MASKED)
        own_top = stat_ref[0, h]
        top = jnp.maximum(own_top, jnp.max(scores, axis=0, keepdims=True))
        raised = jnp.exp(scores - top)
        fade = jnp.exp(own_top - top)
        grad_weights = nt(memory[1], g)
        total = stat_ref[1, h] * fade + jnp.sum(raised, axis=0, keepdims=True)
        delta = stat_ref[2, h] * fade + jnp.sum(raised * grad_weights, axis=0, keepdims=True)
        inverse = 1.0 / total
        delta = delta * inverse
        weights = raised * inverse
        weights_low = weights.astype(BF16)
        grad_scores = (weights * (grad_weights - delta) * scale).astype(BF16)
        w_ref[h] = weights_low
        gs_ref[h] = grad_scores
        fin_ref[0, h] = top
        fin_ref[1, h] = inverse
        fin_ref[2, h] = delta
        for kv, terms in enumerate((nn(grad_scores, q), nn(weights_low, g))):
            terms = terms.astype(BF16)
            swap_ref[0, kv, h] = terms[:slot]
            t2_ref[kv, h] = terms[slot : 2 * slot]
            swap_ref[1, kv, h] = terms[2 * slot : 3 * slot]
            t4_ref[kv, h] = terms[3 * slot :]


def output_kernel(
    place_ref, q_ref, g_ref, kp_ref, vp_ref, near_ref, r2_ref, r2s_ref, r4_ref, r4s_ref,
    w_ref, gs_ref, fin_ref, att_ref, gq_ref, ok_ref, ov_ref,
):
    seg, width = q_ref.shape
    heads = fin_ref.shape[1]
    feat = width // heads
    slot = seg // TAPS
    scale = feat**-0.5
    even = place_ref[0] % 2 == 0
    spot = lax.broadcasted_iota(jnp.int32, (seg, seg), 0)
    query = lax.broadcasted_iota(jnp.int32, (seg, seg), 1)
    allowed = TAPS * (spot % slot) + spot // slot <= query
    for h in range(heads):
        cols = slice(h * feat, (h + 1) * feat)
        memory = []
        for kv in range(2):
            far = r2s_ref[kv, h]
            memory.append(
                jnp.concatenate(
                    [
                        jnp.where(even, far, near_ref[kv, h]),
                        r2_ref[kv, h],
                        jnp.where(even, r4s_ref[kv, h], far),
                        r4_ref[kv, h],
                    ],
                    0,
                )
            )
        q, g, k, v = q_ref[:, cols], g_ref[:, cols], kp_ref[:, cols], vp_ref[:, cols]
        scores = jnp.where(allowed, nt(k, q) * scale, MASKED)
        weights = jnp.exp(scores - fin_ref[0, h]) * fin_ref[1, h]
        grad_weights = nt(v, g)
        weights_low = weights.astype(BF16)
        grad_scores = (weights * (grad_weights - fin_ref[2, h]) * scale).astype(BF16)
        ok_ref[:, cols] = nn(grad_scores, q)
        ov_ref[:, cols] = nn(weights_low, g)
        att = tn(weights_low, v) + tn(w_ref[h], memory[1])
        att_ref[:, cols] = att.astype(BF16)
        gq = tn(grad_scores, k) + tn(gs_ref[h], memory[0])
        gq_ref[:, cols] = gq.astype(BF16)


def sum_kernel(place_ref, near_ref, a_ref, b_ref, kt_ref, vt_ref, mg_ref, mine_ref, other_ref):
    count = mine_ref.shape[0] * 2
    even = place_ref[0] % 2 == 0
    summed = a_ref[...].astype(F32) + b_ref[...].astype(F32)
    near = jnp.where(even, near_ref[0].astype(F32), 0.0)
    low = (summed + near).astype(BF16)
    mg_ref[...] = low
    half = low.shape[0] // 2
    terms = nn(kt_ref[...], low[:half]) + nn(vt_ref[...], low[half:])
    rows = terms.shape[0] // count
    bits = count.bit_length() - 1
    for p in range(0, count, 2):
        spot = int(format(p, "b").zfill(bits)[::-1], 2)
        first = terms[p * rows : (p + 1) * rows]
        second = terms[(p + 1) * rows : (p + 2) * rows]
        mine_ref[spot] = jnp.where(even, first, second)
        other_ref[spot] = jnp.where(even, second, first)


def back_kernel(mgk_ref, mgv_ref, w_ref, ok_ref, ov_ref, gk_ref, gv_ref):
    seg, width = ok_ref.shape
    heads, slot, feat = mgk_ref.shape
    restore = tap_major(seg, inverse=True)
    for mg_ref, own_ref, out_ref in ((mgk_ref, ok_ref, gk_ref), (mgv_ref, ov_ref, gv_ref)):
        back = nt(mg_ref[...].reshape(heads * slot, feat), w_ref[...])
        columns = []
        for h in range(heads):
            head = back[h * slot : (h + 1) * slot]
            columns.append(
                jnp.concatenate([head[:, t * feat : (t + 1) * feat] for t in range(TAPS)], 0)
            )
        total = (own_ref[...] + jnp.concatenate(columns, 1)).astype(BF16)
        out_ref[...] = nn(restore, total).astype(BF16)


def call(kernel, out_shape, grid, in_specs, out_specs, flops, moved, exps=0):
    return pl.pallas_call(
        kernel,
        out_shape=out_shape,
        grid=grid,
        in_specs=in_specs,
        out_specs=out_specs,
        compiler_params=pltpu.CompilerParams(vmem_limit_bytes=VMEM_BYTES),
        cost_estimate=pl.CostEstimate(flops=flops, bytes_accessed=moved, transcendentals=exps),
    )


def local(queries, key_vectors, value_vectors, cotangent, compress_kernel, memory_reach):
    q, k, v, g = queries[0], key_vectors[0], value_vectors[0], cotangent[0]
    seg, width = q.shape
    feat = compress_kernel.shape[1]
    heads = width // feat
    slot = seg // TAPS
    count = lax.axis_size("seq")
    books = lax.axis_size("dp")
    position = lax.axis_index("seq")
    place = jnp.stack([position.astype(jnp.int32), memory_reach[0, 0]])

    group = 4
    grid = (heads // group,)
    cols = pl.BlockSpec((seg, group * feat), lambda i: (0, i))
    whole = pl.BlockSpec(compress_kernel.shape, lambda i: (0, 0))
    small = pl.BlockSpec((2, group, slot, feat), lambda i: (0, i, 0, 0))
    pair = pl.BlockSpec((2, 2, group, slot, feat), lambda i: (0, 0, i, 0, 0))
    stats = pl.BlockSpec((3, group, 1, seg), lambda i: (0, i, 0, 0))
    square = pl.BlockSpec((group, SLOTS * slot, seg), lambda i: (i, 0, 0))
    turned = pl.BlockSpec((TAPS * feat, group * slot), lambda i: (0, i))
    scalars = pl.BlockSpec(memory_space=pltpu.SMEM)
    rows_low = jax.ShapeDtypeStruct((seg, width), BF16)
    rows_full = jax.ShapeDtypeStruct((seg, width), F32)
    packed_shape = jax.ShapeDtypeStruct((2, heads, slot, feat), BF16)
    stat_shape = jax.ShapeDtypeStruct((3, heads, 1, seg), F32)
    square_shape = jax.ShapeDtypeStruct((heads, SLOTS * slot, seg), BF16)
    turned_shape = jax.ShapeDtypeStruct((TAPS * feat, heads * slot), BF16)
    row_bytes = 2 * seg * width
    unit = 2 * heads * seg * seg * feat

    kp, vp, packed = call(
        pack_kernel,
        (rows_low, rows_low, packed_shape),
        grid, [cols, cols, whole], (cols, cols, small), 4 * unit, 5 * row_bytes,
    )(k, v, compress_kernel)

    def shift(value, steps):
        return lax.ppermute(value, "seq", [(s, (s + steps) % count) for s in range(count)])

    def trade(value, bit, axis="seq"):
        size = lax.axis_size(axis)
        return lax.ppermute(value, axis, [(s, s ^ bit) for s in range(size)])

    near = lax.ppermute(packed, "seq", [(s, s + 1) for s in range(0, count, 2)])
    r2 = shift(packed, 2)
    r4 = shift(packed, 4)
    r2s = trade(r2, 1)
    r4s = lax.ppermute(r4, "seq", [(s + 1, s) for s in range(0, count, 2)])

    own_stats, kt, vt = call(
        own_kernel,
        (stat_shape, turned_shape, turned_shape),
        grid, [cols] * 4, (stats, turned, turned), 2 * unit, 6 * row_bytes, heads * seg * seg,
    )(q, g, kp, vp)

    swap, t2, t4, w_mem, gs_mem, final = call(
        memory_kernel,
        (
            jax.ShapeDtypeStruct((2, 2, heads, slot, feat), BF16),
            packed_shape, packed_shape, square_shape, square_shape, stat_shape,
        ),
        grid,
        [scalars, cols, cols, stats] + [small] * 5,
        (pair, small, small, square, square, stats),
        4 * unit, 7 * row_bytes, heads * seg * seg,
    )(place, q, g, own_stats, near, r2, r2s, r4, r4s)

    swapped = trade(swap, 1)
    even = position % 2 == 0
    send2 = (t2.astype(F32) + jnp.where(even, swapped[1], swapped[0]).astype(F32)).astype(BF16)
    send4 = (
        t4.astype(F32) + jnp.where(even, jnp.zeros_like(swapped[1]), swapped[1]).astype(F32)
    ).astype(BF16)
    back2 = shift(send2, -2)
    back4 = shift(send4, -4)

    attended, grad_queries, own_keys, own_values = call(
        output_kernel,
        (rows_low, rows_low, rows_full, rows_full),
        grid,
        [scalars] + [cols] * 4 + [small] * 5 + [square, square, stats],
        (cols, cols, cols, cols),
        8 * unit, 15 * row_bytes, heads * seg * seg,
    )(place, q, g, kp, vp, near, r2, r2s, r4, r4s, w_mem, gs_mem, final)

    flat = (2 * heads * slot, feat)
    kernel_rows = compress_kernel.shape[0]
    half_shape = jax.ShapeDtypeStruct((count // 2, kernel_rows // count, feat), F32)
    vmem = pl.BlockSpec(memory_space=pltpu.VMEM)
    memory_grads, mine, other = call(
        sum_kernel,
        (jax.ShapeDtypeStruct(flat, BF16), half_shape, half_shape),
        (1,),
        [
            scalars,
            pl.BlockSpec((1, *flat), lambda i: (0, 0, 0)),
            vmem, vmem, vmem, vmem,
        ],
        (vmem, vmem, vmem),
        unit, 4 * row_bytes,
    )(place, swapped.reshape(2, *flat), back2.reshape(flat), back4.reshape(flat), kt, vt)

    part = mine + trade(other, 1)
    bit = 2
    while bit < count:
        part = part.reshape(2, -1, *part.shape[1:])
        side = (position // bit) % 2
        kept = lax.dynamic_index_in_dim(part, side, 0, False)
        sent = lax.dynamic_index_in_dim(part, 1 - side, 0, False)
        part = kept + trade(sent, bit)
        bit *= 2
    part = part.reshape(kernel_rows // count, feat)
    bit = 1
    while bit < books:
        part = part + trade(part, bit, "dp")
        bit *= 2

    grads = memory_grads.reshape(2, heads, slot, feat)
    head_rows = pl.BlockSpec((group, slot, feat), lambda i: (i, 0, 0))
    grad_keys, grad_values = call(
        back_kernel,
        (rows_low, rows_low),
        grid, [head_rows, head_rows, whole, cols, cols], (cols, cols), 4 * unit, 7 * row_bytes,
    )(grads[0], grads[1], compress_kernel, own_keys, own_values)
    return (attended[None], grad_queries[None], grad_keys[None], grad_values[None], part)


def solution(mesh):
    rows = P("dp", "seq", None)
    return jax.shard_map(
        local,
        mesh=mesh,
        in_specs=(rows, rows, rows, rows, P(), P("dp", "seq")),
        out_specs=(rows, rows, rows, rows, P("seq", None)),
        check_vma=False,
    )
```

time: 213 us -> 86.7 us (0.41)
  waiting for transfers between devices: 77.1 us -> 28.7 us
  local copies, waits for them, and re-layouts: 42.1 us -> 11.5 us
  matrix products: 24.5 us -> 0 us
  Pallas kernels: 0 us -> 21.2 us
  starting transfers between devices: 38.6 us -> 20.3 us
  between operations: 15.1 us -> 1.56 us
  blocking collectives: 9.4 us -> 0 us
  other arithmetic: 5.59 us -> 2.86 us
    reduce_scatter x1 -> x0, waiting for transfers between devices: 59.2 us -> none  [local(): lax.psum_scatter(kernel_terms, 'seq', scatter_dimension=0, tiled=True)]
    pallas_call x0 -> x6, Pallas kernels: none -> 21.2 us  [the longest x1 6.22 us: local(): call(output_kernel, (rows_low, rows_low, rows_full, rows_full), grid, [sc...]
    dot_general x11 -> x0, matrix products: 21 us -> none  [the longest x1 6.49 us: attend_block(): jnp.einsum('hsl,shd->lhd', grad_scores, query_heads, preferred_element_ty...]
    ppermute x16 -> x13, starting transfers between devices: 38.5 us -> 20.3 us  [the longest x4 11.5 us: shift(): lax.ppermute(value, 'seq', [(s, (s + steps) % count) for s in range(count)])]
    ppermute x16 -> x13, waiting for transfers between devices: 17.8 us -> 28.7 us  [the longest x4 19.5 us: shift(): lax.ppermute(value, 'seq', [(s, (s + steps) % count) for s in range(count)])]
    psum x1 -> x0, blocking collectives: 9.4 us -> none  [local(): grad_kernel = lax.psum(partial_sum, 'dp')]
    squeeze x8 -> x3, local copies, waits for them, and re-layouts: 7.65 us -> 0.03 us  [local(): sent = lax.dynamic_index_in_dim(part, 1 - side, 0, False)]
    reshape x4 -> x0, local copies, waits for them, and re-layouts: 6.44 us -> none  [the longest x2 3.76 us: local(): back_values = jnp.einsum('mhf,tef->mthe', packed_grad_values, kernel, pre...]
  transfers between devices with their start and end apart: 17 -> 13, of which waited for: 5 -> 7; matrix products, arithmetic and copies ran while one was open for 20% -> 0% of each run, Pallas kernels for 0% -> 13%
where the time goes in v1:
time: 86.7 us; the launch traced here: 86.2 us
  waiting for transfers between devices  28.7 us (33%)
  Pallas kernels  21.2 us (24%)
  starting transfers between devices  20.3 us (23%)
  local copies, waits for them, and re-layouts  11.5 us (13%)
  other arithmetic  2.86 us (3%)
  between operations  1.56 us (2%)
    ppermute x4, waiting for transfers between devices, shift(): lax.ppermute(value, 'seq', [(s, (s + steps) % count) for s in range(count)])  19.5 us
    ppermute x4, starting transfers between devices, shift(): lax.ppermute(value, 'seq', [(s, (s + steps) % count) for s in range(count)])  11.5 us
    unnamed x50, local copies, waits for them, and re-layouts  11.5 us
    ppermute x7, waiting for transfers between devices, trade(): return lax.ppermute(value, axis, [(s, s ^ bit) for s in range(size)])  9.19 us
    ppermute x7, starting transfers between devices, trade(): return lax.ppermute(value, axis, [(s, s ^ bit) for s in range(size)])  6.24 us
    pallas_call x1, Pallas kernels, local(): call(output_kernel, (rows_low, rows_low, rows_full, rows_full), grid, [sc...  6.22 us
    pallas_call x1, Pallas kernels, local(): call(memory_kernel, (jax.ShapeDtypeStruct((2, 2, heads, slot, feat), BF16...  5.86 us
    pallas_call x1, Pallas kernels, local(): call(back_kernel, (rows_low, rows_low), grid, [head_rows, head_rows, whol...  3.12 us
  transfers between devices with their start and end apart: 13, of which 7 were waited for; matrix products, arithmetic and copies ran while one was open for 0% of the time, Pallas kernels for 13%

profile of v1, /device:TPU:0, one launch (start us, length us, event | category | flops | bytes accessed | tf_op | source)
XLA Modules:
  0.0 86.2 jit_solution(1000313280782102736)
XLA Ops:
  1.5 1.0 %copy-done.16 = bf16[1,128,2048]{2,1,0:T(8,128)(2,1)S(1)} copy-done((bf16[1,128,2048]{2,1,0:T(8,128)(2,1)S(1)}, bf16[1,128,2048]{2,1,0:T(8,128)(2,1)}, u32[]{:S(2)}) %copy-start.16) | copy-done | bytes 524312
  2.6 1.0 %copy-done.17 = bf16[1,128,2048]{2,1,0:T(8,128)(2,1)S(1)} copy-done((bf16[1,128,2048]{2,1,0:T(8,128)(2,1)S(1)}, bf16[1,128,2048]{2,1,0:T(8,128)(2,1)}, u32[]{:S(2)}) %copy-start.17) | copy-done | bytes 524312
  3.6 2.5 %shard_map.101 = (bf16[128,2048]{1,0:T(8,128)(2,1)S(1)}, bf16[128,2048]{1,0:T(8,128)(2,1)S(1)}, bf16[2,16,32,128]{3,2,1,0:T(8,128)(2,1)}) custom-call(bf16[128,2048]{1,0:T(8,128)(2,1)S(1)} %bitcast.43, bf16[128,2048]{1,0:T(8,128)(2,1)S(1)} %bitcast.44, bf16[512,128]{1,0:T(8,128)(2,1)S(1)} %copy-done.14), custom_call_target="tpu_custom_call" | custom-call | flops 268435456 | bytes 2621440 | tf_op jit(solution)/shard_map/pallas_call | solution.py:261
  6.1 2.9 %collective-permute-start.1 = (bf16[2,16,32,128]{3,2,1,0:T(8,128)(2,1)}, bf16[2,16,32,128]{3,2,1,0:T(8,128)(2,1)S(1)}, u32[]{:S(2)}, u32[]{:S(2)}) collective-permute-start(bf16[2,16,32,128]{3,2,1,0:T(8,128)(2,1)} %get-tuple-element.28), channel_id=1, source_target_pairs={{0,4},{2,6},{4,8},{6,10},{8,12},{10,14},{12,16},{14,18},{16,20},{1... | collective-permute-start | bytes 786440 | tf_op jit(solution)/shard_map/ppermute | solution.py:268
  9.1 1.6 %collective-permute-start.3 = (bf16[2,16,32,128]{3,2,1,0:T(8,128)(2,1)}, bf16[2,16,32,128]{3,2,1,0:T(8,128)(2,1)S(1)}, u32[]{:S(2)}, u32[]{:S(2)}) collective-permute-start(bf16[2,16,32,128]{3,2,1,0:T(8,128)(2,1)} %get-tuple-element.28), channel_id=1, source_target_pairs={{0,8},{2,10},{4,12},{6,14},{8,16},{10,18},{12,20},{14,22},{16,24},... | collective-permute-start | bytes 786440 | tf_op jit(solution)/shard_map/ppermute | solution.py:268
  10.6 1.3 %collective-permute-start = (bf16[2,16,32,128]{3,2,1,0:T(8,128)(2,1)}, bf16[2,16,32,128]{3,2,1,0:T(8,128)(2,1)S(1)}, u32[]{:S(2)}, u32[]{:S(2)}) collective-permute-start(bf16[2,16,32,128]{3,2,1,0:T(8,128)(2,1)} %get-tuple-element.28), channel_id=1, source_target_pairs={{0,2},{4,6},{8,10},{12,14},{16,18},{20,22},{24,26},{28,30},{1,3},{... | collective-permute-start | bytes 786440 | tf_op jit(solution)/shard_map/ppermute | solution.py:274
  11.9 7.5 %collective-permute-done.1.r2_ref = bf16[2,16,32,128]{3,2,1,0:T(8,128)(2,1)S(1)} collective-permute-done((bf16[2,16,32,128]{3,2,1,0:T(8,128)(2,1)}, bf16[2,16,32,128]{3,2,1,0:T(8,128)(2,1)S(1)}, u32[]{:S(2)}, u32[]{:S(2)}) %collective-permute-start.1) | collective-permute-done | bytes 262176 | tf_op jit(solution)/shard_map/ppermute | solution.py:268
  19.5 1.3 %collective-permute-start.4 = (bf16[2,16,32,128]{3,2,1,0:T(8,128)(2,1)S(1)}, bf16[2,16,32,128]{3,2,1,0:T(8,128)(2,1)S(1)}, u32[]{:S(2)}, u32[]{:S(2)}) collective-permute-start(bf16[2,16,32,128]{3,2,1,0:T(8,128)(2,1)S(1)} %collective-permute-done.3.r4_ref), channel_id=1, source_target_pairs={{2,0},{6,4},{10,8},{14,12},{18,16},{22,20},{26,24},{30,28},{3,1},{... | collective-permute-start | bytes 786440 | tf_op jit(solution)/shard_map/ppermute | solution.py:278
  21.4 1.9 %shard_map.102 = (f32[3,16,1,128]{3,2,1,0:T(1,128)S(1)}, bf16[512,512]{1,0:T(8,128)(2,1)S(1)}, bf16[512,512]{1,0:T(8,128)(2,1)S(1)}) custom-call(bf16[128,2048]{1,0:T(8,128)(2,1)S(1)} %bitcast.36, bf16[128,2048]{1,0:T(8,128)(2,1)S(1)} %bitcast.39, bf16[128,2048]{1,0:T(8,128)(2,1)S(1)} %get-tuple-element.26.kp_ref, bf16[128,2048]{1,0:T(8,128)(2,1)S(1)} %get-tuple-element.27.vp_ref), custom_call_target="tpu_custom_call" | custom-call | flops 134217728 | bytes 3145728 | tf_op jit(solution)/shard_map/pallas_call | solution.py:280
  24.2 5.9 %shard_map.103 = (bf16[2,2,16,32,128]{4,3,2,1,0:T(8,128)(2,1)}, bf16[2,16,32,128]{3,2,1,0:T(8,128)(2,1)S(1)}, bf16[2,16,32,128]{3,2,1,0:T(8,128)(2,1)S(1)}, bf16...) custom-call(s32[2]{0:T(128)S(1)} %pad_add_fusion.place_ref, ...), custom_call_target="tpu_custom_call" | custom-call | flops 268435456 | bytes 3670016 | tf_op jit(solution)/shard_map/pallas_call | solution.py:286
  33.7 1.1 %collective-permute-start.5 = (bf16[2,2,16,32,128]{4,3,2,1,0:T(8,128)(2,1)}, bf16[2,2,16,32,128]{4,3,2,1,0:T(8,128)(2,1)S(1)}, u32[]{:S(2)}, u32[]{:S(2)}) collective-permute-start(bf16[2,2,16,32,128]{4,3,2,1,0:T(8,128)(2,1)} %get-tuple-element.35), channel_id=1, source_target_pairs={{0,2},{2,0},{4,6},{6,4},{8,10},{10,8},{12,14},{14,12},{16,18},{18,... | collective-permute-start | bytes 1572872 | tf_op jit(solution)/shard_map/ppermute | solution.py:272
  34.8 1.7 %collective-permute-done.5 = bf16[2,2,16,32,128]{4,3,2,1,0:T(8,128)(2,1)S(1)} collective-permute-done((bf16[2,2,16,32,128]{4,3,2,1,0:T(8,128)(2,1)}, bf16[2,2,16,32,128]{4,3,2,1,0:T(8,128)(2,1)S(1)}, u32[]{:S(2)}, u32[]{:S(2)}) %collective-permute-start.5) | collective-permute-done | bytes 524320 | tf_op jit(solution)/shard_map/ppermute | solution.py:272
  36.6 1.3 %fusion = (bf16[2,16,32,128]{3,2,1,0:T(8,128)(2,1)S(1)}, bf16[2,16,32,128]{3,2,1,0:T(8,128)(2,1)S(1)}) fusion(bf16[2,16,32,128]{3,2,1,0:T(8,128)(2,1)} %copy-done.21, pred[]{:T(512)S(6)} %eq.8, bf16[2,2,16,32,128]{4,3,2,1,0:T(8,128)(2,1)S(1)} %collective-permute-done.5, bf16[2,16,32,128]{3,2,1,0:T(8,128)(2,1)} %copy-done.20), kind=kLoop, calls=%fused_computation.1 | loop fusion | flops 1310720 | bytes 1572865 | tf_op jit(solution)/shard_map/convert_element_type | solution.py:303
  37.9 6.6 %collective-permute-start.6 = (bf16[2,16,32,128]{3,2,1,0:T(8,128)(2,1)S(1)}, bf16[2,16,32,128]{3,2,1,0:T(8,128)(2,1)S(1)}, u32[]{:S(2)}, u32[]{:S(2)}) collective-permute-start(bf16[2,16,32,128]{3,2,1,0:T(8,128)(2,1)S(1)} %get-tuple-element.48), channel_id=1, source_target_pairs={{0,28},{2,30},{4,0},{6,2},{8,4},{10,6},{12,8},{14,10},{16,12},{18,... | collective-permute-start | bytes 786440 | tf_op jit(solution)/shard_map/ppermute | solution.py:268
  44.9 6.2 %collective-permute-done.6 = bf16[2,16,32,128]{3,2,1,0:T(8,128)(2,1)S(1)} collective-permute-done((bf16[2,16,32,128]{3,2,1,0:T(8,128)(2,1)S(1)}, bf16[2,16,32,128]{3,2,1,0:T(8,128)(2,1)S(1)}, u32[]{:S(2)}, u32[]{:S(2)}) %collective-permute-start.6) | collective-permute-done | bytes 262176 | tf_op jit(solution)/shard_map/ppermute | solution.py:268
  51.1 5.8 %collective-permute-done.7 = bf16[2,16,32,128]{3,2,1,0:T(8,128)(2,1)S(1)} collective-permute-done((bf16[2,16,32,128]{3,2,1,0:T(8,128)(2,1)S(1)}, bf16[2,16,32,128]{3,2,1,0:T(8,128)(2,1)S(1)}, u32[]{:S(2)}, u32[]{:S(2)}) %collective-permute-start.7) | collective-permute-done | bytes 262176 | tf_op jit(solution)/shard_map/ppermute | solution.py:268
  56.9 1.7 %shard_map.105 = (bf16[1024,128]{1,0:T(8,128)(2,1)S(1)}, f32[8,32,128]{2,1,0:T(8,128)S(1)}, f32[8,32,128]{2,1,0:T(8,128)}) custom-call(s32[2]{0:T(128)S(1)} %pad_add_fusion.place_ref, bf16[2,1024,128]{2,1,0:T(8,128)(2,1)S(1)} %bitcast.42, bf16[1024,128]{1,0:T(8,128)(2,1)S(1)} %bitcast.47, bf16[1024,128]{1,0:T(8,128)(2,1)S(1)} %bitcast.48, ...), custom_call_target="tpu_custom_call" | custom-call | flops 67108864 | bytes 2097152 | tf_op jit(solution)/shard_map/pallas_call | solution.py:320
  59.3 1.6 %collective-permute-done.8 = f32[8,32,128]{2,1,0:T(8,128)S(1)} collective-permute-done((f32[8,32,128]{2,1,0:T(8,128)}, f32[8,32,128]{2,1,0:T(8,128)S(1)}, u32[]{:S(2)}, u32[]{:S(2)}) %collective-permute-start.8) | collective-permute-done | bytes 131104 | tf_op jit(solution)/shard_map/ppermute | solution.py:272
  61.6 4.2 %collective-permute-done.9 = f32[4,32,128]{2,1,0:T(8,128)S(1)} collective-permute-done((f32[4,32,128]{2,1,0:T(8,128)S(1)}, f32[4,32,128]{2,1,0:T(8,128)S(1)}, u32[]{:S(2)}, u32[]{:S(2)}) %collective-permute-start.9) | collective-permute-done | bytes 65568 | tf_op jit(solution)/shard_map/ppermute | solution.py:272
  69.5 6.2 %shard_map.104 = (bf16[128,2048]{1,0:T(8,128)(2,1)}, bf16[128,2048]{1,0:T(8,128)(2,1)}, f32[128,2048]{1,0:T(8,128)S(1)}, f32[128,2048]{1,0:T(8,128)S(1)}) custom-call(s32[2]{0:T(128)S(1)} %pad_add_fusion.place_ref, bf16[128,2048]{1,0:T(8,128)(2,1)S(1)} %bitcast.38, bf16[128,2048]{1,0:T(8,128)(2,1)S(1)} %bitcast.41, ...), custom_call_target="tpu_custom_call" | custom-call | flops 536870912 | bytes 7864320 | tf_op jit(solution)/shard_map/pallas_call | solution.py:307
  75.7 3.5 %collective-permute-start.11 = (f32[1,32,128]{2,1,0:T(8,128)S(1)}, f32[1,32,128]{2,1,0:T(8,128)S(1)}, u32[]{:S(2)}, u32[]{:S(2)}) collective-permute-start(f32[1,32,128]{2,1,0:T(8,128)S(1)} %constant_dynamic-slice_fusion), channel_id=1, source_target_pairs={{0,16},{2,18},{4,20},{6,22},{8,24},{10,26},{12,28},{14,30},{16,0},... | collective-permute-start | bytes 49160 | tf_op jit(solution)/shard_map/ppermute | solution.py:272
  79.3 1.7 %collective-permute-done.11 = f32[1,32,128]{2,1,0:T(8,128)S(1)} collective-permute-done((f32[1,32,128]{2,1,0:T(8,128)S(1)}, f32[1,32,128]{2,1,0:T(8,128)S(1)}, u32[]{:S(2)}, u32[]{:S(2)}) %collective-permute-start.11) | collective-permute-done | bytes 16416 | tf_op jit(solution)/shard_map/ppermute | solution.py:272
  81.0 1.5 %collective-permute-start.12 = (f32[32,128]{1,0:T(8,128)S(1)}, f32[32,128]{1,0:T(8,128)S(1)}, u32[]{:S(2)}, u32[]{:S(2)}) collective-permute-start(f32[32,128]{1,0:T(8,128)S(1)} %add_bitcast_fusion), channel_id=1, source_target_pairs={{0,1},{1,0},{2,3},{3,2},{4,5},{5,4},{6,7},{7,6},{8,9},{9,8},{10,11... | collective-permute-start | bytes 49160 | tf_op jit(solution)/shard_map/ppermute | solution.py:272
  82.5 3.1 %shard_map.106 = (bf16[128,2048]{1,0:T(8,128)(2,1)}, bf16[128,2048]{1,0:T(8,128)(2,1)}) custom-call(bf16[16,32,128]{2,1,0:T(8,128)(2,1)S(1)} %bitcast.46, bf16[16,32,128]{2,1,0:T(8,128)(2,1)S(1)} %bitcast.45, bf16[512,128]{1,0:T(8,128)(2,1)S(1)} %copy-done.15, f32[128,2048]{1,0:T(8,128)S(1)} %get-tuple-element.41.ok_ref, ...), custom_call_target="tpu_custom_call" | custom-call | flops 268435456 | bytes 3670016 | tf_op jit(solution)/shard_map/pallas_call | solution.py:350
  (69 shorter events, 11.5 us)
Async XLA Ops:
  3.6 17.8 %copy-start = (bf16[1,128,2048]{2,1,0:T(8,128)(2,1)S(1)}, bf16[1,128,2048]{2,1,0:T(8,128)(2,1)}, u32[]{:S(2)}) copy-start(bf16[1,128,2048]{2,1,0:T(8,128)(2,1)} %param.6) | copy-start | bytes 1572868
  3.6 17.8 %copy-start.1 = (bf16[1,128,2048]{2,1,0:T(8,128)(2,1)S(1)}, bf16[1,128,2048]{2,1,0:T(8,128)(2,1)}, u32[]{:S(2)}) copy-start(bf16[1,128,2048]{2,1,0:T(8,128)(2,1)} %param.9) | copy-start | bytes 1572868
  6.1 13.3 %collective-permute-start.1 = (bf16[2,16,32,128]{3,2,1,0:T(8,128)(2,1)}, bf16[2,16,32,128]{3,2,1,0:T(8,128)(2,1)S(1)}, u32[]{:S(2)}, u32[]{:S(2)}) collective-permute-start(bf16[2,16,32,128]{3,2,1,0:T(8,128)(2,1)} %get-tuple-element.28), channel_id=1, source_target_pairs={{0,4},{2,6},{4,8},{6,10},{8,12},{10,14},{12,16},{14,18},{16,20},{1... | collective-permute-start | bytes 786440 | tf_op jit(solution)/shard_map/ppermute | solution.py:268
  9.1 10.4 %collective-permute-start.3 = (bf16[2,16,32,128]{3,2,1,0:T(8,128)(2,1)}, bf16[2,16,32,128]{3,2,1,0:T(8,128)(2,1)S(1)}, u32[]{:S(2)}, u32[]{:S(2)}) collective-permute-start(bf16[2,16,32,128]{3,2,1,0:T(8,128)(2,1)} %get-tuple-element.28), channel_id=1, source_target_pairs={{0,8},{2,10},{4,12},{6,14},{8,16},{10,18},{12,20},{14,22},{16,24},... | collective-permute-start | bytes 786440 | tf_op jit(solution)/shard_map/ppermute | solution.py:268
  10.6 13.5 %collective-permute-start = (bf16[2,16,32,128]{3,2,1,0:T(8,128)(2,1)}, bf16[2,16,32,128]{3,2,1,0:T(8,128)(2,1)S(1)}, u32[]{:S(2)}, u32[]{:S(2)}) collective-permute-start(bf16[2,16,32,128]{3,2,1,0:T(8,128)(2,1)} %get-tuple-element.28), channel_id=1, source_target_pairs={{0,2},{4,6},{8,10},{12,14},{16,18},{20,22},{24,26},{28,30},{1,3},{... | collective-permute-start | bytes 786440 | tf_op jit(solution)/shard_map/ppermute | solution.py:274
  19.4 4.7 %collective-permute-start.2 = (bf16[2,16,32,128]{3,2,1,0:T(8,128)(2,1)S(1)}, bf16[2,16,32,128]{3,2,1,0:T(8,128)(2,1)S(1)}, u32[]{:S(2)}, u32[]{:S(2)}) collective-permute-start(bf16[2,16,32,128]{3,2,1,0:T(8,128)(2,1)S(1)} %collective-permute-done.1.r2_ref), channel_id=1, source_target_pairs={{0,2},{2,0},{4,6},{6,4},{8,10},{10,8},{12,14},{14,12},{16,18},{18,... | collective-permute-start | bytes 786440 | tf_op jit(solution)/shard_map/ppermute | solution.py:272
  19.5 4.7 %collective-permute-start.4 = (bf16[2,16,32,128]{3,2,1,0:T(8,128)(2,1)S(1)}, bf16[2,16,32,128]{3,2,1,0:T(8,128)(2,1)S(1)}, u32[]{:S(2)}, u32[]{:S(2)}) collective-permute-start(bf16[2,16,32,128]{3,2,1,0:T(8,128)(2,1)S(1)} %collective-permute-done.3.r4_ref), channel_id=1, source_target_pairs={{2,0},{6,4},{10,8},{14,12},{18,16},{22,20},{26,24},{30,28},{3,1},{... | collective-permute-start | bytes 786440 | tf_op jit(solution)/shard_map/ppermute | solution.py:278
  24.1 6.0 %copy-start.12 = (bf16[512,512]{1,0:T(8,128)(2,1)}, bf16[512,512]{1,0:T(8,128)(2,1)S(1)}, u32[]{:S(2)}) copy-start(bf16[512,512]{1,0:T(8,128)(2,1)S(1)} %get-tuple-element.39.vt_ref) | copy-start | bytes 1572868
  24.2 5.9 %copy-start.2 = (bf16[2,16,32,128]{3,2,1,0:T(8,128)(2,1)}, bf16[2,16,32,128]{3,2,1,0:T(8,128)(2,1)S(1)}, u32[]{:S(2)}) copy-start(bf16[2,16,32,128]{3,2,1,0:T(8,128)(2,1)S(1)} %collective-permute-done.2.r2s_ref) | copy-start | bytes 786436
  24.2 5.9 %copy-start.4 = (bf16[2,16,32,128]{3,2,1,0:T(8,128)(2,1)}, bf16[2,16,32,128]{3,2,1,0:T(8,128)(2,1)S(1)}, u32[]{:S(2)}) copy-start(bf16[2,16,32,128]{3,2,1,0:T(8,128)(2,1)S(1)} %collective-permute-done.4.r4s_ref) | copy-start | bytes 786436
  33.7 2.9 %collective-permute-start.5 = (bf16[2,2,16,32,128]{4,3,2,1,0:T(8,128)(2,1)}, bf16[2,2,16,32,128]{4,3,2,1,0:T(8,128)(2,1)S(1)}, u32[]{:S(2)}, u32[]{:S(2)}) collective-permute-start(bf16[2,2,16,32,128]{4,3,2,1,0:T(8,128)(2,1)} %get-tuple-element.35), channel_id=1, source_target_pairs={{0,2},{2,0},{4,6},{6,4},{8,10},{10,8},{12,14},{14,12},{16,18},{18,... | collective-permute-start | bytes 1572872 | tf_op jit(solution)/shard_map/ppermute | solution.py:272
  36.6 20.3 %copy-start.11 = (bf16[512,512]{1,0:T(8,128)(2,1)S(1)}, bf16[512,512]{1,0:T(8,128)(2,1)}, u32[]{:S(2)}) copy-start(bf16[512,512]{1,0:T(8,128)(2,1)} %copy-done.10) | copy-start | bytes 1572868
  36.6 20.3 %copy-start.13 = (bf16[512,512]{1,0:T(8,128)(2,1)S(1)}, bf16[512,512]{1,0:T(8,128)(2,1)}, u32[]{:S(2)}) copy-start(bf16[512,512]{1,0:T(8,128)(2,1)} %copy-done.12) | copy-start | bytes 1572868
  37.9 13.2 %collective-permute-start.6 = (bf16[2,16,32,128]{3,2,1,0:T(8,128)(2,1)S(1)}, bf16[2,16,32,128]{3,2,1,0:T(8,128)(2,1)S(1)}, u32[]{:S(2)}, u32[]{:S(2)}) collective-permute-start(bf16[2,16,32,128]{3,2,1,0:T(8,128)(2,1)S(1)} %get-tuple-element.48), channel_id=1, source_target_pairs={{0,28},{2,30},{4,0},{6,2},{8,4},{10,6},{12,8},{14,10},{16,12},{18,... | collective-permute-start | bytes 786440 | tf_op jit(solution)/shard_map/ppermute | solution.py:268
  44.4 12.5 %collective-permute-start.7 = (bf16[2,16,32,128]{3,2,1,0:T(8,128)(2,1)S(1)}, bf16[2,16,32,128]{3,2,1,0:T(8,128)(2,1)S(1)}, u32[]{:S(2)}, u32[]{:S(2)}) collective-permute-start(bf16[2,16,32,128]{3,2,1,0:T(8,128)(2,1)S(1)} %get-tuple-element.47), channel_id=1, source_target_pairs={{0,24},{2,26},{4,28},{6,30},{8,0},{10,2},{12,4},{14,6},{16,8},{18,... | collective-permute-start | bytes 786440 | tf_op jit(solution)/shard_map/ppermute | solution.py:268
  59.3 1.6 %collective-permute-start.8 = (f32[8,32,128]{2,1,0:T(8,128)}, f32[8,32,128]{2,1,0:T(8,128)S(1)}, u32[]{:S(2)}, u32[]{:S(2)}) collective-permute-start(f32[8,32,128]{2,1,0:T(8,128)} %get-tuple-element.46), channel_id=1, source_target_pairs={{0,2},{2,0},{4,6},{6,4},{8,10},{10,8},{12,14},{14,12},{16,18},{18,... | collective-permute-start | bytes 393224 | tf_op jit(solution)/shard_map/ppermute | solution.py:272
  60.9 5.9 %copy-start.5 = (bf16[2,16,32,128]{3,2,1,0:T(8,128)(2,1)S(1)}, bf16[2,16,32,128]{3,2,1,0:T(8,128)(2,1)}, u32[]{:S(2)}) copy-start(bf16[2,16,32,128]{3,2,1,0:T(8,128)(2,1)} %copy-done.4) | copy-start | bytes 786436
  60.9 5.9 %copy-start.3 = (bf16[2,16,32,128]{3,2,1,0:T(8,128)(2,1)S(1)}, bf16[2,16,32,128]{3,2,1,0:T(8,128)(2,1)}, u32[]{:S(2)}) copy-start(bf16[2,16,32,128]{3,2,1,0:T(8,128)(2,1)} %copy-done.2) | copy-start | bytes 786436
  61.5 4.3 %collective-permute-start.9 = (f32[4,32,128]{2,1,0:T(8,128)S(1)}, f32[4,32,128]{2,1,0:T(8,128)S(1)}, u32[]{:S(2)}, u32[]{:S(2)}) collective-permute-start(f32[4,32,128]{2,1,0:T(8,128)S(1)} %dynamic-slice_bitcast_fusion), channel_id=1, source_target_pairs={{0,4},{2,6},{4,0},{6,2},{8,12},{10,14},{12,8},{14,10},{16,20},{18,... | collective-permute-start | bytes 196616 | tf_op jit(solution)/shard_map/ppermute | solution.py:272
  66.7 9.0 %collective-permute-start.10 = (f32[2,32,128]{2,1,0:T(8,128)S(1)}, f32[2,32,128]{2,1,0:T(8,128)S(1)}, u32[]{:S(2)}, u32[]{:S(2)}) collective-permute-start(f32[2,32,128]{2,1,0:T(8,128)S(1)} %dynamic-slice_bitcast_fusion.1), channel_id=1, source_target_pairs={{0,8},{2,10},{4,12},{6,14},{8,0},{10,2},{12,4},{14,6},{16,24},{18,... | collective-permute-start | bytes 98312 | tf_op jit(solution)/shard_map/ppermute | solution.py:272
  69.5 9.8 %copy-start.19 = (bf16[1024,128]{1,0:T(8,128)(2,1)S(1)}, bf16[1024,128]{1,0:T(8,128)(2,1)}, u32[]{:S(2)}) copy-start(bf16[1024,128]{1,0:T(8,128)(2,1)} %copy-done.18) | copy-start | bytes 786436
  75.7 5.2 %collective-permute-start.11 = (f32[1,32,128]{2,1,0:T(8,128)S(1)}, f32[1,32,128]{2,1,0:T(8,128)S(1)}, u32[]{:S(2)}, u32[]{:S(2)}) collective-permute-start(f32[1,32,128]{2,1,0:T(8,128)S(1)} %constant_dynamic-slice_fusion), channel_id=1, source_target_pairs={{0,16},{2,18},{4,20},{6,22},{8,24},{10,26},{12,28},{14,30},{16,0},... | collective-permute-start | bytes 49160 | tf_op jit(solution)/shard_map/ppermute | solution.py:272
  79.2 3.2 %copy-start.15 = (bf16[512,128]{1,0:T(8,128)(2,1)S(1)}, bf16[512,128]{1,0:T(8,128)(2,1)}, u32[]{:S(2)}) copy-start(bf16[512,128]{1,0:T(8,128)(2,1)} %w_ref.3) | copy-start | bytes 393220
  81.0 4.6 %collective-permute-start.12 = (f32[32,128]{1,0:T(8,128)S(1)}, f32[32,128]{1,0:T(8,128)S(1)}, u32[]{:S(2)}, u32[]{:S(2)}) collective-permute-start(f32[32,128]{1,0:T(8,128)S(1)} %add_bitcast_fusion), channel_id=1, source_target_pairs={{0,1},{1,0},{2,3},{3,2},{4,5},{5,4},{6,7},{7,6},{8,9},{9,8},{10,11... | collective-permute-start | bytes 49160 | tf_op jit(solution)/shard_map/ppermute | solution.py:272
  (14 other events, 11.6 us)

commit v2 on v1

--- a/solution.py
+++ b/solution.py
@@ -12,7 +12,7 @@
 TAPS = 4
 SLOTS = 4
 MASKED = -1e30
-VMEM_BYTES = 40 * 2**20
+VMEM_BYTES = 60 * 2**20
 
 
 def nt(a, b):
@@ -32,6 +32,34 @@
     spot = lax.broadcasted_iota(jnp.int32, (seg, seg), 1 if inverse else 0)
     token = lax.broadcasted_iota(jnp.int32, (seg, seg), 0 if inverse else 1)
     return (token == TAPS * (spot % slot) + spot // slot).astype(BF16)
+
+
+def staged(heads, first, second, third):
+    pairs = [range(h, min(h + 2, heads)) for h in range(0, heads, 2)]
+    begun, turned = {}, {}
+    for i in range(len(pairs) + 2):
+        if i < len(pairs):
+            for h in pairs[i]:
+                begun[h] = first(h)
+        if i >= 2:
+            for h in pairs[i - 2]:
+                third(h, *turned.pop(h))
+        if 1 <= i <= len(pairs):
+            for h in pairs[i - 1]:
+                turned[h] = second(h, *begun.pop(h))
+
+
+def memory_rows(kv, h, even, near_ref, r2_ref, r2s_ref, r4_ref, r4s_ref):
+    far = r2s_ref[kv, h]
+    return jnp.concatenate(
+        [
+            jnp.where(even, far, near_ref[kv, h]),
+            r2_ref[kv, h],
+            jnp.where(even, r4s_ref[kv, h], far),
+            r4_ref[kv, h],
+        ],
+        0,
+    )
 
 
 def pack_kernel(k_ref, v_ref, w_ref, kp_ref, vp_ref, packed_ref):
@@ -61,15 +89,23 @@
     spot = lax.broadcasted_iota(jnp.int32, (seg, seg), 0)
     query = lax.broadcasted_iota(jnp.int32, (seg, seg), 1)
     allowed = TAPS * (spot % slot) + spot // slot <= query
-    for h in range(heads):
-        cols = slice(h * feat, (h + 1) * feat)
-        scores = jnp.where(allowed, nt(kp_ref[:, cols], q_ref[:, cols]) * scale, MASKED)
+
+    def cols(h):
+        return slice(h * feat, (h + 1) * feat)
+
+    def first(h):
+        return nt(kp_ref[:, cols(h)], q_ref[:, cols(h)]), nt(vp_ref[:, cols(h)], g_ref[:, cols(h)])
+
+    def second(h, scores, grad_weights):
+        scores = jnp.where(allowed, scores * scale, MASKED)
         top = jnp.max(scores, axis=0, keepdims=True)
         raised = jnp.exp(scores - top)
-        grad_weights = nt(vp_ref[:, cols], g_ref[:, cols])
         stat_ref[0, h] = top
         stat_ref[1, h] = jnp.sum(raised, axis=0, keepdims=True)
         stat_ref[2, h] = jnp.sum(raised * grad_weights, axis=0, keepdims=True)
+        return ()
+
+    staged(heads, first, second, lambda h: None)
     for src, dst in ((kp_ref, kt_ref), (vp_ref, vt_ref)):
         for t in range(TAPS):
             stacked = jnp.concatenate(
@@ -91,33 +127,27 @@
     feat = width // heads
     slot = seg // TAPS
     scale = feat**-0.5
-    position, reach = place_ref[0], place_ref[1]
+    position, reach = lax.axis_index("seq"), place_ref[0, 0]
     even = position % 2 == 0
     slot_of = lax.broadcasted_iota(jnp.int32, (SLOTS * slot, seg), 0) // slot + 1
     allowed = slot_of <= jnp.minimum(reach, position)
-    for h in range(heads):
-        cols = slice(h * feat, (h + 1) * feat)
-        memory = []
-        for kv in range(2):
-            far = r2s_ref[kv, h]
-            memory.append(
-                jnp.concatenate(
-                    [
-                        jnp.where(even, far, near_ref[kv, h]),
-                        r2_ref[kv, h],
-                        jnp.where(even, r4s_ref[kv, h], far),
-                        r4_ref[kv, h],
-                    ],
-                    0,
-                )
-            )
-        q, g = q_ref[:, cols], g_ref[:, cols]
-        scores = jnp.where(allowed, nt(memory[0], q) * scale, MASKED)
+    slots = (near_ref, r2_ref, r2s_ref, r4_ref, r4s_ref)
+
+    def cols(h):
+        return slice(h * feat, (h + 1) * feat)
+
+    def first(h):
+        return (
+            nt(memory_rows(0, h, even, *slots), q_ref[:, cols(h)]),
+            nt(memory_rows(1, h, even, *slots), g_ref[:, cols(h)]),
+        )
+
+    def second(h, scores, grad_weights):
+        scores = jnp.where(allowed, scores * scale, MASKED)
         own_top = stat_ref[0, h]
         top = jnp.maximum(own_top, jnp.max(scores, axis=0, keepdims=True))
         raised = jnp.exp(scores - top)
         fade = jnp.exp(own_top - top)
-        grad_weights = nt(memory[1], g)
         total = stat_ref[1, h] * fade + jnp.sum(raised, axis=0, keepdims=True)
         delta = stat_ref[2, h] * fade + jnp.sum(raised * grad_weights, axis=0, keepdims=True)
         inverse = 1.0 / total
@@ -130,12 +160,18 @@
         fin_ref[0, h] = top
         fin_ref[1, h] = inverse
         fin_ref[2, h] = delta
-        for kv, terms in enumerate((nn(grad_scores, q), nn(weights_low, g))):
+        return grad_scores, weights_low
+
+    def third(h, grad_scores, weights_low):
+        pair = (nn(grad_scores, q_ref[:, cols(h)]), nn(weights_low, g_ref[:, cols(h)]))
+        for kv, terms in enumerate(pair):
             terms = terms.astype(BF16)
             swap_ref[0, kv, h] = terms[:slot]
             t2_ref[kv, h] = terms[slot : 2 * slot]
             swap_ref[1, kv, h] = terms[2 * slot : 3 * slot]
             t4_ref[kv, h] = terms[3 * slot :]
+
+    staged(heads, first, second, third)
 
 
 def output_kernel(
@@ -147,43 +183,38 @@
     feat = width // heads
     slot = seg // TAPS
     scale = feat**-0.5
-    even = place_ref[0] % 2 == 0
+    even = lax.axis_index("seq") % 2 == 0
     spot = lax.broadcasted_iota(jnp.int32, (seg, seg), 0)
     query = lax.broadcasted_iota(jnp.int32, (seg, seg), 1)
     allowed = TAPS * (spot % slot) + spot // slot <= query
-    for h in range(heads):
-        cols = slice(h * feat, (h + 1) * feat)
-        memory = []
-        for kv in range(2):
-            far = r2s_ref[kv, h]
-            memory.append(
-                jnp.concatenate(
-                    [
-                        jnp.where(even, far, near_ref[kv, h]),
-                        r2_ref[kv, h],
-                        jnp.where(even, r4s_ref[kv, h], far),
-                        r4_ref[kv, h],
-                    ],
-                    0,
-                )
-            )
-        q, g, k, v = q_ref[:, cols], g_ref[:, cols], kp_ref[:, cols], vp_ref[:, cols]
-        scores = jnp.where(allowed, nt(k, q) * scale, MASKED)
+    slots = (near_ref, r2_ref, r2s_ref, r4_ref, r4s_ref)
+
+    def cols(h):
+        return slice(h * feat, (h + 1) * feat)
+
+    def first(h):
+        return nt(kp_ref[:, cols(h)], q_ref[:, cols(h)]), nt(vp_ref[:, cols(h)], g_ref[:, cols(h)])
+
+    def second(h, scores, grad_weights):
+        scores = jnp.where(allowed, scores * scale, MASKED)
         weights = jnp.exp(scores - fin_ref[0, h]) * fin_ref[1, h]
-        grad_weights = nt(v, g)
-        weights_low = weights.astype(BF16)
         grad_scores = (weights * (grad_weights - fin_ref[2, h]) * scale).astype(BF16)
-        ok_ref[:, cols] = nn(grad_scores, q)
-        ov_ref[:, cols] = nn(weights_low, g)
-        att = tn(weights_low, v) + tn(w_ref[h], memory[1])
-        att_ref[:, cols] = att.astype(BF16)
-        gq = tn(grad_scores, k) + tn(gs_ref[h], memory[0])
-        gq_ref[:, cols] = gq.astype(BF16)
+        return grad_scores, weights.astype(BF16)
+
+    def third(h, grad_scores, weights_low):
+        ok_ref[:, cols(h)] = nn(grad_scores, q_ref[:, cols(h)])
+        ov_ref[:, cols(h)] = nn(weights_low, g_ref[:, cols(h)])
+        att = tn(weights_low, vp_ref[:, cols(h)]) + tn(w_ref[h], memory_rows(1, h, even, *slots))
+        att_ref[:, cols(h)] = att.astype(BF16)
+        gq = tn(grad_scores, kp_ref[:, cols(h)]) + tn(gs_ref[h], memory_rows(0, h, even, *slots))
+        gq_ref[:, cols(h)] = gq.astype(BF16)
+
+    staged(heads, first, second, third)
 
 
 def sum_kernel(place_ref, near_ref, a_ref, b_ref, kt_ref, vt_ref, mg_ref, mine_ref, other_ref):
     count = mine_ref.shape[0] * 2
-    even = place_ref[0] % 2 == 0
+    even = lax.axis_index("seq") % 2 == 0
     summed = a_ref[...].astype(F32) + b_ref[...].astype(F32)
     near = jnp.where(even, near_ref[0].astype(F32), 0.0)
     low = (summed + near).astype(BF16)
@@ -237,9 +268,9 @@
     count = lax.axis_size("seq")
     books = lax.axis_size("dp")
     position = lax.axis_index("seq")
-    place = jnp.stack([position.astype(jnp.int32), memory_reach[0, 0]])
-
-    group = 4
+    place = memory_reach
+
+    group = 8
     grid = (heads // group,)
     cols = pl.BlockSpec((seg, group * feat), lambda i: (0, i))
     whole = pl.BlockSpec(compress_kernel.shape, lambda i: (0, 0))
@@ -274,7 +305,6 @@
     near = lax.ppermute(packed, "seq", [(s, s + 1) for s in range(0, count, 2)])
     r2 = shift(packed, 2)
     r4 = shift(packed, 4)
-    r2s = trade(r2, 1)
     r4s = lax.ppermute(r4, "seq", [(s + 1, s) for s in range(0, count, 2)])
 
     own_stats, kt, vt = call(
@@ -282,6 +312,9 @@
         (stat_shape, turned_shape, turned_shape),
         grid, [cols] * 4, (stats, turned, turned), 2 * unit, 6 * row_bytes, heads * seg * seg,
     )(q, g, kp, vp)
+
+    r2, own_stats, kt, vt = lax.optimization_barrier((r2, own_stats, kt, vt))
+    r2s = trade(r2, 1)
 
     swap, t2, t4, w_mem, gs_mem, final = call(
         memory_kernel,
@@ -313,6 +346,9 @@
         8 * unit, 15 * row_bytes, heads * seg * seg,
     )(place, q, g, kp, vp, near, r2, r2s, r4, r4s, w_mem, gs_mem, final)
 
+    back2, back4, own_keys, own_values = lax.optimization_barrier(
+        (back2, back4, own_keys, own_values)
+    )
     flat = (2 * heads * slot, feat)
     kernel_rows = compress_kernel.shape[0]
     half_shape = jax.ShapeDtypeStruct((count // 2, kernel_rows // count, feat), F32)

time: 86.7 us -> 72 us (0.83)
  local copies, waits for them, and re-layouts: 11.5 us -> 2.16 us
  waiting for transfers between devices: 28.7 us -> 26.4 us
  starting transfers between devices: 20.3 us -> 18.4 us
  Pallas kernels: 21.2 us -> 20.3 us
    unnamed x50 -> x18, local copies, waits for them, and re-layouts: 11.5 us -> 1.42 us
    ppermute x4, waiting for transfers between devices: 19.5 us -> 11.7 us  [shift(): lax.ppermute(value, 'seq', [(s, (s + steps) % count) for s in range(count)])]
    ppermute x7, waiting for transfers between devices: 9.19 us -> 13.2 us  [trade(): return lax.ppermute(value, axis, [(s, s ^ bit) for s in range(size)])]
    pallas_call x1, Pallas kernels: 5.86 us -> 3.85 us  [local(): call(memory_kernel, (jax.ShapeDtypeStruct((2, 2, heads, slot, feat), BF16...]
    ppermute x7, starting transfers between devices: 6.24 us -> 4.29 us  [trade(): return lax.ppermute(value, axis, [(s, s ^ bit) for s in range(size)])]
    pallas_call x1, Pallas kernels: 6.22 us -> 4.69 us  [local(): call(output_kernel, (rows_low, rows_low, rows_full, rows_full), grid, [sc...]
    ppermute x1, waiting for transfers between devices: 0.01 us -> 1.44 us  [local(): r4s = lax.ppermute(r4, 'seq', [(s + 1, s) for s in range(0, count, 2)])]
    pallas_call x1, Pallas kernels: 1.87 us -> 3.16 us  [local(): call(own_kernel, (stat_shape, turned_shape, turned_shape), grid, [cols] *...]
  transfers between devices with their start and end apart: 13 -> 13, of which waited for: 7 -> 9; matrix products, arithmetic and copies ran while one was open for 0% -> 1% of each run, Pallas kernels for 13% -> 16%
where the time goes in v2:
time: 72 us; the launch traced here: 71.7 us
  waiting for transfers between devices  26.4 us (37%)
  Pallas kernels  20.3 us (28%)
  starting transfers between devices  18.4 us (26%)
  other arithmetic  2.95 us (4%)
  local copies, waits for them, and re-layouts  2.16 us (3%)
  between operations  1.53 us (2%)
    ppermute x7, waiting for transfers between devices, trade(): return lax.ppermute(value, axis, [(s, s ^ bit) for s in range(size)])  13.2 us
    ppermute x4, waiting for transfers between devices, shift(): lax.ppermute(value, 'seq', [(s, (s + steps) % count) for s in range(count)])  11.7 us
    ppermute x4, starting transfers between devices, shift(): lax.ppermute(value, 'seq', [(s, (s + steps) % count) for s in range(count)])  11.5 us
    pallas_call x1, Pallas kernels, local(): call(output_kernel, (rows_low, rows_low, rows_full, rows_full), grid, [sc...  4.69 us
    ppermute x7, starting transfers between devices, trade(): return lax.ppermute(value, axis, [(s, s ^ bit) for s in range(size)])  4.29 us
    pallas_call x1, Pallas kernels, local(): call(memory_kernel, (jax.ShapeDtypeStruct((2, 2, heads, slot, feat), BF16...  3.85 us
    pallas_call x1, Pallas kernels, local(): call(back_kernel, (rows_low, rows_low), grid, [head_rows, head_rows, whol...  3.38 us
    pallas_call x1, Pallas kernels, local(): call(own_kernel, (stat_shape, turned_shape, turned_shape), grid, [cols] *...  3.16 us
  transfers between devices with their start and end apart: 13, of which 9 were waited for; matrix products, arithmetic and copies ran while one was open for 1% of the time, Pallas kernels for 16%

profile of v2, /device:TPU:0, one launch (start us, length us, event | category | flops | bytes accessed | tf_op | source)
XLA Modules:
  0.0 71.7 jit_solution(1821818407878360405)
XLA Ops:
  0.6 2.6 %shard_map.101 = (bf16[128,2048]{1,0:T(8,128)(2,1)}, bf16[128,2048]{1,0:T(8,128)(2,1)}, bf16[2,16,32,128]{3,2,1,0:T(8,128)(2,1)}) custom-call(bf16[128,2048]{1,0:T(8,128)(2,1)} %bitcast.42, bf16[128,2048]{1,0:T(8,128)(2,1)} %bitcast.43, bf16[512,128]{1,0:T(8,128)(2,1)} %w_ref.3), custom_call_target="tpu_custom_call" | custom-call | flops 268435456 | bytes 2621440 | tf_op jit(solution)/shard_map/pallas_call | solution.py:292
  3.3 2.9 %collective-permute-start.1 = (bf16[2,16,32,128]{3,2,1,0:T(8,128)(2,1)}, bf16[2,16,32,128]{3,2,1,0:T(8,128)(2,1)S(1)}, u32[]{:S(2)}, u32[]{:S(2)}) collective-permute-start(bf16[2,16,32,128]{3,2,1,0:T(8,128)(2,1)} %get-tuple-element.36), channel_id=1, source_target_pairs={{0,4},{2,6},{4,8},{6,10},{8,12},{10,14},{12,16},{14,18},{16,20},{1... | collective-permute-start | bytes 786440 | tf_op jit(solution)/shard_map/ppermute | solution.py:299
  6.2 1.6 %collective-permute-start.3 = (bf16[2,16,32,128]{3,2,1,0:T(8,128)(2,1)}, bf16[2,16,32,128]{3,2,1,0:T(8,128)(2,1)S(1)}, u32[]{:S(2)}, u32[]{:S(2)}) collective-permute-start(bf16[2,16,32,128]{3,2,1,0:T(8,128)(2,1)} %get-tuple-element.36), channel_id=1, source_target_pairs={{0,8},{2,10},{4,12},{6,14},{8,16},{10,18},{12,20},{14,22},{16,24},... | collective-permute-start | bytes 786440 | tf_op jit(solution)/shard_map/ppermute | solution.py:299
  7.8 1.3 %collective-permute-start = (bf16[2,16,32,128]{3,2,1,0:T(8,128)(2,1)}, bf16[2,16,32,128]{3,2,1,0:T(8,128)(2,1)S(1)}, u32[]{:S(2)}, u32[]{:S(2)}) collective-permute-start(bf16[2,16,32,128]{3,2,1,0:T(8,128)(2,1)} %get-tuple-element.36), channel_id=1, source_target_pairs={{0,2},{4,6},{8,10},{12,14},{16,18},{20,22},{24,26},{28,30},{1,3},{... | collective-permute-start | bytes 786440 | tf_op jit(solution)/shard_map/ppermute | solution.py:305
  9.1 3.2 %shard_map.102 = (f32[3,16,1,128]{3,2,1,0:T(1,128)}, bf16[512,512]{1,0:T(8,128)(2,1)}, bf16[512,512]{1,0:T(8,128)(2,1)}) custom-call(bf16[128,2048]{1,0:T(8,128)(2,1)} %bitcast.33, bf16[128,2048]{1,0:T(8,128)(2,1)} %bitcast.36, bf16[128,2048]{1,0:T(8,128)(2,1)} %get-tuple-element.34.kp_ref, bf16[128,2048]{1,0:T(8,128)(2,1)} %get-tuple-element.35.vp_ref), custom_call_target="tpu_custom_call" | custom-call | flops 134217728 | bytes 3145728 | tf_op jit(solution)/shard_map/pallas_call | solution.py:310
  12.2 4.3 %collective-permute-done.1.r2_ref = bf16[2,16,32,128]{3,2,1,0:T(8,128)(2,1)S(1)} collective-permute-done((bf16[2,16,32,128]{3,2,1,0:T(8,128)(2,1)}, bf16[2,16,32,128]{3,2,1,0:T(8,128)(2,1)S(1)}, u32[]{:S(2)}, u32[]{:S(2)}) %collective-permute-start.1) | collective-permute-done | bytes 262176 | tf_op jit(solution)/shard_map/ppermute | solution.py:299
  16.6 1.3 %collective-permute-start.4 = (bf16[2,16,32,128]{3,2,1,0:T(8,128)(2,1)S(1)}, bf16[2,16,32,128]{3,2,1,0:T(8,128)(2,1)S(1)}, u32[]{:S(2)}, u32[]{:S(2)}) collective-permute-start(bf16[2,16,32,128]{3,2,1,0:T(8,128)(2,1)S(1)} %collective-permute-done.3.r4_ref), channel_id=1, source_target_pairs={{2,0},{6,4},{10,8},{14,12},{18,16},{22,20},{26,24},{30,28},{3,1},{... | collective-permute-start | bytes 786440 | tf_op jit(solution)/shard_map/ppermute | solution.py:308
  18.6 1.4 %collective-permute-done.4.r4s_ref = bf16[2,16,32,128]{3,2,1,0:T(8,128)(2,1)S(1)} collective-permute-done((bf16[2,16,32,128]{3,2,1,0:T(8,128)(2,1)S(1)}, bf16[2,16,32,128]{3,2,1,0:T(8,128)(2,1)S(1)}, u32[]{:S(2)}, u32[]{:S(2)}) %collective-permute-start.4) | collective-permute-done | bytes 262176 | tf_op jit(solution)/shard_map/ppermute | solution.py:308
  20.8 3.9 %shard_map.103 = (bf16[2,2,16,32,128]{4,3,2,1,0:T(8,128)(2,1)}, bf16[2,16,32,128]{3,2,1,0:T(8,128)(2,1)}, bf16[2,16,32,128]{3,2,1,0:T(8,128)(2,1)}, bf16[16,128,...) custom-call(s32[1,1]{1,0:T(1,128)S(6)} %copy.11.place_ref, ...), custom_call_target="tpu_custom_call" | custom-call | flops 268435456 | bytes 3670016 | tf_op jit(solution)/shard_map/pallas_call | solution.py:319
  25.1 1.7 %collective-permute-done.5 = bf16[2,2,16,32,128]{4,3,2,1,0:T(8,128)(2,1)S(1)} collective-permute-done((bf16[2,2,16,32,128]{4,3,2,1,0:T(8,128)(2,1)}, bf16[2,2,16,32,128]{4,3,2,1,0:T(8,128)(2,1)S(1)}, u32[]{:S(2)}, u32[]{:S(2)}) %collective-permute-start.5) | collective-permute-done | bytes 524320 | tf_op jit(solution)/shard_map/ppermute | solution.py:303
  26.9 1.4 %fusion = (bf16[2,16,32,128]{3,2,1,0:T(8,128)(2,1)S(1)}, bf16[2,16,32,128]{3,2,1,0:T(8,128)(2,1)S(1)}) fusion(bf16[2,16,32,128]{3,2,1,0:T(8,128)(2,1)} %get-tuple-element.49, pred[]{:T(512)S(6)} %eq.8, bf16[2,2,16,32,128]{4,3,2,1,0:T(8,128)(2,1)S(1)} %collective-permute-done.5, bf16[2,16,32,128]{3,2,1,0:T(8,128)(2,1)} %get-tuple-element.48), kind=kLoop, calls=%fused_computation.1 | loop fusion | flops 1310720 | bytes 1572865 | tf_op jit(solution)/shard_map/convert_element_type | solution.py:336
  28.3 6.5 %collective-permute-start.6 = (bf16[2,16,32,128]{3,2,1,0:T(8,128)(2,1)S(1)}, bf16[2,16,32,128]{3,2,1,0:T(8,128)(2,1)S(1)}, u32[]{:S(2)}, u32[]{:S(2)}) collective-permute-start(bf16[2,16,32,128]{3,2,1,0:T(8,128)(2,1)S(1)} %get-tuple-element.64), channel_id=1, source_target_pairs={{0,28},{2,30},{4,0},{6,2},{8,4},{10,6},{12,8},{14,10},{16,12},{18,... | collective-permute-start | bytes 786440 | tf_op jit(solution)/shard_map/ppermute | solution.py:299
  35.3 4.7 %shard_map.104 = (bf16[128,2048]{1,0:T(8,128)(2,1)}, bf16[128,2048]{1,0:T(8,128)(2,1)}, f32[128,2048]{1,0:T(8,128)}, f32[128,2048]{1,0:T(8,128)}) custom-call(s32[1,1]{1,0:T(1,128)S(6)} %copy.11.place_ref, bf16[128,2048]{1,0:T(8,128)(2,1)} %bitcast.35, bf16[128,2048]{1,0:T(8,128)(2,1)} %bitcast.38, bf16[128,2048]{1,0:T(8,128)(2,1)} %get-tuple-element.34.kp_ref, ...), custom_call_target="tpu_custom_call" | custom-call | flops 536870912 | bytes 7864320 | tf_op jit(solution)/shard_map/pallas_call | solution.py:340
  40.0 1.5 %collective-permute-done.6 = bf16[2,16,32,128]{3,2,1,0:T(8,128)(2,1)S(1)} collective-permute-done((bf16[2,16,32,128]{3,2,1,0:T(8,128)(2,1)S(1)}, bf16[2,16,32,128]{3,2,1,0:T(8,128)(2,1)S(1)}, u32[]{:S(2)}, u32[]{:S(2)}) %collective-permute-start.6) | collective-permute-done | bytes 262176 | tf_op jit(solution)/shard_map/ppermute | solution.py:299
  41.5 5.8 %collective-permute-done.7 = bf16[2,16,32,128]{3,2,1,0:T(8,128)(2,1)S(1)} collective-permute-done((bf16[2,16,32,128]{3,2,1,0:T(8,128)(2,1)S(1)}, bf16[2,16,32,128]{3,2,1,0:T(8,128)(2,1)S(1)}, u32[]{:S(2)}, u32[]{:S(2)}) %collective-permute-start.7) | collective-permute-done | bytes 262176 | tf_op jit(solution)/shard_map/ppermute | solution.py:299
  48.0 2.6 %shard_map.105 = (bf16[1024,128]{1,0:T(8,128)(2,1)}, f32[8,32,128]{2,1,0:T(8,128)}, f32[8,32,128]{2,1,0:T(8,128)}) custom-call(s32[1,1]{1,0:T(1,128)S(6)} %copy.11.place_ref, bf16[2,1024,128]{2,1,0:T(8,128)(2,1)} %bitcast.39, bf16[1024,128]{1,0:T(8,128)(2,1)} %bitcast.46, bf16[1024,128]{1,0:T(8,128)(2,1)} %bitcast.47, ...), custom_call_target="tpu_custom_call" | custom-call | flops 67108864 | bytes 2097152 | tf_op jit(solution)/shard_map/pallas_call | solution.py:356
  50.6 1.6 %collective-permute-done.8 = f32[8,32,128]{2,1,0:T(8,128)S(1)} collective-permute-done((f32[8,32,128]{2,1,0:T(8,128)}, f32[8,32,128]{2,1,0:T(8,128)S(1)}, u32[]{:S(2)}, u32[]{:S(2)}) %collective-permute-start.8) | collective-permute-done | bytes 131104 | tf_op jit(solution)/shard_map/ppermute | solution.py:303
  52.2 0.9 %add.64 = f32[8,32,128]{2,1,0:T(8,128)S(1)} add(f32[8,32,128]{2,1,0:T(8,128)} %get-tuple-element.61, f32[8,32,128]{2,1,0:T(8,128)S(1)} %collective-permute-done.8) | non-fusion elementwise | flops 32768 | bytes 393216 | tf_op jit(solution)/shard_map/add | solution.py:369
  53.2 4.2 %collective-permute-done.9 = f32[4,32,128]{2,1,0:T(8,128)S(1)} collective-permute-done((f32[4,32,128]{2,1,0:T(8,128)S(1)}, f32[4,32,128]{2,1,0:T(8,128)S(1)}, u32[]{:S(2)}, u32[]{:S(2)}) %collective-permute-start.9) | collective-permute-done | bytes 65568 | tf_op jit(solution)/shard_map/ppermute | solution.py:303
  57.6 3.9 %collective-permute-done.10 = f32[2,32,128]{2,1,0:T(8,128)S(1)} collective-permute-done((f32[2,32,128]{2,1,0:T(8,128)S(1)}, f32[2,32,128]{2,1,0:T(8,128)S(1)}, u32[]{:S(2)}, u32[]{:S(2)}) %collective-permute-start.10) | collective-permute-done | bytes 32800 | tf_op jit(solution)/shard_map/ppermute | solution.py:303
  61.5 2.1 %collective-permute-start.11 = (f32[1,32,128]{2,1,0:T(8,128)S(1)}, f32[1,32,128]{2,1,0:T(8,128)S(1)}, u32[]{:S(2)}, u32[]{:S(2)}) collective-permute-start(f32[1,32,128]{2,1,0:T(8,128)S(1)} %constant_dynamic-slice_fusion), channel_id=1, source_target_pairs={{0,16},{2,18},{4,20},{6,22},{8,24},{10,26},{12,28},{14,30},{16,0},... | collective-permute-start | bytes 49160 | tf_op jit(solution)/shard_map/ppermute | solution.py:303
  64.3 1.9 %collective-permute-done.11 = f32[1,32,128]{2,1,0:T(8,128)S(1)} collective-permute-done((f32[1,32,128]{2,1,0:T(8,128)S(1)}, f32[1,32,128]{2,1,0:T(8,128)S(1)}, u32[]{:S(2)}, u32[]{:S(2)}) %collective-permute-start.11) | collective-permute-done | bytes 16416 | tf_op jit(solution)/shard_map/ppermute | solution.py:303
  66.2 1.5 %collective-permute-start.12 = (f32[32,128]{1,0:T(8,128)S(1)}, f32[32,128]{1,0:T(8,128)S(1)}, u32[]{:S(2)}, u32[]{:S(2)}) collective-permute-start(f32[32,128]{1,0:T(8,128)S(1)} %add_bitcast_fusion), channel_id=1, source_target_pairs={{0,1},{1,0},{2,3},{3,2},{4,5},{5,4},{6,7},{7,6},{8,9},{9,8},{10,11... | collective-permute-start | bytes 49160 | tf_op jit(solution)/shard_map/ppermute | solution.py:303
  67.7 3.4 %shard_map.106 = (bf16[128,2048]{1,0:T(8,128)(2,1)}, bf16[128,2048]{1,0:T(8,128)(2,1)}) custom-call(bf16[16,32,128]{2,1,0:T(8,128)(2,1)} %bitcast.45, bf16[16,32,128]{2,1,0:T(8,128)(2,1)} %bitcast.44, bf16[512,128]{1,0:T(8,128)(2,1)} %w_ref.3, f32[128,2048]{1,0:T(8,128)} %get-tuple-element.57.ok_ref, f32[128,2048]{1,0:T(8,128)} %get-tuple-element.58.ov_ref), custom_call_target="tpu_custom_call" | custom-call | flops 268435456 | bytes 3670016 | tf_op jit(solution)/shard_map/pallas_call | solution.py:386
  (36 shorter events, 3.9 us)
Async XLA Ops:
  3.3 13.3 %collective-permute-start.1 = (bf16[2,16,32,128]{3,2,1,0:T(8,128)(2,1)}, bf16[2,16,32,128]{3,2,1,0:T(8,128)(2,1)S(1)}, u32[]{:S(2)}, u32[]{:S(2)}) collective-permute-start(bf16[2,16,32,128]{3,2,1,0:T(8,128)(2,1)} %get-tuple-element.36), channel_id=1, source_target_pairs={{0,4},{2,6},{4,8},{6,10},{8,12},{10,14},{12,16},{14,18},{16,20},{1... | collective-permute-start | bytes 786440 | tf_op jit(solution)/shard_map/ppermute | solution.py:299
  6.2 10.4 %collective-permute-start.3 = (bf16[2,16,32,128]{3,2,1,0:T(8,128)(2,1)}, bf16[2,16,32,128]{3,2,1,0:T(8,128)(2,1)S(1)}, u32[]{:S(2)}, u32[]{:S(2)}) collective-permute-start(bf16[2,16,32,128]{3,2,1,0:T(8,128)(2,1)} %get-tuple-element.36), channel_id=1, source_target_pairs={{0,8},{2,10},{4,12},{6,14},{8,16},{10,18},{12,20},{14,22},{16,24},... | collective-permute-start | bytes 786440 | tf_op jit(solution)/shard_map/ppermute | solution.py:299
  7.8 10.8 %collective-permute-start = (bf16[2,16,32,128]{3,2,1,0:T(8,128)(2,1)}, bf16[2,16,32,128]{3,2,1,0:T(8,128)(2,1)S(1)}, u32[]{:S(2)}, u32[]{:S(2)}) collective-permute-start(bf16[2,16,32,128]{3,2,1,0:T(8,128)(2,1)} %get-tuple-element.36), channel_id=1, source_target_pairs={{0,2},{4,6},{8,10},{12,14},{16,18},{20,22},{24,26},{28,30},{1,3},{... | collective-permute-start | bytes 786440 | tf_op jit(solution)/shard_map/ppermute | solution.py:305
  16.6 3.5 %copy-start.1 = (bf16[2,16,32,128]{3,2,1,0:T(8,128)(2,1)}, bf16[2,16,32,128]{3,2,1,0:T(8,128)(2,1)S(1)}, u32[]{:S(2)}) copy-start(bf16[2,16,32,128]{3,2,1,0:T(8,128)(2,1)S(1)} %collective-permute-done.1.r2_ref) | copy-start | bytes 786436
  16.6 2.0 %collective-permute-start.2 = (bf16[2,16,32,128]{3,2,1,0:T(8,128)(2,1)S(1)}, bf16[2,16,32,128]{3,2,1,0:T(8,128)(2,1)S(1)}, u32[]{:S(2)}, u32[]{:S(2)}) collective-permute-start(bf16[2,16,32,128]{3,2,1,0:T(8,128)(2,1)S(1)} %collective-permute-done.1.r2_ref), channel_id=1, source_target_pairs={{0,2},{2,0},{4,6},{6,4},{8,10},{10,8},{12,14},{14,12},{16,18},{18,... | collective-permute-start | bytes 786440 | tf_op jit(solution)/shard_map/ppermute | solution.py:303
  16.6 3.4 %copy-start.2 = (bf16[2,16,32,128]{3,2,1,0:T(8,128)(2,1)}, bf16[2,16,32,128]{3,2,1,0:T(8,128)(2,1)S(1)}, u32[]{:S(2)}) copy-start(bf16[2,16,32,128]{3,2,1,0:T(8,128)(2,1)S(1)} %collective-permute-done.3.r4_ref) | copy-start | bytes 786436
  16.6 3.4 %collective-permute-start.4 = (bf16[2,16,32,128]{3,2,1,0:T(8,128)(2,1)S(1)}, bf16[2,16,32,128]{3,2,1,0:T(8,128)(2,1)S(1)}, u32[]{:S(2)}, u32[]{:S(2)}) collective-permute-start(bf16[2,16,32,128]{3,2,1,0:T(8,128)(2,1)S(1)} %collective-permute-done.3.r4_ref), channel_id=1, source_target_pairs={{2,0},{6,4},{10,8},{14,12},{18,16},{22,20},{26,24},{30,28},{3,1},{... | collective-permute-start | bytes 786440 | tf_op jit(solution)/shard_map/ppermute | solution.py:308
  18.6 1.5 %copy-start.3 = (bf16[2,16,32,128]{3,2,1,0:T(8,128)(2,1)}, bf16[2,16,32,128]{3,2,1,0:T(8,128)(2,1)S(1)}, u32[]{:S(2)}) copy-start(bf16[2,16,32,128]{3,2,1,0:T(8,128)(2,1)S(1)} %collective-permute-done.near_ref) | copy-start | bytes 786436
  18.6 1.5 %copy-start.4 = (bf16[2,16,32,128]{3,2,1,0:T(8,128)(2,1)}, bf16[2,16,32,128]{3,2,1,0:T(8,128)(2,1)S(1)}, u32[]{:S(2)}) copy-start(bf16[2,16,32,128]{3,2,1,0:T(8,128)(2,1)S(1)} %collective-permute-done.2.r2s_ref) | copy-start | bytes 786436
  20.1 0.7 copy-start.5
  24.6 2.2 %collective-permute-start.5 = (bf16[2,2,16,32,128]{4,3,2,1,0:T(8,128)(2,1)}, bf16[2,2,16,32,128]{4,3,2,1,0:T(8,128)(2,1)S(1)}, u32[]{:S(2)}, u32[]{:S(2)}) collective-permute-start(bf16[2,2,16,32,128]{4,3,2,1,0:T(8,128)(2,1)} %get-tuple-element.47), channel_id=1, source_target_pairs={{0,2},{2,0},{4,6},{6,4},{8,10},{10,8},{12,14},{14,12},{16,18},{18,... | collective-permute-start | bytes 1572872 | tf_op jit(solution)/shard_map/ppermute | solution.py:303
  26.9 1.4 %copy-start = (bf16[2,2,16,32,128]{4,3,2,1,0:T(8,128)(2,1)}, bf16[2,2,16,32,128]{4,3,2,1,0:T(8,128)(2,1)S(1)}, u32[]{:S(2)}) copy-start(bf16[2,2,16,32,128]{4,3,2,1,0:T(8,128)(2,1)S(1)} %collective-permute-done.5) | copy-start | bytes 1572868
  28.3 13.2 %collective-permute-start.6 = (bf16[2,16,32,128]{3,2,1,0:T(8,128)(2,1)S(1)}, bf16[2,16,32,128]{3,2,1,0:T(8,128)(2,1)S(1)}, u32[]{:S(2)}, u32[]{:S(2)}) collective-permute-start(bf16[2,16,32,128]{3,2,1,0:T(8,128)(2,1)S(1)} %get-tuple-element.64), channel_id=1, source_target_pairs={{0,28},{2,30},{4,0},{6,2},{8,4},{10,6},{12,8},{14,10},{16,12},{18,... | collective-permute-start | bytes 786440 | tf_op jit(solution)/shard_map/ppermute | solution.py:299
  34.8 12.5 %collective-permute-start.7 = (bf16[2,16,32,128]{3,2,1,0:T(8,128)(2,1)S(1)}, bf16[2,16,32,128]{3,2,1,0:T(8,128)(2,1)S(1)}, u32[]{:S(2)}, u32[]{:S(2)}) collective-permute-start(bf16[2,16,32,128]{3,2,1,0:T(8,128)(2,1)S(1)} %get-tuple-element.63), channel_id=1, source_target_pairs={{0,24},{2,26},{4,28},{6,30},{8,0},{10,2},{12,4},{14,6},{16,8},{18,... | collective-permute-start | bytes 786440 | tf_op jit(solution)/shard_map/ppermute | solution.py:299
  41.5 5.8 %copy-start.6 = (bf16[2,16,32,128]{3,2,1,0:T(8,128)(2,1)}, bf16[2,16,32,128]{3,2,1,0:T(8,128)(2,1)S(1)}, u32[]{:S(2)}) copy-start(bf16[2,16,32,128]{3,2,1,0:T(8,128)(2,1)S(1)} %collective-permute-done.6) | copy-start | bytes 786436
  47.3 0.7 copy-start.7
  50.6 1.6 %collective-permute-start.8 = (f32[8,32,128]{2,1,0:T(8,128)}, f32[8,32,128]{2,1,0:T(8,128)S(1)}, u32[]{:S(2)}, u32[]{:S(2)}) collective-permute-start(f32[8,32,128]{2,1,0:T(8,128)} %get-tuple-element.62), channel_id=1, source_target_pairs={{0,2},{2,0},{4,6},{6,4},{8,10},{10,8},{12,14},{14,12},{16,18},{18,... | collective-permute-start | bytes 393224 | tf_op jit(solution)/shard_map/ppermute | solution.py:303
  53.1 10.5 %copy-start.8 = (bf16[1024,128]{1,0:T(8,128)(2,1)S(1)}, bf16[1024,128]{1,0:T(8,128)(2,1)}, u32[]{:S(2)}) copy-start(bf16[1024,128]{1,0:T(8,128)(2,1)} %get-tuple-element.56) | copy-start | bytes 786436
  53.1 4.3 %collective-permute-start.9 = (f32[4,32,128]{2,1,0:T(8,128)S(1)}, f32[4,32,128]{2,1,0:T(8,128)S(1)}, u32[]{:S(2)}, u32[]{:S(2)}) collective-permute-start(f32[4,32,128]{2,1,0:T(8,128)S(1)} %dynamic-slice_bitcast_fusion), channel_id=1, source_target_pairs={{0,4},{2,6},{4,0},{6,2},{8,12},{10,14},{12,8},{14,10},{16,20},{18,... | collective-permute-start | bytes 196616 | tf_op jit(solution)/shard_map/ppermute | solution.py:303
  57.5 4.0 %collective-permute-start.10 = (f32[2,32,128]{2,1,0:T(8,128)S(1)}, f32[2,32,128]{2,1,0:T(8,128)S(1)}, u32[]{:S(2)}, u32[]{:S(2)}) collective-permute-start(f32[2,32,128]{2,1,0:T(8,128)S(1)} %dynamic-slice_bitcast_fusion.1), channel_id=1, source_target_pairs={{0,8},{2,10},{4,12},{6,14},{8,0},{10,2},{12,4},{14,6},{16,24},{18,... | collective-permute-start | bytes 98312 | tf_op jit(solution)/shard_map/ppermute | solution.py:303
  61.5 4.7 %collective-permute-start.11 = (f32[1,32,128]{2,1,0:T(8,128)S(1)}, f32[1,32,128]{2,1,0:T(8,128)S(1)}, u32[]{:S(2)}, u32[]{:S(2)}) collective-permute-start(f32[1,32,128]{2,1,0:T(8,128)S(1)} %constant_dynamic-slice_fusion), channel_id=1, source_target_pairs={{0,16},{2,18},{4,20},{6,22},{8,24},{10,26},{12,28},{14,30},{16,0},... | collective-permute-start | bytes 49160 | tf_op jit(solution)/shard_map/ppermute | solution.py:303
  66.2 4.9 %collective-permute-start.12 = (f32[32,128]{1,0:T(8,128)S(1)}, f32[32,128]{1,0:T(8,128)S(1)}, u32[]{:S(2)}, u32[]{:S(2)}) collective-permute-start(f32[32,128]{1,0:T(8,128)S(1)} %add_bitcast_fusion), channel_id=1, source_target_pairs={{0,1},{1,0},{2,3},{3,2},{4,5},{5,4},{6,7},{7,6},{8,9},{9,8},{10,11... | collective-permute-start | bytes 49160 | tf_op jit(solution)/shard_map/ppermute | solution.py:303

commit v3 on v2

v3 whole, which is shorter than its diff:
```python
import jax
import jax.numpy as jnp
from jax import lax
from jax.experimental import pallas as pl
from jax.experimental.pallas import tpu as pltpu
from jax.sharding import PartitionSpec as P

F32 = jnp.float32
BF16 = jnp.bfloat16
TAPS = 4
MASKED = -1e30
VMEM_BYTES = 24 * 2**20
PIECES = 1
BLOCKS = 5


def nt(a, b):
    return lax.dot_general(a, b, (((1,), (1,)), ((), ())), preferred_element_type=F32)


def nn(a, b):
    return lax.dot_general(a, b, (((1,), (0,)), ((), ())), preferred_element_type=F32)


def tn(a, b):
    return lax.dot_general(a, b, (((0,), (0,)), ((), ())), preferred_element_type=F32)


def tap_major(seg, inverse=False):
    slot = seg // TAPS
    spot = lax.broadcasted_iota(jnp.int32, (seg, seg), 1 if inverse else 0)
    token = lax.broadcasted_iota(jnp.int32, (seg, seg), 0 if inverse else 1)
    return (token == TAPS * (spot % slot) + spot // slot).astype(BF16)


def causal(seg):
    slot = seg // TAPS
    spot = lax.broadcasted_iota(jnp.int32, (seg, seg), 0)
    query = lax.broadcasted_iota(jnp.int32, (seg, seg), 1)
    return TAPS * (spot % slot) + spot // slot <= query


def head(h, feat):
    return slice(h * feat, (h + 1) * feat)


def staged(items, first, second, third, size=2):
    groups = [items[i : i + size] for i in range(0, len(items), size)]
    begun, turned = {}, {}
    for i in range(len(groups) + 2):
        if i < len(groups):
            for item in groups[i]:
                begun[item] = first(item)
        if i >= 2:
            for item in groups[i - 2]:
                third(item, *turned.pop(item))
        if 1 <= i <= len(groups):
            for item in groups[i - 1]:
                turned[item] = second(item, *begun.pop(item))


def tap_rows(rows, heads, feat):
    slot = rows.shape[0] // TAPS
    return jnp.concatenate(
        [
            jnp.concatenate(
                [rows[t * slot : (t + 1) * slot, head(h, feat)] for t in range(TAPS)], 1
            )
            for h in range(heads)
        ],
        0,
    )


def pack_kernel(reach_ref, k_hbm, v_hbm, q_hbm, g_hbm, w_hbm, *refs):
    *packed_refs, give_ref, rows_ref, w_ref, sems = refs
    seg, width = k_hbm.shape
    feat = w_hbm.shape[1]
    heads = width // feat
    slot = seg // TAPS
    share = heads // 2 // len(packed_refs)
    order = tap_major(seg)
    parts = [
        (half, i, kv)
        for half in range(2)
        for i in range(len(packed_refs))
        for kv in range(2)
    ]
    copies = []
    for n, (half, i, kv) in enumerate(parts):
        cols = pl.ds((half * len(packed_refs) + i) * share * feat, share * feat)
        copies.append(
            pltpu.make_async_copy(
                (k_hbm, v_hbm)[kv].at[:, cols], rows_ref.at[kv, :, cols], sems.at[n]
            )
        )
    copies.append(pltpu.make_async_copy(w_hbm, w_ref, sems.at[len(parts)]))
    for n in (0, 1, len(parts), *range(2, len(parts))):
        copies[n].start()
    start = pl.multiple_of((1 - lax.axis_index("seq") % 2) * (width // 2), width // 2)
    given = [
        pltpu.make_async_copy(
            src.at[:, pl.ds(start, width // 2)],
            give_ref.at[pl.ds(i * seg, seg)],
            sems.at[len(parts) + 1 + i],
        )
        for i, src in enumerate((k_hbm, v_hbm, q_hbm, g_hbm))
    ]
    for copy in given:
        copy.start()
    tail = (give_ref.shape[0] - 4 * seg, give_ref.shape[1])
    reach = jnp.full(tail, reach_ref[0, 0], jnp.int32)
    give_ref[4 * seg :] = reach.astype(F32).astype(BF16)
    for n, (half, i, kv) in enumerate(parts):
        copies[n].wait()
        begin = (half * len(packed_refs) + i) * share * feat
        rows = nn(order, rows_ref[kv, :, begin : begin + share * feat]).astype(BF16)
        if n == 0:
            copies[-1].wait()
        packed = nn(tap_rows(rows, share, feat), w_ref[...]).astype(BF16)
        packed_refs[i][kv, half] = packed.reshape(share, slot, feat)
    for copy in given:
        copy.wait()


def own_kernel(
    reach_ref, k_ref, v_ref, q_ref, g_ref, got_ref, w_ref,
    kv_ref, near_ref, stat_ref, kt_ref, vt_ref, bias_ref,
):
    seg, width = q_ref.shape
    feat = w_ref.shape[1]
    heads = width // feat
    slot = seg // TAPS
    scale = feat**-0.5
    mine = lax.axis_index("seq")
    partner = mine + 1 - 2 * (mine % 2)
    even = mine % 2 == 0
    sources = (mine - mine % 2, mine - 2, partner - 2, mine - 4, partner - 4)
    reach = jnp.full((slot, seg), reach_ref[0, 0], jnp.int32).astype(F32)
    reach_s = jnp.broadcast_to(got_ref[4 * seg : 4 * seg + 1, :seg].astype(F32), (slot, seg))
    for b, source in enumerate(sources):
        for u, (reader, limit) in enumerate(((mine, reach), (partner, reach_s))):
            steps = reader - source
            near_enough = (steps >= 1) & (steps <= 4) & (source >= 0)
            wanted = jnp.full((slot, seg), jnp.where(near_enough, steps, 9), jnp.int32)
            bias_ref[b * slot : (b + 1) * slot, u * seg : (u + 1) * seg] = jnp.where(
                wanted.astype(F32) <= limit, 0.0, MASKED
            )
    allowed = causal(seg)
    order = tap_major(seg)
    for kv, src in enumerate((k_ref, v_ref)):
        kv_ref[kv, 0] = nn(order, src[...]).astype(BF16)
        kv_ref[kv, 1] = nn(order, got_ref[kv * seg : (kv + 1) * seg]).astype(BF16)
    queries = (q_ref, got_ref.at[2 * seg : 3 * seg])
    grads = (g_ref, got_ref.at[3 * seg : 4 * seg])

    def first(item):
        h, u = item
        cols = head(h, feat)
        return (
            nt(kv_ref[0, u, :, cols], queries[u][:, cols]),
            nt(kv_ref[1, u, :, cols], grads[u][:, cols]),
        )

    def second(item, scores, grad_weights):
        h, u = item
        scores = jnp.where(allowed, scores * scale, MASKED)
        top = jnp.max(scores, axis=0, keepdims=True)
        raised = jnp.exp(scores - top)
        side = slice(u * seg, (u + 1) * seg)
        stat_ref[0, h, :, side] = top
        stat_ref[1, h, :, side] = jnp.sum(raised, axis=0, keepdims=True)
        stat_ref[2, h, :, side] = jnp.sum(raised * grad_weights, axis=0, keepdims=True)
        return ()

    staged([(h, u) for h in range(heads) for u in range(2)], first, second, lambda item: None, 4)
    rows = [
        tap_rows(jnp.where(even, kv_ref[kv, 0], kv_ref[kv, 1]), heads, feat) for kv in range(2)
    ]
    near = nn(jnp.concatenate(rows, 0), w_ref[...]).astype(BF16)
    near_ref[...] = near.reshape(near_ref.shape)
    for kv, dst in enumerate((kt_ref, vt_ref)):
        for u in range(2):
            lanes = slice(u * heads * slot, (u + 1) * heads * slot)
            for t in range(TAPS):
                part = kv_ref[kv, u, t * slot : (t + 1) * slot, :]
                stacked = jnp.concatenate([part[:, head(h, feat)] for h in range(heads)], 0)
                dst[t * feat : (t + 1) * feat, lanes] = stacked.T


def memory_rows(kv, h, slots):
    near_ref, *far_refs = slots
    return jnp.concatenate([near_ref[kv, h]] + [ref[kv, 0, h] for ref in far_refs], 0)


def memory_kernel(
    bias_ref, q_ref, qs_ref, g_ref, gs_ref, stat_ref,
    near_ref, r2_ref, r2s_ref, r4_ref, r4s_ref,
    t0_ref, t2_ref, t4_ref, w_ref, d_ref, fin_ref,
):
    seg, width = q_ref.shape
    heads = stat_ref.shape[1]
    feat = width // heads
    slot = seg // TAPS
    scale = feat**-0.5
    slots = (near_ref, r2_ref, r2s_ref, r4_ref, r4s_ref)

    def both(a_ref, b_ref, h):
        return jnp.concatenate([a_ref[:, head(h, feat)], b_ref[:, head(h, feat)]], 0)

    def first(h):
        return (
            nt(memory_rows(0, h, slots), both(q_ref, qs_ref, h)),
            nt(memory_rows(1, h, slots), both(g_ref, gs_ref, h)),
        )

    def second(h, scores, grad_weights):
        bias = bias_ref[...]
        scores = jnp.where(bias < 0.0, MASKED, scores * scale)
        own_top = stat_ref[0, h]
        top = jnp.maximum(own_top, jnp.max(scores, axis=0, keepdims=True))
        raised = jnp.exp(scores - top)
        fade = jnp.exp(own_top - top)
        total = stat_ref[1, h] * fade + jnp.sum(raised, axis=0, keepdims=True)
        delta = stat_ref[2, h] * fade + jnp.sum(raised * grad_weights, axis=0, keepdims=True)
        inverse = 1.0 / total
        delta = delta * inverse
        weights = raised * inverse
        weights_low = weights.astype(BF16)
        grad_scores = (weights * (grad_weights - delta) * scale).astype(BF16)
        w_ref[h] = weights_low
        d_ref[h] = grad_scores
        fin_ref[0, h] = top
        fin_ref[1, h] = inverse
        fin_ref[2, h] = delta
        return grad_scores, weights_low

    def third(h, grad_scores, weights_low):
        pair = (nn(grad_scores, both(q_ref, qs_ref, h)), nn(weights_low, both(g_ref, gs_ref, h)))
        for kv, terms in enumerate(pair):
            t0_ref[kv, h] = terms[:slot]
            terms = terms.astype(BF16)
            for i, (ref, u) in enumerate(((t2_ref, 0), (t2_ref, 1), (t4_ref, 0), (t4_ref, 1))):
                ref[u, kv, h] = terms[(i + 1) * slot : (i + 2) * slot]

    staged(list(range(heads)), first, second, third)


def output_kernel(*refs):
    q_ref, qs_ref, g_ref, gs_ref, kv_ref, near_ref = refs[:6]
    count = (len(refs) - 6 - 4) // 7
    pieces = [refs[6 + 7 * i : 13 + 7 * i] for i in range(count)]
    att_ref, gq_ref, give_ref, terms_ref = refs[-4:]
    seg, width = q_ref.shape
    feat = near_ref.shape[3]
    heads = width // feat
    share = heads // count
    scale = feat**-0.5
    allowed = causal(seg)
    queries, grads = (q_ref, qs_ref), (g_ref, gs_ref)

    def first(item):
        h, u = item
        cols = head(h, feat)
        return (
            nt(kv_ref[0, u, :, cols], queries[u][:, cols]),
            nt(kv_ref[1, u, :, cols], grads[u][:, cols]),
        )

    def second(item, scores, grad_weights):
        h, u = item
        fin_ref = pieces[h // share][6]
        side = slice(u * seg, (u + 1) * seg)
        top, inverse, delta = (fin_ref[i, h % share, :, side] for i in range(3))
        scores = jnp.where(allowed, scores * scale, MASKED)
        weights = jnp.exp(scores - top) * inverse
        grad_scores = (weights * (grad_weights - delta) * scale).astype(BF16)
        return grad_scores, weights.astype(BF16)

    def third(item, grad_scores, weights_low):
        h, u = item
        cols = head(h, feat)
        side = slice(u * seg, (u + 1) * seg)
        *far, w_ref, d_ref, _ = pieces[h // share]
        terms_ref[0, u, :, cols] = nn(grad_scores, queries[u][:, cols])
        terms_ref[1, u, :, cols] = nn(weights_low, grads[u][:, cols])

        def whole(kv, own, memory):
            rows = [near_ref[kv, h]] + [ref[kv, 0, h % share] for ref in far]
            return tn(own, kv_ref[kv, u, :, cols]) + tn(memory, jnp.concatenate(rows, 0))

        att = whole(1, weights_low, w_ref[h % share, :, side]).astype(BF16)
        gq = whole(0, grad_scores, d_ref[h % share, :, side]).astype(BF16)
        if u == 0:
            att_ref[:, cols] = att
            gq_ref[:, cols] = gq
        else:
            give_ref[0, :, cols] = att
            give_ref[1, :, cols] = gq

    staged([(h, u) for h in range(heads) for u in range(2)], first, second, third, 4)


def sum_kernel(kt_ref, vt_ref, *refs):
    mg_ref, mine_ref, other_ref = refs[-3:]
    pieces = [refs[i : i + 3] for i in range(0, len(refs) - 3, 3)]
    count = mine_ref.shape[0] * 2
    feat = mine_ref.shape[2]
    even = lax.axis_index("seq") % 2 == 0
    share, slot = pieces[0][0].shape[1:3]
    terms = jnp.zeros((kt_ref.shape[0], feat), F32)
    for kv, turned_ref in enumerate((kt_ref, vt_ref)):
        rows = []
        for u in range(2):
            for i, (t0_ref, a_ref, b_ref) in enumerate(pieces):
                near = jnp.where(even == (u == 0), t0_ref[kv], 0.0)
                low = (near + a_ref[u, kv].astype(F32) + b_ref[u, kv].astype(F32)).astype(BF16)
                mg_ref[kv, u, i * share : (i + 1) * share] = low
                rows.append(low.reshape(share * slot, feat))
        terms = terms + nn(turned_ref[...], jnp.concatenate(rows, 0))
    rows = terms.shape[0] // count
    bits = count.bit_length() - 1
    for p in range(0, count, 2):
        spot = int(format(p, "b").zfill(bits)[::-1], 2)
        first = terms[p * rows : (p + 1) * rows]
        second = terms[(p + 1) * rows : (p + 2) * rows]
        mine_ref[spot] = jnp.where(even, first, second)
        other_ref[spot] = jnp.where(even, second, first)


def back_kernel(mg_ref, w_ref, terms_ref, gk_ref, gv_ref, give_ref):
    seg = terms_ref.shape[2]
    heads, slot, feat = mg_ref.shape[2:]
    restore = tap_major(seg, inverse=True)
    for kv, out_ref in enumerate((gk_ref, gv_ref)):
        for u in range(2):
            back = nt(mg_ref[kv, u].reshape(heads * slot, feat), w_ref[...])
            columns = []
            for h in range(heads):
                rows = back[h * slot : (h + 1) * slot]
                columns.append(
                    jnp.concatenate([rows[:, head(t, feat)] for t in range(TAPS)], 0)
                )
            total = (terms_ref[kv, u] + jnp.concatenate(columns, 1)).astype(BF16)
            result = nn(restore, total).astype(BF16)
            if u == 0:
                out_ref[...] = result
            else:
                give_ref[kv] = result


def finish_kernel(a_in, b_in, got_ref, a_ref, b_ref, sems):
    del a_in, b_in
    width = got_ref.shape[2]
    start = pl.multiple_of((1 - lax.axis_index("seq") % 2) * width, width)
    copies = [
        pltpu.make_async_copy(got_ref.at[i], dst.at[:, pl.ds(start, width)], sems.at[i])
        for i, dst in enumerate((a_ref, b_ref))
    ]
    for copy in copies:
        copy.start()
    for copy in copies:
        copy.wait()


def call(kernel, out_shape, in_specs, out_specs, flops, moved, exps=0, scratch=(), aliases=None):
    return pl.pallas_call(
        kernel,
        out_shape=out_shape,
        grid=(1,),
        in_specs=in_specs,
        out_specs=out_specs,
        scratch_shapes=scratch,
        input_output_aliases=aliases or {},
        compiler_params=pltpu.CompilerParams(vmem_limit_bytes=VMEM_BYTES),
        cost_estimate=pl.CostEstimate(flops=flops, bytes_accessed=moved, transcendentals=exps),
    )


def local(queries, key_vectors, value_vectors, cotangent, compress_kernel, memory_reach):
    q, k, v, g = queries[0], key_vectors[0], value_vectors[0], cotangent[0]
    seg, width = q.shape
    feat = compress_kernel.shape[1]
    heads = width // feat
    half = heads // 2
    share = half // PIECES
    slot = seg // TAPS
    span = BLOCKS * slot
    count = lax.axis_size("seq")
    books = lax.axis_size("dp")
    position = lax.axis_index("seq")
    row_bytes = 2 * seg * width
    unit = 2 * heads * seg * seg * feat

    def side():
        return lax.axis_index("seq") % 2

    def shift(value, steps):
        return lax.ppermute(value, "seq", [(s, (s + steps) % count) for s in range(count)])

    def trade(value):
        return lax.ppermute(value, "seq", [(s, s ^ 1) for s in range(count)])

    def in_hbm(value):
        return pltpu.with_memory_space_constraint(value, pltpu.HBM)

    def shape(dims, kind=BF16):
        return jax.ShapeDtypeStruct(dims, kind)

    def full(dims):
        return pl.BlockSpec(dims, lambda i: (0,) * len(dims))

    scalars = pl.BlockSpec(memory_space=pltpu.SMEM)
    mine_cols = pl.BlockSpec((seg, half * feat), lambda i: (0, side()))
    other_cols = pl.BlockSpec((seg, half * feat), lambda i: (0, 1 - side()))
    far = pl.BlockSpec((2, 1, share, slot, feat), lambda i: (0, side(), 0, 0, 0))
    kernel_spec = full(compress_kernel.shape)

    hbm = pl.BlockSpec(memory_space=pltpu.HBM)
    rows = 4 * seg + 16
    *packed, give = call(
        pack_kernel,
        [shape((2, 2, share, slot, feat))] * PIECES + [shape((rows, half * feat))],
        [scalars] + [hbm] * 5,
        [full((2, 2, share, slot, feat))] * PIECES + [full((rows, half * feat))],
        3 * unit, 5 * row_bytes,
        scratch=[
            pltpu.VMEM((2, seg, width), BF16),
            pltpu.VMEM(compress_kernel.shape, BF16),
            pltpu.SemaphoreType.DMA((4 * PIECES + 5,)),
        ],
    )(memory_reach, *[in_hbm(a) for a in (k, v, q, g, compress_kernel)])
    got = trade(give)

    r2, r4 = [], []
    for piece in packed:
        r2.append(shift(piece, 2))
        r4.append(shift(piece, 4))
    kvp, near, own_stats, kt, vt, bias = call(
        own_kernel,
        (
            shape((2, 2, seg, half * feat)),
            shape((2, half, slot, feat)),
            shape((3, half, 1, 2 * seg), F32),
            shape((TAPS * feat, heads * slot)),
            shape((TAPS * feat, heads * slot)),
            shape((span, 2 * seg), F32),
        ),
        [scalars] + [mine_cols] * 4 + [full((rows, half * feat)), kernel_spec],
        (
            full((2, 2, seg, half * feat)),
            full((2, half, slot, feat)),
            full((3, half, 1, 2 * seg)),
            full((TAPS * feat, heads * slot)),
            full((TAPS * feat, heads * slot)),
            full((span, 2 * seg)),
        ),
        5 * unit, 8 * row_bytes, heads * seg * seg,
    )(memory_reach, k, v, q, g, got, compress_kernel)

    pieces, sums, terms = [], [], []
    for i in range(PIECES):
        if i == 0:
            first2, own_stats, near = lax.optimization_barrier((r2[0], own_stats, near))
            r2[0] = first2
        else:
            r2[i], r4[i], t2, t4 = lax.optimization_barrier((r2[i], r4[i], *terms[-1]))
            terms[-1] = (t2, t4)
        slots = [r2[i], trade(r2[i]), r4[i], trade(r4[i])]
        cols = pl.BlockSpec((seg, share * feat), lambda s, i=i: (0, side() * PIECES + i))
        got_q = pl.BlockSpec((seg, share * feat), lambda s, i=i: (2, i))
        got_g = pl.BlockSpec((seg, share * feat), lambda s, i=i: (3, i))
        stats = pl.BlockSpec((3, share, 1, 2 * seg), lambda s, i=i: (0, i, 0, 0))
        near_spec = pl.BlockSpec((2, share, slot, feat), lambda s, i=i: (0, i, 0, 0))
        t0, t2, t4, w_mem, d_mem, final = call(
            memory_kernel,
            (
                shape((2, share, slot, feat), F32),
                shape((2, 2, share, slot, feat)),
                shape((2, 2, share, slot, feat)),
                shape((share, span, 2 * seg)),
                shape((share, span, 2 * seg)),
                shape((3, share, 1, 2 * seg), F32),
            ),
            [full((span, 2 * seg)), cols, got_q, cols, got_g, stats, near_spec] + [far] * 4,
            (
                full((2, share, slot, feat)),
                full((2, 2, share, slot, feat)),
                full((2, 2, share, slot, feat)),
                full((share, span, 2 * seg)),
                full((share, span, 2 * seg)),
                full((3, share, 1, 2 * seg)),
            ),
            4 * unit // PIECES, 8 * row_bytes // PIECES, heads * seg * seg,
        )(bias, q, got, g, got, own_stats, near, *slots)
        sums.append([t0])
        terms.append((t2, t4))
        pieces.append([*slots, w_mem, d_mem, final])

    for total, (t2, t4) in zip(sums, terms):
        total += [shift(t2, -2), shift(t4, -4)]
    piece_specs = [
        far, far, far, far,
        full((share, span, 2 * seg)), full((share, span, 2 * seg)), full((3, share, 1, 2 * seg)),
    ]
    attended, grad_queries, give_first, own_terms = call(
        output_kernel,
        (
            shape((seg, width)),
            shape((seg, width)),
            shape((2, seg, half * feat)),
            shape((2, 2, seg, half * feat), F32),
        ),
        [
            mine_cols,
            pl.BlockSpec((seg, half * feat), lambda i: (2, 0)),
            mine_cols,
            pl.BlockSpec((seg, half * feat), lambda i: (3, 0)),
        ]
        + [full((2, 2, seg, half * feat)), full((2, half, slot, feat))]
        + piece_specs * PIECES,
        (
            mine_cols, mine_cols,
            full((2, seg, half * feat)),
            full((2, 2, seg, half * feat)),
        ),
        8 * unit, 12 * row_bytes, heads * seg * seg,
    )(q, got, g, got, kvp, near, *[a for piece in pieces for a in piece])

    def finish(a, b, give):
        anywhere = pl.BlockSpec(memory_space=pl.ANY)
        return call(
            finish_kernel,
            (shape((seg, width)), shape((seg, width))),
            [anywhere] * 3,
            (anywhere, anywhere),
            0, 2 * row_bytes,
            scratch=[pltpu.SemaphoreType.DMA((2,))],
            aliases={0: 0, 1: 1},
        )(a, b, trade(give))

    attended, grad_queries = finish(attended, grad_queries, give_first)
    sums[-1][2], own_terms = lax.optimization_barrier((sums[-1][2], own_terms))
    kernel_rows = compress_kernel.shape[0]
    half_dims = (count // 2, kernel_rows // count, feat)
    sum_specs = [
        full((2, share, slot, feat)),
        full((2, 2, share, slot, feat)),
        full((2, 2, share, slot, feat)),
    ]
    memory_grads, mine, other = call(
        sum_kernel,
        (shape((2, 2, half, slot, feat)), shape(half_dims, F32), shape(half_dims, F32)),
        [full((TAPS * feat, heads * slot))] * 2 + sum_specs * PIECES,
        (full((2, 2, half, slot, feat)), full(half_dims), full(half_dims)),
        unit, 4 * row_bytes,
    )(kt, vt, *[a for piece in sums for a in piece])

    grad_keys, grad_values, give_last = call(
        back_kernel,
        (shape((seg, width)), shape((seg, width)), shape((2, seg, half * feat))),
        [full((2, 2, half, slot, feat)), kernel_spec, full((2, 2, seg, half * feat))],
        (mine_cols, mine_cols, full((2, seg, half * feat))),
        4 * unit, 7 * row_bytes,
    )(memory_grads, compress_kernel, own_terms)

    grad_keys, grad_values = finish(grad_keys, grad_values, give_last)
    part = mine + trade(other)
    part, (attended, grad_queries, grad_keys, grad_values) = reduce_rest(
        part, position, count, books, [(attended, grad_queries), (grad_keys, grad_values)]
    )
    return (attended[None], grad_queries[None], grad_keys[None], grad_values[None], part)


def reduce_rest(part, position, count, books, beside):
    bits = []
    step = 2
    while step < count:
        bits.append(("seq", step))
        step *= 2
    step = 1
    while step < books:
        bits.append(("dp", step))
        step *= 2
    for i in range(0, len(bits), 2):
        phase = bits[i : i + 2]
        split = [step for axis, step in phase if axis == "seq"]
        part = part.reshape(2 ** len(split), -1, *part.shape[1:])
        mine = jnp.int32(0)
        for step in split:
            mine = mine * 2 + (position // step) % 2
        arrived = []
        for mask in range(1, 2 ** len(phase)):
            flip, seq_xor, dp_xor = 0, 0, 0
            for j, (axis, step) in enumerate(phase):
                chosen = (mask >> (len(phase) - 1 - j)) & 1
                if axis == "seq":
                    flip = flip * 2 + chosen
                    seq_xor |= chosen * step
                else:
                    dp_xor |= chosen * step
            sent = lax.dynamic_index_in_dim(part, mine ^ flip, 0, False)
            pairs = [
                (s * books + d, (s ^ seq_xor) * books + (d ^ dp_xor))
                for s in range(count)
                for d in range(books)
            ]
            arrived.append(lax.ppermute(sent, ("seq", "dp"), pairs))
        part = lax.dynamic_index_in_dim(part, mine, 0, False)
        if i // 2 < len(beside):
            arrived[0], *beside[i // 2] = lax.optimization_barrier(
                (arrived[0], *beside[i // 2])
            )
        for piece in arrived:
            part = part + piece
    return part.reshape(-1, part.shape[-1]), [array for arrays in beside for array in arrays]


def solution(mesh):
    rows = P("dp", "seq", None)
    return jax.shard_map(
        local,
        mesh=mesh,
        in_specs=(rows, rows, rows, rows, P(), P("dp", "seq")),
        out_specs=(rows, rows, rows, rows, P("seq", None)),
        check_vma=False,
    )
```

time: 72 us -> 57.2 us (0.79)
  Pallas kernels: 20.3 us -> 12.1 us
  starting transfers between devices: 18.4 us -> 15.3 us
  other arithmetic: 2.95 us -> 0.64 us
  local copies, waits for them, and re-layouts: 2.16 us -> 0.05 us
  waiting for transfers between devices: 26.4 us -> 27.5 us
    ppermute x4, waiting for transfers between devices: 11.7 us -> 20 us  [shift(): lax.ppermute(value, 'seq', [(s, (s + steps) % count) for s in range(count)])]
    pallas_call x6 -> x8, Pallas kernels: 20.3 us -> 12.1 us  [the longest x1 2.83 us: local(): call(output_kernel, (shape((seg, width)), shape((seg, width)), shape((2,...]
    ppermute x9 -> x12, waiting for transfers between devices: 14.7 us -> 7.55 us  [the longest x6 6.01 us: reduce_rest(): arrived.append(lax.ppermute(sent, ('seq', 'dp'), pairs))]
    ppermute x4, starting transfers between devices: 11.5 us -> 5.98 us  [shift(): lax.ppermute(value, 'seq', [(s, (s + steps) % count) for s in range(count)])]
    ppermute x9 -> x12, starting transfers between devices: 6.88 us -> 9.32 us  [the longest x6 8.23 us: reduce_rest(): arrived.append(lax.ppermute(sent, ('seq', 'dp'), pairs))]
    add x4 -> x2, other arithmetic: 1.55 us -> 0.03 us  [the longest x1 0.02 us: local(): part = mine + trade(other)]
    unnamed x18 -> x10, local copies, waits for them, and re-layouts: 1.42 us -> 0.02 us
    convert_element_type x1 -> x0, other arithmetic: 1.39 us -> none  [local(): send4 = (t4.astype(F32) + jnp.where(even, jnp.zeros_like(swapped[1]), swa...]
  transfers between devices with their start and end apart: 13 -> 16, of which waited for: 9 -> 7; matrix products, arithmetic and copies ran while one was open for 1% -> 0% of each run, Pallas kernels for 16% -> 14%
where the time goes in v3:
time: 57.2 us; the launch traced here: 57.1 us
  waiting for transfers between devices  27.5 us (48%)
  starting transfers between devices  15.3 us (27%)
  Pallas kernels  12.1 us (21%)
  between operations  1.47 us (3%)
  other arithmetic  0.64 us (1%)
    ppermute x4, waiting for transfers between devices, shift(): lax.ppermute(value, 'seq', [(s, (s + steps) % count) for s in range(count)])  20 us
    ppermute x6, starting transfers between devices, reduce_rest(): arrived.append(lax.ppermute(sent, ('seq', 'dp'), pairs))  8.23 us
    ppermute x6, waiting for transfers between devices, reduce_rest(): arrived.append(lax.ppermute(sent, ('seq', 'dp'), pairs))  6.01 us
    ppermute x4, starting transfers between devices, shift(): lax.ppermute(value, 'seq', [(s, (s + steps) % count) for s in range(count)])  5.98 us
    pallas_call x1, Pallas kernels, local(): call(output_kernel, (shape((seg, width)), shape((seg, width)), shape((2,...  2.83 us
    pallas_call x1, Pallas kernels, local(): call(pack_kernel, [shape((2, 2, share, slot, feat))] * PIECES + [shape((r...  2.74 us
    pallas_call x1, Pallas kernels, local(): call(back_kernel, (shape((seg, width)), shape((seg, width)), shape((2, se...  1.76 us
    pallas_call x2, Pallas kernels, finish(): call(finish_kernel, (shape((seg, width)), shape((seg, width))), [anywhere...  1.61 us
  transfers between devices with their start and end apart: 16, of which 7 were waited for; matrix products, arithmetic and copies ran while one was open for 0% of the time, Pallas kernels for 14%

profile of v3, /device:TPU:0, one launch (start us, length us, event | category | flops | bytes accessed | tf_op | source)
XLA Modules:
  0.0 57.1 jit_solution(15679183576804360878)
XLA Ops:
  1.3 2.7 %shard_map.101 = (bf16[2,2,8,32,128]{4,3,2,1,0:T(8,128)(2,1)S(1)}, bf16[528,1024]{1,0:T(8,128)(2,1)S(1)}) custom-call(s32[1,1]{1,0:T(1,128)S(6)} %copy.19.reach_ref, bf16[128,2048]{1,0:T(8,128)(2,1)} %bitcast.31, bf16[128,2048]{1,0:T(8,128)(2,1)} %bitcast.33, bf16[128,2048]{1,0:T(8,128)(2,1)} %bitcast.23, bf16[128,2048]{1,0:T(8,128)(2,1)} %bitcast.27, ...), custom_call_target="tpu_custom_call" | custom-call | flops 201326592 | bytes 2621440 | tf_op jit(solution)/shard_map/pallas_call | solution.py:421
  4.1 0.5 collective-permute-start
  4.6 2.6 %collective-permute-start.3 = (bf16[2,2,8,32,128]{4,3,2,1,0:T(8,128)(2,1)S(1)}, bf16[2,2,8,32,128]{4,3,2,1,0:T(8,128)(2,1)S(1)}, u32[]{:S(2)}, u32[]{:S(2)}) collective-permute-start(bf16[2,2,8,32,128]{4,3,2,1,0:T(8,128)(2,1)S(1)} %get-tuple-element.48), channel_id=1, source_target_pairs={{0,8},{2,10},{4,12},{6,14},{8,16},{10,18},{12,20},{14,22},{16,24},... | collective-permute-start | bytes 786440 | tf_op jit(solution)/shard_map/ppermute | solution.py:399
  7.2 1.5 %collective-permute-start.1 = (bf16[2,2,8,32,128]{4,3,2,1,0:T(8,128)(2,1)S(1)}, bf16[2,2,8,32,128]{4,3,2,1,0:T(8,128)(2,1)S(1)}, u32[]{:S(2)}, u32[]{:S(2)}) collective-permute-start(bf16[2,2,8,32,128]{4,3,2,1,0:T(8,128)(2,1)S(1)} %get-tuple-element.48), channel_id=1, source_target_pairs={{0,4},{2,6},{4,8},{6,10},{8,12},{10,14},{12,16},{14,18},{16,20},{1... | collective-permute-start | bytes 786440 | tf_op jit(solution)/shard_map/ppermute | solution.py:399
  8.7 7.4 %collective-permute-done.3.r4_ref.refs_8_ = bf16[2,2,8,32,128]{4,3,2,1,0:T(8,128)(2,1)S(1)} collective-permute-done((bf16[2,2,8,32,128]{4,3,2,1,0:T(8,128)(2,1)S(1)}, bf16[2,2,8,32,128]{4,3,2,1,0:T(8,128)(2,1)S(1)}, u32[]{:S(2)}, u32[]{:S(2)}) %collective-permute-start.3) | collective-permute-done | bytes 262176 | tf_op jit(solution)/shard_map/ppermute | solution.py:399
  16.2 1.2 %shard_map.102 = (bf16[2,2,128,1024]{3,2,1,0:T(8,128)(2,1)S(1)}, bf16[2,8,32,128]{3,2,1,0:T(8,128)(2,1)S(1)}, f32[3,8,1,256]{3,2,1,0:T(1,128)S(1)}, bf16[512,512...) custom-call(s32[1,1]{1,0:T(1,128)S(6)} %copy.19.reach_ref, bf16[128,2048]{1,0:T(8,128)(2,1)S(1)} %bitcast.32, ...), custom_call_target="tpu_custom_call" | custom-call | flops 335544320 | bytes 4194304 | tf_op jit(solution)/shard_map/pallas_call | solution.py:439
  17.5 5.2 %collective-permute-done.1.r2_ref.refs_6_ = bf16[2,2,8,32,128]{4,3,2,1,0:T(8,128)(2,1)S(1)} collective-permute-done((bf16[2,2,8,32,128]{4,3,2,1,0:T(8,128)(2,1)S(1)}, bf16[2,2,8,32,128]{4,3,2,1,0:T(8,128)(2,1)S(1)}, u32[]{:S(2)}, u32[]{:S(2)}) %collective-permute-start.1) | collective-permute-done | bytes 262176 | tf_op jit(solution)/shard_map/ppermute | solution.py:399
  22.7 1.5 %collective-permute-done.2.r2s_ref.refs_7_ = bf16[2,2,8,32,128]{4,3,2,1,0:T(8,128)(2,1)S(1)} collective-permute-done((bf16[2,2,8,32,128]{4,3,2,1,0:T(8,128)(2,1)S(1)}, bf16[2,2,8,32,128]{4,3,2,1,0:T(8,128)(2,1)S(1)}, u32[]{:S(2)}, u32[]{:S(2)}) %collective-permute-start.2) | collective-permute-done | bytes 262176 | tf_op jit(solution)/shard_map/ppermute | solution.py:402
  24.3 1.4 %shard_map.103 = (f32[2,8,32,128]{3,2,1,0:T(8,128)S(1)}, bf16[2,2,8,32,128]{4,3,2,1,0:T(8,128)(2,1)S(1)}, bf16[2,2,8,32,128]{4,3,2,1,0:T(8,128)(2,1)S(1)}, bf16[...) custom-call(f32[160,256]{1,0:T(8,128)S(1)} %get-tuple-element.47.bias_ref, ...), custom_call_target="tpu_custom_call" | custom-call | flops 268435456 | bytes 4194304 | tf_op jit(solution)/shard_map/pallas_call | solution.py:475
  25.8 1.8 %collective-permute-start.6 = (bf16[2,2,8,32,128]{4,3,2,1,0:T(8,128)(2,1)S(1)}, bf16[2,2,8,32,128]{4,3,2,1,0:T(8,128)(2,1)S(1)}, u32[]{:S(2)}, u32[]{:S(2)}) collective-permute-start(bf16[2,2,8,32,128]{4,3,2,1,0:T(8,128)(2,1)S(1)} %get-tuple-element.56), channel_id=1, source_target_pairs={{0,24},{2,26},{4,28},{6,30},{8,0},{10,2},{12,4},{14,6},{16,8},{18,... | collective-permute-start | bytes 786440 | tf_op jit(solution)/shard_map/ppermute | solution.py:399
  27.6 2.8 %shard_map.104 = (bf16[128,2048]{1,0:T(8,128)(2,1)}, bf16[128,2048]{1,0:T(8,128)(2,1)}, bf16[2,128,1024]{2,1,0:T(8,128)(2,1)S(1)}, f32[2,2,128,1024]{3,2,1,0:T(8,128)S(1)}) custom-call(bf16[128,2048]{1,0:T(8,128)(2,1)S(1)} %bitcast.26, bf16[528,1024]{1,0:T(8,128)(2,1)S(1)} %collective-permute-done.got_ref.qs_ref.gs_ref.refs_1_.refs_3_, ...), custom_call_target="tpu_custom_call" | custom-call | flops 536870912 | bytes 6291456 | tf_op jit(solution)/shard_map/pallas_call | solution.py:506
  30.4 7.3 %collective-permute-done.6.refs_2_ = bf16[2,2,8,32,128]{4,3,2,1,0:T(8,128)(2,1)S(1)} collective-permute-done((bf16[2,2,8,32,128]{4,3,2,1,0:T(8,128)(2,1)S(1)}, bf16[2,2,8,32,128]{4,3,2,1,0:T(8,128)(2,1)S(1)}, u32[]{:S(2)}, u32[]{:S(2)}) %collective-permute-start.6) | collective-permute-done | bytes 262176 | tf_op jit(solution)/shard_map/ppermute | solution.py:399
  38.2 1.8 %shard_map.107 = (bf16[128,2048]{1,0:T(8,128)(2,1)}, bf16[128,2048]{1,0:T(8,128)(2,1)}, bf16[2,128,1024]{2,1,0:T(8,128)(2,1)S(1)}) custom-call(bf16[2,2,8,32,128]{4,3,2,1,0:T(8,128)(2,1)S(1)} %get-tuple-element.73.mg_ref, bf16[512,128]{1,0:T(8,128)(2,1)S(1)} %copy-done.4, f32[2,2,128,1024]{3,2,1,0:T(8,128)S(1)} %get-tuple-element.74.terms_ref), custom_call_target="tpu_custom_call" | custom-call | flops 268435456 | bytes 3670016 | tf_op jit(solution)/shard_map/pallas_call | solution.py:559
  40.0 0.5 collective-permute-start.13
  40.5 1.6 %collective-permute-start.8 = (f32[2,32,128]{2,1,0:T(8,128)S(1)}, f32[2,32,128]{2,1,0:T(8,128)S(1)}, u32[]{:S(2)}, u32[]{:S(2)}) collective-permute-start(f32[2,32,128]{2,1,0:T(8,128)S(1)} %get-tuple-element.85), channel_id=1, source_target_pairs={{0,8},{1,9},{2,10},{3,11},{4,12},{5,13},{6,14},{7,15},{8,0},{9,1},... | collective-permute-start | bytes 98312 | tf_op jit(solution)/shard_map/ppermute | solution.py:608
  42.2 1.9 %collective-permute-start.10 = (f32[2,32,128]{2,1,0:T(8,128)S(1)}, f32[2,32,128]{2,1,0:T(8,128)S(1)}, u32[]{:S(2)}, u32[]{:S(2)}) collective-permute-start(f32[2,32,128]{2,1,0:T(8,128)S(1)} %get-tuple-element.83), channel_id=1, source_target_pairs={{0,4},{1,5},{2,6},{3,7},{4,0},{5,1},{6,2},{7,3},{8,12},{9,13},{10,... | collective-permute-start | bytes 98312 | tf_op jit(solution)/shard_map/ppermute | solution.py:608
  44.1 0.8 %shard_map.106 = (bf16[128,2048]{1,0:T(8,128)(2,1)}, bf16[128,2048]{1,0:T(8,128)(2,1)}) custom-call(bf16[128,2048]{1,0:T(8,128)(2,1)} %get-tuple-element.65.a_in, bf16[128,2048]{1,0:T(8,128)(2,1)} %get-tuple-element.66.b_in, bf16[2,128,1024]{2,1,0:T(8,128)(2,1)S(1)} %collective-permute-done.9.got_ref), custom_call_target="tpu_custom_call", output_to_operand_aliasing={{0}: (0, {}), {1}: (1, {})} | custom-call | bytes 1048576 | tf_op jit(solution)/shard_map/pallas_call | solution.py:532
  44.9 2.1 %collective-permute-done.11 = f32[2,32,128]{2,1,0:T(8,128)S(1)} collective-permute-done((f32[2,32,128]{2,1,0:T(8,128)S(1)}, f32[2,32,128]{2,1,0:T(8,128)S(1)}, u32[]{:S(2)}, u32[]{:S(2)}) %collective-permute-start.11) | collective-permute-done | bytes 32800 | tf_op jit(solution)/shard_map/ppermute | solution.py:608
  47.0 1.6 %collective-permute-start.12 = (f32[1,32,128]{2,1,0:T(8,128)S(1)}, f32[1,32,128]{2,1,0:T(8,128)S(1)}, u32[]{:S(2)}, u32[]{:S(2)}) collective-permute-start(f32[1,32,128]{2,1,0:T(8,128)S(1)} %get-tuple-element.87), channel_id=1, source_target_pairs={{0,1},{1,0},{2,3},{3,2},{4,5},{5,4},{6,7},{7,6},{8,9},{9,8},{10,11... | collective-permute-start | bytes 49160 | tf_op jit(solution)/shard_map/ppermute | solution.py:608
  48.6 3.0 %collective-permute-start.15 = (f32[1,32,128]{2,1,0:T(8,128)S(1)}, f32[1,32,128]{2,1,0:T(8,128)S(1)}, u32[]{:S(2)}, u32[]{:S(2)}) collective-permute-start(f32[1,32,128]{2,1,0:T(8,128)S(1)} %get-tuple-element.86), channel_id=1, source_target_pairs={{0,17},{1,16},{2,19},{3,18},{4,21},{5,20},{6,23},{7,22},{8,25},{9,... | collective-permute-start | bytes 49160 | tf_op jit(solution)/shard_map/ppermute | solution.py:608
  51.7 0.8 %shard_map.108 = (bf16[128,2048]{1,0:T(8,128)(2,1)}, bf16[128,2048]{1,0:T(8,128)(2,1)}) custom-call(bf16[128,2048]{1,0:T(8,128)(2,1)} %get-tuple-element.75.a_in, bf16[128,2048]{1,0:T(8,128)(2,1)} %get-tuple-element.76.b_in, bf16[2,128,1024]{2,1,0:T(8,128)(2,1)S(1)} %collective-permute-done.13.got_ref), custom_call_target="tpu_custom_call", output_to_operand_aliasing={{0}: (0, {}), {1}: (1, {})} | custom-call | bytes 1048576 | tf_op jit(solution)/shard_map/pallas_call | solution.py:532
  52.5 1.6 %collective-permute-done.15 = f32[1,32,128]{2,1,0:T(8,128)S(1)} collective-permute-done((f32[1,32,128]{2,1,0:T(8,128)S(1)}, f32[1,32,128]{2,1,0:T(8,128)S(1)}, u32[]{:S(2)}, u32[]{:S(2)}) %collective-permute-start.15) | collective-permute-done | bytes 16416 | tf_op jit(solution)/shard_map/ppermute | solution.py:608
  54.2 2.3 %collective-permute-done.14 = f32[1,32,128]{2,1,0:T(8,128)S(1)} collective-permute-done((f32[1,32,128]{2,1,0:T(8,128)S(1)}, f32[1,32,128]{2,1,0:T(8,128)S(1)}, u32[]{:S(2)}, u32[]{:S(2)}) %collective-permute-start.14) | collective-permute-done | bytes 16416 | tf_op jit(solution)/shard_map/ppermute | solution.py:608
  56.5 0.6 %add_bitcast_fusion = f32[32,128]{1,0:T(8,128)} fusion(f32[1,32,128]{2,1,0:T(8,128)S(1)} %collective-permute-done.15, f32[1,32,128]{2,1,0:T(8,128)S(1)} %collective-permute-done.14, f32[1,32,128]{2,1,0:T(8,128)S(1)} %get-tuple-element.87, f32[1,32,128]{2,1,0:T(8,128)S(1)} %collective-permute-done.12), kind=kLoop, calls=%fused_computation.6 | loop fusion | flops 12288 | bytes 81920 | tf_op jit(solution)/shard_map/reshape | solution.py:616
  (31 shorter events, 0.8 us)
Async XLA Ops:
  1.3 14.9 %copy-start = (bf16[1,128,2048]{2,1,0:T(8,128)(2,1)S(1)}, bf16[1,128,2048]{2,1,0:T(8,128)(2,1)}, u32[]{:S(2)}) copy-start(bf16[1,128,2048]{2,1,0:T(8,128)(2,1)} %param.6) | copy-start | bytes 1572868
  1.3 14.9 %copy-start.1 = (bf16[1,128,2048]{2,1,0:T(8,128)(2,1)S(1)}, bf16[1,128,2048]{2,1,0:T(8,128)(2,1)}, u32[]{:S(2)}) copy-start(bf16[1,128,2048]{2,1,0:T(8,128)(2,1)} %param.9) | copy-start | bytes 1572868
  1.3 14.9 %copy-start.2 = (bf16[1,128,2048]{2,1,0:T(8,128)(2,1)S(1)}, bf16[1,128,2048]{2,1,0:T(8,128)(2,1)}, u32[]{:S(2)}) copy-start(bf16[1,128,2048]{2,1,0:T(8,128)(2,1)} %param.7) | copy-start | bytes 1572868
  1.3 14.9 %copy-start.3 = (bf16[1,128,2048]{2,1,0:T(8,128)(2,1)S(1)}, bf16[1,128,2048]{2,1,0:T(8,128)(2,1)}, u32[]{:S(2)}) copy-start(bf16[1,128,2048]{2,1,0:T(8,128)(2,1)} %param.8) | copy-start | bytes 1572868
  1.3 14.9 %copy-start.4 = (bf16[512,128]{1,0:T(8,128)(2,1)S(1)}, bf16[512,128]{1,0:T(8,128)(2,1)}, u32[]{:S(2)}) copy-start(bf16[512,128]{1,0:T(8,128)(2,1)} %w_ref.3) | copy-start | bytes 393220
  4.1 12.1 %collective-permute-start = (bf16[528,1024]{1,0:T(8,128)(2,1)S(1)}, bf16[528,1024]{1,0:T(8,128)(2,1)S(1)}, u32[]{:S(2)}, u32[]{:S(2)}) collective-permute-start(bf16[528,1024]{1,0:T(8,128)(2,1)S(1)} %get-tuple-element.44), channel_id=1, source_target_pairs={{0,2},{2,0},{4,6},{6,4},{8,10},{10,8},{12,14},{14,12},{16,18},{18,... | collective-permute-start | bytes 3244040 | tf_op jit(solution)/shard_map/ppermute | solution.py:402
  4.6 11.6 %collective-permute-start.3 = (bf16[2,2,8,32,128]{4,3,2,1,0:T(8,128)(2,1)S(1)}, bf16[2,2,8,32,128]{4,3,2,1,0:T(8,128)(2,1)S(1)}, u32[]{:S(2)}, u32[]{:S(2)}) collective-permute-start(bf16[2,2,8,32,128]{4,3,2,1,0:T(8,128)(2,1)S(1)} %get-tuple-element.48), channel_id=1, source_target_pairs={{0,8},{2,10},{4,12},{6,14},{8,16},{10,18},{12,20},{14,22},{16,24},... | collective-permute-start | bytes 786440 | tf_op jit(solution)/shard_map/ppermute | solution.py:399
  7.2 15.5 %collective-permute-start.1 = (bf16[2,2,8,32,128]{4,3,2,1,0:T(8,128)(2,1)S(1)}, bf16[2,2,8,32,128]{4,3,2,1,0:T(8,128)(2,1)S(1)}, u32[]{:S(2)}, u32[]{:S(2)}) collective-permute-start(bf16[2,2,8,32,128]{4,3,2,1,0:T(8,128)(2,1)S(1)} %get-tuple-element.48), channel_id=1, source_target_pairs={{0,4},{2,6},{4,8},{6,10},{8,12},{10,14},{12,16},{14,18},{16,20},{1... | collective-permute-start | bytes 786440 | tf_op jit(solution)/shard_map/ppermute | solution.py:399
  16.2 6.5 %collective-permute-start.4 = (bf16[2,2,8,32,128]{4,3,2,1,0:T(8,128)(2,1)S(1)}, bf16[2,2,8,32,128]{4,3,2,1,0:T(8,128)(2,1)S(1)}, u32[]{:S(2)}, u32[]{:S(2)}) collective-permute-start(bf16[2,2,8,32,128]{4,3,2,1,0:T(8,128)(2,1)S(1)} %collective-permute-done.3.r4_ref.refs_8_), channel_id=1, source_target_pairs={{0,2},{2,0},{4,6},{6,4},{8,10},{10,8},{12,14},{14,12},{16,18},{18,... | collective-permute-start | bytes 786440 | tf_op jit(solution)/shard_map/ppermute | solution.py:402
  22.7 1.5 %collective-permute-start.2 = (bf16[2,2,8,32,128]{4,3,2,1,0:T(8,128)(2,1)S(1)}, bf16[2,2,8,32,128]{4,3,2,1,0:T(8,128)(2,1)S(1)}, u32[]{:S(2)}, u32[]{:S(2)}) collective-permute-start(bf16[2,2,8,32,128]{4,3,2,1,0:T(8,128)(2,1)S(1)} %collective-permute-done.1.r2_ref.refs_6_), channel_id=1, source_target_pairs={{0,2},{2,0},{4,6},{6,4},{8,10},{10,8},{12,14},{14,12},{16,18},{18,... | collective-permute-start | bytes 786440 | tf_op jit(solution)/shard_map/ppermute | solution.py:402
  25.7 12.0 %collective-permute-start.5 = (bf16[2,2,8,32,128]{4,3,2,1,0:T(8,128)(2,1)S(1)}, bf16[2,2,8,32,128]{4,3,2,1,0:T(8,128)(2,1)S(1)}, u32[]{:S(2)}, u32[]{:S(2)}) collective-permute-start(bf16[2,2,8,32,128]{4,3,2,1,0:T(8,128)(2,1)S(1)} %get-tuple-element.55), channel_id=1, source_target_pairs={{0,28},{2,30},{4,0},{6,2},{8,4},{10,6},{12,8},{14,10},{16,12},{18,... | collective-permute-start | bytes 786440 | tf_op jit(solution)/shard_map/ppermute | solution.py:399
  25.8 11.9 %collective-permute-start.6 = (bf16[2,2,8,32,128]{4,3,2,1,0:T(8,128)(2,1)S(1)}, bf16[2,2,8,32,128]{4,3,2,1,0:T(8,128)(2,1)S(1)}, u32[]{:S(2)}, u32[]{:S(2)}) collective-permute-start(bf16[2,2,8,32,128]{4,3,2,1,0:T(8,128)(2,1)S(1)} %get-tuple-element.56), channel_id=1, source_target_pairs={{0,24},{2,26},{4,28},{6,30},{8,0},{10,2},{12,4},{14,6},{16,8},{18,... | collective-permute-start | bytes 786440 | tf_op jit(solution)/shard_map/ppermute | solution.py:399
  30.4 13.7 %collective-permute-start.9 = (bf16[2,128,1024]{2,1,0:T(8,128)(2,1)S(1)}, bf16[2,128,1024]{2,1,0:T(8,128)(2,1)S(1)}, u32[]{:S(2)}, u32[]{:S(2)}) collective-permute-start(bf16[2,128,1024]{2,1,0:T(8,128)(2,1)S(1)} %get-tuple-element.67), channel_id=1, source_target_pairs={{0,2},{2,0},{4,6},{6,4},{8,10},{10,8},{12,14},{14,12},{16,18},{18,... | collective-permute-start | bytes 1572872 | tf_op jit(solution)/shard_map/ppermute | solution.py:402
  38.2 2.3 %collective-permute-start.7 = (f32[8,32,128]{2,1,0:T(8,128)S(1)}, f32[8,32,128]{2,1,0:T(8,128)S(1)}, u32[]{:S(2)}, u32[]{:S(2)}) collective-permute-start(f32[8,32,128]{2,1,0:T(8,128)S(1)} %get-tuple-element.64), channel_id=1, source_target_pairs={{0,2},{2,0},{4,6},{6,4},{8,10},{10,8},{12,14},{14,12},{16,18},{18,... | collective-permute-start | bytes 393224 | tf_op jit(solution)/shard_map/ppermute | solution.py:402
  40.0 11.7 %collective-permute-start.13 = (bf16[2,128,1024]{2,1,0:T(8,128)(2,1)S(1)}, bf16[2,128,1024]{2,1,0:T(8,128)(2,1)S(1)}, u32[]{:S(2)}, u32[]{:S(2)}) collective-permute-start(bf16[2,128,1024]{2,1,0:T(8,128)(2,1)S(1)} %get-tuple-element.77), channel_id=1, source_target_pairs={{0,2},{2,0},{4,6},{6,4},{8,10},{10,8},{12,14},{14,12},{16,18},{18,... | collective-permute-start | bytes 1572872 | tf_op jit(solution)/shard_map/ppermute | solution.py:402
  40.5 4.4 %collective-permute-start.8 = (f32[2,32,128]{2,1,0:T(8,128)S(1)}, f32[2,32,128]{2,1,0:T(8,128)S(1)}, u32[]{:S(2)}, u32[]{:S(2)}) collective-permute-start(f32[2,32,128]{2,1,0:T(8,128)S(1)} %get-tuple-element.85), channel_id=1, source_target_pairs={{0,8},{1,9},{2,10},{3,11},{4,12},{5,13},{6,14},{7,15},{8,0},{9,1},... | collective-permute-start | bytes 98312 | tf_op jit(solution)/shard_map/ppermute | solution.py:608
  42.2 4.8 %collective-permute-start.11 = (f32[2,32,128]{2,1,0:T(8,128)S(1)}, f32[2,32,128]{2,1,0:T(8,128)S(1)}, u32[]{:S(2)}, u32[]{:S(2)}) collective-permute-start(f32[2,32,128]{2,1,0:T(8,128)S(1)} %get-tuple-element.84), channel_id=1, source_target_pairs={{0,12},{1,13},{2,14},{3,15},{4,8},{5,9},{6,10},{7,11},{8,4},{9,5},... | collective-permute-start | bytes 98312 | tf_op jit(solution)/shard_map/ppermute | solution.py:608
  42.2 4.8 %collective-permute-start.10 = (f32[2,32,128]{2,1,0:T(8,128)S(1)}, f32[2,32,128]{2,1,0:T(8,128)S(1)}, u32[]{:S(2)}, u32[]{:S(2)}) collective-permute-start(f32[2,32,128]{2,1,0:T(8,128)S(1)} %get-tuple-element.83), channel_id=1, source_target_pairs={{0,4},{1,5},{2,6},{3,7},{4,0},{5,1},{6,2},{7,3},{8,12},{9,13},{10,... | collective-permute-start | bytes 98312 | tf_op jit(solution)/shard_map/ppermute | solution.py:608
  47.0 5.5 %collective-permute-start.12 = (f32[1,32,128]{2,1,0:T(8,128)S(1)}, f32[1,32,128]{2,1,0:T(8,128)S(1)}, u32[]{:S(2)}, u32[]{:S(2)}) collective-permute-start(f32[1,32,128]{2,1,0:T(8,128)S(1)} %get-tuple-element.87), channel_id=1, source_target_pairs={{0,1},{1,0},{2,3},{3,2},{4,5},{5,4},{6,7},{7,6},{8,9},{9,8},{10,11... | collective-permute-start | bytes 49160 | tf_op jit(solution)/shard_map/ppermute | solution.py:608
  48.6 5.6 %collective-permute-start.15 = (f32[1,32,128]{2,1,0:T(8,128)S(1)}, f32[1,32,128]{2,1,0:T(8,128)S(1)}, u32[]{:S(2)}, u32[]{:S(2)}) collective-permute-start(f32[1,32,128]{2,1,0:T(8,128)S(1)} %get-tuple-element.86), channel_id=1, source_target_pairs={{0,17},{1,16},{2,19},{3,18},{4,21},{5,20},{6,23},{7,22},{8,25},{9,... | collective-permute-start | bytes 49160 | tf_op jit(solution)/shard_map/ppermute | solution.py:608
  51.7 4.8 %collective-permute-start.14 = (f32[1,32,128]{2,1,0:T(8,128)S(1)}, f32[1,32,128]{2,1,0:T(8,128)S(1)}, u32[]{:S(2)}, u32[]{:S(2)}) collective-permute-start(f32[1,32,128]{2,1,0:T(8,128)S(1)} %get-tuple-element.86), channel_id=1, source_target_pairs={{0,16},{1,17},{2,18},{3,19},{4,20},{5,21},{6,22},{7,23},{8,24},{9,... | collective-permute-start | bytes 49160 | tf_op jit(solution)/shard_map/ppermute | solution.py:608

commit v4 on v3

--- a/solution.py
+++ b/solution.py
@@ -10,7 +10,6 @@
 TAPS = 4
 MASKED = -1e30
 VMEM_BYTES = 24 * 2**20
-PIECES = 1
 BLOCKS = 5
 
 
@@ -72,59 +71,47 @@
     )
 
 
-def pack_kernel(reach_ref, k_hbm, v_hbm, q_hbm, g_hbm, w_hbm, *refs):
-    *packed_refs, give_ref, rows_ref, w_ref, sems = refs
+def pack_kernel(
+    reach_ref, k_hbm, v_hbm, q_hbm, g_hbm, w_hbm,
+    mine_ref, other_ref, give_ref, rows_ref, w_ref, sems,
+):
     seg, width = k_hbm.shape
     feat = w_hbm.shape[1]
-    heads = width // feat
+    half = width // 2
+    heads = half // feat
     slot = seg // TAPS
-    share = heads // 2 // len(packed_refs)
     order = tap_major(seg)
-    parts = [
-        (half, i, kv)
-        for half in range(2)
-        for i in range(len(packed_refs))
-        for kv in range(2)
+    core = lax.axis_index("seq") % 2
+    begin = [pl.multiple_of(core * half, half), pl.multiple_of((1 - core) * half, half)]
+    steps = [(part, kv) for part in range(2) for kv in range(2)]
+    pairs = [
+        ((k_hbm, v_hbm)[kv].at[:, pl.ds(begin[part], half)], rows_ref.at[part, kv])
+        for part, kv in steps
     ]
-    copies = []
-    for n, (half, i, kv) in enumerate(parts):
-        cols = pl.ds((half * len(packed_refs) + i) * share * feat, share * feat)
-        copies.append(
-            pltpu.make_async_copy(
-                (k_hbm, v_hbm)[kv].at[:, cols], rows_ref.at[kv, :, cols], sems.at[n]
-            )
-        )
-    copies.append(pltpu.make_async_copy(w_hbm, w_ref, sems.at[len(parts)]))
-    for n in (0, 1, len(parts), *range(2, len(parts))):
-        copies[n].start()
-    start = pl.multiple_of((1 - lax.axis_index("seq") % 2) * (width // 2), width // 2)
-    given = [
-        pltpu.make_async_copy(
-            src.at[:, pl.ds(start, width // 2)],
-            give_ref.at[pl.ds(i * seg, seg)],
-            sems.at[len(parts) + 1 + i],
-        )
-        for i, src in enumerate((k_hbm, v_hbm, q_hbm, g_hbm))
+    pairs.insert(2, (w_hbm, w_ref))
+    pairs += [
+        (src.at[:, pl.ds(begin[1], half)], give_ref.at[pl.ds((2 + i) * seg, seg)])
+        for i, src in enumerate((q_hbm, g_hbm))
     ]
-    for copy in given:
+    copies = [pltpu.make_async_copy(*pair, sems.at[n]) for n, pair in enumerate(pairs)]
+    for copy in copies:
         copy.start()
-    tail = (give_ref.shape[0] - 4 * seg, give_ref.shape[1])
-    reach = jnp.full(tail, reach_ref[0, 0], jnp.int32)
-    give_ref[4 * seg :] = reach.astype(F32).astype(BF16)
-    for n, (half, i, kv) in enumerate(parts):
-        copies[n].wait()
-        begin = (half * len(packed_refs) + i) * share * feat
-        rows = nn(order, rows_ref[kv, :, begin : begin + share * feat]).astype(BF16)
+    for n, (part, kv) in enumerate(steps):
+        copies[n if n < 2 else n + 1].wait()
+        rows = nn(order, rows_ref[part, kv]).astype(BF16)
         if n == 0:
-            copies[-1].wait()
-        packed = nn(tap_rows(rows, share, feat), w_ref[...]).astype(BF16)
-        packed_refs[i][kv, half] = packed.reshape(share, slot, feat)
-    for copy in given:
+            copies[2].wait()
+        packed = nn(tap_rows(rows, heads, feat), w_ref[...]).astype(BF16)
+        (mine_ref, other_ref)[part][kv] = packed.reshape(heads, slot, feat)
+        if part == 1:
+            give_ref[kv * seg : (kv + 1) * seg] = rows_ref[part, kv]
+    for copy in copies[5:]:
         copy.wait()
+    give_ref[4 * seg :] = reach_ref[...]
 
 
 def own_kernel(
-    reach_ref, k_ref, v_ref, q_ref, g_ref, got_ref, w_ref,
+    k_ref, v_ref, q_ref, g_ref, reach_ref, got_ref, w_ref,
     kv_ref, near_ref, stat_ref, kt_ref, vt_ref, bias_ref,
 ):
     seg, width = q_ref.shape
@@ -136,7 +123,7 @@
     partner = mine + 1 - 2 * (mine % 2)
     even = mine % 2 == 0
     sources = (mine - mine % 2, mine - 2, partner - 2, mine - 4, partner - 4)
-    reach = jnp.full((slot, seg), reach_ref[0, 0], jnp.int32).astype(F32)
+    reach = jnp.broadcast_to(reach_ref[:1].astype(F32), (slot, seg))
     reach_s = jnp.broadcast_to(got_ref[4 * seg : 4 * seg + 1, :seg].astype(F32), (slot, seg))
     for b, source in enumerate(sources):
         for u, (reader, limit) in enumerate(((mine, reach), (partner, reach_s))):
@@ -189,8 +176,7 @@
 
 
 def memory_rows(kv, h, slots):
-    near_ref, *far_refs = slots
-    return jnp.concatenate([near_ref[kv, h]] + [ref[kv, 0, h] for ref in far_refs], 0)
+    return jnp.concatenate([ref[kv, h] for ref in slots], 0)
 
 
 def memory_kernel(
@@ -240,21 +226,19 @@
         for kv, terms in enumerate(pair):
             t0_ref[kv, h] = terms[:slot]
             terms = terms.astype(BF16)
-            for i, (ref, u) in enumerate(((t2_ref, 0), (t2_ref, 1), (t4_ref, 0), (t4_ref, 1))):
-                ref[u, kv, h] = terms[(i + 1) * slot : (i + 2) * slot]
+            for i in range(4):
+                (t2_ref, t4_ref)[i // 2][i % 2, kv, h] = terms[(i + 1) * slot : (i + 2) * slot]
 
     staged(list(range(heads)), first, second, third)
 
 
 def output_kernel(*refs):
-    q_ref, qs_ref, g_ref, gs_ref, kv_ref, near_ref = refs[:6]
-    count = (len(refs) - 6 - 4) // 7
-    pieces = [refs[6 + 7 * i : 13 + 7 * i] for i in range(count)]
-    att_ref, gq_ref, give_ref, terms_ref = refs[-4:]
+    q_ref, qs_ref, g_ref, gs_ref, kv_ref = refs[:5]
+    slots = refs[5 : 5 + BLOCKS]
+    w_ref, d_ref, fin_ref, att_ref, gq_ref, give_ref, terms_ref = refs[5 + BLOCKS :]
     seg, width = q_ref.shape
-    feat = near_ref.shape[3]
+    feat = slots[0].shape[3]
     heads = width // feat
-    share = heads // count
     scale = feat**-0.5
     allowed = causal(seg)
     queries, grads = (q_ref, qs_ref), (g_ref, gs_ref)
@@ -269,9 +253,8 @@
 
     def second(item, scores, grad_weights):
         h, u = item
-        fin_ref = pieces[h // share][6]
         side = slice(u * seg, (u + 1) * seg)
-        top, inverse, delta = (fin_ref[i, h % share, :, side] for i in range(3))
+        top, inverse, delta = (fin_ref[i, h, :, side] for i in range(3))
         scores = jnp.where(allowed, scores * scale, MASKED)
         weights = jnp.exp(scores - top) * inverse
         grad_scores = (weights * (grad_weights - delta) * scale).astype(BF16)
@@ -281,16 +264,14 @@
         h, u = item
         cols = head(h, feat)
         side = slice(u * seg, (u + 1) * seg)
-        *far, w_ref, d_ref, _ = pieces[h // share]
         terms_ref[0, u, :, cols] = nn(grad_scores, queries[u][:, cols])
         terms_ref[1, u, :, cols] = nn(weights_low, grads[u][:, cols])
 
         def whole(kv, own, memory):
-            rows = [near_ref[kv, h]] + [ref[kv, 0, h % share] for ref in far]
-            return tn(own, kv_ref[kv, u, :, cols]) + tn(memory, jnp.concatenate(rows, 0))
-
-        att = whole(1, weights_low, w_ref[h % share, :, side]).astype(BF16)
-        gq = whole(0, grad_scores, d_ref[h % share, :, side]).astype(BF16)
+            return tn(own, kv_ref[kv, u, :, cols]) + tn(memory, memory_rows(kv, h, slots))
+
+        att = whole(1, weights_low, w_ref[h, :, side]).astype(BF16)
+        gq = whole(0, grad_scores, d_ref[h, :, side]).astype(BF16)
         if u == 0:
             att_ref[:, cols] = att
             gq_ref[:, cols] = gq
@@ -301,22 +282,18 @@
     staged([(h, u) for h in range(heads) for u in range(2)], first, second, third, 4)
 
 
-def sum_kernel(kt_ref, vt_ref, *refs):
-    mg_ref, mine_ref, other_ref = refs[-3:]
-    pieces = [refs[i : i + 3] for i in range(0, len(refs) - 3, 3)]
+def sum_kernel(kt_ref, vt_ref, t0_ref, b4_ref, b2_ref, mg_ref, mine_ref, other_ref):
     count = mine_ref.shape[0] * 2
     feat = mine_ref.shape[2]
     even = lax.axis_index("seq") % 2 == 0
-    share, slot = pieces[0][0].shape[1:3]
     terms = jnp.zeros((kt_ref.shape[0], feat), F32)
     for kv, turned_ref in enumerate((kt_ref, vt_ref)):
         rows = []
         for u in range(2):
-            for i, (t0_ref, a_ref, b_ref) in enumerate(pieces):
-                near = jnp.where(even == (u == 0), t0_ref[kv], 0.0)
-                low = (near + a_ref[u, kv].astype(F32) + b_ref[u, kv].astype(F32)).astype(BF16)
-                mg_ref[kv, u, i * share : (i + 1) * share] = low
-                rows.append(low.reshape(share * slot, feat))
+            low = jnp.where(even == (u == 0), t0_ref[kv], 0.0)
+            low = (low + b2_ref[u, kv].astype(F32) + b4_ref[u, kv].astype(F32)).astype(BF16)
+            mg_ref[kv, u] = low
+            rows.append(low.reshape(-1, feat))
         terms = terms + nn(turned_ref[...], jnp.concatenate(rows, 0))
     rows = terms.shape[0] // count
     bits = count.bit_length() - 1
@@ -383,7 +360,6 @@
     feat = compress_kernel.shape[1]
     heads = width // feat
     half = heads // 2
-    share = half // PIECES
     slot = seg // TAPS
     span = BLOCKS * slot
     count = lax.axis_size("seq")
@@ -398,8 +374,11 @@
     def shift(value, steps):
         return lax.ppermute(value, "seq", [(s, (s + steps) % count) for s in range(count)])
 
-    def trade(value):
-        return lax.ppermute(value, "seq", [(s, s ^ 1) for s in range(count)])
+    def cross(value, steps):
+        return lax.ppermute(value, "seq", [(s, ((s ^ 1) + steps) % count) for s in range(count)])
+
+    def trade(value, flip=1):
+        return lax.ppermute(value, "seq", [(s, s ^ flip) for s in range(count)])
 
     def in_hbm(value):
         return pltpu.with_memory_space_constraint(value, pltpu.HBM)
@@ -410,32 +389,30 @@
     def full(dims):
         return pl.BlockSpec(dims, lambda i: (0,) * len(dims))
 
-    scalars = pl.BlockSpec(memory_space=pltpu.SMEM)
     mine_cols = pl.BlockSpec((seg, half * feat), lambda i: (0, side()))
-    other_cols = pl.BlockSpec((seg, half * feat), lambda i: (0, 1 - side()))
-    far = pl.BlockSpec((2, 1, share, slot, feat), lambda i: (0, side(), 0, 0, 0))
     kernel_spec = full(compress_kernel.shape)
 
     hbm = pl.BlockSpec(memory_space=pltpu.HBM)
     rows = 4 * seg + 16
-    *packed, give = call(
+    half_dims = (2, half, slot, feat)
+    packed_mine, packed_other, give = call(
         pack_kernel,
-        [shape((2, 2, share, slot, feat))] * PIECES + [shape((rows, half * feat))],
-        [scalars] + [hbm] * 5,
-        [full((2, 2, share, slot, feat))] * PIECES + [full((rows, half * feat))],
+        (shape(half_dims), shape(half_dims), shape((rows, half * feat))),
+        [full((16, half * feat))] + [hbm] * 5,
+        (full(half_dims), full(half_dims), full((rows, half * feat))),
         3 * unit, 5 * row_bytes,
         scratch=[
-            pltpu.VMEM((2, seg, width), BF16),
+            pltpu.VMEM((2, 2, seg, half * feat), BF16),
             pltpu.VMEM(compress_kernel.shape, BF16),
-            pltpu.SemaphoreType.DMA((4 * PIECES + 5,)),
+            pltpu.SemaphoreType.DMA((7,)),
         ],
-    )(memory_reach, *[in_hbm(a) for a in (k, v, q, g, compress_kernel)])
+    )(jnp.full((16, half * feat), memory_reach[0, 0].astype(BF16)), *[in_hbm(a) for a in (k, v, q, g, compress_kernel)])
     got = trade(give)
 
-    r2, r4 = [], []
-    for piece in packed:
-        r2.append(shift(piece, 2))
-        r4.append(shift(piece, 4))
+    r4 = shift(packed_mine, 4)
+    r2 = shift(packed_mine, 2)
+    r4s = cross(packed_other, 4)
+    r2s = cross(packed_other, 2)
     kvp, near, own_stats, kt, vt, bias = call(
         own_kernel,
         (
@@ -446,7 +423,12 @@
             shape((TAPS * feat, heads * slot)),
             shape((span, 2 * seg), F32),
         ),
-        [scalars] + [mine_cols] * 4 + [full((rows, half * feat)), kernel_spec],
+        [mine_cols] * 4
+        + [
+            pl.BlockSpec((16, seg), lambda i: (4 * seg // 16, 0)),
+            full((rows, half * feat)),
+            kernel_spec,
+        ],
         (
             full((2, 2, seg, half * feat)),
             full((2, half, slot, feat)),
@@ -455,54 +437,27 @@
             full((TAPS * feat, heads * slot)),
             full((span, 2 * seg)),
         ),
-        5 * unit, 8 * row_bytes, heads * seg * seg,
-    )(memory_reach, k, v, q, g, got, compress_kernel)
-
-    pieces, sums, terms = [], [], []
-    for i in range(PIECES):
-        if i == 0:
-            first2, own_stats, near = lax.optimization_barrier((r2[0], own_stats, near))
-            r2[0] = first2
-        else:
-            r2[i], r4[i], t2, t4 = lax.optimization_barrier((r2[i], r4[i], *terms[-1]))
-            terms[-1] = (t2, t4)
-        slots = [r2[i], trade(r2[i]), r4[i], trade(r4[i])]
-        cols = pl.BlockSpec((seg, share * feat), lambda s, i=i: (0, side() * PIECES + i))
-        got_q = pl.BlockSpec((seg, share * feat), lambda s, i=i: (2, i))
-        got_g = pl.BlockSpec((seg, share * feat), lambda s, i=i: (3, i))
-        stats = pl.BlockSpec((3, share, 1, 2 * seg), lambda s, i=i: (0, i, 0, 0))
-        near_spec = pl.BlockSpec((2, share, slot, feat), lambda s, i=i: (0, i, 0, 0))
-        t0, t2, t4, w_mem, d_mem, final = call(
-            memory_kernel,
-            (
-                shape((2, share, slot, feat), F32),
-                shape((2, 2, share, slot, feat)),
-                shape((2, 2, share, slot, feat)),
-                shape((share, span, 2 * seg)),
-                shape((share, span, 2 * seg)),
-                shape((3, share, 1, 2 * seg), F32),
-            ),
-            [full((span, 2 * seg)), cols, got_q, cols, got_g, stats, near_spec] + [far] * 4,
-            (
-                full((2, share, slot, feat)),
-                full((2, 2, share, slot, feat)),
-                full((2, 2, share, slot, feat)),
-                full((share, span, 2 * seg)),
-                full((share, span, 2 * seg)),
-                full((3, share, 1, 2 * seg)),
-            ),
-            4 * unit // PIECES, 8 * row_bytes // PIECES, heads * seg * seg,
-        )(bias, q, got, g, got, own_stats, near, *slots)
-        sums.append([t0])
-        terms.append((t2, t4))
-        pieces.append([*slots, w_mem, d_mem, final])
-
-    for total, (t2, t4) in zip(sums, terms):
-        total += [shift(t2, -2), shift(t4, -4)]
-    piece_specs = [
-        far, far, far, far,
-        full((share, span, 2 * seg)), full((share, span, 2 * seg)), full((3, share, 1, 2 * seg)),
-    ]
+        unit, 8 * row_bytes, heads * seg * seg,
+    )(k, v, q, g, give, got, compress_kernel)
+
+    slots = [near, r2, r2s, r4, r4s]
+    got_q = pl.BlockSpec((seg, half * feat), lambda i: (2, 0))
+    got_g = pl.BlockSpec((seg, half * feat), lambda i: (3, 0))
+    one = (2, half, slot, feat)
+    soft = (half, span, 2 * seg)
+    stats = (3, half, 1, 2 * seg)
+    pair = (2, 2, half, slot, feat)
+    t0, t2, t4, w_mem, d_mem, final = call(
+        memory_kernel,
+        (shape(one, F32), *[shape(pair)] * 2, shape(soft), shape(soft), shape(stats, F32)),
+        [full((span, 2 * seg)), mine_cols, got_q, mine_cols, got_g, full(stats)]
+        + [full(one)] * BLOCKS,
+        (full(one), *[full(pair)] * 2, full(soft), full(soft), full(stats)),
+        4 * unit, 8 * row_bytes, heads * seg * seg,
+    )(bias, q, got, g, got, own_stats, *slots)
+
+    back4 = shift(t4, -4)
+    back2 = shift(t2, -2)
     attended, grad_queries, give_first, own_terms = call(
         output_kernel,
         (
@@ -511,21 +466,16 @@
             shape((2, seg, half * feat)),
             shape((2, 2, seg, half * feat), F32),
         ),
-        [
-            mine_cols,
-            pl.BlockSpec((seg, half * feat), lambda i: (2, 0)),
-            mine_cols,
-            pl.BlockSpec((seg, half * feat), lambda i: (3, 0)),
-        ]
-        + [full((2, 2, seg, half * feat)), full((2, half, slot, feat))]
-        + piece_specs * PIECES,
+        [mine_cols, got_q, mine_cols, got_g, full((2, 2, seg, half * feat))]
+        + [full(one)] * BLOCKS
+        + [full(soft), full(soft), full(stats)],
         (
             mine_cols, mine_cols,
             full((2, seg, half * feat)),
             full((2, 2, seg, half * feat)),
         ),
         8 * unit, 12 * row_bytes, heads * seg * seg,
-    )(q, got, g, got, kvp, near, *[a for piece in pieces for a in piece])
+    )(q, got, g, got, kvp, *slots, w_mem, d_mem, final)
 
     def finish(a, b, give):
         anywhere = pl.BlockSpec(memory_space=pl.ANY)
@@ -540,26 +490,22 @@
         )(a, b, trade(give))
 
     attended, grad_queries = finish(attended, grad_queries, give_first)
-    sums[-1][2], own_terms = lax.optimization_barrier((sums[-1][2], own_terms))
+    back2, own_terms = lax.optimization_barrier((back2, own_terms))
     kernel_rows = compress_kernel.shape[0]
-    half_dims = (count // 2, kernel_rows // count, feat)
-    sum_specs = [
-        full((2, share, slot, feat)),
-        full((2, 2, share, slot, feat)),
-        full((2, 2, share, slot, feat)),
-    ]
+    split = (count // 2, kernel_rows // count, feat)
+    turned = full((TAPS * feat, heads * slot))
     memory_grads, mine, other = call(
         sum_kernel,
-        (shape((2, 2, half, slot, feat)), shape(half_dims, F32), shape(half_dims, F32)),
-        [full((TAPS * feat, heads * slot))] * 2 + sum_specs * PIECES,
-        (full((2, 2, half, slot, feat)), full(half_dims), full(half_dims)),
+        (shape(pair), shape(split, F32), shape(split, F32)),
+        [turned] * 2 + [full(one)] + [full(pair)] * 2,
+        (full(pair), full(split), full(split)),
         unit, 4 * row_bytes,
-    )(kt, vt, *[a for piece in sums for a in piece])
+    )(kt, vt, t0, back4, back2)
 
     grad_keys, grad_values, give_last = call(
         back_kernel,
         (shape((seg, width)), shape((seg, width)), shape((2, seg, half * feat))),
-        [full((2, 2, half, slot, feat)), kernel_spec, full((2, 2, seg, half * feat))],
+        [full(pair), kernel_spec, full((2, 2, seg, half * feat))],
         (mine_cols, mine_cols, full((2, seg, half * feat))),
         4 * unit, 7 * row_bytes,
     )(memory_grads, compress_kernel, own_terms)

time: 57.2 us -> 51.7 us (0.904)
  waiting for transfers between devices: 27.5 us -> 14.4 us
  starting transfers between devices: 15.3 us -> 22.9 us
    ppermute x4, waiting for transfers between devices: 20 us -> 5.73 us  [shift(): lax.ppermute(value, 'seq', [(s, (s + steps) % count) for s in range(count)])]
    ppermute x4, starting transfers between devices: 5.98 us -> 10.4 us  [shift(): lax.ppermute(value, 'seq', [(s, (s + steps) % count) for s in range(count)])]
    ppermute x6, starting transfers between devices: 1.09 us -> 3.65 us  [the longest x2 2.56 us: cross(): lax.ppermute(value, 'seq', [(s, ((s ^ 1) + steps) % count) for s in range...]
    ppermute x6, waiting for transfers between devices: 1.54 us -> 3.72 us  [the longest x2 3.71 us: cross(): lax.ppermute(value, 'seq', [(s, ((s ^ 1) + steps) % count) for s in range...]
    ppermute x6, waiting for transfers between devices: 6.01 us -> 4.93 us  [reduce_rest(): arrived.append(lax.ppermute(sent, ('seq', 'dp'), pairs))]
    ppermute x6, starting transfers between devices: 8.23 us -> 8.92 us  [reduce_rest(): arrived.append(lax.ppermute(sent, ('seq', 'dp'), pairs))]
  transfers between devices with their start and end apart: 16 -> 16, of which waited for: 7 -> 7; matrix products, arithmetic and copies ran while one was open for 0% -> 0% of each run, Pallas kernels for 14% -> 15%
where the time goes in v4:
time: 51.7 us; the launch traced here: 51.5 us
  starting transfers between devices  22.9 us (44%)
  waiting for transfers between devices  14.4 us (28%)
  Pallas kernels  12.1 us (23%)
  between operations  1.46 us (3%)
  other arithmetic  0.64 us (1%)
    ppermute x4, starting transfers between devices, shift(): lax.ppermute(value, 'seq', [(s, (s + steps) % count) for s in range(count)])  10.4 us
    ppermute x6, starting transfers between devices, reduce_rest(): arrived.append(lax.ppermute(sent, ('seq', 'dp'), pairs))  8.92 us
    ppermute x4, waiting for transfers between devices, shift(): lax.ppermute(value, 'seq', [(s, (s + steps) % count) for s in range(count)])  5.73 us
    ppermute x6, waiting for transfers between devices, reduce_rest(): arrived.append(lax.ppermute(sent, ('seq', 'dp'), pairs))  4.93 us
    ppermute x2, waiting for transfers between devices, cross(): lax.ppermute(value, 'seq', [(s, ((s ^ 1) + steps) % count) for s in range...  3.71 us
    pallas_call x1, Pallas kernels, local(): call(output_kernel, (shape((seg, width)), shape((seg, width)), shape((2,...  2.82 us
    pallas_call x1, Pallas kernels, local(): call(pack_kernel, (shape(half_dims), shape(half_dims), shape((rows, half...  2.73 us
    ppermute x2, starting transfers between devices, cross(): lax.ppermute(value, 'seq', [(s, ((s ^ 1) + steps) % count) for s in range...  2.56 us
  transfers between devices with their start and end apart: 16, of which 7 were waited for; matrix products, arithmetic and copies ran while one was open for 0% of the time, Pallas kernels for 15%

profile of v4, /device:TPU:0, one launch (start us, length us, event | category | flops | bytes accessed | tf_op | source)
XLA Modules:
  0.0 51.5 jit_solution(8666406170054514599)
XLA Ops:
  1.4 2.7 %shard_map.101 = (bf16[2,8,32,128]{3,2,1,0:T(8,128)(2,1)S(1)}, bf16[2,8,32,128]{3,2,1,0:T(8,128)(2,1)S(1)}, bf16[528,1024]{1,0:T(8,128)(2,1)S(1)}) custom-call(bf16[16,1024]{1,0:T(8,128)(2,1)S(1)} %broadcast_in_dim.15.reach_ref, bf16[128,2048]{1,0:T(8,128)(2,1)} %bitcast.32, bf16[128,2048]{1,0:T(8,128)(2,1)} %bitcast.34, bf16[128,2048]{1,0:T(8,128)(2,1)} %bitcast.24, ...), custom_call_target="tpu_custom_call" | custom-call | flops 201326592 | bytes 2621440 | tf_op jit(solution)/shard_map/pallas_call | solution.py:398
  4.6 2.5 %collective-permute-start.1 = (bf16[2,8,32,128]{3,2,1,0:T(8,128)(2,1)S(1)}, bf16[2,8,32,128]{3,2,1,0:T(8,128)(2,1)S(1)}, u32[]{:S(2)}, u32[]{:S(2)}) collective-permute-start(bf16[2,8,32,128]{3,2,1,0:T(8,128)(2,1)S(1)} %get-tuple-element.48), channel_id=1, source_target_pairs={{0,4},{2,6},{4,8},{6,10},{8,12},{10,14},{12,16},{14,18},{16,20},{1... | collective-permute-start | bytes 393224 | tf_op jit(solution)/shard_map/ppermute | solution.py:375
  7.2 1.3 %collective-permute-start.2 = (bf16[2,8,32,128]{3,2,1,0:T(8,128)(2,1)S(1)}, bf16[2,8,32,128]{3,2,1,0:T(8,128)(2,1)S(1)}, u32[]{:S(2)}, u32[]{:S(2)}) collective-permute-start(bf16[2,8,32,128]{3,2,1,0:T(8,128)(2,1)S(1)} %get-tuple-element.49), channel_id=1, source_target_pairs={{0,6},{2,4},{4,10},{6,8},{8,14},{10,12},{12,18},{14,16},{16,22},{1... | collective-permute-start | bytes 393224 | tf_op jit(solution)/shard_map/ppermute | solution.py:378
  8.5 1.6 %collective-permute-start.3 = (bf16[2,8,32,128]{3,2,1,0:T(8,128)(2,1)S(1)}, bf16[2,8,32,128]{3,2,1,0:T(8,128)(2,1)S(1)}, u32[]{:S(2)}, u32[]{:S(2)}) collective-permute-start(bf16[2,8,32,128]{3,2,1,0:T(8,128)(2,1)S(1)} %get-tuple-element.48), channel_id=1, source_target_pairs={{0,8},{2,10},{4,12},{6,14},{8,16},{10,18},{12,20},{14,22},{16,24},... | collective-permute-start | bytes 393224 | tf_op jit(solution)/shard_map/ppermute | solution.py:375
  10.1 1.2 %collective-permute-start.4 = (bf16[2,8,32,128]{3,2,1,0:T(8,128)(2,1)S(1)}, bf16[2,8,32,128]{3,2,1,0:T(8,128)(2,1)S(1)}, u32[]{:S(2)}, u32[]{:S(2)}) collective-permute-start(bf16[2,8,32,128]{3,2,1,0:T(8,128)(2,1)S(1)} %get-tuple-element.49), channel_id=1, source_target_pairs={{0,10},{2,8},{4,14},{6,12},{8,18},{10,16},{12,22},{14,20},{16,26},... | collective-permute-start | bytes 393224 | tf_op jit(solution)/shard_map/ppermute | solution.py:378
  11.3 1.2 %shard_map.102 = (bf16[2,2,128,1024]{3,2,1,0:T(8,128)(2,1)S(1)}, bf16[2,8,32,128]{3,2,1,0:T(8,128)(2,1)S(1)}, f32[3,8,1,256]{3,2,1,0:T(1,128)S(1)}, bf16[512,512...) custom-call(bf16[128,2048]{1,0:T(8,128)(2,1)S(1)} %bitcast.33, ...), custom_call_target="tpu_custom_call" | custom-call | flops 67108864 | bytes 4194304 | tf_op jit(solution)/shard_map/pallas_call | solution.py:416
  12.6 2.0 %collective-permute-done.1.r2_ref.refs_6_ = bf16[2,8,32,128]{3,2,1,0:T(8,128)(2,1)S(1)} collective-permute-done((bf16[2,8,32,128]{3,2,1,0:T(8,128)(2,1)S(1)}, bf16[2,8,32,128]{3,2,1,0:T(8,128)(2,1)S(1)}, u32[]{:S(2)}, u32[]{:S(2)}) %collective-permute-start.1) | collective-permute-done | bytes 131104 | tf_op jit(solution)/shard_map/ppermute | solution.py:375
  14.6 2.3 %collective-permute-done.2.r2s_ref.refs_7_ = bf16[2,8,32,128]{3,2,1,0:T(8,128)(2,1)S(1)} collective-permute-done((bf16[2,8,32,128]{3,2,1,0:T(8,128)(2,1)S(1)}, bf16[2,8,32,128]{3,2,1,0:T(8,128)(2,1)S(1)}, u32[]{:S(2)}, u32[]{:S(2)}) %collective-permute-start.2) | collective-permute-done | bytes 131104 | tf_op jit(solution)/shard_map/ppermute | solution.py:378
  16.9 1.4 %collective-permute-done.4.r4s_ref.refs_9_ = bf16[2,8,32,128]{3,2,1,0:T(8,128)(2,1)S(1)} collective-permute-done((bf16[2,8,32,128]{3,2,1,0:T(8,128)(2,1)S(1)}, bf16[2,8,32,128]{3,2,1,0:T(8,128)(2,1)S(1)}, u32[]{:S(2)}, u32[]{:S(2)}) %collective-permute-start.4) | collective-permute-done | bytes 131104 | tf_op jit(solution)/shard_map/ppermute | solution.py:378
  18.3 1.4 %shard_map.103 = (f32[2,8,32,128]{3,2,1,0:T(8,128)S(1)}, bf16[2,2,8,32,128]{4,3,2,1,0:T(8,128)(2,1)S(1)}, bf16[2,2,8,32,128]{4,3,2,1,0:T(8,128)(2,1)S(1)}, bf16[...) custom-call(f32[160,256]{1,0:T(8,128)S(1)} %get-tuple-element.45.bias_ref, ...), custom_call_target="tpu_custom_call" | custom-call | flops 268435456 | bytes 4194304 | tf_op jit(solution)/shard_map/pallas_call | solution.py:450
  20.2 5.7 %collective-permute-start.6 = (bf16[2,2,8,32,128]{4,3,2,1,0:T(8,128)(2,1)S(1)}, bf16[2,2,8,32,128]{4,3,2,1,0:T(8,128)(2,1)S(1)}, u32[]{:S(2)}, u32[]{:S(2)}) collective-permute-start(bf16[2,2,8,32,128]{4,3,2,1,0:T(8,128)(2,1)S(1)} %get-tuple-element.52), channel_id=1, source_target_pairs={{0,28},{2,30},{4,0},{6,2},{8,4},{10,6},{12,8},{14,10},{16,12},{18,... | collective-permute-start | bytes 786440 | tf_op jit(solution)/shard_map/ppermute | solution.py:375
  25.9 2.8 %shard_map.104 = (bf16[128,2048]{1,0:T(8,128)(2,1)}, bf16[128,2048]{1,0:T(8,128)(2,1)}, bf16[2,128,1024]{2,1,0:T(8,128)(2,1)S(1)}, f32[2,2,128,1024]{3,2,1,0:T(8,128)S(1)}) custom-call(bf16[128,2048]{1,0:T(8,128)(2,1)S(1)} %bitcast.27, bf16[528,1024]{1,0:T(8,128)(2,1)S(1)} %collective-permute-done.got_ref.qs_ref.gs_ref.refs_1_.refs_3_, ...), custom_call_target="tpu_custom_call" | custom-call | flops 536870912 | bytes 6291456 | tf_op jit(solution)/shard_map/pallas_call | solution.py:461
  28.8 3.8 %collective-permute-done.6.b2_ref = bf16[2,2,8,32,128]{4,3,2,1,0:T(8,128)(2,1)S(1)} collective-permute-done((bf16[2,2,8,32,128]{4,3,2,1,0:T(8,128)(2,1)S(1)}, bf16[2,2,8,32,128]{4,3,2,1,0:T(8,128)(2,1)S(1)}, u32[]{:S(2)}, u32[]{:S(2)}) %collective-permute-start.6) | collective-permute-done | bytes 262176 | tf_op jit(solution)/shard_map/ppermute | solution.py:375
  33.1 1.8 %shard_map.107 = (bf16[128,2048]{1,0:T(8,128)(2,1)}, bf16[128,2048]{1,0:T(8,128)(2,1)}, bf16[2,128,1024]{2,1,0:T(8,128)(2,1)S(1)}) custom-call(bf16[2,2,8,32,128]{4,3,2,1,0:T(8,128)(2,1)S(1)} %get-tuple-element.69.mg_ref, bf16[512,128]{1,0:T(8,128)(2,1)S(1)} %copy-done.4, f32[2,2,128,1024]{3,2,1,0:T(8,128)S(1)} %get-tuple-element.70.terms_ref), custom_call_target="tpu_custom_call" | custom-call | flops 268435456 | bytes 3670016 | tf_op jit(solution)/shard_map/pallas_call | solution.py:505
  35.4 1.1 %collective-permute-start.8 = (f32[2,32,128]{2,1,0:T(8,128)S(1)}, f32[2,32,128]{2,1,0:T(8,128)S(1)}, u32[]{:S(2)}, u32[]{:S(2)}) collective-permute-start(f32[2,32,128]{2,1,0:T(8,128)S(1)} %get-tuple-element.81), channel_id=1, source_target_pairs={{0,8},{1,9},{2,10},{3,11},{4,12},{5,13},{6,14},{7,15},{8,0},{9,1},... | collective-permute-start | bytes 98312 | tf_op jit(solution)/shard_map/ppermute | solution.py:554
  36.5 3.4 %collective-permute-start.11 = (f32[2,32,128]{2,1,0:T(8,128)S(1)}, f32[2,32,128]{2,1,0:T(8,128)S(1)}, u32[]{:S(2)}, u32[]{:S(2)}) collective-permute-start(f32[2,32,128]{2,1,0:T(8,128)S(1)} %get-tuple-element.80), channel_id=1, source_target_pairs={{0,12},{1,13},{2,14},{3,15},{4,8},{5,9},{6,10},{7,11},{8,4},{9,5},... | collective-permute-start | bytes 98312 | tf_op jit(solution)/shard_map/ppermute | solution.py:554
  39.8 0.8 %shard_map.106 = (bf16[128,2048]{1,0:T(8,128)(2,1)}, bf16[128,2048]{1,0:T(8,128)(2,1)}) custom-call(bf16[128,2048]{1,0:T(8,128)(2,1)} %get-tuple-element.61.a_in, bf16[128,2048]{1,0:T(8,128)(2,1)} %get-tuple-element.62.b_in, bf16[2,128,1024]{2,1,0:T(8,128)(2,1)S(1)} %collective-permute-done.9.got_ref), custom_call_target="tpu_custom_call", output_to_operand_aliasing={{0}: (0, {}), {1}: (1, {})} | custom-call | bytes 1048576 | tf_op jit(solution)/shard_map/pallas_call | solution.py:482
  40.7 1.4 %collective-permute-done.11 = f32[2,32,128]{2,1,0:T(8,128)S(1)} collective-permute-done((f32[2,32,128]{2,1,0:T(8,128)S(1)}, f32[2,32,128]{2,1,0:T(8,128)S(1)}, u32[]{:S(2)}, u32[]{:S(2)}) %collective-permute-start.11) | collective-permute-done | bytes 32800 | tf_op jit(solution)/shard_map/ppermute | solution.py:554
  42.1 1.7 %collective-permute-done.10 = f32[2,32,128]{2,1,0:T(8,128)S(1)} collective-permute-done((f32[2,32,128]{2,1,0:T(8,128)S(1)}, f32[2,32,128]{2,1,0:T(8,128)S(1)}, u32[]{:S(2)}, u32[]{:S(2)}) %collective-permute-start.10) | collective-permute-done | bytes 32800 | tf_op jit(solution)/shard_map/ppermute | solution.py:554
  43.8 1.6 %collective-permute-start.12 = (f32[1,32,128]{2,1,0:T(8,128)S(1)}, f32[1,32,128]{2,1,0:T(8,128)S(1)}, u32[]{:S(2)}, u32[]{:S(2)}) collective-permute-start(f32[1,32,128]{2,1,0:T(8,128)S(1)} %get-tuple-element.83), channel_id=1, source_target_pairs={{0,1},{1,0},{2,3},{3,2},{4,5},{5,4},{6,7},{7,6},{8,9},{9,8},{10,11... | collective-permute-start | bytes 49160 | tf_op jit(solution)/shard_map/ppermute | solution.py:554
  45.4 0.9 %collective-permute-start.15 = (f32[1,32,128]{2,1,0:T(8,128)S(1)}, f32[1,32,128]{2,1,0:T(8,128)S(1)}, u32[]{:S(2)}, u32[]{:S(2)}) collective-permute-start(f32[1,32,128]{2,1,0:T(8,128)S(1)} %get-tuple-element.82), channel_id=1, source_target_pairs={{0,17},{1,16},{2,19},{3,18},{4,21},{5,20},{6,23},{7,22},{8,25},{9,... | collective-permute-start | bytes 49160 | tf_op jit(solution)/shard_map/ppermute | solution.py:554
  46.2 2.0 %collective-permute-start.14 = (f32[1,32,128]{2,1,0:T(8,128)S(1)}, f32[1,32,128]{2,1,0:T(8,128)S(1)}, u32[]{:S(2)}, u32[]{:S(2)}) collective-permute-start(f32[1,32,128]{2,1,0:T(8,128)S(1)} %get-tuple-element.82), channel_id=1, source_target_pairs={{0,16},{1,17},{2,18},{3,19},{4,20},{5,21},{6,22},{7,23},{8,24},{9,... | collective-permute-start | bytes 49160 | tf_op jit(solution)/shard_map/ppermute | solution.py:554
  48.2 0.8 %shard_map.108 = (bf16[128,2048]{1,0:T(8,128)(2,1)}, bf16[128,2048]{1,0:T(8,128)(2,1)}) custom-call(bf16[128,2048]{1,0:T(8,128)(2,1)} %get-tuple-element.71.a_in, bf16[128,2048]{1,0:T(8,128)(2,1)} %get-tuple-element.72.b_in, bf16[2,128,1024]{2,1,0:T(8,128)(2,1)S(1)} %collective-permute-done.13.got_ref), custom_call_target="tpu_custom_call", output_to_operand_aliasing={{0}: (0, {}), {1}: (1, {})} | custom-call | bytes 1048576 | tf_op jit(solution)/shard_map/pallas_call | solution.py:482
  49.1 1.8 %collective-permute-done.15 = f32[1,32,128]{2,1,0:T(8,128)S(1)} collective-permute-done((f32[1,32,128]{2,1,0:T(8,128)S(1)}, f32[1,32,128]{2,1,0:T(8,128)S(1)}, u32[]{:S(2)}, u32[]{:S(2)}) %collective-permute-start.15) | collective-permute-done | bytes 16416 | tf_op jit(solution)/shard_map/ppermute | solution.py:554
  (32 shorter events, 2.8 us)
Async XLA Ops:
  1.3 10.0 %copy-start = (bf16[1,128,2048]{2,1,0:T(8,128)(2,1)S(1)}, bf16[1,128,2048]{2,1,0:T(8,128)(2,1)}, u32[]{:S(2)}) copy-start(bf16[1,128,2048]{2,1,0:T(8,128)(2,1)} %param.6) | copy-start | bytes 1572868
  1.3 10.0 %copy-start.1 = (bf16[1,128,2048]{2,1,0:T(8,128)(2,1)S(1)}, bf16[1,128,2048]{2,1,0:T(8,128)(2,1)}, u32[]{:S(2)}) copy-start(bf16[1,128,2048]{2,1,0:T(8,128)(2,1)} %param.9) | copy-start | bytes 1572868
  1.3 10.0 %copy-start.2 = (bf16[1,128,2048]{2,1,0:T(8,128)(2,1)S(1)}, bf16[1,128,2048]{2,1,0:T(8,128)(2,1)}, u32[]{:S(2)}) copy-start(bf16[1,128,2048]{2,1,0:T(8,128)(2,1)} %param.7) | copy-start | bytes 1572868
  1.3 10.0 %copy-start.3 = (bf16[1,128,2048]{2,1,0:T(8,128)(2,1)S(1)}, bf16[1,128,2048]{2,1,0:T(8,128)(2,1)}, u32[]{:S(2)}) copy-start(bf16[1,128,2048]{2,1,0:T(8,128)(2,1)} %param.8) | copy-start | bytes 1572868
  1.3 10.0 %copy-start.4 = (bf16[512,128]{1,0:T(8,128)(2,1)S(1)}, bf16[512,128]{1,0:T(8,128)(2,1)}, u32[]{:S(2)}) copy-start(bf16[512,128]{1,0:T(8,128)(2,1)} %w_ref.3) | copy-start | bytes 393220
  4.1 7.2 %collective-permute-start = (bf16[528,1024]{1,0:T(8,128)(2,1)S(1)}, bf16[528,1024]{1,0:T(8,128)(2,1)S(1)}, u32[]{:S(2)}, u32[]{:S(2)}) collective-permute-start(bf16[528,1024]{1,0:T(8,128)(2,1)S(1)} %get-tuple-element.42.reach_ref), channel_id=1, source_target_pairs={{0,2},{2,0},{4,6},{6,4},{8,10},{10,8},{12,14},{14,12},{16,18},{18,... | collective-permute-start | bytes 3244040 | tf_op jit(solution)/shard_map/ppermute | solution.py:381
  4.6 9.9 %collective-permute-start.1 = (bf16[2,8,32,128]{3,2,1,0:T(8,128)(2,1)S(1)}, bf16[2,8,32,128]{3,2,1,0:T(8,128)(2,1)S(1)}, u32[]{:S(2)}, u32[]{:S(2)}) collective-permute-start(bf16[2,8,32,128]{3,2,1,0:T(8,128)(2,1)S(1)} %get-tuple-element.48), channel_id=1, source_target_pairs={{0,4},{2,6},{4,8},{6,10},{8,12},{10,14},{12,16},{14,18},{16,20},{1... | collective-permute-start | bytes 393224 | tf_op jit(solution)/shard_map/ppermute | solution.py:375
  7.2 9.7 %collective-permute-start.2 = (bf16[2,8,32,128]{3,2,1,0:T(8,128)(2,1)S(1)}, bf16[2,8,32,128]{3,2,1,0:T(8,128)(2,1)S(1)}, u32[]{:S(2)}, u32[]{:S(2)}) collective-permute-start(bf16[2,8,32,128]{3,2,1,0:T(8,128)(2,1)S(1)} %get-tuple-element.49), channel_id=1, source_target_pairs={{0,6},{2,4},{4,10},{6,8},{8,14},{10,12},{12,18},{14,16},{16,22},{1... | collective-permute-start | bytes 393224 | tf_op jit(solution)/shard_map/ppermute | solution.py:378
  8.5 8.4 %collective-permute-start.3 = (bf16[2,8,32,128]{3,2,1,0:T(8,128)(2,1)S(1)}, bf16[2,8,32,128]{3,2,1,0:T(8,128)(2,1)S(1)}, u32[]{:S(2)}, u32[]{:S(2)}) collective-permute-start(bf16[2,8,32,128]{3,2,1,0:T(8,128)(2,1)S(1)} %get-tuple-element.48), channel_id=1, source_target_pairs={{0,8},{2,10},{4,12},{6,14},{8,16},{10,18},{12,20},{14,22},{16,24},... | collective-permute-start | bytes 393224 | tf_op jit(solution)/shard_map/ppermute | solution.py:375
  10.1 8.2 %collective-permute-start.4 = (bf16[2,8,32,128]{3,2,1,0:T(8,128)(2,1)S(1)}, bf16[2,8,32,128]{3,2,1,0:T(8,128)(2,1)S(1)}, u32[]{:S(2)}, u32[]{:S(2)}) collective-permute-start(bf16[2,8,32,128]{3,2,1,0:T(8,128)(2,1)S(1)} %get-tuple-element.49), channel_id=1, source_target_pairs={{0,10},{2,8},{4,14},{6,12},{8,18},{10,16},{12,22},{14,20},{16,26},... | collective-permute-start | bytes 393224 | tf_op jit(solution)/shard_map/ppermute | solution.py:378
  19.7 12.8 %collective-permute-start.5 = (bf16[2,2,8,32,128]{4,3,2,1,0:T(8,128)(2,1)S(1)}, bf16[2,2,8,32,128]{4,3,2,1,0:T(8,128)(2,1)S(1)}, u32[]{:S(2)}, u32[]{:S(2)}) collective-permute-start(bf16[2,2,8,32,128]{4,3,2,1,0:T(8,128)(2,1)S(1)} %get-tuple-element.51), channel_id=1, source_target_pairs={{0,24},{2,26},{4,28},{6,30},{8,0},{10,2},{12,4},{14,6},{16,8},{18,... | collective-permute-start | bytes 786440 | tf_op jit(solution)/shard_map/ppermute | solution.py:375
  20.2 12.3 %collective-permute-start.6 = (bf16[2,2,8,32,128]{4,3,2,1,0:T(8,128)(2,1)S(1)}, bf16[2,2,8,32,128]{4,3,2,1,0:T(8,128)(2,1)S(1)}, u32[]{:S(2)}, u32[]{:S(2)}) collective-permute-start(bf16[2,2,8,32,128]{4,3,2,1,0:T(8,128)(2,1)S(1)} %get-tuple-element.52), channel_id=1, source_target_pairs={{0,28},{2,30},{4,0},{6,2},{8,4},{10,6},{12,8},{14,10},{16,12},{18,... | collective-permute-start | bytes 786440 | tf_op jit(solution)/shard_map/ppermute | solution.py:375
  28.8 11.1 %collective-permute-start.9 = (bf16[2,128,1024]{2,1,0:T(8,128)(2,1)S(1)}, bf16[2,128,1024]{2,1,0:T(8,128)(2,1)S(1)}, u32[]{:S(2)}, u32[]{:S(2)}) collective-permute-start(bf16[2,128,1024]{2,1,0:T(8,128)(2,1)S(1)} %get-tuple-element.63), channel_id=1, source_target_pairs={{0,2},{2,0},{4,6},{6,4},{8,10},{10,8},{12,14},{14,12},{16,18},{18,... | collective-permute-start | bytes 1572872 | tf_op jit(solution)/shard_map/ppermute | solution.py:381
  33.0 2.3 %collective-permute-start.7 = (f32[8,32,128]{2,1,0:T(8,128)S(1)}, f32[8,32,128]{2,1,0:T(8,128)S(1)}, u32[]{:S(2)}, u32[]{:S(2)}) collective-permute-start(f32[8,32,128]{2,1,0:T(8,128)S(1)} %get-tuple-element.60), channel_id=1, source_target_pairs={{0,2},{2,0},{4,6},{6,4},{8,10},{10,8},{12,14},{14,12},{16,18},{18,... | collective-permute-start | bytes 393224 | tf_op jit(solution)/shard_map/ppermute | solution.py:381
  34.8 13.4 %collective-permute-start.13 = (bf16[2,128,1024]{2,1,0:T(8,128)(2,1)S(1)}, bf16[2,128,1024]{2,1,0:T(8,128)(2,1)S(1)}, u32[]{:S(2)}, u32[]{:S(2)}) collective-permute-start(bf16[2,128,1024]{2,1,0:T(8,128)(2,1)S(1)} %get-tuple-element.73), channel_id=1, source_target_pairs={{0,2},{2,0},{4,6},{6,4},{8,10},{10,8},{12,14},{14,12},{16,18},{18,... | collective-permute-start | bytes 1572872 | tf_op jit(solution)/shard_map/ppermute | solution.py:381
  35.4 5.3 %collective-permute-start.8 = (f32[2,32,128]{2,1,0:T(8,128)S(1)}, f32[2,32,128]{2,1,0:T(8,128)S(1)}, u32[]{:S(2)}, u32[]{:S(2)}) collective-permute-start(f32[2,32,128]{2,1,0:T(8,128)S(1)} %get-tuple-element.81), channel_id=1, source_target_pairs={{0,8},{1,9},{2,10},{3,11},{4,12},{5,13},{6,14},{7,15},{8,0},{9,1},... | collective-permute-start | bytes 98312 | tf_op jit(solution)/shard_map/ppermute | solution.py:554
  36.5 5.6 %collective-permute-start.11 = (f32[2,32,128]{2,1,0:T(8,128)S(1)}, f32[2,32,128]{2,1,0:T(8,128)S(1)}, u32[]{:S(2)}, u32[]{:S(2)}) collective-permute-start(f32[2,32,128]{2,1,0:T(8,128)S(1)} %get-tuple-element.80), channel_id=1, source_target_pairs={{0,12},{1,13},{2,14},{3,15},{4,8},{5,9},{6,10},{7,11},{8,4},{9,5},... | collective-permute-start | bytes 98312 | tf_op jit(solution)/shard_map/ppermute | solution.py:554
  39.8 3.9 %collective-permute-start.10 = (f32[2,32,128]{2,1,0:T(8,128)S(1)}, f32[2,32,128]{2,1,0:T(8,128)S(1)}, u32[]{:S(2)}, u32[]{:S(2)}) collective-permute-start(f32[2,32,128]{2,1,0:T(8,128)S(1)} %get-tuple-element.79), channel_id=1, source_target_pairs={{0,4},{1,5},{2,6},{3,7},{4,0},{5,1},{6,2},{7,3},{8,12},{9,13},{10,... | collective-permute-start | bytes 98312 | tf_op jit(solution)/shard_map/ppermute | solution.py:554
  43.8 5.3 %collective-permute-start.12 = (f32[1,32,128]{2,1,0:T(8,128)S(1)}, f32[1,32,128]{2,1,0:T(8,128)S(1)}, u32[]{:S(2)}, u32[]{:S(2)}) collective-permute-start(f32[1,32,128]{2,1,0:T(8,128)S(1)} %get-tuple-element.83), channel_id=1, source_target_pairs={{0,1},{1,0},{2,3},{3,2},{4,5},{5,4},{6,7},{7,6},{8,9},{9,8},{10,11... | collective-permute-start | bytes 49160 | tf_op jit(solution)/shard_map/ppermute | solution.py:554
  45.4 5.5 %collective-permute-start.15 = (f32[1,32,128]{2,1,0:T(8,128)S(1)}, f32[1,32,128]{2,1,0:T(8,128)S(1)}, u32[]{:S(2)}, u32[]{:S(2)}) collective-permute-start(f32[1,32,128]{2,1,0:T(8,128)S(1)} %get-tuple-element.82), channel_id=1, source_target_pairs={{0,17},{1,16},{2,19},{3,18},{4,21},{5,20},{6,23},{7,22},{8,25},{9,... | collective-permute-start | bytes 49160 | tf_op jit(solution)/shard_map/ppermute | solution.py:554
  46.2 4.7 %collective-permute-start.14 = (f32[1,32,128]{2,1,0:T(8,128)S(1)}, f32[1,32,128]{2,1,0:T(8,128)S(1)}, u32[]{:S(2)}, u32[]{:S(2)}) collective-permute-start(f32[1,32,128]{2,1,0:T(8,128)S(1)} %get-tuple-element.82), channel_id=1, source_target_pairs={{0,16},{1,17},{2,18},{3,19},{4,20},{5,21},{6,22},{7,23},{8,24},{9,... | collective-permute-start | bytes 49160 | tf_op jit(solution)/shard_map/ppermute | solution.py:554

commit v5 on v4

--- a/solution.py
+++ b/solution.py
@@ -72,7 +72,7 @@
 
 
 def pack_kernel(
-    reach_ref, k_hbm, v_hbm, q_hbm, g_hbm, w_hbm,
+    k_hbm, v_hbm, q_hbm, g_hbm, w_hbm,
     mine_ref, other_ref, give_ref, rows_ref, w_ref, sems,
 ):
     seg, width = k_hbm.shape
@@ -96,22 +96,22 @@
     copies = [pltpu.make_async_copy(*pair, sems.at[n]) for n, pair in enumerate(pairs)]
     for copy in copies:
         copy.start()
+    sorted_rows = []
     for n, (part, kv) in enumerate(steps):
         copies[n if n < 2 else n + 1].wait()
-        rows = nn(order, rows_ref[part, kv]).astype(BF16)
-        if n == 0:
-            copies[2].wait()
+        sorted_rows.append(nn(order, rows_ref[part, kv]).astype(BF16))
+    copies[2].wait()
+    for (part, kv), rows in zip(steps, sorted_rows):
         packed = nn(tap_rows(rows, heads, feat), w_ref[...]).astype(BF16)
         (mine_ref, other_ref)[part][kv] = packed.reshape(heads, slot, feat)
         if part == 1:
             give_ref[kv * seg : (kv + 1) * seg] = rows_ref[part, kv]
     for copy in copies[5:]:
         copy.wait()
-    give_ref[4 * seg :] = reach_ref[...]
 
 
 def own_kernel(
-    k_ref, v_ref, q_ref, g_ref, reach_ref, got_ref, w_ref,
+    reach_ref, reach_s_ref, k_ref, v_ref, q_ref, g_ref, got_ref, w_ref,
     kv_ref, near_ref, stat_ref, kt_ref, vt_ref, bias_ref,
 ):
     seg, width = q_ref.shape
@@ -123,15 +123,12 @@
     partner = mine + 1 - 2 * (mine % 2)
     even = mine % 2 == 0
     sources = (mine - mine % 2, mine - 2, partner - 2, mine - 4, partner - 4)
-    reach = jnp.broadcast_to(reach_ref[:1].astype(F32), (slot, seg))
-    reach_s = jnp.broadcast_to(got_ref[4 * seg : 4 * seg + 1, :seg].astype(F32), (slot, seg))
     for b, source in enumerate(sources):
-        for u, (reader, limit) in enumerate(((mine, reach), (partner, reach_s))):
+        for u, (reader, limit) in enumerate(((mine, reach_ref), (partner, reach_s_ref))):
             steps = reader - source
-            near_enough = (steps >= 1) & (steps <= 4) & (source >= 0)
-            wanted = jnp.full((slot, seg), jnp.where(near_enough, steps, 9), jnp.int32)
-            bias_ref[b * slot : (b + 1) * slot, u * seg : (u + 1) * seg] = jnp.where(
-                wanted.astype(F32) <= limit, 0.0, MASKED
+            shown = (steps >= 1) & (steps <= jnp.minimum(limit[0, 0], 4)) & (source >= 0)
+            bias_ref[b * slot : (b + 1) * slot, u * seg : (u + 1) * seg] = jnp.full(
+                (slot, seg), jnp.where(shown, 0.0, MASKED), F32
             )
     allowed = causal(seg)
     order = tap_major(seg)
@@ -235,7 +232,8 @@
 def output_kernel(*refs):
     q_ref, qs_ref, g_ref, gs_ref, kv_ref = refs[:5]
     slots = refs[5 : 5 + BLOCKS]
-    w_ref, d_ref, fin_ref, att_ref, gq_ref, give_ref, terms_ref = refs[5 + BLOCKS :]
+    w_ref, d_ref, fin_ref, *results = refs[5 + BLOCKS :]
+    att_ref, gq_ref, givea_ref, giveg_ref, terms_ref = results
     seg, width = q_ref.shape
     feat = slots[0].shape[3]
     heads = width // feat
@@ -276,13 +274,21 @@
             att_ref[:, cols] = att
             gq_ref[:, cols] = gq
         else:
-            give_ref[0, :, cols] = att
-            give_ref[1, :, cols] = gq
+            givea_ref[:, cols] = att
+            giveg_ref[:, cols] = gq
 
     staged([(h, u) for h in range(heads) for u in range(2)], first, second, third, 4)
 
 
-def sum_kernel(kt_ref, vt_ref, t0_ref, b4_ref, b2_ref, mg_ref, mine_ref, other_ref):
+def first_sum_kernel(t0_ref, b4_ref, low_ref):
+    even = lax.axis_index("seq") % 2 == 0
+    for kv in range(2):
+        for u in range(2):
+            low = jnp.where(even == (u == 0), t0_ref[kv], 0.0)
+            low_ref[u, kv] = low + b4_ref[u, kv].astype(F32)
+
+
+def sum_kernel(kt_ref, vt_ref, low_ref, b2_ref, mg_ref, mine_ref, other_ref):
     count = mine_ref.shape[0] * 2
     feat = mine_ref.shape[2]
     even = lax.axis_index("seq") % 2 == 0
@@ -290,8 +296,7 @@
     for kv, turned_ref in enumerate((kt_ref, vt_ref)):
         rows = []
         for u in range(2):
-            low = jnp.where(even == (u == 0), t0_ref[kv], 0.0)
-            low = (low + b2_ref[u, kv].astype(F32) + b4_ref[u, kv].astype(F32)).astype(BF16)
+            low = (low_ref[u, kv] + b2_ref[u, kv].astype(F32)).astype(BF16)
             mg_ref[kv, u] = low
             rows.append(low.reshape(-1, feat))
         terms = terms + nn(turned_ref[...], jnp.concatenate(rows, 0))
@@ -302,10 +307,10 @@
         first = terms[p * rows : (p + 1) * rows]
         second = terms[(p + 1) * rows : (p + 2) * rows]
         mine_ref[spot] = jnp.where(even, first, second)
-        other_ref[spot] = jnp.where(even, second, first)
-
-
-def back_kernel(mg_ref, w_ref, terms_ref, gk_ref, gv_ref, give_ref):
+        other_ref[spot] = jnp.where(even, second, first).astype(BF16)
+
+
+def back_kernel(mg_ref, w_ref, terms_ref, gk_ref, gv_ref, givek_ref, givev_ref):
     seg = terms_ref.shape[2]
     heads, slot, feat = mg_ref.shape[2:]
     restore = tap_major(seg, inverse=True)
@@ -323,16 +328,16 @@
             if u == 0:
                 out_ref[...] = result
             else:
-                give_ref[kv] = result
-
-
-def finish_kernel(a_in, b_in, got_ref, a_ref, b_ref, sems):
+                (givek_ref, givev_ref)[kv][...] = result
+
+
+def finish_kernel(a_in, b_in, got_a, got_b, a_ref, b_ref, sems):
     del a_in, b_in
-    width = got_ref.shape[2]
+    width = got_a.shape[1]
     start = pl.multiple_of((1 - lax.axis_index("seq") % 2) * width, width)
     copies = [
-        pltpu.make_async_copy(got_ref.at[i], dst.at[:, pl.ds(start, width)], sems.at[i])
-        for i, dst in enumerate((a_ref, b_ref))
+        pltpu.make_async_copy(got, dst.at[:, pl.ds(start, width)], sems.at[i])
+        for i, (got, dst) in enumerate(((got_a, a_ref), (got_b, b_ref)))
     ]
     for copy in copies:
         copy.start()
@@ -393,12 +398,12 @@
     kernel_spec = full(compress_kernel.shape)
 
     hbm = pl.BlockSpec(memory_space=pltpu.HBM)
-    rows = 4 * seg + 16
+    rows = 4 * seg
     half_dims = (2, half, slot, feat)
     packed_mine, packed_other, give = call(
         pack_kernel,
         (shape(half_dims), shape(half_dims), shape((rows, half * feat))),
-        [full((16, half * feat))] + [hbm] * 5,
+        [hbm] * 5,
         (full(half_dims), full(half_dims), full((rows, half * feat))),
         3 * unit, 5 * row_bytes,
         scratch=[
@@ -406,13 +411,15 @@
             pltpu.VMEM(compress_kernel.shape, BF16),
             pltpu.SemaphoreType.DMA((7,)),
         ],
-    )(jnp.full((16, half * feat), memory_reach[0, 0].astype(BF16)), *[in_hbm(a) for a in (k, v, q, g, compress_kernel)])
+    )(*[in_hbm(a) for a in (k, v, q, g, compress_kernel)])
     got = trade(give)
 
     r4 = shift(packed_mine, 4)
     r2 = shift(packed_mine, 2)
     r4s = cross(packed_other, 4)
     r2s = cross(packed_other, 2)
+    got, late_reach = lax.optimization_barrier((got, memory_reach))
+    scalar = pl.BlockSpec(memory_space=pltpu.SMEM)
     kvp, near, own_stats, kt, vt, bias = call(
         own_kernel,
         (
@@ -423,12 +430,7 @@
             shape((TAPS * feat, heads * slot)),
             shape((span, 2 * seg), F32),
         ),
-        [mine_cols] * 4
-        + [
-            pl.BlockSpec((16, seg), lambda i: (4 * seg // 16, 0)),
-            full((rows, half * feat)),
-            kernel_spec,
-        ],
+        [scalar] * 2 + [mine_cols] * 4 + [full((rows, half * feat)), kernel_spec],
         (
             full((2, 2, seg, half * feat)),
             full((2, half, slot, feat)),
@@ -438,7 +440,7 @@
             full((span, 2 * seg)),
         ),
         unit, 8 * row_bytes, heads * seg * seg,
-    )(k, v, q, g, give, got, compress_kernel)
+    )(late_reach, trade(late_reach), k, v, q, g, got, compress_kernel)
 
     slots = [near, r2, r2s, r4, r4s]
     got_q = pl.BlockSpec((seg, half * feat), lambda i: (2, 0))
@@ -458,12 +460,13 @@
 
     back4 = shift(t4, -4)
     back2 = shift(t2, -2)
-    attended, grad_queries, give_first, own_terms = call(
+    attended, grad_queries, give_a, give_g, own_terms = call(
         output_kernel,
         (
             shape((seg, width)),
             shape((seg, width)),
-            shape((2, seg, half * feat)),
+            shape((seg, half * feat)),
+            shape((seg, half * feat)),
             shape((2, 2, seg, half * feat), F32),
         ),
         [mine_cols, got_q, mine_cols, got_g, full((2, 2, seg, half * feat))]
@@ -471,47 +474,51 @@
         + [full(soft), full(soft), full(stats)],
         (
             mine_cols, mine_cols,
-            full((2, seg, half * feat)),
+            full((seg, half * feat)),
+            full((seg, half * feat)),
             full((2, 2, seg, half * feat)),
         ),
         8 * unit, 12 * row_bytes, heads * seg * seg,
     )(q, got, g, got, kvp, *slots, w_mem, d_mem, final)
 
-    def finish(a, b, give):
+    def finish(a, b, give_a, give_b):
         anywhere = pl.BlockSpec(memory_space=pl.ANY)
         return call(
             finish_kernel,
             (shape((seg, width)), shape((seg, width))),
-            [anywhere] * 3,
+            [anywhere] * 4,
             (anywhere, anywhere),
             0, 2 * row_bytes,
             scratch=[pltpu.SemaphoreType.DMA((2,))],
             aliases={0: 0, 1: 1},
-        )(a, b, trade(give))
-
-    attended, grad_queries = finish(attended, grad_queries, give_first)
-    back2, own_terms = lax.optimization_barrier((back2, own_terms))
+        )(a, b, trade(give_a), trade(give_b))
+
+    attended, grad_queries = finish(attended, grad_queries, give_a, give_g)
     kernel_rows = compress_kernel.shape[0]
     split = (count // 2, kernel_rows // count, feat)
     turned = full((TAPS * feat, heads * slot))
+    low = call(
+        first_sum_kernel, shape(pair, F32), [full(one), full(pair)], full(pair), 0, 2 * row_bytes * 10
+    )(t0, back4)
+    low, own_terms = lax.optimization_barrier((low, own_terms))
     memory_grads, mine, other = call(
         sum_kernel,
-        (shape(pair), shape(split, F32), shape(split, F32)),
-        [turned] * 2 + [full(one)] + [full(pair)] * 2,
+        (shape(pair), shape(split, F32), shape(split)),
+        [turned] * 2 + [full(pair)] * 2,
         (full(pair), full(split), full(split)),
         unit, 4 * row_bytes,
-    )(kt, vt, t0, back4, back2)
-
-    grad_keys, grad_values, give_last = call(
+    )(kt, vt, low, back2)
+
+    grad_keys, grad_values, give_k, give_v = call(
         back_kernel,
-        (shape((seg, width)), shape((seg, width)), shape((2, seg, half * feat))),
+        (shape((seg, width)), shape((seg, width)), *[shape((seg, half * feat))] * 2),
         [full(pair), kernel_spec, full((2, 2, seg, half * feat))],
-        (mine_cols, mine_cols, full((2, seg, half * feat))),
+        (mine_cols, mine_cols, *[full((seg, half * feat))] * 2),
         4 * unit, 7 * row_bytes,
     )(memory_grads, compress_kernel, own_terms)
 
-    grad_keys, grad_values = finish(grad_keys, grad_values, give_last)
-    part = mine + trade(other)
+    grad_keys, grad_values = finish(grad_keys, grad_values, give_k, give_v)
+    part = mine + trade(other).astype(F32)
     part, (attended, grad_queries, grad_keys, grad_values) = reduce_rest(
         part, position, count, books, [(attended, grad_queries), (grad_keys, grad_values)]
     )
@@ -551,14 +558,14 @@
                 for s in range(count)
                 for d in range(books)
             ]
-            arrived.append(lax.ppermute(sent, ("seq", "dp"), pairs))
+            arrived.append(lax.ppermute(sent.astype(BF16), ("seq", "dp"), pairs))
         part = lax.dynamic_index_in_dim(part, mine, 0, False)
         if i // 2 < len(beside):
             arrived[0], *beside[i // 2] = lax.optimization_barrier(
                 (arrived[0], *beside[i // 2])
             )
         for piece in arrived:
-            part = part + piece
+            part = part + piece.astype(F32)
     return part.reshape(-1, part.shape[-1]), [array for arrays in beside for array in arrays]
 
 

time: 51.7 us -> 49.5 us (0.957)
  waiting for transfers between devices: 14.4 us -> 10.5 us
  starting transfers between devices: 22.9 us -> 24 us
    ppermute x6, waiting for transfers between devices: 4.93 us -> 2.4 us  [reduce_rest(): arrived.append(lax.ppermute(sent.astype(BF16), ('seq', 'dp'), pairs))]
    ppermute x4, waiting for transfers between devices: 5.73 us -> 3.69 us  [shift(): lax.ppermute(value, 'seq', [(s, (s + steps) % count) for s in range(count)])]
    ppermute x4 -> x7, waiting for transfers between devices: 0.01 us -> 1.53 us  [trade(): return lax.ppermute(value, 'seq', [(s, s ^ flip) for s in range(count)])]
    ppermute x4 -> x7, starting transfers between devices: 1.09 us -> 2.19 us  [trade(): return lax.ppermute(value, 'seq', [(s, s ^ flip) for s in range(count)])]
    ppermute x2, waiting for transfers between devices: 3.71 us -> 2.92 us  [cross(): lax.ppermute(value, 'seq', [(s, ((s ^ 1) + steps) % count) for s in range...]
    pallas_call x1, Pallas kernels: 1.23 us -> 1.86 us  [local(): call(own_kernel, (shape((2, 2, seg, half * feat)), shape((2, half, slot,...]
    pallas_call x3 -> x4, Pallas kernels: 5.05 us -> 5.09 us  [the longest x1 2.81 us: local(): call(output_kernel, (shape((seg, width)), shape((seg, width)), shape((seg...]
  transfers between devices with their start and end apart: 16 -> 19, of which waited for: 7 -> 7; matrix products, arithmetic and copies ran while one was open for 0% -> 0% of each run, Pallas kernels for 15% -> 16%
where the time goes in v5:
time: 49.5 us; the launch traced here: 49.3 us
  starting transfers between devices  24 us (48%)
  Pallas kernels  12.5 us (25%)
  waiting for transfers between devices  10.5 us (21%)
  between operations  1.58 us (3%)
  other arithmetic  0.64 us (1%)
    ppermute x4, starting transfers between devices, shift(): lax.ppermute(value, 'seq', [(s, (s + steps) % count) for s in range(count)])  10.4 us
    ppermute x6, starting transfers between devices, reduce_rest(): arrived.append(lax.ppermute(sent.astype(BF16), ('seq', 'dp'), pairs))  8.91 us
    ppermute x4, waiting for transfers between devices, shift(): lax.ppermute(value, 'seq', [(s, (s + steps) % count) for s in range(count)])  3.69 us
    ppermute x2, waiting for transfers between devices, cross(): lax.ppermute(value, 'seq', [(s, ((s ^ 1) + steps) % count) for s in range...  2.92 us
    pallas_call x1, Pallas kernels, local(): call(output_kernel, (shape((seg, width)), shape((seg, width)), shape((seg...  2.81 us
    ppermute x2, starting transfers between devices, cross(): lax.ppermute(value, 'seq', [(s, ((s ^ 1) + steps) % count) for s in range...  2.55 us
    pallas_call x1, Pallas kernels, local(): call(pack_kernel, (shape(half_dims), shape(half_dims), shape((rows, half...  2.5 us
    ppermute x6, waiting for transfers between devices, reduce_rest(): arrived.append(lax.ppermute(sent.astype(BF16), ('seq', 'dp'), pairs))  2.4 us
  transfers between devices with their start and end apart: 19, of which 7 were waited for; matrix products, arithmetic and copies ran while one was open for 0% of the time, Pallas kernels for 16%

profile of v5, /device:TPU:0, one launch (start us, length us, event | category | flops | bytes accessed | tf_op | source)
XLA Modules:
  0.0 49.3 jit_solution(13483641674155882998)
XLA Ops:
  0.7 2.5 %shard_map.101 = (bf16[2,8,32,128]{3,2,1,0:T(8,128)(2,1)S(1)}, bf16[2,8,32,128]{3,2,1,0:T(8,128)(2,1)S(1)}, bf16[512,1024]{1,0:T(8,128)(2,1)S(1)}) custom-call(bf16[128,2048]{1,0:T(8,128)(2,1)} %bitcast.31, bf16[128,2048]{1,0:T(8,128)(2,1)} %bitcast.33, bf16[128,2048]{1,0:T(8,128)(2,1)} %bitcast.23, bf16[128,2048]{1,0:T(8,128)(2,1)} %bitcast.27, ...), custom_call_target="tpu_custom_call" | custom-call | flops 201326592 | bytes 2621440 | tf_op jit(solution)/shard_map/pallas_call | solution.py:403
  3.7 2.6 %collective-permute-start.2 = (bf16[2,8,32,128]{3,2,1,0:T(8,128)(2,1)S(1)}, bf16[2,8,32,128]{3,2,1,0:T(8,128)(2,1)S(1)}, u32[]{:S(2)}, u32[]{:S(2)}) collective-permute-start(bf16[2,8,32,128]{3,2,1,0:T(8,128)(2,1)S(1)} %get-tuple-element.54), channel_id=1, source_target_pairs={{0,4},{2,6},{4,8},{6,10},{8,12},{10,14},{12,16},{14,18},{16,20},{1... | collective-permute-start | bytes 393224 | tf_op jit(solution)/shard_map/ppermute | solution.py:380
  6.3 1.3 %collective-permute-start.3 = (bf16[2,8,32,128]{3,2,1,0:T(8,128)(2,1)S(1)}, bf16[2,8,32,128]{3,2,1,0:T(8,128)(2,1)S(1)}, u32[]{:S(2)}, u32[]{:S(2)}) collective-permute-start(bf16[2,8,32,128]{3,2,1,0:T(8,128)(2,1)S(1)} %get-tuple-element.55), channel_id=1, source_target_pairs={{0,6},{2,4},{4,10},{6,8},{8,14},{10,12},{12,18},{14,16},{16,22},{1... | collective-permute-start | bytes 393224 | tf_op jit(solution)/shard_map/ppermute | solution.py:383
  7.6 1.6 %collective-permute-start.4 = (bf16[2,8,32,128]{3,2,1,0:T(8,128)(2,1)S(1)}, bf16[2,8,32,128]{3,2,1,0:T(8,128)(2,1)S(1)}, u32[]{:S(2)}, u32[]{:S(2)}) collective-permute-start(bf16[2,8,32,128]{3,2,1,0:T(8,128)(2,1)S(1)} %get-tuple-element.54), channel_id=1, source_target_pairs={{0,8},{2,10},{4,12},{6,14},{8,16},{10,18},{12,20},{14,22},{16,24},... | collective-permute-start | bytes 393224 | tf_op jit(solution)/shard_map/ppermute | solution.py:380
  9.2 1.2 %collective-permute-start.5 = (bf16[2,8,32,128]{3,2,1,0:T(8,128)(2,1)S(1)}, bf16[2,8,32,128]{3,2,1,0:T(8,128)(2,1)S(1)}, u32[]{:S(2)}, u32[]{:S(2)}) collective-permute-start(bf16[2,8,32,128]{3,2,1,0:T(8,128)(2,1)S(1)} %get-tuple-element.55), channel_id=1, source_target_pairs={{0,10},{2,8},{4,14},{6,12},{8,18},{10,16},{12,22},{14,20},{16,26},... | collective-permute-start | bytes 393224 | tf_op jit(solution)/shard_map/ppermute | solution.py:383
  11.6 1.0 %collective-permute-done.1.reach_s_ref = s32[1,1]{1,0:T(1,128)} collective-permute-done((s32[1,1]{1,0:T(1,128)}, s32[1,1]{1,0:T(1,128)}, u32[]{:S(2)}, u32[]{:S(2)}) %collective-permute-start.1) | collective-permute-done | bytes 36 | tf_op jit(solution)/shard_map/ppermute | solution.py:386
  12.6 1.9 %shard_map.102 = (bf16[2,2,128,1024]{3,2,1,0:T(8,128)(2,1)S(1)}, bf16[2,8,32,128]{3,2,1,0:T(8,128)(2,1)S(1)}, f32[3,8,1,256]{3,2,1,0:T(1,128)S(1)}, bf16[512,512...) custom-call(s32[1,1]{1,0:T(1,128)S(6)} %copy.19.reach_ref, ...), custom_call_target="tpu_custom_call" | custom-call | flops 67108864 | bytes 4194304 | tf_op jit(solution)/shard_map/pallas_call | solution.py:423
  14.4 1.5 %collective-permute-done.3.r2s_ref.refs_7_ = bf16[2,8,32,128]{3,2,1,0:T(8,128)(2,1)S(1)} collective-permute-done((bf16[2,8,32,128]{3,2,1,0:T(8,128)(2,1)S(1)}, bf16[2,8,32,128]{3,2,1,0:T(8,128)(2,1)S(1)}, u32[]{:S(2)}, u32[]{:S(2)}) %collective-permute-start.3) | collective-permute-done | bytes 131104 | tf_op jit(solution)/shard_map/ppermute | solution.py:383
  16.0 1.4 %collective-permute-done.5.r4s_ref.refs_9_ = bf16[2,8,32,128]{3,2,1,0:T(8,128)(2,1)S(1)} collective-permute-done((bf16[2,8,32,128]{3,2,1,0:T(8,128)(2,1)S(1)}, bf16[2,8,32,128]{3,2,1,0:T(8,128)(2,1)S(1)}, u32[]{:S(2)}, u32[]{:S(2)}) %collective-permute-start.5) | collective-permute-done | bytes 131104 | tf_op jit(solution)/shard_map/ppermute | solution.py:383
  17.4 1.4 %shard_map.103 = (f32[2,8,32,128]{3,2,1,0:T(8,128)S(1)}, bf16[2,2,8,32,128]{4,3,2,1,0:T(8,128)(2,1)S(1)}, bf16[2,2,8,32,128]{4,3,2,1,0:T(8,128)(2,1)S(1)}, bf16[...) custom-call(f32[160,256]{1,0:T(8,128)S(1)} %get-tuple-element.51.bias_ref, ...), custom_call_target="tpu_custom_call" | custom-call | flops 268435456 | bytes 4194304 | tf_op jit(solution)/shard_map/pallas_call | solution.py:452
  19.3 5.7 %collective-permute-start.7 = (bf16[2,2,8,32,128]{4,3,2,1,0:T(8,128)(2,1)S(1)}, bf16[2,2,8,32,128]{4,3,2,1,0:T(8,128)(2,1)S(1)}, u32[]{:S(2)}, u32[]{:S(2)}) collective-permute-start(bf16[2,2,8,32,128]{4,3,2,1,0:T(8,128)(2,1)S(1)} %get-tuple-element.64), channel_id=1, source_target_pairs={{0,28},{2,30},{4,0},{6,2},{8,4},{10,6},{12,8},{14,10},{16,12},{18,... | collective-permute-start | bytes 786440 | tf_op jit(solution)/shard_map/ppermute | solution.py:380
  25.0 2.8 %shard_map.105 = (bf16[128,2048]{1,0:T(8,128)(2,1)}, bf16[128,2048]{1,0:T(8,128)(2,1)}, bf16[128,1024]{1,0:T(8,128)(2,1)S(1)}, bf16[128,1024]{1,0:T(8,128)(2,1)S(1)}, f32[2,2,128,1024]{3,2,1,0:T(8,128)S(1)}) custom-call(bf16[128,2048]{1,0:T(8,128)(2,1)S(1)} %bitcast.26, bf16[512,1024]{1,0:T(8,128)(2,1)S(1)} %collective-permute-done.got_ref.qs_ref.gs_ref.refs_1_.refs_3_, ...), custom_call_target="tpu_custom_call" | custom-call | flops 536870912 | bytes 6291456 | tf_op jit(solution)/shard_map/pallas_call | solution.py:463
  27.9 3.7 %collective-permute-done.7.b2_ref = bf16[2,2,8,32,128]{4,3,2,1,0:T(8,128)(2,1)S(1)} collective-permute-done((bf16[2,2,8,32,128]{4,3,2,1,0:T(8,128)(2,1)S(1)}, bf16[2,2,8,32,128]{4,3,2,1,0:T(8,128)(2,1)S(1)}, u32[]{:S(2)}, u32[]{:S(2)}) %collective-permute-start.7) | collective-permute-done | bytes 262176 | tf_op jit(solution)/shard_map/ppermute | solution.py:380
  33.4 1.1 %collective-permute-start.9 = (bf16[2,32,128]{2,1,0:T(8,128)(2,1)S(1)}, bf16[2,32,128]{2,1,0:T(8,128)(2,1)S(1)}, u32[]{:S(2)}, u32[]{:S(2)}) collective-permute-start(bf16[2,32,128]{2,1,0:T(8,128)(2,1)S(1)} %get-tuple-element.89), channel_id=1, source_target_pairs={{0,8},{1,9},{2,10},{3,11},{4,12},{5,13},{6,14},{7,15},{8,0},{9,1},... | collective-permute-start | bytes 49160 | tf_op jit(solution)/shard_map/ppermute | solution.py:561
  34.5 3.4 %collective-permute-start.13 = (bf16[2,32,128]{2,1,0:T(8,128)(2,1)S(1)}, bf16[2,32,128]{2,1,0:T(8,128)(2,1)S(1)}, u32[]{:S(2)}, u32[]{:S(2)}) collective-permute-start(bf16[2,32,128]{2,1,0:T(8,128)(2,1)S(1)} %get-tuple-element.88), channel_id=1, source_target_pairs={{0,12},{1,13},{2,14},{3,15},{4,8},{5,9},{6,10},{7,11},{8,4},{9,5},... | collective-permute-start | bytes 49160 | tf_op jit(solution)/shard_map/ppermute | solution.py:561
  37.9 1.8 %shard_map.108 = (bf16[128,2048]{1,0:T(8,128)(2,1)}, bf16[128,2048]{1,0:T(8,128)(2,1)}, bf16[128,1024]{1,0:T(8,128)(2,1)S(1)}, bf16[128,1024]{1,0:T(8,128)(2,1)S(1)}) custom-call(bf16[2,2,8,32,128]{4,3,2,1,0:T(8,128)(2,1)S(1)} %get-tuple-element.76.mg_ref, bf16[512,128]{1,0:T(8,128)(2,1)S(1)} %copy-done.4, f32[2,2,128,1024]{3,2,1,0:T(8,128)S(1)} %get-tuple-element.77.terms_ref), custom_call_target="tpu_custom_call" | custom-call | flops 268435456 | bytes 3670016 | tf_op jit(solution)/shard_map/pallas_call | solution.py:512
  40.2 0.8 %shard_map.107 = (bf16[128,2048]{1,0:T(8,128)(2,1)}, bf16[128,2048]{1,0:T(8,128)(2,1)}) custom-call(bf16[128,2048]{1,0:T(8,128)(2,1)} %get-tuple-element.67.a_in, bf16[128,2048]{1,0:T(8,128)(2,1)} %get-tuple-element.68.b_in, bf16[128,1024]{1,0:T(8,128)(2,1)S(1)} %collective-permute-done.10.got_a, ...), custom_call_target="tpu_custom_call", output_to_operand_aliasing={{0}: (0, {}), {1}: (1, {})} | custom-call | bytes 1048576 | tf_op jit(solution)/shard_map/pallas_call | solution.py:486
  41.0 0.6 %collective-permute-done.12 = bf16[2,32,128]{2,1,0:T(8,128)(2,1)S(1)} collective-permute-done((bf16[2,32,128]{2,1,0:T(8,128)(2,1)S(1)}, bf16[2,32,128]{2,1,0:T(8,128)(2,1)S(1)}, u32[]{:S(2)}, u32[]{:S(2)}) %collective-permute-start.12) | collective-permute-done | bytes 16416 | tf_op jit(solution)/shard_map/ppermute | solution.py:561
  41.7 1.6 %collective-permute-start.14 = (bf16[1,32,128]{2,1,0:T(8,128)(2,1)S(1)}, bf16[1,32,128]{2,1,0:T(8,128)(2,1)S(1)}, u32[]{:S(2)}, u32[]{:S(2)}) collective-permute-start(bf16[1,32,128]{2,1,0:T(8,128)(2,1)S(1)} %get-tuple-element.91), channel_id=1, source_target_pairs={{0,1},{1,0},{2,3},{3,2},{4,5},{5,4},{6,7},{7,6},{8,9},{9,8},{10,11... | collective-permute-start | bytes 24584 | tf_op jit(solution)/shard_map/ppermute | solution.py:561
  43.3 0.9 %collective-permute-start.18 = (bf16[1,32,128]{2,1,0:T(8,128)(2,1)S(1)}, bf16[1,32,128]{2,1,0:T(8,128)(2,1)S(1)}, u32[]{:S(2)}, u32[]{:S(2)}) collective-permute-start(bf16[1,32,128]{2,1,0:T(8,128)(2,1)S(1)} %get-tuple-element.90), channel_id=1, source_target_pairs={{0,17},{1,16},{2,19},{3,18},{4,21},{5,20},{6,23},{7,22},{8,25},{9,... | collective-permute-start | bytes 24584 | tf_op jit(solution)/shard_map/ppermute | solution.py:561
  44.1 2.0 %collective-permute-start.17 = (bf16[1,32,128]{2,1,0:T(8,128)(2,1)S(1)}, bf16[1,32,128]{2,1,0:T(8,128)(2,1)S(1)}, u32[]{:S(2)}, u32[]{:S(2)}) collective-permute-start(bf16[1,32,128]{2,1,0:T(8,128)(2,1)S(1)} %get-tuple-element.90), channel_id=1, source_target_pairs={{0,16},{1,17},{2,18},{3,19},{4,20},{5,21},{6,22},{7,23},{8,24},{9,... | collective-permute-start | bytes 24584 | tf_op jit(solution)/shard_map/ppermute | solution.py:561
  46.1 0.8 %shard_map.109 = (bf16[128,2048]{1,0:T(8,128)(2,1)}, bf16[128,2048]{1,0:T(8,128)(2,1)}) custom-call(bf16[128,2048]{1,0:T(8,128)(2,1)} %get-tuple-element.78.a_in, bf16[128,2048]{1,0:T(8,128)(2,1)} %get-tuple-element.79.b_in, bf16[128,1024]{1,0:T(8,128)(2,1)S(1)} %collective-permute-done.15.got_a, ...), custom_call_target="tpu_custom_call", output_to_operand_aliasing={{0}: (0, {}), {1}: (1, {})} | custom-call | bytes 1048576 | tf_op jit(solution)/shard_map/pallas_call | solution.py:486
  47.0 1.8 %collective-permute-done.18 = bf16[1,32,128]{2,1,0:T(8,128)(2,1)S(1)} collective-permute-done((bf16[1,32,128]{2,1,0:T(8,128)(2,1)S(1)}, bf16[1,32,128]{2,1,0:T(8,128)(2,1)S(1)}, u32[]{:S(2)}, u32[]{:S(2)}) %collective-permute-start.18) | collective-permute-done | bytes 8224 | tf_op jit(solution)/shard_map/ppermute | solution.py:561
  48.7 0.6 %add_bitcast_fusion = f32[32,128]{1,0:T(8,128)} fusion(bf16[1,32,128]{2,1,0:T(8,128)(2,1)S(1)} %collective-permute-done.18, bf16[1,32,128]{2,1,0:T(8,128)(2,1)S(1)} %collective-permute-done.17, bf16[1,32,128]{2,1,0:T(8,128)(2,1)S(1)} %collective-permute-done.14, f32[2,32,128]{2,1,0:T(8,128)S(1)} %fusion.1, s32[]{:T(128)S(6)} %select_n.57), kind=kLoop, calls=%fused_computation.10 | loop fusion | flops 24576 | bytes 57348 | tf_op jit(solution)/shard_map/reshape | solution.py:569
  (38 shorter events, 3.9 us)
Async XLA Ops:
  0.6 11.9 %copy-start.2 = (bf16[1,128,2048]{2,1,0:T(8,128)(2,1)S(1)}, bf16[1,128,2048]{2,1,0:T(8,128)(2,1)}, u32[]{:S(2)}) copy-start(bf16[1,128,2048]{2,1,0:T(8,128)(2,1)} %param.7) | copy-start | bytes 1572868
  0.6 11.9 %copy-start.3 = (bf16[1,128,2048]{2,1,0:T(8,128)(2,1)S(1)}, bf16[1,128,2048]{2,1,0:T(8,128)(2,1)}, u32[]{:S(2)}) copy-start(bf16[1,128,2048]{2,1,0:T(8,128)(2,1)} %param.8) | copy-start | bytes 1572868
  0.7 11.9 %copy-start = (bf16[1,128,2048]{2,1,0:T(8,128)(2,1)S(1)}, bf16[1,128,2048]{2,1,0:T(8,128)(2,1)}, u32[]{:S(2)}) copy-start(bf16[1,128,2048]{2,1,0:T(8,128)(2,1)} %param.6) | copy-start | bytes 1572868
  0.7 11.9 %copy-start.1 = (bf16[1,128,2048]{2,1,0:T(8,128)(2,1)S(1)}, bf16[1,128,2048]{2,1,0:T(8,128)(2,1)}, u32[]{:S(2)}) copy-start(bf16[1,128,2048]{2,1,0:T(8,128)(2,1)} %param.9) | copy-start | bytes 1572868
  0.7 11.9 %copy-start.4 = (bf16[512,128]{1,0:T(8,128)(2,1)S(1)}, bf16[512,128]{1,0:T(8,128)(2,1)}, u32[]{:S(2)}) copy-start(bf16[512,128]{1,0:T(8,128)(2,1)} %w_ref.3) | copy-start | bytes 393220
  3.2 7.9 %collective-permute-start = (bf16[512,1024]{1,0:T(8,128)(2,1)S(1)}, bf16[512,1024]{1,0:T(8,128)(2,1)S(1)}, u32[]{:S(2)}, u32[]{:S(2)}) collective-permute-start(bf16[512,1024]{1,0:T(8,128)(2,1)S(1)} %get-tuple-element.46), channel_id=1, source_target_pairs={{0,2},{2,0},{4,6},{6,4},{8,10},{10,8},{12,14},{14,12},{16,18},{18,... | collective-permute-start | bytes 3145736 | tf_op jit(solution)/shard_map/ppermute | solution.py:386
  3.7 10.7 %collective-permute-start.2 = (bf16[2,8,32,128]{3,2,1,0:T(8,128)(2,1)S(1)}, bf16[2,8,32,128]{3,2,1,0:T(8,128)(2,1)S(1)}, u32[]{:S(2)}, u32[]{:S(2)}) collective-permute-start(bf16[2,8,32,128]{3,2,1,0:T(8,128)(2,1)S(1)} %get-tuple-element.54), channel_id=1, source_target_pairs={{0,4},{2,6},{4,8},{6,10},{8,12},{10,14},{12,16},{14,18},{16,20},{1... | collective-permute-start | bytes 393224 | tf_op jit(solution)/shard_map/ppermute | solution.py:380
  6.3 9.7 %collective-permute-start.3 = (bf16[2,8,32,128]{3,2,1,0:T(8,128)(2,1)S(1)}, bf16[2,8,32,128]{3,2,1,0:T(8,128)(2,1)S(1)}, u32[]{:S(2)}, u32[]{:S(2)}) collective-permute-start(bf16[2,8,32,128]{3,2,1,0:T(8,128)(2,1)S(1)} %get-tuple-element.55), channel_id=1, source_target_pairs={{0,6},{2,4},{4,10},{6,8},{8,14},{10,12},{12,18},{14,16},{16,22},{1... | collective-permute-start | bytes 393224 | tf_op jit(solution)/shard_map/ppermute | solution.py:383
  7.6 8.4 %collective-permute-start.4 = (bf16[2,8,32,128]{3,2,1,0:T(8,128)(2,1)S(1)}, bf16[2,8,32,128]{3,2,1,0:T(8,128)(2,1)S(1)}, u32[]{:S(2)}, u32[]{:S(2)}) collective-permute-start(bf16[2,8,32,128]{3,2,1,0:T(8,128)(2,1)S(1)} %get-tuple-element.54), channel_id=1, source_target_pairs={{0,8},{2,10},{4,12},{6,14},{8,16},{10,18},{12,20},{14,22},{16,24},... | collective-permute-start | bytes 393224 | tf_op jit(solution)/shard_map/ppermute | solution.py:380
  9.2 8.2 %collective-permute-start.5 = (bf16[2,8,32,128]{3,2,1,0:T(8,128)(2,1)S(1)}, bf16[2,8,32,128]{3,2,1,0:T(8,128)(2,1)S(1)}, u32[]{:S(2)}, u32[]{:S(2)}) collective-permute-start(bf16[2,8,32,128]{3,2,1,0:T(8,128)(2,1)S(1)} %get-tuple-element.55), channel_id=1, source_target_pairs={{0,10},{2,8},{4,14},{6,12},{8,18},{10,16},{12,22},{14,20},{16,26},... | collective-permute-start | bytes 393224 | tf_op jit(solution)/shard_map/ppermute | solution.py:383
  11.1 1.5 %collective-permute-start.1 = (s32[1,1]{1,0:T(1,128)}, s32[1,1]{1,0:T(1,128)}, u32[]{:S(2)}, u32[]{:S(2)}) collective-permute-start(s32[1,1]{1,0:T(1,128)} %param.11), channel_id=1, source_target_pairs={{0,2},{2,0},{4,6},{6,4},{8,10},{10,8},{12,14},{14,12},{16,18},{18,... | collective-permute-start | bytes 20 | tf_op jit(solution)/shard_map/ppermute | solution.py:386
  18.8 9.1 %collective-permute-start.6 = (bf16[2,2,8,32,128]{4,3,2,1,0:T(8,128)(2,1)S(1)}, bf16[2,2,8,32,128]{4,3,2,1,0:T(8,128)(2,1)S(1)}, u32[]{:S(2)}, u32[]{:S(2)}) collective-permute-start(bf16[2,2,8,32,128]{4,3,2,1,0:T(8,128)(2,1)S(1)} %get-tuple-element.57), channel_id=1, source_target_pairs={{0,24},{2,26},{4,28},{6,30},{8,0},{10,2},{12,4},{14,6},{16,8},{18,... | collective-permute-start | bytes 786440 | tf_op jit(solution)/shard_map/ppermute | solution.py:380
  19.3 12.3 %collective-permute-start.7 = (bf16[2,2,8,32,128]{4,3,2,1,0:T(8,128)(2,1)S(1)}, bf16[2,2,8,32,128]{4,3,2,1,0:T(8,128)(2,1)S(1)}, u32[]{:S(2)}, u32[]{:S(2)}) collective-permute-start(bf16[2,2,8,32,128]{4,3,2,1,0:T(8,128)(2,1)S(1)} %get-tuple-element.64), channel_id=1, source_target_pairs={{0,28},{2,30},{4,0},{6,2},{8,4},{10,6},{12,8},{14,10},{16,12},{18,... | collective-permute-start | bytes 786440 | tf_op jit(solution)/shard_map/ppermute | solution.py:380
  32.1 1.3 %collective-permute-start.8 = (bf16[8,32,128]{2,1,0:T(8,128)(2,1)S(1)}, bf16[8,32,128]{2,1,0:T(8,128)(2,1)S(1)}, u32[]{:S(2)}, u32[]{:S(2)}) collective-permute-start(bf16[8,32,128]{2,1,0:T(8,128)(2,1)S(1)} %get-tuple-element.66), channel_id=1, source_target_pairs={{0,2},{2,0},{4,6},{6,4},{8,10},{10,8},{12,14},{14,12},{16,18},{18,... | collective-permute-start | bytes 196616 | tf_op jit(solution)/shard_map/ppermute | solution.py:386
  32.3 7.4 %collective-permute-start.10 = (bf16[128,1024]{1,0:T(8,128)(2,1)S(1)}, bf16[128,1024]{1,0:T(8,128)(2,1)S(1)}, u32[]{:S(2)}, u32[]{:S(2)}) collective-permute-start(bf16[128,1024]{1,0:T(8,128)(2,1)S(1)} %get-tuple-element.69), channel_id=1, source_target_pairs={{0,2},{2,0},{4,6},{6,4},{8,10},{10,8},{12,14},{14,12},{16,18},{18,... | collective-permute-start | bytes 786440 | tf_op jit(solution)/shard_map/ppermute | solution.py:386
  32.7 7.0 %collective-permute-start.11 = (bf16[128,1024]{1,0:T(8,128)(2,1)S(1)}, bf16[128,1024]{1,0:T(8,128)(2,1)S(1)}, u32[]{:S(2)}, u32[]{:S(2)}) collective-permute-start(bf16[128,1024]{1,0:T(8,128)(2,1)S(1)} %get-tuple-element.70), channel_id=1, source_target_pairs={{0,2},{2,0},{4,6},{6,4},{8,10},{10,8},{12,14},{14,12},{16,18},{18,... | collective-permute-start | bytes 786440 | tf_op jit(solution)/shard_map/ppermute | solution.py:386
  33.4 7.6 %collective-permute-start.9 = (bf16[2,32,128]{2,1,0:T(8,128)(2,1)S(1)}, bf16[2,32,128]{2,1,0:T(8,128)(2,1)S(1)}, u32[]{:S(2)}, u32[]{:S(2)}) collective-permute-start(bf16[2,32,128]{2,1,0:T(8,128)(2,1)S(1)} %get-tuple-element.89), channel_id=1, source_target_pairs={{0,8},{1,9},{2,10},{3,11},{4,12},{5,13},{6,14},{7,15},{8,0},{9,1},... | collective-permute-start | bytes 49160 | tf_op jit(solution)/shard_map/ppermute | solution.py:561
  34.5 6.5 %collective-permute-start.13 = (bf16[2,32,128]{2,1,0:T(8,128)(2,1)S(1)}, bf16[2,32,128]{2,1,0:T(8,128)(2,1)S(1)}, u32[]{:S(2)}, u32[]{:S(2)}) collective-permute-start(bf16[2,32,128]{2,1,0:T(8,128)(2,1)S(1)} %get-tuple-element.88), channel_id=1, source_target_pairs={{0,12},{1,13},{2,14},{3,15},{4,8},{5,9},{6,10},{7,11},{8,4},{9,5},... | collective-permute-start | bytes 49160 | tf_op jit(solution)/shard_map/ppermute | solution.py:561
  37.9 3.7 %collective-permute-start.12 = (bf16[2,32,128]{2,1,0:T(8,128)(2,1)S(1)}, bf16[2,32,128]{2,1,0:T(8,128)(2,1)S(1)}, u32[]{:S(2)}, u32[]{:S(2)}) collective-permute-start(bf16[2,32,128]{2,1,0:T(8,128)(2,1)S(1)} %get-tuple-element.87), channel_id=1, source_target_pairs={{0,4},{1,5},{2,6},{3,7},{4,0},{5,1},{6,2},{7,3},{8,12},{9,13},{10,... | collective-permute-start | bytes 49160 | tf_op jit(solution)/shard_map/ppermute | solution.py:561
  39.7 6.5 %collective-permute-start.15 = (bf16[128,1024]{1,0:T(8,128)(2,1)S(1)}, bf16[128,1024]{1,0:T(8,128)(2,1)S(1)}, u32[]{:S(2)}, u32[]{:S(2)}) collective-permute-start(bf16[128,1024]{1,0:T(8,128)(2,1)S(1)} %get-tuple-element.80), channel_id=1, source_target_pairs={{0,2},{2,0},{4,6},{6,4},{8,10},{10,8},{12,14},{14,12},{16,18},{18,... | collective-permute-start | bytes 786440 | tf_op jit(solution)/shard_map/ppermute | solution.py:386
  39.7 6.5 %collective-permute-start.16 = (bf16[128,1024]{1,0:T(8,128)(2,1)S(1)}, bf16[128,1024]{1,0:T(8,128)(2,1)S(1)}, u32[]{:S(2)}, u32[]{:S(2)}) collective-permute-start(bf16[128,1024]{1,0:T(8,128)(2,1)S(1)} %get-tuple-element.81), channel_id=1, source_target_pairs={{0,2},{2,0},{4,6},{6,4},{8,10},{10,8},{12,14},{14,12},{16,18},{18,... | collective-permute-start | bytes 786440 | tf_op jit(solution)/shard_map/ppermute | solution.py:386
  41.7 5.3 %collective-permute-start.14 = (bf16[1,32,128]{2,1,0:T(8,128)(2,1)S(1)}, bf16[1,32,128]{2,1,0:T(8,128)(2,1)S(1)}, u32[]{:S(2)}, u32[]{:S(2)}) collective-permute-start(bf16[1,32,128]{2,1,0:T(8,128)(2,1)S(1)} %get-tuple-element.91), channel_id=1, source_target_pairs={{0,1},{1,0},{2,3},{3,2},{4,5},{5,4},{6,7},{7,6},{8,9},{9,8},{10,11... | collective-permute-start | bytes 24584 | tf_op jit(solution)/shard_map/ppermute | solution.py:561
  43.3 5.4 %collective-permute-start.18 = (bf16[1,32,128]{2,1,0:T(8,128)(2,1)S(1)}, bf16[1,32,128]{2,1,0:T(8,128)(2,1)S(1)}, u32[]{:S(2)}, u32[]{:S(2)}) collective-permute-start(bf16[1,32,128]{2,1,0:T(8,128)(2,1)S(1)} %get-tuple-element.90), channel_id=1, source_target_pairs={{0,17},{1,16},{2,19},{3,18},{4,21},{5,20},{6,23},{7,22},{8,25},{9,... | collective-permute-start | bytes 24584 | tf_op jit(solution)/shard_map/ppermute | solution.py:561
  44.1 4.6 %collective-permute-start.17 = (bf16[1,32,128]{2,1,0:T(8,128)(2,1)S(1)}, bf16[1,32,128]{2,1,0:T(8,128)(2,1)S(1)}, u32[]{:S(2)}, u32[]{:S(2)}) collective-permute-start(bf16[1,32,128]{2,1,0:T(8,128)(2,1)S(1)} %get-tuple-element.90), channel_id=1, source_target_pairs={{0,16},{1,17},{2,18},{3,19},{4,20},{5,21},{6,22},{7,23},{8,24},{9,... | collective-permute-start | bytes 24584 | tf_op jit(solution)/shard_map/ppermute | solution.py:561

commit v6 on v5

--- a/solution.py
+++ b/solution.py
@@ -99,11 +99,17 @@
     sorted_rows = []
     for n, (part, kv) in enumerate(steps):
         copies[n if n < 2 else n + 1].wait()
-        sorted_rows.append(nn(order, rows_ref[part, kv]).astype(BF16))
     copies[2].wait()
-    for (part, kv), rows in zip(steps, sorted_rows):
-        packed = nn(tap_rows(rows, heads, feat), w_ref[...]).astype(BF16)
-        (mine_ref, other_ref)[part][kv] = packed.reshape(heads, slot, feat)
+    every = jnp.concatenate([rows_ref[part, kv] for part, kv in steps], 1)
+    every = nn(order, every).astype(BF16)
+    half_width = heads * feat
+    sorted_rows = [
+        every[:, n * half_width : (n + 1) * half_width] for n in range(len(steps))
+    ]
+    rows = jnp.concatenate([tap_rows(rows, heads, feat) for rows in sorted_rows], 0)
+    packed = nn(rows, w_ref[...]).astype(BF16).reshape(len(steps), heads, slot, feat)
+    for n, (part, kv) in enumerate(steps):
+        (mine_ref, other_ref)[part][kv] = packed[n]
         if part == 1:
             give_ref[kv * seg : (kv + 1) * seg] = rows_ref[part, kv]
     for copy in copies[5:]:
@@ -314,21 +320,18 @@
     seg = terms_ref.shape[2]
     heads, slot, feat = mg_ref.shape[2:]
     restore = tap_major(seg, inverse=True)
-    for kv, out_ref in enumerate((gk_ref, gv_ref)):
-        for u in range(2):
-            back = nt(mg_ref[kv, u].reshape(heads * slot, feat), w_ref[...])
-            columns = []
-            for h in range(heads):
-                rows = back[h * slot : (h + 1) * slot]
-                columns.append(
-                    jnp.concatenate([rows[:, head(t, feat)] for t in range(TAPS)], 0)
-                )
-            total = (terms_ref[kv, u] + jnp.concatenate(columns, 1)).astype(BF16)
-            result = nn(restore, total).astype(BF16)
-            if u == 0:
-                out_ref[...] = result
-            else:
-                (givek_ref, givev_ref)[kv][...] = result
+    parts = [(kv, u) for kv in range(2) for u in range(2)]
+    backs = [nt(mg_ref[kv, u].reshape(heads * slot, feat), w_ref[...]) for kv, u in parts]
+    totals = []
+    for (kv, u), back in zip(parts, backs):
+        columns = []
+        for h in range(heads):
+            rows = back[h * slot : (h + 1) * slot]
+            columns.append(jnp.concatenate([rows[:, head(t, feat)] for t in range(TAPS)], 0))
+        totals.append((terms_ref[kv, u] + jnp.concatenate(columns, 1)).astype(BF16))
+    for (kv, u), total in zip(parts, totals):
+        result = nn(restore, total).astype(BF16)
+        ((gk_ref, gv_ref), (givek_ref, givev_ref))[u][kv][...] = result
 
 
 def finish_kernel(a_in, b_in, got_a, got_b, a_ref, b_ref, sems):
@@ -520,7 +523,7 @@
     grad_keys, grad_values = finish(grad_keys, grad_values, give_k, give_v)
     part = mine + trade(other).astype(F32)
     part, (attended, grad_queries, grad_keys, grad_values) = reduce_rest(
-        part, position, count, books, [(attended, grad_queries), (grad_keys, grad_values)]
+        part, position, count, books, (attended, grad_queries, grad_keys, grad_values)
     )
     return (attended[None], grad_queries[None], grad_keys[None], grad_values[None], part)
 
@@ -560,13 +563,11 @@
             ]
             arrived.append(lax.ppermute(sent.astype(BF16), ("seq", "dp"), pairs))
         part = lax.dynamic_index_in_dim(part, mine, 0, False)
-        if i // 2 < len(beside):
-            arrived[0], *beside[i // 2] = lax.optimization_barrier(
-                (arrived[0], *beside[i // 2])
-            )
+        if i + 2 >= len(bits):
+            arrived[0], *beside = lax.optimization_barrier((arrived[0], *beside))
         for piece in arrived:
             part = part + piece.astype(F32)
-    return part.reshape(-1, part.shape[-1]), [array for arrays in beside for array in arrays]
+    return part.reshape(-1, part.shape[-1]), beside
 
 
 def solution(mesh):

time: 49.5 us -> 49.1 us (level)
  Pallas kernels: 12.5 us -> 11.8 us
  waiting for transfers between devices: 10.5 us -> 11.2 us
    ppermute x6, waiting for transfers between devices: 2.4 us -> 3.04 us  [reduce_rest(): arrived.append(lax.ppermute(sent.astype(BF16), ('seq', 'dp'), pairs))]
  transfers between devices with their start and end apart: 19 -> 19, of which waited for: 7 -> 9; matrix products, arithmetic and copies ran while one was open for 0% -> 0% of each run, Pallas kernels for 16% -> 16%
where the time goes in v6:
time: 49.1 us; the launch traced here: 48.9 us
  starting transfers between devices  23.6 us (48%)
  Pallas kernels  11.8 us (24%)
  waiting for transfers between devices  11.2 us (23%)
  between operations  1.57 us (3%)
  other arithmetic  0.64 us (1%)
    ppermute x4, starting transfers between devices, shift(): lax.ppermute(value, 'seq', [(s, (s + steps) % count) for s in range(count)])  10.4 us
    ppermute x6, starting transfers between devices, reduce_rest(): arrived.append(lax.ppermute(sent.astype(BF16), ('seq', 'dp'), pairs))  8.91 us
    ppermute x4, waiting for transfers between devices, shift(): lax.ppermute(value, 'seq', [(s, (s + steps) % count) for s in range(count)])  3.7 us
    ppermute x6, waiting for transfers between devices, reduce_rest(): arrived.append(lax.ppermute(sent.astype(BF16), ('seq', 'dp'), pairs))  3.04 us
    ppermute x2, waiting for transfers between devices, cross(): lax.ppermute(value, 'seq', [(s, ((s ^ 1) + steps) % count) for s in range...  2.92 us
    pallas_call x1, Pallas kernels, local(): call(output_kernel, (shape((seg, width)), shape((seg, width)), shape((seg...  2.81 us
    ppermute x2, starting transfers between devices, cross(): lax.ppermute(value, 'seq', [(s, ((s ^ 1) + steps) % count) for s in range...  2.55 us
    pallas_call x1, Pallas kernels, local(): call(pack_kernel, (shape(half_dims), shape(half_dims), shape((rows, half...  2.19 us
  transfers between devices with their start and end apart: 19, of which 9 were waited for; matrix products, arithmetic and copies ran while one was open for 0% of the time, Pallas kernels for 16%

profile of v6, /device:TPU:0, one launch (start us, length us, event | category | flops | bytes accessed | tf_op | source)
XLA Modules:
  0.0 48.9 jit_solution(8247095134883977374)
XLA Ops:
  0.7 2.2 %shard_map.101 = (bf16[2,8,32,128]{3,2,1,0:T(8,128)(2,1)S(1)}, bf16[2,8,32,128]{3,2,1,0:T(8,128)(2,1)S(1)}, bf16[512,1024]{1,0:T(8,128)(2,1)S(1)}) custom-call(bf16[128,2048]{1,0:T(8,128)(2,1)} %bitcast.31, bf16[128,2048]{1,0:T(8,128)(2,1)} %bitcast.33, bf16[128,2048]{1,0:T(8,128)(2,1)} %bitcast.23, bf16[128,2048]{1,0:T(8,128)(2,1)} %bitcast.27, ...), custom_call_target="tpu_custom_call" | custom-call | flops 201326592 | bytes 2621440 | tf_op jit(solution)/shard_map/pallas_call | solution.py:406
  3.4 2.6 %collective-permute-start.2 = (bf16[2,8,32,128]{3,2,1,0:T(8,128)(2,1)S(1)}, bf16[2,8,32,128]{3,2,1,0:T(8,128)(2,1)S(1)}, u32[]{:S(2)}, u32[]{:S(2)}) collective-permute-start(bf16[2,8,32,128]{3,2,1,0:T(8,128)(2,1)S(1)} %get-tuple-element.53), channel_id=1, source_target_pairs={{0,4},{2,6},{4,8},{6,10},{8,12},{10,14},{12,16},{14,18},{16,20},{1... | collective-permute-start | bytes 393224 | tf_op jit(solution)/shard_map/ppermute | solution.py:383
  6.0 1.3 %collective-permute-start.3 = (bf16[2,8,32,128]{3,2,1,0:T(8,128)(2,1)S(1)}, bf16[2,8,32,128]{3,2,1,0:T(8,128)(2,1)S(1)}, u32[]{:S(2)}, u32[]{:S(2)}) collective-permute-start(bf16[2,8,32,128]{3,2,1,0:T(8,128)(2,1)S(1)} %get-tuple-element.54), channel_id=1, source_target_pairs={{0,6},{2,4},{4,10},{6,8},{8,14},{10,12},{12,18},{14,16},{16,22},{1... | collective-permute-start | bytes 393224 | tf_op jit(solution)/shard_map/ppermute | solution.py:386
  7.3 1.6 %collective-permute-start.4 = (bf16[2,8,32,128]{3,2,1,0:T(8,128)(2,1)S(1)}, bf16[2,8,32,128]{3,2,1,0:T(8,128)(2,1)S(1)}, u32[]{:S(2)}, u32[]{:S(2)}) collective-permute-start(bf16[2,8,32,128]{3,2,1,0:T(8,128)(2,1)S(1)} %get-tuple-element.53), channel_id=1, source_target_pairs={{0,8},{2,10},{4,12},{6,14},{8,16},{10,18},{12,20},{14,22},{16,24},... | collective-permute-start | bytes 393224 | tf_op jit(solution)/shard_map/ppermute | solution.py:383
  8.8 1.2 %collective-permute-start.5 = (bf16[2,8,32,128]{3,2,1,0:T(8,128)(2,1)S(1)}, bf16[2,8,32,128]{3,2,1,0:T(8,128)(2,1)S(1)}, u32[]{:S(2)}, u32[]{:S(2)}) collective-permute-start(bf16[2,8,32,128]{3,2,1,0:T(8,128)(2,1)S(1)} %get-tuple-element.54), channel_id=1, source_target_pairs={{0,10},{2,8},{4,14},{6,12},{8,18},{10,16},{12,22},{14,20},{16,26},... | collective-permute-start | bytes 393224 | tf_op jit(solution)/shard_map/ppermute | solution.py:386
  11.3 1.0 %collective-permute-done.1.reach_s_ref = s32[1,1]{1,0:T(1,128)} collective-permute-done((s32[1,1]{1,0:T(1,128)}, s32[1,1]{1,0:T(1,128)}, u32[]{:S(2)}, u32[]{:S(2)}) %collective-permute-start.1) | collective-permute-done | bytes 36 | tf_op jit(solution)/shard_map/ppermute | solution.py:389
  12.3 1.9 %shard_map.102 = (bf16[2,2,128,1024]{3,2,1,0:T(8,128)(2,1)S(1)}, bf16[2,8,32,128]{3,2,1,0:T(8,128)(2,1)S(1)}, f32[3,8,1,256]{3,2,1,0:T(1,128)S(1)}, bf16[512,512...) custom-call(s32[1,1]{1,0:T(1,128)S(6)} %copy.19.reach_ref, ...), custom_call_target="tpu_custom_call" | custom-call | flops 67108864 | bytes 4194304 | tf_op jit(solution)/shard_map/pallas_call | solution.py:426
  14.1 1.5 %collective-permute-done.3.r2s_ref.refs_7_ = bf16[2,8,32,128]{3,2,1,0:T(8,128)(2,1)S(1)} collective-permute-done((bf16[2,8,32,128]{3,2,1,0:T(8,128)(2,1)S(1)}, bf16[2,8,32,128]{3,2,1,0:T(8,128)(2,1)S(1)}, u32[]{:S(2)}, u32[]{:S(2)}) %collective-permute-start.3) | collective-permute-done | bytes 131104 | tf_op jit(solution)/shard_map/ppermute | solution.py:386
  15.7 1.4 %collective-permute-done.5.r4s_ref.refs_9_ = bf16[2,8,32,128]{3,2,1,0:T(8,128)(2,1)S(1)} collective-permute-done((bf16[2,8,32,128]{3,2,1,0:T(8,128)(2,1)S(1)}, bf16[2,8,32,128]{3,2,1,0:T(8,128)(2,1)S(1)}, u32[]{:S(2)}, u32[]{:S(2)}) %collective-permute-start.5) | collective-permute-done | bytes 131104 | tf_op jit(solution)/shard_map/ppermute | solution.py:386
  17.1 1.4 %shard_map.103 = (f32[2,8,32,128]{3,2,1,0:T(8,128)S(1)}, bf16[2,2,8,32,128]{4,3,2,1,0:T(8,128)(2,1)S(1)}, bf16[2,2,8,32,128]{4,3,2,1,0:T(8,128)(2,1)S(1)}, bf16[...) custom-call(f32[160,256]{1,0:T(8,128)S(1)} %get-tuple-element.50.bias_ref, ...), custom_call_target="tpu_custom_call" | custom-call | flops 268435456 | bytes 4194304 | tf_op jit(solution)/shard_map/pallas_call | solution.py:455
  19.0 5.7 %collective-permute-start.7 = (bf16[2,2,8,32,128]{4,3,2,1,0:T(8,128)(2,1)S(1)}, bf16[2,2,8,32,128]{4,3,2,1,0:T(8,128)(2,1)S(1)}, u32[]{:S(2)}, u32[]{:S(2)}) collective-permute-start(bf16[2,2,8,32,128]{4,3,2,1,0:T(8,128)(2,1)S(1)} %get-tuple-element.63), channel_id=1, source_target_pairs={{0,28},{2,30},{4,0},{6,2},{8,4},{10,6},{12,8},{14,10},{16,12},{18,... | collective-permute-start | bytes 786440 | tf_op jit(solution)/shard_map/ppermute | solution.py:383
  24.7 2.8 %shard_map.105 = (bf16[128,2048]{1,0:T(8,128)(2,1)}, bf16[128,2048]{1,0:T(8,128)(2,1)}, bf16[128,1024]{1,0:T(8,128)(2,1)S(1)}, bf16[128,1024]{1,0:T(8,128)(2,1)S(1)}, f32[2,2,128,1024]{3,2,1,0:T(8,128)S(1)}) custom-call(bf16[128,2048]{1,0:T(8,128)(2,1)S(1)} %bitcast.26, bf16[512,1024]{1,0:T(8,128)(2,1)S(1)} %collective-permute-done.got_ref.qs_ref.gs_ref.refs_1_.refs_3_, ...), custom_call_target="tpu_custom_call" | custom-call | flops 536870912 | bytes 6291456 | tf_op jit(solution)/shard_map/pallas_call | solution.py:466
  27.6 3.7 %collective-permute-done.7.b2_ref = bf16[2,2,8,32,128]{4,3,2,1,0:T(8,128)(2,1)S(1)} collective-permute-done((bf16[2,2,8,32,128]{4,3,2,1,0:T(8,128)(2,1)S(1)}, bf16[2,2,8,32,128]{4,3,2,1,0:T(8,128)(2,1)S(1)}, u32[]{:S(2)}, u32[]{:S(2)}) %collective-permute-start.7) | collective-permute-done | bytes 262176 | tf_op jit(solution)/shard_map/ppermute | solution.py:383
  33.1 2.5 %collective-permute-start.11 = (bf16[2,32,128]{2,1,0:T(8,128)(2,1)S(1)}, bf16[2,32,128]{2,1,0:T(8,128)(2,1)S(1)}, u32[]{:S(2)}, u32[]{:S(2)}) collective-permute-start(bf16[2,32,128]{2,1,0:T(8,128)(2,1)S(1)} %get-tuple-element.86), channel_id=1, source_target_pairs={{0,12},{1,13},{2,14},{3,15},{4,8},{5,9},{6,10},{7,11},{8,4},{9,5},... | collective-permute-start | bytes 49160 | tf_op jit(solution)/shard_map/ppermute | solution.py:564
  36.2 1.4 %collective-permute-start.9 = (bf16[2,32,128]{2,1,0:T(8,128)(2,1)S(1)}, bf16[2,32,128]{2,1,0:T(8,128)(2,1)S(1)}, u32[]{:S(2)}, u32[]{:S(2)}) collective-permute-start(bf16[2,32,128]{2,1,0:T(8,128)(2,1)S(1)} %get-tuple-element.85), channel_id=1, source_target_pairs={{0,8},{1,9},{2,10},{3,11},{4,12},{5,13},{6,14},{7,15},{8,0},{9,1},... | collective-permute-start | bytes 49160 | tf_op jit(solution)/shard_map/ppermute | solution.py:564
  37.6 1.4 %shard_map.108 = (bf16[128,2048]{1,0:T(8,128)(2,1)}, bf16[128,2048]{1,0:T(8,128)(2,1)}, bf16[128,1024]{1,0:T(8,128)(2,1)S(1)}, bf16[128,1024]{1,0:T(8,128)(2,1)S(1)}) custom-call(bf16[2,2,8,32,128]{4,3,2,1,0:T(8,128)(2,1)S(1)} %get-tuple-element.72.mg_ref, bf16[512,128]{1,0:T(8,128)(2,1)S(1)} %copy-done.4, f32[2,2,128,1024]{3,2,1,0:T(8,128)S(1)} %get-tuple-element.73.terms_ref), custom_call_target="tpu_custom_call" | custom-call | flops 268435456 | bytes 3670016 | tf_op jit(solution)/shard_map/pallas_call | solution.py:515
  40.0 1.6 %collective-permute-start.12 = (bf16[1,32,128]{2,1,0:T(8,128)(2,1)S(1)}, bf16[1,32,128]{2,1,0:T(8,128)(2,1)S(1)}, u32[]{:S(2)}, u32[]{:S(2)}) collective-permute-start(bf16[1,32,128]{2,1,0:T(8,128)(2,1)S(1)} %get-tuple-element.89), channel_id=1, source_target_pairs={{0,1},{1,0},{2,3},{3,2},{4,5},{5,4},{6,7},{7,6},{8,9},{9,8},{10,11... | collective-permute-start | bytes 24584 | tf_op jit(solution)/shard_map/ppermute | solution.py:564
  41.6 2.2 %collective-permute-start.18 = (bf16[1,32,128]{2,1,0:T(8,128)(2,1)S(1)}, bf16[1,32,128]{2,1,0:T(8,128)(2,1)S(1)}, u32[]{:S(2)}, u32[]{:S(2)}) collective-permute-start(bf16[1,32,128]{2,1,0:T(8,128)(2,1)S(1)} %get-tuple-element.88), channel_id=1, source_target_pairs={{0,17},{1,16},{2,19},{3,18},{4,21},{5,20},{6,23},{7,22},{8,25},{9,... | collective-permute-start | bytes 24584 | tf_op jit(solution)/shard_map/ppermute | solution.py:564
  43.8 0.7 %collective-permute-start.17 = (bf16[1,32,128]{2,1,0:T(8,128)(2,1)S(1)}, bf16[1,32,128]{2,1,0:T(8,128)(2,1)S(1)}, u32[]{:S(2)}, u32[]{:S(2)}) collective-permute-start(bf16[1,32,128]{2,1,0:T(8,128)(2,1)S(1)} %get-tuple-element.88), channel_id=1, source_target_pairs={{0,16},{1,17},{2,18},{3,19},{4,20},{5,21},{6,22},{7,23},{8,24},{9,... | collective-permute-start | bytes 24584 | tf_op jit(solution)/shard_map/ppermute | solution.py:564
  44.5 0.8 %shard_map.107 = (bf16[128,2048]{1,0:T(8,128)(2,1)}, bf16[128,2048]{1,0:T(8,128)(2,1)}) custom-call(bf16[128,2048]{1,0:T(8,128)(2,1)} %get-tuple-element.66.a_in, bf16[128,2048]{1,0:T(8,128)(2,1)} %get-tuple-element.67.b_in, bf16[128,1024]{1,0:T(8,128)(2,1)S(1)} %collective-permute-done.13.got_a, ...), custom_call_target="tpu_custom_call", output_to_operand_aliasing={{0}: (0, {}), {1}: (1, {})} | custom-call | bytes 1048576 | tf_op jit(solution)/shard_map/pallas_call | solution.py:489
  45.3 0.8 %shard_map.109 = (bf16[128,2048]{1,0:T(8,128)(2,1)}, bf16[128,2048]{1,0:T(8,128)(2,1)}) custom-call(bf16[128,2048]{1,0:T(8,128)(2,1)} %get-tuple-element.74.a_in, bf16[128,2048]{1,0:T(8,128)(2,1)} %get-tuple-element.75.b_in, bf16[128,1024]{1,0:T(8,128)(2,1)S(1)} %collective-permute-done.15.got_a, ...), custom_call_target="tpu_custom_call", output_to_operand_aliasing={{0}: (0, {}), {1}: (1, {})} | custom-call | bytes 1048576 | tf_op jit(solution)/shard_map/pallas_call | solution.py:489
  46.1 0.9 %collective-permute-done.18 = bf16[1,32,128]{2,1,0:T(8,128)(2,1)S(1)} collective-permute-done((bf16[1,32,128]{2,1,0:T(8,128)(2,1)S(1)}, bf16[1,32,128]{2,1,0:T(8,128)(2,1)S(1)}, u32[]{:S(2)}, u32[]{:S(2)}) %collective-permute-start.18) | collective-permute-done | bytes 8224 | tf_op jit(solution)/shard_map/ppermute | solution.py:564
  47.0 1.3 %collective-permute-done.17 = bf16[1,32,128]{2,1,0:T(8,128)(2,1)S(1)} collective-permute-done((bf16[1,32,128]{2,1,0:T(8,128)(2,1)S(1)}, bf16[1,32,128]{2,1,0:T(8,128)(2,1)S(1)}, u32[]{:S(2)}, u32[]{:S(2)}) %collective-permute-start.17) | collective-permute-done | bytes 8224 | tf_op jit(solution)/shard_map/ppermute | solution.py:564
  48.3 0.6 %add_bitcast_fusion = f32[32,128]{1,0:T(8,128)} fusion(bf16[1,32,128]{2,1,0:T(8,128)(2,1)S(1)} %collective-permute-done.18, bf16[1,32,128]{2,1,0:T(8,128)(2,1)S(1)} %collective-permute-done.17, bf16[1,32,128]{2,1,0:T(8,128)(2,1)S(1)} %collective-permute-done.12, f32[2,32,128]{2,1,0:T(8,128)S(1)} %fusion.1, s32[]{:T(128)S(6)} %select_n.57), kind=kLoop, calls=%fused_computation.10 | loop fusion | flops 24576 | bytes 57348 | tf_op jit(solution)/shard_map/reshape | solution.py:570
  (38 shorter events, 4.9 us)
Async XLA Ops:
  0.6 11.6 %copy-start.2 = (bf16[1,128,2048]{2,1,0:T(8,128)(2,1)S(1)}, bf16[1,128,2048]{2,1,0:T(8,128)(2,1)}, u32[]{:S(2)}) copy-start(bf16[1,128,2048]{2,1,0:T(8,128)(2,1)} %param.7) | copy-start | bytes 1572868
  0.6 11.6 %copy-start.3 = (bf16[1,128,2048]{2,1,0:T(8,128)(2,1)S(1)}, bf16[1,128,2048]{2,1,0:T(8,128)(2,1)}, u32[]{:S(2)}) copy-start(bf16[1,128,2048]{2,1,0:T(8,128)(2,1)} %param.8) | copy-start | bytes 1572868
  0.7 11.6 %copy-start = (bf16[1,128,2048]{2,1,0:T(8,128)(2,1)S(1)}, bf16[1,128,2048]{2,1,0:T(8,128)(2,1)}, u32[]{:S(2)}) copy-start(bf16[1,128,2048]{2,1,0:T(8,128)(2,1)} %param.6) | copy-start | bytes 1572868
  0.7 11.6 %copy-start.1 = (bf16[1,128,2048]{2,1,0:T(8,128)(2,1)S(1)}, bf16[1,128,2048]{2,1,0:T(8,128)(2,1)}, u32[]{:S(2)}) copy-start(bf16[1,128,2048]{2,1,0:T(8,128)(2,1)} %param.9) | copy-start | bytes 1572868
  0.7 11.6 %copy-start.4 = (bf16[512,128]{1,0:T(8,128)(2,1)S(1)}, bf16[512,128]{1,0:T(8,128)(2,1)}, u32[]{:S(2)}) copy-start(bf16[512,128]{1,0:T(8,128)(2,1)} %w_ref.3) | copy-start | bytes 393220
  2.9 7.9 %collective-permute-start = (bf16[512,1024]{1,0:T(8,128)(2,1)S(1)}, bf16[512,1024]{1,0:T(8,128)(2,1)S(1)}, u32[]{:S(2)}, u32[]{:S(2)}) collective-permute-start(bf16[512,1024]{1,0:T(8,128)(2,1)S(1)} %get-tuple-element.45), channel_id=1, source_target_pairs={{0,2},{2,0},{4,6},{6,4},{8,10},{10,8},{12,14},{14,12},{16,18},{18,... | collective-permute-start | bytes 3145736 | tf_op jit(solution)/shard_map/ppermute | solution.py:389
  3.4 10.7 %collective-permute-start.2 = (bf16[2,8,32,128]{3,2,1,0:T(8,128)(2,1)S(1)}, bf16[2,8,32,128]{3,2,1,0:T(8,128)(2,1)S(1)}, u32[]{:S(2)}, u32[]{:S(2)}) collective-permute-start(bf16[2,8,32,128]{3,2,1,0:T(8,128)(2,1)S(1)} %get-tuple-element.53), channel_id=1, source_target_pairs={{0,4},{2,6},{4,8},{6,10},{8,12},{10,14},{12,16},{14,18},{16,20},{1... | collective-permute-start | bytes 393224 | tf_op jit(solution)/shard_map/ppermute | solution.py:383
  6.0 9.7 %collective-permute-start.3 = (bf16[2,8,32,128]{3,2,1,0:T(8,128)(2,1)S(1)}, bf16[2,8,32,128]{3,2,1,0:T(8,128)(2,1)S(1)}, u32[]{:S(2)}, u32[]{:S(2)}) collective-permute-start(bf16[2,8,32,128]{3,2,1,0:T(8,128)(2,1)S(1)} %get-tuple-element.54), channel_id=1, source_target_pairs={{0,6},{2,4},{4,10},{6,8},{8,14},{10,12},{12,18},{14,16},{16,22},{1... | collective-permute-start | bytes 393224 | tf_op jit(solution)/shard_map/ppermute | solution.py:386
  7.3 8.4 %collective-permute-start.4 = (bf16[2,8,32,128]{3,2,1,0:T(8,128)(2,1)S(1)}, bf16[2,8,32,128]{3,2,1,0:T(8,128)(2,1)S(1)}, u32[]{:S(2)}, u32[]{:S(2)}) collective-permute-start(bf16[2,8,32,128]{3,2,1,0:T(8,128)(2,1)S(1)} %get-tuple-element.53), channel_id=1, source_target_pairs={{0,8},{2,10},{4,12},{6,14},{8,16},{10,18},{12,20},{14,22},{16,24},... | collective-permute-start | bytes 393224 | tf_op jit(solution)/shard_map/ppermute | solution.py:383
  8.8 8.2 %collective-permute-start.5 = (bf16[2,8,32,128]{3,2,1,0:T(8,128)(2,1)S(1)}, bf16[2,8,32,128]{3,2,1,0:T(8,128)(2,1)S(1)}, u32[]{:S(2)}, u32[]{:S(2)}) collective-permute-start(bf16[2,8,32,128]{3,2,1,0:T(8,128)(2,1)S(1)} %get-tuple-element.54), channel_id=1, source_target_pairs={{0,10},{2,8},{4,14},{6,12},{8,18},{10,16},{12,22},{14,20},{16,26},... | collective-permute-start | bytes 393224 | tf_op jit(solution)/shard_map/ppermute | solution.py:386
  10.8 1.5 %collective-permute-start.1 = (s32[1,1]{1,0:T(1,128)}, s32[1,1]{1,0:T(1,128)}, u32[]{:S(2)}, u32[]{:S(2)}) collective-permute-start(s32[1,1]{1,0:T(1,128)} %param.11), channel_id=1, source_target_pairs={{0,2},{2,0},{4,6},{6,4},{8,10},{10,8},{12,14},{14,12},{16,18},{18,... | collective-permute-start | bytes 20 | tf_op jit(solution)/shard_map/ppermute | solution.py:389
  18.5 9.0 %collective-permute-start.6 = (bf16[2,2,8,32,128]{4,3,2,1,0:T(8,128)(2,1)S(1)}, bf16[2,2,8,32,128]{4,3,2,1,0:T(8,128)(2,1)S(1)}, u32[]{:S(2)}, u32[]{:S(2)}) collective-permute-start(bf16[2,2,8,32,128]{4,3,2,1,0:T(8,128)(2,1)S(1)} %get-tuple-element.56), channel_id=1, source_target_pairs={{0,24},{2,26},{4,28},{6,30},{8,0},{10,2},{12,4},{14,6},{16,8},{18,... | collective-permute-start | bytes 786440 | tf_op jit(solution)/shard_map/ppermute | solution.py:383
  19.0 12.3 %collective-permute-start.7 = (bf16[2,2,8,32,128]{4,3,2,1,0:T(8,128)(2,1)S(1)}, bf16[2,2,8,32,128]{4,3,2,1,0:T(8,128)(2,1)S(1)}, u32[]{:S(2)}, u32[]{:S(2)}) collective-permute-start(bf16[2,2,8,32,128]{4,3,2,1,0:T(8,128)(2,1)S(1)} %get-tuple-element.63), channel_id=1, source_target_pairs={{0,28},{2,30},{4,0},{6,2},{8,4},{10,6},{12,8},{14,10},{16,12},{18,... | collective-permute-start | bytes 786440 | tf_op jit(solution)/shard_map/ppermute | solution.py:383
  31.8 1.3 %collective-permute-start.8 = (bf16[8,32,128]{2,1,0:T(8,128)(2,1)S(1)}, bf16[8,32,128]{2,1,0:T(8,128)(2,1)S(1)}, u32[]{:S(2)}, u32[]{:S(2)}) collective-permute-start(bf16[8,32,128]{2,1,0:T(8,128)(2,1)S(1)} %get-tuple-element.65), channel_id=1, source_target_pairs={{0,2},{2,0},{4,6},{6,4},{8,10},{10,8},{12,14},{14,12},{16,18},{18,... | collective-permute-start | bytes 196616 | tf_op jit(solution)/shard_map/ppermute | solution.py:389
  32.0 9.6 %collective-permute-start.13 = (bf16[128,1024]{1,0:T(8,128)(2,1)S(1)}, bf16[128,1024]{1,0:T(8,128)(2,1)S(1)}, u32[]{:S(2)}, u32[]{:S(2)}) collective-permute-start(bf16[128,1024]{1,0:T(8,128)(2,1)S(1)} %get-tuple-element.68), channel_id=1, source_target_pairs={{0,2},{2,0},{4,6},{6,4},{8,10},{10,8},{12,14},{14,12},{16,18},{18,... | collective-permute-start | bytes 786440 | tf_op jit(solution)/shard_map/ppermute | solution.py:389
  32.4 11.4 %collective-permute-start.14 = (bf16[128,1024]{1,0:T(8,128)(2,1)S(1)}, bf16[128,1024]{1,0:T(8,128)(2,1)S(1)}, u32[]{:S(2)}, u32[]{:S(2)}) collective-permute-start(bf16[128,1024]{1,0:T(8,128)(2,1)S(1)} %get-tuple-element.69), channel_id=1, source_target_pairs={{0,2},{2,0},{4,6},{6,4},{8,10},{10,8},{12,14},{14,12},{16,18},{18,... | collective-permute-start | bytes 786440 | tf_op jit(solution)/shard_map/ppermute | solution.py:389
  33.1 5.8 %collective-permute-start.11 = (bf16[2,32,128]{2,1,0:T(8,128)(2,1)S(1)}, bf16[2,32,128]{2,1,0:T(8,128)(2,1)S(1)}, u32[]{:S(2)}, u32[]{:S(2)}) collective-permute-start(bf16[2,32,128]{2,1,0:T(8,128)(2,1)S(1)} %get-tuple-element.86), channel_id=1, source_target_pairs={{0,12},{1,13},{2,14},{3,15},{4,8},{5,9},{6,10},{7,11},{8,4},{9,5},... | collective-permute-start | bytes 49160 | tf_op jit(solution)/shard_map/ppermute | solution.py:564
  35.6 3.7 %collective-permute-start.10 = (bf16[2,32,128]{2,1,0:T(8,128)(2,1)S(1)}, bf16[2,32,128]{2,1,0:T(8,128)(2,1)S(1)}, u32[]{:S(2)}, u32[]{:S(2)}) collective-permute-start(bf16[2,32,128]{2,1,0:T(8,128)(2,1)S(1)} %get-tuple-element.87), channel_id=1, source_target_pairs={{0,4},{1,5},{2,6},{3,7},{4,0},{5,1},{6,2},{7,3},{8,12},{9,13},{10,... | collective-permute-start | bytes 49160 | tf_op jit(solution)/shard_map/ppermute | solution.py:564
  36.2 3.7 %collective-permute-start.9 = (bf16[2,32,128]{2,1,0:T(8,128)(2,1)S(1)}, bf16[2,32,128]{2,1,0:T(8,128)(2,1)S(1)}, u32[]{:S(2)}, u32[]{:S(2)}) collective-permute-start(bf16[2,32,128]{2,1,0:T(8,128)(2,1)S(1)} %get-tuple-element.85), channel_id=1, source_target_pairs={{0,8},{1,9},{2,10},{3,11},{4,12},{5,13},{6,14},{7,15},{8,0},{9,1},... | collective-permute-start | bytes 49160 | tf_op jit(solution)/shard_map/ppermute | solution.py:564
  39.0 6.3 %collective-permute-start.15 = (bf16[128,1024]{1,0:T(8,128)(2,1)S(1)}, bf16[128,1024]{1,0:T(8,128)(2,1)S(1)}, u32[]{:S(2)}, u32[]{:S(2)}) collective-permute-start(bf16[128,1024]{1,0:T(8,128)(2,1)S(1)} %get-tuple-element.76), channel_id=1, source_target_pairs={{0,2},{2,0},{4,6},{6,4},{8,10},{10,8},{12,14},{14,12},{16,18},{18,... | collective-permute-start | bytes 786440 | tf_op jit(solution)/shard_map/ppermute | solution.py:389
  39.4 5.9 %collective-permute-start.16 = (bf16[128,1024]{1,0:T(8,128)(2,1)S(1)}, bf16[128,1024]{1,0:T(8,128)(2,1)S(1)}, u32[]{:S(2)}, u32[]{:S(2)}) collective-permute-start(bf16[128,1024]{1,0:T(8,128)(2,1)S(1)} %get-tuple-element.77), channel_id=1, source_target_pairs={{0,2},{2,0},{4,6},{6,4},{8,10},{10,8},{12,14},{14,12},{16,18},{18,... | collective-permute-start | bytes 786440 | tf_op jit(solution)/shard_map/ppermute | solution.py:389
  40.0 6.1 %collective-permute-start.12 = (bf16[1,32,128]{2,1,0:T(8,128)(2,1)S(1)}, bf16[1,32,128]{2,1,0:T(8,128)(2,1)S(1)}, u32[]{:S(2)}, u32[]{:S(2)}) collective-permute-start(bf16[1,32,128]{2,1,0:T(8,128)(2,1)S(1)} %get-tuple-element.89), channel_id=1, source_target_pairs={{0,1},{1,0},{2,3},{3,2},{4,5},{5,4},{6,7},{7,6},{8,9},{9,8},{10,11... | collective-permute-start | bytes 24584 | tf_op jit(solution)/shard_map/ppermute | solution.py:564
  41.6 5.4 %collective-permute-start.18 = (bf16[1,32,128]{2,1,0:T(8,128)(2,1)S(1)}, bf16[1,32,128]{2,1,0:T(8,128)(2,1)S(1)}, u32[]{:S(2)}, u32[]{:S(2)}) collective-permute-start(bf16[1,32,128]{2,1,0:T(8,128)(2,1)S(1)} %get-tuple-element.88), channel_id=1, source_target_pairs={{0,17},{1,16},{2,19},{3,18},{4,21},{5,20},{6,23},{7,22},{8,25},{9,... | collective-permute-start | bytes 24584 | tf_op jit(solution)/shard_map/ppermute | solution.py:564
  43.8 4.6 %collective-permute-start.17 = (bf16[1,32,128]{2,1,0:T(8,128)(2,1)S(1)}, bf16[1,32,128]{2,1,0:T(8,128)(2,1)S(1)}, u32[]{:S(2)}, u32[]{:S(2)}) collective-permute-start(bf16[1,32,128]{2,1,0:T(8,128)(2,1)S(1)} %get-tuple-element.88), channel_id=1, source_target_pairs={{0,16},{1,17},{2,18},{3,19},{4,20},{5,21},{6,22},{7,23},{8,24},{9,... | collective-permute-start | bytes 24584 | tf_op jit(solution)/shard_map/ppermute | solution.py:564

commit v7 on v6

--- a/solution.py
+++ b/solution.py
@@ -8,6 +8,7 @@
 F32 = jnp.float32
 BF16 = jnp.bfloat16
 TAPS = 4
+PLANE = 4
 MASKED = -1e30
 VMEM_BYTES = 24 * 2**20
 BLOCKS = 5
@@ -116,6 +117,17 @@
         copy.wait()
 
 
+def choose_kernel(own_ref, got_ref, out_ref):
+    first_chip = lax.axis_index("seq") % PLANE < 2
+    out_ref[...] = jnp.where(first_chip, own_ref[...], got_ref[...])
+
+
+def join_kernel(a_ref, b_ref, out_ref):
+    slot = a_ref.shape[2]
+    out_ref[:, :, :slot] = a_ref[...]
+    out_ref[:, :, slot:] = b_ref[...]
+
+
 def own_kernel(
     reach_ref, reach_s_ref, k_ref, v_ref, q_ref, g_ref, got_ref, w_ref,
     kv_ref, near_ref, stat_ref, kt_ref, vt_ref, bias_ref,
@@ -128,7 +140,7 @@
     mine = lax.axis_index("seq")
     partner = mine + 1 - 2 * (mine % 2)
     even = mine % 2 == 0
-    sources = (mine - mine % 2, mine - 2, partner - 2, mine - 4, partner - 4)
+    sources = (mine - mine % 2, mine - 2, mine - 4, partner - 2, partner - 4)
     for b, source in enumerate(sources):
         for u, (reader, limit) in enumerate(((mine, reach_ref), (partner, reach_s_ref))):
             steps = reader - source
@@ -184,15 +196,15 @@
 
 def memory_kernel(
     bias_ref, q_ref, qs_ref, g_ref, gs_ref, stat_ref,
-    near_ref, r2_ref, r2s_ref, r4_ref, r4s_ref,
-    t0_ref, t2_ref, t4_ref, w_ref, d_ref, fin_ref,
+    near_ref, joined_ref, r2s_ref, r4s_ref,
+    t0_ref, t2k_ref, t2v_ref, t4k_ref, t4v_ref, w_ref, d_ref, fin_ref,
 ):
     seg, width = q_ref.shape
     heads = stat_ref.shape[1]
     feat = width // heads
     slot = seg // TAPS
     scale = feat**-0.5
-    slots = (near_ref, r2_ref, r2s_ref, r4_ref, r4s_ref)
+    slots = (near_ref, joined_ref, r2s_ref, r4s_ref)
 
     def both(a_ref, b_ref, h):
         return jnp.concatenate([a_ref[:, head(h, feat)], b_ref[:, head(h, feat)]], 0)
@@ -230,15 +242,15 @@
             t0_ref[kv, h] = terms[:slot]
             terms = terms.astype(BF16)
             for i in range(4):
-                (t2_ref, t4_ref)[i // 2][i % 2, kv, h] = terms[(i + 1) * slot : (i + 2) * slot]
+                ((t2k_ref, t2v_ref), (t4k_ref, t4v_ref))[i % 2][kv][i // 2, h] = terms[(i + 1) * slot : (i + 2) * slot]
 
     staged(list(range(heads)), first, second, third)
 
 
 def output_kernel(*refs):
     q_ref, qs_ref, g_ref, gs_ref, kv_ref = refs[:5]
-    slots = refs[5 : 5 + BLOCKS]
-    w_ref, d_ref, fin_ref, *results = refs[5 + BLOCKS :]
+    slots = refs[5:9]
+    w_ref, d_ref, fin_ref, *results = refs[9:]
     att_ref, gq_ref, givea_ref, giveg_ref, terms_ref = results
     seg, width = q_ref.shape
     feat = slots[0].shape[3]
@@ -286,15 +298,23 @@
     staged([(h, u) for h in range(heads) for u in range(2)], first, second, third, 4)
 
 
-def first_sum_kernel(t0_ref, b4_ref, low_ref):
-    even = lax.axis_index("seq") % 2 == 0
-    for kv in range(2):
-        for u in range(2):
-            low = jnp.where(even == (u == 0), t0_ref[kv], 0.0)
-            low_ref[u, kv] = low + b4_ref[u, kv].astype(F32)
-
-
-def sum_kernel(kt_ref, vt_ref, low_ref, b2_ref, mg_ref, mine_ref, other_ref):
+def relay_kernel(own_ref, passed_ref, out_ref):
+    first_chip = lax.axis_index("seq") % PLANE < 2
+    passed = jnp.where(first_chip, 0.0, passed_ref[...].astype(F32))
+    out_ref[...] = (own_ref[...].astype(F32) + passed).astype(BF16)
+
+
+def first_sum_kernel(t0_ref, k4_ref, k2_ref, v2_ref, low_ref):
+    position = lax.axis_index("seq")
+    even = position % 2 == 0
+    first_chip = position % PLANE < 2
+    for u in range(2):
+        near = [jnp.where(even == (u == 0), t0_ref[kv], 0.0) for kv in range(2)]
+        low_ref[0, u] = near[0] + k4_ref[u].astype(F32) + k2_ref[u].astype(F32)
+        low_ref[1, u] = near[1] + jnp.where(first_chip, v2_ref[u].astype(F32), 0.0)
+
+
+def sum_kernel(kt_ref, vt_ref, low_ref, v4_ref, mg_ref, mine_ref, other_ref):
     count = mine_ref.shape[0] * 2
     feat = mine_ref.shape[2]
     even = lax.axis_index("seq") % 2 == 0
@@ -302,7 +322,10 @@
     for kv, turned_ref in enumerate((kt_ref, vt_ref)):
         rows = []
         for u in range(2):
-            low = (low_ref[u, kv] + b2_ref[u, kv].astype(F32)).astype(BF16)
+            low = low_ref[kv, u]
+            if kv == 1:
+                low = low + v4_ref[u].astype(F32)
+            low = low.astype(BF16)
             mg_ref[kv, u] = low
             rows.append(low.reshape(-1, feat))
         terms = terms + nn(turned_ref[...], jnp.concatenate(rows, 0))
@@ -382,6 +405,15 @@
     def shift(value, steps):
         return lax.ppermute(value, "seq", [(s, (s + steps) % count) for s in range(count)])
 
+    def shift_part(value, steps):
+        return lax.ppermute(
+            value, "seq", [(s, s + steps) for s in range(count) if 0 <= s + steps < count]
+        )
+
+    def cross_part(value, steps):
+        pairs = [(s, (s ^ 1) + steps) for s in range(count)]
+        return lax.ppermute(value, "seq", [(s, t) for s, t in pairs if t < count])
+
     def cross(value, steps):
         return lax.ppermute(value, "seq", [(s, ((s ^ 1) + steps) % count) for s in range(count)])
 
@@ -417,10 +449,17 @@
     )(*[in_hbm(a) for a in (k, v, q, g, compress_kernel)])
     got = trade(give)
 
+    r4s = cross(packed_other, 4)
+    r2 = shift(packed_mine, 2)
     r4 = shift(packed_mine, 4)
-    r2 = shift(packed_mine, 2)
-    r4s = cross(packed_other, 4)
-    r2s = cross(packed_other, 2)
+    plane = range(0, count, PLANE)
+    r2s = lax.ppermute(
+        call(
+            choose_kernel, shape(half_dims), [full(half_dims)] * 2, full(half_dims), 0, row_bytes
+        )(packed_other, r4s),
+        "seq",
+        [(p + s, p + t) for p in plane for s, t in ((0, 3), (1, 2), (2, 0), (3, 1))],
+    )
     got, late_reach = lax.optimization_barrier((got, memory_reach))
     scalar = pl.BlockSpec(memory_space=pltpu.SMEM)
     kvp, near, own_stats, kt, vt, bias = call(
@@ -445,24 +484,33 @@
         unit, 8 * row_bytes, heads * seg * seg,
     )(late_reach, trade(late_reach), k, v, q, g, got, compress_kernel)
 
-    slots = [near, r2, r2s, r4, r4s]
+    r2, own_stats = lax.optimization_barrier((r2, own_stats))
+    joined_dims = (2, half, 2 * slot, feat)
+    joined = call(
+        join_kernel, shape(joined_dims), [full(half_dims)] * 2, full(joined_dims), 0, 10 * row_bytes
+    )(r2, r4)
+    slots = [near, joined, r2s, r4s]
     got_q = pl.BlockSpec((seg, half * feat), lambda i: (2, 0))
     got_g = pl.BlockSpec((seg, half * feat), lambda i: (3, 0))
     one = (2, half, slot, feat)
     soft = (half, span, 2 * seg)
     stats = (3, half, 1, 2 * seg)
     pair = (2, 2, half, slot, feat)
-    t0, t2, t4, w_mem, d_mem, final = call(
+    t0, t2k, t2v, t4k, t4v, w_mem, d_mem, final = call(
         memory_kernel,
-        (shape(one, F32), *[shape(pair)] * 2, shape(soft), shape(soft), shape(stats, F32)),
+        (shape(one, F32), *[shape(one)] * 4, shape(soft), shape(soft), shape(stats, F32)),
         [full((span, 2 * seg)), mine_cols, got_q, mine_cols, got_g, full(stats)]
-        + [full(one)] * BLOCKS,
-        (full(one), *[full(pair)] * 2, full(soft), full(soft), full(stats)),
+        + [full(one), full(joined_dims), full(one), full(one)],
+        (full(one), *[full(one)] * 4, full(soft), full(soft), full(stats)),
         4 * unit, 8 * row_bytes, heads * seg * seg,
     )(bias, q, got, g, got, own_stats, *slots)
 
-    back4 = shift(t4, -4)
-    back2 = shift(t2, -2)
+    v2 = trade(t2v, 2)
+    k4 = shift_part(t4k, -4)
+    k2 = shift(t2k, -2)
+    v4 = shift_part(
+        call(relay_kernel, shape(one), [full(one)] * 2, full(one), 0, row_bytes)(t4v, v2), -4
+    )
     attended, grad_queries, give_a, give_g, own_terms = call(
         output_kernel,
         (
@@ -473,7 +521,7 @@
             shape((2, 2, seg, half * feat), F32),
         ),
         [mine_cols, got_q, mine_cols, got_g, full((2, 2, seg, half * feat))]
-        + [full(one)] * BLOCKS
+        + [full(one), full(joined_dims), full(one), full(one)]
         + [full(soft), full(soft), full(stats)],
         (
             mine_cols, mine_cols,
@@ -501,16 +549,20 @@
     split = (count // 2, kernel_rows // count, feat)
     turned = full((TAPS * feat, heads * slot))
     low = call(
-        first_sum_kernel, shape(pair, F32), [full(one), full(pair)], full(pair), 0, 2 * row_bytes * 10
-    )(t0, back4)
+        first_sum_kernel,
+        shape(pair, F32),
+        [full(one)] * 4,
+        full(pair),
+        0, 4 * row_bytes,
+    )(t0, k4, k2, v2)
     low, own_terms = lax.optimization_barrier((low, own_terms))
     memory_grads, mine, other = call(
         sum_kernel,
         (shape(pair), shape(split, F32), shape(split)),
-        [turned] * 2 + [full(pair)] * 2,
+        [turned] * 2 + [full(pair), full(one)],
         (full(pair), full(split), full(split)),
         unit, 4 * row_bytes,
-    )(kt, vt, low, back2)
+    )(kt, vt, low, v4)
 
     grad_keys, grad_values, give_k, give_v = call(
         back_kernel,

time: 49.1 us -> 48.7 us (level)
  waiting for transfers between devices: 11.2 us -> 10.2 us
  starting transfers between devices: 23.6 us -> 24.1 us
    ppermute x0 -> x3, starting transfers between devices: none -> 4.22 us  [the longest x2 2.57 us: shift_part(): lax.ppermute(value, 'seq', [(s, s + steps) for s in range(count) if 0 <=...]
    ppermute x0 -> x3, waiting for transfers between devices: none -> 3.69 us  [the longest x2 2.6 us: shift_part(): lax.ppermute(value, 'seq', [(s, s + steps) for s in range(count) if 0 <=...]
    ppermute x4 -> x3, waiting for transfers between devices: 3.7 us -> 0.01 us  [shift(): lax.ppermute(value, 'seq', [(s, (s + steps) % count) for s in range(count)])]
    ppermute x4 -> x3, starting transfers between devices: 10.4 us -> 6.74 us  [shift(): lax.ppermute(value, 'seq', [(s, (s + steps) % count) for s in range(count)])]
    ppermute x6, waiting for transfers between devices: 3.04 us -> 0.97 us  [reduce_rest(): arrived.append(lax.ppermute(sent.astype(BF16), ('seq', 'dp'), pairs))]
    ppermute x7 -> x8, waiting for transfers between devices: 1.53 us -> 2.74 us  [trade(): return lax.ppermute(value, 'seq', [(s, s ^ flip) for s in range(count)])]
    ppermute x6, starting transfers between devices: 8.91 us -> 8.01 us  [reduce_rest(): arrived.append(lax.ppermute(sent.astype(BF16), ('seq', 'dp'), pairs))]
    ppermute x7 -> x8, starting transfers between devices: 1.81 us -> 2.42 us  [trade(): return lax.ppermute(value, 'seq', [(s, s ^ flip) for s in range(count)])]
  transfers between devices with their start and end apart: 19 -> 21, of which waited for: 9 -> 7; matrix products, arithmetic and copies ran while one was open for 0% -> 0% of each run, Pallas kernels for 16% -> 16%
where the time goes in v7:
time: 48.7 us; the launch traced here: 48.5 us
  starting transfers between devices  24.1 us (49%)
  Pallas kernels  11.9 us (24%)
  waiting for transfers between devices  10.2 us (21%)
  between operations  1.63 us (3%)
  other arithmetic  0.64 us (1%)
    ppermute x6, starting transfers between devices, reduce_rest(): arrived.append(lax.ppermute(sent.astype(BF16), ('seq', 'dp'), pairs))  8.01 us
    ppermute x3, starting transfers between devices, shift(): lax.ppermute(value, 'seq', [(s, (s + steps) % count) for s in range(count)])  6.74 us
    pallas_call x1, Pallas kernels, local(): call(output_kernel, (shape((seg, width)), shape((seg, width)), shape((seg...  2.85 us
    ppermute x1, waiting for transfers between devices, cross(): lax.ppermute(value, 'seq', [(s, ((s ^ 1) + steps) % count) for s in range...  2.77 us
    ppermute x8, waiting for transfers between devices, trade(): return lax.ppermute(value, 'seq', [(s, s ^ flip) for s in range(count)])  2.74 us
    ppermute x1, starting transfers between devices, cross(): lax.ppermute(value, 'seq', [(s, ((s ^ 1) + steps) % count) for s in range...  2.68 us
    ppermute x2, waiting for transfers between devices, shift_part(): lax.ppermute(value, 'seq', [(s, s + steps) for s in range(count) if 0 <=...  2.6 us
    ppermute x2, starting transfers between devices, shift_part(): lax.ppermute(value, 'seq', [(s, s + steps) for s in range(count) if 0 <=...  2.57 us
  transfers between devices with their start and end apart: 21, of which 7 were waited for; matrix products, arithmetic and copies ran while one was open for 0% of the time, Pallas kernels for 16%

profile of v7, /device:TPU:0, one launch (start us, length us, event | category | flops | bytes accessed | tf_op | source)
XLA Modules:
  0.0 48.5 jit_solution(8524700180681127465)
XLA Ops:
  0.7 2.2 %shard_map.101 = (bf16[2,8,32,128]{3,2,1,0:T(8,128)(2,1)S(1)}, bf16[2,8,32,128]{3,2,1,0:T(8,128)(2,1)S(1)}, bf16[512,1024]{1,0:T(8,128)(2,1)S(1)}) custom-call(bf16[128,2048]{1,0:T(8,128)(2,1)} %bitcast.31, bf16[128,2048]{1,0:T(8,128)(2,1)} %bitcast.33, bf16[128,2048]{1,0:T(8,128)(2,1)} %bitcast.23, bf16[128,2048]{1,0:T(8,128)(2,1)} %bitcast.27, ...), custom_call_target="tpu_custom_call" | custom-call | flops 201326592 | bytes 2621440 | tf_op jit(solution)/shard_map/pallas_call | solution.py:438
  3.4 2.7 %collective-permute-start.4 = (bf16[2,8,32,128]{3,2,1,0:T(8,128)(2,1)S(1)}, bf16[2,8,32,128]{3,2,1,0:T(8,128)(2,1)S(1)}, u32[]{:S(2)}, u32[]{:S(2)}) collective-permute-start(bf16[2,8,32,128]{3,2,1,0:T(8,128)(2,1)S(1)} %get-tuple-element.60.own_ref), channel_id=1, source_target_pairs={{0,10},{2,8},{4,14},{6,12},{8,18},{10,16},{12,22},{14,20},{16,26},... | collective-permute-start | bytes 393224 | tf_op jit(solution)/shard_map/ppermute | solution.py:418
  6.1 1.5 %collective-permute-start.2 = (bf16[2,8,32,128]{3,2,1,0:T(8,128)(2,1)S(1)}, bf16[2,8,32,128]{3,2,1,0:T(8,128)(2,1)S(1)}, u32[]{:S(2)}, u32[]{:S(2)}) collective-permute-start(bf16[2,8,32,128]{3,2,1,0:T(8,128)(2,1)S(1)} %get-tuple-element.55), channel_id=1, source_target_pairs={{0,4},{2,6},{4,8},{6,10},{8,12},{10,14},{12,16},{14,18},{16,20},{1... | collective-permute-start | bytes 393224 | tf_op jit(solution)/shard_map/ppermute | solution.py:406
  7.6 1.6 %collective-permute-start.3 = (bf16[2,8,32,128]{3,2,1,0:T(8,128)(2,1)S(1)}, bf16[2,8,32,128]{3,2,1,0:T(8,128)(2,1)S(1)}, u32[]{:S(2)}, u32[]{:S(2)}) collective-permute-start(bf16[2,8,32,128]{3,2,1,0:T(8,128)(2,1)S(1)} %get-tuple-element.55), channel_id=1, source_target_pairs={{0,8},{2,10},{4,12},{6,14},{8,16},{10,18},{12,20},{14,22},{16,24},... | collective-permute-start | bytes 393224 | tf_op jit(solution)/shard_map/ppermute | solution.py:406
  9.2 2.8 %collective-permute-done.4.got_ref.r4s_ref.refs_8_ = bf16[2,8,32,128]{3,2,1,0:T(8,128)(2,1)S(1)} collective-permute-done((bf16[2,8,32,128]{3,2,1,0:T(8,128)(2,1)S(1)}, bf16[2,8,32,128]{3,2,1,0:T(8,128)(2,1)S(1)}, u32[]{:S(2)}, u32[]{:S(2)}) %collective-permute-start.4) | collective-permute-done | bytes 131104 | tf_op jit(solution)/shard_map/ppermute | solution.py:418
  12.0 1.7 %collective-permute-start.5 = (bf16[2,8,32,128]{3,2,1,0:T(8,128)(2,1)S(1)}, bf16[2,8,32,128]{3,2,1,0:T(8,128)(2,1)S(1)}, u32[]{:S(2)}, u32[]{:S(2)}) collective-permute-start(bf16[2,8,32,128]{3,2,1,0:T(8,128)(2,1)S(1)} %shard_map.104), channel_id=1, source_target_pairs={{0,6},{2,4},{4,0},{6,2},{8,14},{10,12},{12,8},{14,10},{16,22},{18,... | collective-permute-start | bytes 393224 | tf_op jit(solution)/shard_map/ppermute | solution.py:456
  14.4 1.4 %collective-permute-done.1.reach_s_ref = s32[1,1]{1,0:T(1,128)} collective-permute-done((s32[1,1]{1,0:T(1,128)}, s32[1,1]{1,0:T(1,128)}, u32[]{:S(2)}, u32[]{:S(2)}) %collective-permute-start.1) | collective-permute-done | bytes 36 | tf_op jit(solution)/shard_map/ppermute | solution.py:421
  15.8 1.8 %shard_map.102 = (bf16[2,2,128,1024]{3,2,1,0:T(8,128)(2,1)S(1)}, bf16[2,8,32,128]{3,2,1,0:T(8,128)(2,1)S(1)}, f32[3,8,1,256]{3,2,1,0:T(1,128)S(1)}, bf16[512,512...) custom-call(s32[1,1]{1,0:T(1,128)S(6)} %copy.19.reach_ref, ...), custom_call_target="tpu_custom_call" | custom-call | flops 67108864 | bytes 4194304 | tf_op jit(solution)/shard_map/pallas_call | solution.py:465
  17.6 1.1 %collective-permute-done.5.r2s_ref.refs_7_ = bf16[2,8,32,128]{3,2,1,0:T(8,128)(2,1)S(1)} collective-permute-done((bf16[2,8,32,128]{3,2,1,0:T(8,128)(2,1)S(1)}, bf16[2,8,32,128]{3,2,1,0:T(8,128)(2,1)S(1)}, u32[]{:S(2)}, u32[]{:S(2)}) %collective-permute-start.5) | collective-permute-done | bytes 131104 | tf_op jit(solution)/shard_map/ppermute | solution.py:456
  18.7 1.4 %shard_map.105 = (f32[2,8,32,128]{3,2,1,0:T(8,128)S(1)}, bf16[2,8,32,128]{3,2,1,0:T(8,128)(2,1)S(1)}, bf16[2,8,32,128]{3,2,1,0:T(8,128)(2,1)S(1)}, bf16[2,8,32,1...) custom-call(f32[160,256]{1,0:T(8,128)S(1)} %get-tuple-element.54.bia, ...), custom_call_target="tpu_custom_call" | custom-call | flops 268435456 | bytes 4194304 | tf_op jit(solution)/shard_map/pallas_call | solution.py:499
  20.8 1.3 %collective-permute-start.6 = (bf16[2,8,32,128]{3,2,1,0:T(8,128)(2,1)S(1)}, bf16[2,8,32,128]{3,2,1,0:T(8,128)(2,1)S(1)}, u32[]{:S(2)}, u32[]{:S(2)}) collective-permute-start(bf16[2,8,32,128]{3,2,1,0:T(8,128)(2,1)S(1)} %get-tuple-element.62), channel_id=1, source_target_pairs={{8,0},{10,2},{12,4},{14,6},{16,8},{18,10},{20,12},{22,14},{24,16},... | collective-permute-start | bytes 393224 | tf_op jit(solution)/shard_map/ppermute | solution.py:409
  22.1 3.7 %collective-permute-start.7 = (bf16[2,8,32,128]{3,2,1,0:T(8,128)(2,1)S(1)}, bf16[2,8,32,128]{3,2,1,0:T(8,128)(2,1)S(1)}, u32[]{:S(2)}, u32[]{:S(2)}) collective-permute-start(bf16[2,8,32,128]{3,2,1,0:T(8,128)(2,1)S(1)} %get-tuple-element.63), channel_id=1, source_target_pairs={{0,28},{2,30},{4,0},{6,2},{8,4},{10,6},{12,8},{14,10},{16,12},{18,... | collective-permute-start | bytes 393224 | tf_op jit(solution)/shard_map/ppermute | solution.py:406
  25.8 0.8 %collective-permute-done.8.v2_ref.passed_ref = bf16[2,8,32,128]{3,2,1,0:T(8,128)(2,1)S(1)} collective-permute-done((bf16[2,8,32,128]{3,2,1,0:T(8,128)(2,1)S(1)}, bf16[2,8,32,128]{3,2,1,0:T(8,128)(2,1)S(1)}, u32[]{:S(2)}, u32[]{:S(2)}) %collective-permute-start.8) | collective-permute-done | bytes 131104 | tf_op jit(solution)/shard_map/ppermute | solution.py:421
  26.6 1.3 %collective-permute-start.9 = (bf16[2,8,32,128]{3,2,1,0:T(8,128)(2,1)S(1)}, bf16[2,8,32,128]{3,2,1,0:T(8,128)(2,1)S(1)}, u32[]{:S(2)}, u32[]{:S(2)}) collective-permute-start(bf16[2,8,32,128]{3,2,1,0:T(8,128)(2,1)S(1)} %shard_map.108), channel_id=1, source_target_pairs={{8,0},{10,2},{12,4},{14,6},{16,8},{18,10},{20,12},{22,14},{24,16},... | collective-permute-start | bytes 393224 | tf_op jit(solution)/shard_map/ppermute | solution.py:409
  27.9 2.9 %shard_map.107 = (bf16[128,2048]{1,0:T(8,128)(2,1)}, bf16[128,2048]{1,0:T(8,128)(2,1)}, bf16[128,1024]{1,0:T(8,128)(2,1)S(1)}, bf16[128,1024]{1,0:T(8,128)(2,1)S(1)}, f32[2,2,128,1024]{3,2,1,0:T(8,128)S(1)}) custom-call(bf16[128,2048]{1,0:T(8,128)(2,1)S(1)} %bitcast.26, bf16[512,1024]{1,0:T(8,128)(2,1)S(1)} %collective-permute-done.got_ref.qs_ref.gs_ref.refs_1_.refs_3_, ...), custom_call_target="tpu_custom_call" | custom-call | flops 536870912 | bytes 6291456 | tf_op jit(solution)/shard_map/pallas_call | solution.py:514
  30.9 2.6 %collective-permute-done.9.v4_ref = bf16[2,8,32,128]{3,2,1,0:T(8,128)(2,1)S(1)} collective-permute-done((bf16[2,8,32,128]{3,2,1,0:T(8,128)(2,1)S(1)}, bf16[2,8,32,128]{3,2,1,0:T(8,128)(2,1)S(1)}, u32[]{:S(2)}, u32[]{:S(2)}) %collective-permute-start.9) | collective-permute-done | bytes 131104 | tf_op jit(solution)/shard_map/ppermute | solution.py:409
  35.4 1.0 %collective-permute-start.13 = (bf16[2,32,128]{2,1,0:T(8,128)(2,1)S(1)}, bf16[2,32,128]{2,1,0:T(8,128)(2,1)S(1)}, u32[]{:S(2)}, u32[]{:S(2)}) collective-permute-start(bf16[2,32,128]{2,1,0:T(8,128)(2,1)S(1)} %get-tuple-element.94), channel_id=1, source_target_pairs={{0,12},{1,13},{2,14},{3,15},{4,8},{5,9},{6,10},{7,11},{8,4},{9,5},... | collective-permute-start | bytes 49160 | tf_op jit(solution)/shard_map/ppermute | solution.py:616
  36.4 2.4 %collective-permute-start.12 = (bf16[2,32,128]{2,1,0:T(8,128)(2,1)S(1)}, bf16[2,32,128]{2,1,0:T(8,128)(2,1)S(1)}, u32[]{:S(2)}, u32[]{:S(2)}) collective-permute-start(bf16[2,32,128]{2,1,0:T(8,128)(2,1)S(1)} %get-tuple-element.95), channel_id=1, source_target_pairs={{0,4},{1,5},{2,6},{3,7},{4,0},{5,1},{6,2},{7,3},{8,12},{9,13},{10,... | collective-permute-start | bytes 49160 | tf_op jit(solution)/shard_map/ppermute | solution.py:616
  38.9 1.4 %shard_map.111 = (bf16[128,2048]{1,0:T(8,128)(2,1)}, bf16[128,2048]{1,0:T(8,128)(2,1)}, bf16[128,1024]{1,0:T(8,128)(2,1)S(1)}, bf16[128,1024]{1,0:T(8,128)(2,1)S(1)}) custom-call(bf16[2,2,8,32,128]{4,3,2,1,0:T(8,128)(2,1)S(1)} %get-tuple-element.80.mg_ref, bf16[512,128]{1,0:T(8,128)(2,1)S(1)} %copy-done.4, f32[2,2,128,1024]{3,2,1,0:T(8,128)S(1)} %get-tuple-element.81.terms_ref), custom_call_target="tpu_custom_call" | custom-call | flops 268435456 | bytes 3670016 | tf_op jit(solution)/shard_map/pallas_call | solution.py:567
  40.8 1.6 %collective-permute-start.14 = (bf16[1,32,128]{2,1,0:T(8,128)(2,1)S(1)}, bf16[1,32,128]{2,1,0:T(8,128)(2,1)S(1)}, u32[]{:S(2)}, u32[]{:S(2)}) collective-permute-start(bf16[1,32,128]{2,1,0:T(8,128)(2,1)S(1)} %get-tuple-element.97), channel_id=1, source_target_pairs={{0,1},{1,0},{2,3},{3,2},{4,5},{5,4},{6,7},{7,6},{8,9},{9,8},{10,11... | collective-permute-start | bytes 24584 | tf_op jit(solution)/shard_map/ppermute | solution.py:616
  43.0 2.3 %collective-permute-start.19 = (bf16[1,32,128]{2,1,0:T(8,128)(2,1)S(1)}, bf16[1,32,128]{2,1,0:T(8,128)(2,1)S(1)}, u32[]{:S(2)}, u32[]{:S(2)}) collective-permute-start(bf16[1,32,128]{2,1,0:T(8,128)(2,1)S(1)} %get-tuple-element.96), channel_id=1, source_target_pairs={{0,16},{1,17},{2,18},{3,19},{4,20},{5,21},{6,22},{7,23},{8,24},{9,... | collective-permute-start | bytes 24584 | tf_op jit(solution)/shard_map/ppermute | solution.py:616
  45.3 0.8 %shard_map.110 = (bf16[128,2048]{1,0:T(8,128)(2,1)}, bf16[128,2048]{1,0:T(8,128)(2,1)}) custom-call(bf16[128,2048]{1,0:T(8,128)(2,1)} %get-tuple-element.74.a_in, bf16[128,2048]{1,0:T(8,128)(2,1)} %get-tuple-element.75.b_in, bf16[128,1024]{1,0:T(8,128)(2,1)S(1)} %collective-permute-done.15.got_a, ...), custom_call_target="tpu_custom_call", output_to_operand_aliasing={{0}: (0, {}), {1}: (1, {})} | custom-call | bytes 1048576 | tf_op jit(solution)/shard_map/pallas_call | solution.py:537
  46.1 0.8 %shard_map.112 = (bf16[128,2048]{1,0:T(8,128)(2,1)}, bf16[128,2048]{1,0:T(8,128)(2,1)}) custom-call(bf16[128,2048]{1,0:T(8,128)(2,1)} %get-tuple-element.82.a_in, bf16[128,2048]{1,0:T(8,128)(2,1)} %get-tuple-element.83.b_in, bf16[128,1024]{1,0:T(8,128)(2,1)S(1)} %collective-permute-done.17.got_a, ...), custom_call_target="tpu_custom_call", output_to_operand_aliasing={{0}: (0, {}), {1}: (1, {})} | custom-call | bytes 1048576 | tf_op jit(solution)/shard_map/pallas_call | solution.py:537
  46.9 1.0 %collective-permute-done.20 = bf16[1,32,128]{2,1,0:T(8,128)(2,1)S(1)} collective-permute-done((bf16[1,32,128]{2,1,0:T(8,128)(2,1)S(1)}, bf16[1,32,128]{2,1,0:T(8,128)(2,1)S(1)}, u32[]{:S(2)}, u32[]{:S(2)}) %collective-permute-start.20) | collective-permute-done | bytes 8224 | tf_op jit(solution)/shard_map/ppermute | solution.py:616
  (45 shorter events, 5.1 us)
Async XLA Ops:
  0.6 15.1 %copy-start.4 = (bf16[512,128]{1,0:T(8,128)(2,1)S(1)}, bf16[512,128]{1,0:T(8,128)(2,1)}, u32[]{:S(2)}) copy-start(bf16[512,128]{1,0:T(8,128)(2,1)} %w_ref.3) | copy-start | bytes 393220
  0.6 15.1 %copy-start.1 = (bf16[1,128,2048]{2,1,0:T(8,128)(2,1)S(1)}, bf16[1,128,2048]{2,1,0:T(8,128)(2,1)}, u32[]{:S(2)}) copy-start(bf16[1,128,2048]{2,1,0:T(8,128)(2,1)} %param.9) | copy-start | bytes 1572868
  0.7 15.1 %copy-start.3 = (bf16[1,128,2048]{2,1,0:T(8,128)(2,1)S(1)}, bf16[1,128,2048]{2,1,0:T(8,128)(2,1)}, u32[]{:S(2)}) copy-start(bf16[1,128,2048]{2,1,0:T(8,128)(2,1)} %param.8) | copy-start | bytes 1572868
  2.9 11.4 %collective-permute-start = (bf16[512,1024]{1,0:T(8,128)(2,1)S(1)}, bf16[512,1024]{1,0:T(8,128)(2,1)S(1)}, u32[]{:S(2)}, u32[]{:S(2)}) collective-permute-start(bf16[512,1024]{1,0:T(8,128)(2,1)S(1)} %get-tuple-element.49), channel_id=1, source_target_pairs={{0,2},{2,0},{4,6},{6,4},{8,10},{10,8},{12,14},{14,12},{16,18},{18,... | collective-permute-start | bytes 3145736 | tf_op jit(solution)/shard_map/ppermute | solution.py:421
  3.4 8.5 %collective-permute-start.4 = (bf16[2,8,32,128]{3,2,1,0:T(8,128)(2,1)S(1)}, bf16[2,8,32,128]{3,2,1,0:T(8,128)(2,1)S(1)}, u32[]{:S(2)}, u32[]{:S(2)}) collective-permute-start(bf16[2,8,32,128]{3,2,1,0:T(8,128)(2,1)S(1)} %get-tuple-element.60.own_ref), channel_id=1, source_target_pairs={{0,10},{2,8},{4,14},{6,12},{8,18},{10,16},{12,22},{14,20},{16,26},... | collective-permute-start | bytes 393224 | tf_op jit(solution)/shard_map/ppermute | solution.py:418
  6.1 11.5 %collective-permute-start.2 = (bf16[2,8,32,128]{3,2,1,0:T(8,128)(2,1)S(1)}, bf16[2,8,32,128]{3,2,1,0:T(8,128)(2,1)S(1)}, u32[]{:S(2)}, u32[]{:S(2)}) collective-permute-start(bf16[2,8,32,128]{3,2,1,0:T(8,128)(2,1)S(1)} %get-tuple-element.55), channel_id=1, source_target_pairs={{0,4},{2,6},{4,8},{6,10},{8,12},{10,14},{12,16},{14,18},{16,20},{1... | collective-permute-start | bytes 393224 | tf_op jit(solution)/shard_map/ppermute | solution.py:406
  7.6 10.0 %collective-permute-start.3 = (bf16[2,8,32,128]{3,2,1,0:T(8,128)(2,1)S(1)}, bf16[2,8,32,128]{3,2,1,0:T(8,128)(2,1)S(1)}, u32[]{:S(2)}, u32[]{:S(2)}) collective-permute-start(bf16[2,8,32,128]{3,2,1,0:T(8,128)(2,1)S(1)} %get-tuple-element.55), channel_id=1, source_target_pairs={{0,8},{2,10},{4,12},{6,14},{8,16},{10,18},{12,20},{14,22},{16,24},... | collective-permute-start | bytes 393224 | tf_op jit(solution)/shard_map/ppermute | solution.py:406
  12.0 6.7 %collective-permute-start.5 = (bf16[2,8,32,128]{3,2,1,0:T(8,128)(2,1)S(1)}, bf16[2,8,32,128]{3,2,1,0:T(8,128)(2,1)S(1)}, u32[]{:S(2)}, u32[]{:S(2)}) collective-permute-start(bf16[2,8,32,128]{3,2,1,0:T(8,128)(2,1)S(1)} %shard_map.104), channel_id=1, source_target_pairs={{0,6},{2,4},{4,0},{6,2},{8,14},{10,12},{12,8},{14,10},{16,22},{18,... | collective-permute-start | bytes 393224 | tf_op jit(solution)/shard_map/ppermute | solution.py:456
  14.3 1.5 %collective-permute-start.1 = (s32[1,1]{1,0:T(1,128)}, s32[1,1]{1,0:T(1,128)}, u32[]{:S(2)}, u32[]{:S(2)}) collective-permute-start(s32[1,1]{1,0:T(1,128)} %param.11), channel_id=1, source_target_pairs={{0,2},{2,0},{4,6},{6,4},{8,10},{10,8},{12,14},{14,12},{16,18},{18,... | collective-permute-start | bytes 20 | tf_op jit(solution)/shard_map/ppermute | solution.py:421
  20.2 6.4 %collective-permute-start.8 = (bf16[2,8,32,128]{3,2,1,0:T(8,128)(2,1)S(1)}, bf16[2,8,32,128]{3,2,1,0:T(8,128)(2,1)S(1)}, u32[]{:S(2)}, u32[]{:S(2)}) collective-permute-start(bf16[2,8,32,128]{3,2,1,0:T(8,128)(2,1)S(1)} %get-tuple-element.64), channel_id=1, source_target_pairs={{0,4},{2,6},{4,0},{6,2},{8,12},{10,14},{12,8},{14,10},{16,20},{18,... | collective-permute-start | bytes 393224 | tf_op jit(solution)/shard_map/ppermute | solution.py:421
  20.8 10.0 %collective-permute-start.6 = (bf16[2,8,32,128]{3,2,1,0:T(8,128)(2,1)S(1)}, bf16[2,8,32,128]{3,2,1,0:T(8,128)(2,1)S(1)}, u32[]{:S(2)}, u32[]{:S(2)}) collective-permute-start(bf16[2,8,32,128]{3,2,1,0:T(8,128)(2,1)S(1)} %get-tuple-element.62), channel_id=1, source_target_pairs={{8,0},{10,2},{12,4},{14,6},{16,8},{18,10},{20,12},{22,14},{24,16},... | collective-permute-start | bytes 393224 | tf_op jit(solution)/shard_map/ppermute | solution.py:409
  22.1 8.7 %collective-permute-start.7 = (bf16[2,8,32,128]{3,2,1,0:T(8,128)(2,1)S(1)}, bf16[2,8,32,128]{3,2,1,0:T(8,128)(2,1)S(1)}, u32[]{:S(2)}, u32[]{:S(2)}) collective-permute-start(bf16[2,8,32,128]{3,2,1,0:T(8,128)(2,1)S(1)} %get-tuple-element.63), channel_id=1, source_target_pairs={{0,28},{2,30},{4,0},{6,2},{8,4},{10,6},{12,8},{14,10},{16,12},{18,... | collective-permute-start | bytes 393224 | tf_op jit(solution)/shard_map/ppermute | solution.py:406
  26.6 6.9 %collective-permute-start.9 = (bf16[2,8,32,128]{3,2,1,0:T(8,128)(2,1)S(1)}, bf16[2,8,32,128]{3,2,1,0:T(8,128)(2,1)S(1)}, u32[]{:S(2)}, u32[]{:S(2)}) collective-permute-start(bf16[2,8,32,128]{3,2,1,0:T(8,128)(2,1)S(1)} %shard_map.108), channel_id=1, source_target_pairs={{8,0},{10,2},{12,4},{14,6},{16,8},{18,10},{20,12},{22,14},{24,16},... | collective-permute-start | bytes 393224 | tf_op jit(solution)/shard_map/ppermute | solution.py:409
  34.0 1.3 %collective-permute-start.10 = (bf16[8,32,128]{2,1,0:T(8,128)(2,1)S(1)}, bf16[8,32,128]{2,1,0:T(8,128)(2,1)S(1)}, u32[]{:S(2)}, u32[]{:S(2)}) collective-permute-start(bf16[8,32,128]{2,1,0:T(8,128)(2,1)S(1)} %get-tuple-element.73), channel_id=1, source_target_pairs={{0,2},{2,0},{4,6},{6,4},{8,10},{10,8},{12,14},{14,12},{16,18},{18,... | collective-permute-start | bytes 196616 | tf_op jit(solution)/shard_map/ppermute | solution.py:421
  34.1 8.3 %collective-permute-start.15 = (bf16[128,1024]{1,0:T(8,128)(2,1)S(1)}, bf16[128,1024]{1,0:T(8,128)(2,1)S(1)}, u32[]{:S(2)}, u32[]{:S(2)}) collective-permute-start(bf16[128,1024]{1,0:T(8,128)(2,1)S(1)} %get-tuple-element.76), channel_id=1, source_target_pairs={{0,2},{2,0},{4,6},{6,4},{8,10},{10,8},{12,14},{14,12},{16,18},{18,... | collective-permute-start | bytes 786440 | tf_op jit(solution)/shard_map/ppermute | solution.py:421
  34.5 8.5 %collective-permute-start.16 = (bf16[128,1024]{1,0:T(8,128)(2,1)S(1)}, bf16[128,1024]{1,0:T(8,128)(2,1)S(1)}, u32[]{:S(2)}, u32[]{:S(2)}) collective-permute-start(bf16[128,1024]{1,0:T(8,128)(2,1)S(1)} %get-tuple-element.77), channel_id=1, source_target_pairs={{0,2},{2,0},{4,6},{6,4},{8,10},{10,8},{12,14},{14,12},{16,18},{18,... | collective-permute-start | bytes 786440 | tf_op jit(solution)/shard_map/ppermute | solution.py:421
  35.3 4.9 %collective-permute-start.11 = (bf16[2,32,128]{2,1,0:T(8,128)(2,1)S(1)}, bf16[2,32,128]{2,1,0:T(8,128)(2,1)S(1)}, u32[]{:S(2)}, u32[]{:S(2)}) collective-permute-start(bf16[2,32,128]{2,1,0:T(8,128)(2,1)S(1)} %get-tuple-element.93), channel_id=1, source_target_pairs={{0,8},{1,9},{2,10},{3,11},{4,12},{5,13},{6,14},{7,15},{8,0},{9,1},... | collective-permute-start | bytes 49160 | tf_op jit(solution)/shard_map/ppermute | solution.py:616
  35.4 4.8 %collective-permute-start.13 = (bf16[2,32,128]{2,1,0:T(8,128)(2,1)S(1)}, bf16[2,32,128]{2,1,0:T(8,128)(2,1)S(1)}, u32[]{:S(2)}, u32[]{:S(2)}) collective-permute-start(bf16[2,32,128]{2,1,0:T(8,128)(2,1)S(1)} %get-tuple-element.94), channel_id=1, source_target_pairs={{0,12},{1,13},{2,14},{3,15},{4,8},{5,9},{6,10},{7,11},{8,4},{9,5},... | collective-permute-start | bytes 49160 | tf_op jit(solution)/shard_map/ppermute | solution.py:616
  36.4 4.3 %collective-permute-start.12 = (bf16[2,32,128]{2,1,0:T(8,128)(2,1)S(1)}, bf16[2,32,128]{2,1,0:T(8,128)(2,1)S(1)}, u32[]{:S(2)}, u32[]{:S(2)}) collective-permute-start(bf16[2,32,128]{2,1,0:T(8,128)(2,1)S(1)} %get-tuple-element.95), channel_id=1, source_target_pairs={{0,4},{1,5},{2,6},{3,7},{4,0},{5,1},{6,2},{7,3},{8,12},{9,13},{10,... | collective-permute-start | bytes 49160 | tf_op jit(solution)/shard_map/ppermute | solution.py:616
  40.3 5.8 %collective-permute-start.17 = (bf16[128,1024]{1,0:T(8,128)(2,1)S(1)}, bf16[128,1024]{1,0:T(8,128)(2,1)S(1)}, u32[]{:S(2)}, u32[]{:S(2)}) collective-permute-start(bf16[128,1024]{1,0:T(8,128)(2,1)S(1)} %get-tuple-element.84), channel_id=1, source_target_pairs={{0,2},{2,0},{4,6},{6,4},{8,10},{10,8},{12,14},{14,12},{16,18},{18,... | collective-permute-start | bytes 786440 | tf_op jit(solution)/shard_map/ppermute | solution.py:421
  40.3 5.8 %collective-permute-start.18 = (bf16[128,1024]{1,0:T(8,128)(2,1)S(1)}, bf16[128,1024]{1,0:T(8,128)(2,1)S(1)}, u32[]{:S(2)}, u32[]{:S(2)}) collective-permute-start(bf16[128,1024]{1,0:T(8,128)(2,1)S(1)} %get-tuple-element.85), channel_id=1, source_target_pairs={{0,2},{2,0},{4,6},{6,4},{8,10},{10,8},{12,14},{14,12},{16,18},{18,... | collective-permute-start | bytes 786440 | tf_op jit(solution)/shard_map/ppermute | solution.py:421
  40.8 6.1 %collective-permute-start.14 = (bf16[1,32,128]{2,1,0:T(8,128)(2,1)S(1)}, bf16[1,32,128]{2,1,0:T(8,128)(2,1)S(1)}, u32[]{:S(2)}, u32[]{:S(2)}) collective-permute-start(bf16[1,32,128]{2,1,0:T(8,128)(2,1)S(1)} %get-tuple-element.97), channel_id=1, source_target_pairs={{0,1},{1,0},{2,3},{3,2},{4,5},{5,4},{6,7},{7,6},{8,9},{9,8},{10,11... | collective-permute-start | bytes 24584 | tf_op jit(solution)/shard_map/ppermute | solution.py:616
  42.4 5.5 %collective-permute-start.20 = (bf16[1,32,128]{2,1,0:T(8,128)(2,1)S(1)}, bf16[1,32,128]{2,1,0:T(8,128)(2,1)S(1)}, u32[]{:S(2)}, u32[]{:S(2)}) collective-permute-start(bf16[1,32,128]{2,1,0:T(8,128)(2,1)S(1)} %get-tuple-element.96), channel_id=1, source_target_pairs={{0,17},{1,16},{2,19},{3,18},{4,21},{5,20},{6,23},{7,22},{8,25},{9,... | collective-permute-start | bytes 24584 | tf_op jit(solution)/shard_map/ppermute | solution.py:616
  43.0 4.9 %collective-permute-start.19 = (bf16[1,32,128]{2,1,0:T(8,128)(2,1)S(1)}, bf16[1,32,128]{2,1,0:T(8,128)(2,1)S(1)}, u32[]{:S(2)}, u32[]{:S(2)}) collective-permute-start(bf16[1,32,128]{2,1,0:T(8,128)(2,1)S(1)} %get-tuple-element.96), channel_id=1, source_target_pairs={{0,16},{1,17},{2,18},{3,19},{4,20},{5,21},{6,22},{7,23},{8,24},{9,... | collective-permute-start | bytes 24584 | tf_op jit(solution)/shard_map/ppermute | solution.py:616
  (2 other events, 30.2 us)

commit v8 on v7

--- a/solution.py
+++ b/solution.py
@@ -216,8 +216,7 @@
         )
 
     def second(h, scores, grad_weights):
-        bias = bias_ref[...]
-        scores = jnp.where(bias < 0.0, MASKED, scores * scale)
+        scores = scores * scale + bias_ref[...]
         own_top = stat_ref[0, h]
         top = jnp.maximum(own_top, jnp.max(scores, axis=0, keepdims=True))
         raised = jnp.exp(scores - top)
@@ -284,7 +283,8 @@
         terms_ref[1, u, :, cols] = nn(weights_low, grads[u][:, cols])
 
         def whole(kv, own, memory):
-            return tn(own, kv_ref[kv, u, :, cols]) + tn(memory, memory_rows(kv, h, slots))
+            rows = jnp.concatenate([kv_ref[kv, u, :, cols], memory_rows(kv, h, slots)], 0)
+            return tn(jnp.concatenate([own, memory], 0), rows)
 
         att = whole(1, weights_low, w_ref[h, :, side]).astype(BF16)
         gq = whole(0, grad_scores, d_ref[h, :, side]).astype(BF16)

time: 48.7 us -> 48.7 us (level)
  no operation moved by 1% of the time
where the time goes in v8:
time: 48.7 us; the launch traced here: 48.5 us
  starting transfers between devices  24.1 us (49%)
  Pallas kernels  11.9 us (24%)
  waiting for transfers between devices  10.2 us (21%)
  between operations  1.63 us (3%)
  other arithmetic  0.64 us (1%)
    ppermute x6, starting transfers between devices, reduce_rest(): arrived.append(lax.ppermute(sent.astype(BF16), ('seq', 'dp'), pairs))  8.01 us
    ppermute x3, starting transfers between devices, shift(): lax.ppermute(value, 'seq', [(s, (s + steps) % count) for s in range(count)])  6.74 us
    pallas_call x1, Pallas kernels, local(): call(output_kernel, (shape((seg, width)), shape((seg, width)), shape((seg...  2.85 us
    ppermute x1, waiting for transfers between devices, cross(): lax.ppermute(value, 'seq', [(s, ((s ^ 1) + steps) % count) for s in range...  2.77 us
    ppermute x8, waiting for transfers between devices, trade(): return lax.ppermute(value, 'seq', [(s, s ^ flip) for s in range(count)])  2.74 us
    ppermute x1, starting transfers between devices, cross(): lax.ppermute(value, 'seq', [(s, ((s ^ 1) + steps) % count) for s in range...  2.68 us
    ppermute x2, waiting for transfers between devices, shift_part(): lax.ppermute(value, 'seq', [(s, s + steps) for s in range(count) if 0 <=...  2.61 us
    ppermute x2, starting transfers between devices, shift_part(): lax.ppermute(value, 'seq', [(s, s + steps) for s in range(count) if 0 <=...  2.57 us
  transfers between devices with their start and end apart: 21, of which 7 were waited for; matrix products, arithmetic and copies ran while one was open for 0% of the time, Pallas kernels for 16%

profile of v8, /device:TPU:0, one launch (start us, length us, event | category | flops | bytes accessed | tf_op | source)
XLA Modules:
  0.0 48.5 jit_solution(11770176428446393820)
XLA Ops:
  0.7 2.2 %shard_map.101 = (bf16[2,8,32,128]{3,2,1,0:T(8,128)(2,1)S(1)}, bf16[2,8,32,128]{3,2,1,0:T(8,128)(2,1)S(1)}, bf16[512,1024]{1,0:T(8,128)(2,1)S(1)}) custom-call(bf16[128,2048]{1,0:T(8,128)(2,1)} %bitcast.31, bf16[128,2048]{1,0:T(8,128)(2,1)} %bitcast.33, bf16[128,2048]{1,0:T(8,128)(2,1)} %bitcast.23, bf16[128,2048]{1,0:T(8,128)(2,1)} %bitcast.27, ...), custom_call_target="tpu_custom_call" | custom-call | flops 201326592 | bytes 2621440 | tf_op jit(solution)/shard_map/pallas_call | solution.py:438
  3.4 2.7 %collective-permute-start.4 = (bf16[2,8,32,128]{3,2,1,0:T(8,128)(2,1)S(1)}, bf16[2,8,32,128]{3,2,1,0:T(8,128)(2,1)S(1)}, u32[]{:S(2)}, u32[]{:S(2)}) collective-permute-start(bf16[2,8,32,128]{3,2,1,0:T(8,128)(2,1)S(1)} %get-tuple-element.60.own_ref), channel_id=1, source_target_pairs={{0,10},{2,8},{4,14},{6,12},{8,18},{10,16},{12,22},{14,20},{16,26},... | collective-permute-start | bytes 393224 | tf_op jit(solution)/shard_map/ppermute | solution.py:418
  6.1 1.5 %collective-permute-start.2 = (bf16[2,8,32,128]{3,2,1,0:T(8,128)(2,1)S(1)}, bf16[2,8,32,128]{3,2,1,0:T(8,128)(2,1)S(1)}, u32[]{:S(2)}, u32[]{:S(2)}) collective-permute-start(bf16[2,8,32,128]{3,2,1,0:T(8,128)(2,1)S(1)} %get-tuple-element.55), channel_id=1, source_target_pairs={{0,4},{2,6},{4,8},{6,10},{8,12},{10,14},{12,16},{14,18},{16,20},{1... | collective-permute-start | bytes 393224 | tf_op jit(solution)/shard_map/ppermute | solution.py:406
  7.6 1.6 %collective-permute-start.3 = (bf16[2,8,32,128]{3,2,1,0:T(8,128)(2,1)S(1)}, bf16[2,8,32,128]{3,2,1,0:T(8,128)(2,1)S(1)}, u32[]{:S(2)}, u32[]{:S(2)}) collective-permute-start(bf16[2,8,32,128]{3,2,1,0:T(8,128)(2,1)S(1)} %get-tuple-element.55), channel_id=1, source_target_pairs={{0,8},{2,10},{4,12},{6,14},{8,16},{10,18},{12,20},{14,22},{16,24},... | collective-permute-start | bytes 393224 | tf_op jit(solution)/shard_map/ppermute | solution.py:406
  9.2 2.8 %collective-permute-done.4.got_ref.r4s_ref.refs_8_ = bf16[2,8,32,128]{3,2,1,0:T(8,128)(2,1)S(1)} collective-permute-done((bf16[2,8,32,128]{3,2,1,0:T(8,128)(2,1)S(1)}, bf16[2,8,32,128]{3,2,1,0:T(8,128)(2,1)S(1)}, u32[]{:S(2)}, u32[]{:S(2)}) %collective-permute-start.4) | collective-permute-done | bytes 131104 | tf_op jit(solution)/shard_map/ppermute | solution.py:418
  12.0 1.7 %collective-permute-start.5 = (bf16[2,8,32,128]{3,2,1,0:T(8,128)(2,1)S(1)}, bf16[2,8,32,128]{3,2,1,0:T(8,128)(2,1)S(1)}, u32[]{:S(2)}, u32[]{:S(2)}) collective-permute-start(bf16[2,8,32,128]{3,2,1,0:T(8,128)(2,1)S(1)} %shard_map.104), channel_id=1, source_target_pairs={{0,6},{2,4},{4,0},{6,2},{8,14},{10,12},{12,8},{14,10},{16,22},{18,... | collective-permute-start | bytes 393224 | tf_op jit(solution)/shard_map/ppermute | solution.py:456
  14.4 1.4 %collective-permute-done.1.reach_s_ref = s32[1,1]{1,0:T(1,128)} collective-permute-done((s32[1,1]{1,0:T(1,128)}, s32[1,1]{1,0:T(1,128)}, u32[]{:S(2)}, u32[]{:S(2)}) %collective-permute-start.1) | collective-permute-done | bytes 36 | tf_op jit(solution)/shard_map/ppermute | solution.py:421
  15.8 1.8 %shard_map.102 = (bf16[2,2,128,1024]{3,2,1,0:T(8,128)(2,1)S(1)}, bf16[2,8,32,128]{3,2,1,0:T(8,128)(2,1)S(1)}, f32[3,8,1,256]{3,2,1,0:T(1,128)S(1)}, bf16[512,512...) custom-call(s32[1,1]{1,0:T(1,128)S(6)} %copy.19.reach_ref, ...), custom_call_target="tpu_custom_call" | custom-call | flops 67108864 | bytes 4194304 | tf_op jit(solution)/shard_map/pallas_call | solution.py:465
  17.6 1.1 %collective-permute-done.5.r2s_ref.refs_7_ = bf16[2,8,32,128]{3,2,1,0:T(8,128)(2,1)S(1)} collective-permute-done((bf16[2,8,32,128]{3,2,1,0:T(8,128)(2,1)S(1)}, bf16[2,8,32,128]{3,2,1,0:T(8,128)(2,1)S(1)}, u32[]{:S(2)}, u32[]{:S(2)}) %collective-permute-start.5) | collective-permute-done | bytes 131104 | tf_op jit(solution)/shard_map/ppermute | solution.py:456
  18.7 1.4 %shard_map.105 = (f32[2,8,32,128]{3,2,1,0:T(8,128)S(1)}, bf16[2,8,32,128]{3,2,1,0:T(8,128)(2,1)S(1)}, bf16[2,8,32,128]{3,2,1,0:T(8,128)(2,1)S(1)}, bf16[2,8,32,1...) custom-call(f32[160,256]{1,0:T(8,128)S(1)} %get-tuple-element.54.bia, ...), custom_call_target="tpu_custom_call" | custom-call | flops 268435456 | bytes 4194304 | tf_op jit(solution)/shard_map/pallas_call | solution.py:499
  20.8 1.3 %collective-permute-start.6 = (bf16[2,8,32,128]{3,2,1,0:T(8,128)(2,1)S(1)}, bf16[2,8,32,128]{3,2,1,0:T(8,128)(2,1)S(1)}, u32[]{:S(2)}, u32[]{:S(2)}) collective-permute-start(bf16[2,8,32,128]{3,2,1,0:T(8,128)(2,1)S(1)} %get-tuple-element.62), channel_id=1, source_target_pairs={{8,0},{10,2},{12,4},{14,6},{16,8},{18,10},{20,12},{22,14},{24,16},... | collective-permute-start | bytes 393224 | tf_op jit(solution)/shard_map/ppermute | solution.py:409
  22.1 3.7 %collective-permute-start.7 = (bf16[2,8,32,128]{3,2,1,0:T(8,128)(2,1)S(1)}, bf16[2,8,32,128]{3,2,1,0:T(8,128)(2,1)S(1)}, u32[]{:S(2)}, u32[]{:S(2)}) collective-permute-start(bf16[2,8,32,128]{3,2,1,0:T(8,128)(2,1)S(1)} %get-tuple-element.63), channel_id=1, source_target_pairs={{0,28},{2,30},{4,0},{6,2},{8,4},{10,6},{12,8},{14,10},{16,12},{18,... | collective-permute-start | bytes 393224 | tf_op jit(solution)/shard_map/ppermute | solution.py:406
  25.7 0.8 %collective-permute-done.8.v2_ref.passed_ref = bf16[2,8,32,128]{3,2,1,0:T(8,128)(2,1)S(1)} collective-permute-done((bf16[2,8,32,128]{3,2,1,0:T(8,128)(2,1)S(1)}, bf16[2,8,32,128]{3,2,1,0:T(8,128)(2,1)S(1)}, u32[]{:S(2)}, u32[]{:S(2)}) %collective-permute-start.8) | collective-permute-done | bytes 131104 | tf_op jit(solution)/shard_map/ppermute | solution.py:421
  26.6 1.3 %collective-permute-start.9 = (bf16[2,8,32,128]{3,2,1,0:T(8,128)(2,1)S(1)}, bf16[2,8,32,128]{3,2,1,0:T(8,128)(2,1)S(1)}, u32[]{:S(2)}, u32[]{:S(2)}) collective-permute-start(bf16[2,8,32,128]{3,2,1,0:T(8,128)(2,1)S(1)} %shard_map.108), channel_id=1, source_target_pairs={{8,0},{10,2},{12,4},{14,6},{16,8},{18,10},{20,12},{22,14},{24,16},... | collective-permute-start | bytes 393224 | tf_op jit(solution)/shard_map/ppermute | solution.py:409
  27.9 2.9 %shard_map.107 = (bf16[128,2048]{1,0:T(8,128)(2,1)}, bf16[128,2048]{1,0:T(8,128)(2,1)}, bf16[128,1024]{1,0:T(8,128)(2,1)S(1)}, bf16[128,1024]{1,0:T(8,128)(2,1)S(1)}, f32[2,2,128,1024]{3,2,1,0:T(8,128)S(1)}) custom-call(bf16[128,2048]{1,0:T(8,128)(2,1)S(1)} %bitcast.26, bf16[512,1024]{1,0:T(8,128)(2,1)S(1)} %collective-permute-done.got_ref.qs_ref.gs_ref.refs_1_.refs_3_, ...), custom_call_target="tpu_custom_call" | custom-call | flops 536870912 | bytes 6291456 | tf_op jit(solution)/shard_map/pallas_call | solution.py:514
  30.8 2.6 %collective-permute-done.9.v4_ref = bf16[2,8,32,128]{3,2,1,0:T(8,128)(2,1)S(1)} collective-permute-done((bf16[2,8,32,128]{3,2,1,0:T(8,128)(2,1)S(1)}, bf16[2,8,32,128]{3,2,1,0:T(8,128)(2,1)S(1)}, u32[]{:S(2)}, u32[]{:S(2)}) %collective-permute-start.9) | collective-permute-done | bytes 131104 | tf_op jit(solution)/shard_map/ppermute | solution.py:409
  35.4 1.0 %collective-permute-start.13 = (bf16[2,32,128]{2,1,0:T(8,128)(2,1)S(1)}, bf16[2,32,128]{2,1,0:T(8,128)(2,1)S(1)}, u32[]{:S(2)}, u32[]{:S(2)}) collective-permute-start(bf16[2,32,128]{2,1,0:T(8,128)(2,1)S(1)} %get-tuple-element.94), channel_id=1, source_target_pairs={{0,12},{1,13},{2,14},{3,15},{4,8},{5,9},{6,10},{7,11},{8,4},{9,5},... | collective-permute-start | bytes 49160 | tf_op jit(solution)/shard_map/ppermute | solution.py:616
  36.4 2.4 %collective-permute-start.12 = (bf16[2,32,128]{2,1,0:T(8,128)(2,1)S(1)}, bf16[2,32,128]{2,1,0:T(8,128)(2,1)S(1)}, u32[]{:S(2)}, u32[]{:S(2)}) collective-permute-start(bf16[2,32,128]{2,1,0:T(8,128)(2,1)S(1)} %get-tuple-element.95), channel_id=1, source_target_pairs={{0,4},{1,5},{2,6},{3,7},{4,0},{5,1},{6,2},{7,3},{8,12},{9,13},{10,... | collective-permute-start | bytes 49160 | tf_op jit(solution)/shard_map/ppermute | solution.py:616
  38.8 1.4 %shard_map.111 = (bf16[128,2048]{1,0:T(8,128)(2,1)}, bf16[128,2048]{1,0:T(8,128)(2,1)}, bf16[128,1024]{1,0:T(8,128)(2,1)S(1)}, bf16[128,1024]{1,0:T(8,128)(2,1)S(1)}) custom-call(bf16[2,2,8,32,128]{4,3,2,1,0:T(8,128)(2,1)S(1)} %get-tuple-element.80.mg_ref, bf16[512,128]{1,0:T(8,128)(2,1)S(1)} %copy-done.4, f32[2,2,128,1024]{3,2,1,0:T(8,128)S(1)} %get-tuple-element.81.terms_ref), custom_call_target="tpu_custom_call" | custom-call | flops 268435456 | bytes 3670016 | tf_op jit(solution)/shard_map/pallas_call | solution.py:567
  40.8 1.6 %collective-permute-start.14 = (bf16[1,32,128]{2,1,0:T(8,128)(2,1)S(1)}, bf16[1,32,128]{2,1,0:T(8,128)(2,1)S(1)}, u32[]{:S(2)}, u32[]{:S(2)}) collective-permute-start(bf16[1,32,128]{2,1,0:T(8,128)(2,1)S(1)} %get-tuple-element.97), channel_id=1, source_target_pairs={{0,1},{1,0},{2,3},{3,2},{4,5},{5,4},{6,7},{7,6},{8,9},{9,8},{10,11... | collective-permute-start | bytes 24584 | tf_op jit(solution)/shard_map/ppermute | solution.py:616
  42.9 2.3 %collective-permute-start.19 = (bf16[1,32,128]{2,1,0:T(8,128)(2,1)S(1)}, bf16[1,32,128]{2,1,0:T(8,128)(2,1)S(1)}, u32[]{:S(2)}, u32[]{:S(2)}) collective-permute-start(bf16[1,32,128]{2,1,0:T(8,128)(2,1)S(1)} %get-tuple-element.96), channel_id=1, source_target_pairs={{0,16},{1,17},{2,18},{3,19},{4,20},{5,21},{6,22},{7,23},{8,24},{9,... | collective-permute-start | bytes 24584 | tf_op jit(solution)/shard_map/ppermute | solution.py:616
  45.2 0.8 %shard_map.110 = (bf16[128,2048]{1,0:T(8,128)(2,1)}, bf16[128,2048]{1,0:T(8,128)(2,1)}) custom-call(bf16[128,2048]{1,0:T(8,128)(2,1)} %get-tuple-element.74.a_in, bf16[128,2048]{1,0:T(8,128)(2,1)} %get-tuple-element.75.b_in, bf16[128,1024]{1,0:T(8,128)(2,1)S(1)} %collective-permute-done.15.got_a, ...), custom_call_target="tpu_custom_call", output_to_operand_aliasing={{0}: (0, {}), {1}: (1, {})} | custom-call | bytes 1048576 | tf_op jit(solution)/shard_map/pallas_call | solution.py:537
  46.0 0.8 %shard_map.112 = (bf16[128,2048]{1,0:T(8,128)(2,1)}, bf16[128,2048]{1,0:T(8,128)(2,1)}) custom-call(bf16[128,2048]{1,0:T(8,128)(2,1)} %get-tuple-element.82.a_in, bf16[128,2048]{1,0:T(8,128)(2,1)} %get-tuple-element.83.b_in, bf16[128,1024]{1,0:T(8,128)(2,1)S(1)} %collective-permute-done.17.got_a, ...), custom_call_target="tpu_custom_call", output_to_operand_aliasing={{0}: (0, {}), {1}: (1, {})} | custom-call | bytes 1048576 | tf_op jit(solution)/shard_map/pallas_call | solution.py:537
  46.9 1.0 %collective-permute-done.20 = bf16[1,32,128]{2,1,0:T(8,128)(2,1)S(1)} collective-permute-done((bf16[1,32,128]{2,1,0:T(8,128)(2,1)S(1)}, bf16[1,32,128]{2,1,0:T(8,128)(2,1)S(1)}, u32[]{:S(2)}, u32[]{:S(2)}) %collective-permute-start.20) | collective-permute-done | bytes 8224 | tf_op jit(solution)/shard_map/ppermute | solution.py:616
  (45 shorter events, 5.1 us)
Async XLA Ops:
  0.6 15.1 %copy-start.4 = (bf16[512,128]{1,0:T(8,128)(2,1)S(1)}, bf16[512,128]{1,0:T(8,128)(2,1)}, u32[]{:S(2)}) copy-start(bf16[512,128]{1,0:T(8,128)(2,1)} %w_ref.3) | copy-start | bytes 393220
  0.6 15.1 %copy-start.1 = (bf16[1,128,2048]{2,1,0:T(8,128)(2,1)S(1)}, bf16[1,128,2048]{2,1,0:T(8,128)(2,1)}, u32[]{:S(2)}) copy-start(bf16[1,128,2048]{2,1,0:T(8,128)(2,1)} %param.9) | copy-start | bytes 1572868
  0.7 15.1 %copy-start.3 = (bf16[1,128,2048]{2,1,0:T(8,128)(2,1)S(1)}, bf16[1,128,2048]{2,1,0:T(8,128)(2,1)}, u32[]{:S(2)}) copy-start(bf16[1,128,2048]{2,1,0:T(8,128)(2,1)} %param.8) | copy-start | bytes 1572868
  2.9 11.4 %collective-permute-start = (bf16[512,1024]{1,0:T(8,128)(2,1)S(1)}, bf16[512,1024]{1,0:T(8,128)(2,1)S(1)}, u32[]{:S(2)}, u32[]{:S(2)}) collective-permute-start(bf16[512,1024]{1,0:T(8,128)(2,1)S(1)} %get-tuple-element.49), channel_id=1, source_target_pairs={{0,2},{2,0},{4,6},{6,4},{8,10},{10,8},{12,14},{14,12},{16,18},{18,... | collective-permute-start | bytes 3145736 | tf_op jit(solution)/shard_map/ppermute | solution.py:421
  3.4 8.5 %collective-permute-start.4 = (bf16[2,8,32,128]{3,2,1,0:T(8,128)(2,1)S(1)}, bf16[2,8,32,128]{3,2,1,0:T(8,128)(2,1)S(1)}, u32[]{:S(2)}, u32[]{:S(2)}) collective-permute-start(bf16[2,8,32,128]{3,2,1,0:T(8,128)(2,1)S(1)} %get-tuple-element.60.own_ref), channel_id=1, source_target_pairs={{0,10},{2,8},{4,14},{6,12},{8,18},{10,16},{12,22},{14,20},{16,26},... | collective-permute-start | bytes 393224 | tf_op jit(solution)/shard_map/ppermute | solution.py:418
  6.1 11.5 %collective-permute-start.2 = (bf16[2,8,32,128]{3,2,1,0:T(8,128)(2,1)S(1)}, bf16[2,8,32,128]{3,2,1,0:T(8,128)(2,1)S(1)}, u32[]{:S(2)}, u32[]{:S(2)}) collective-permute-start(bf16[2,8,32,128]{3,2,1,0:T(8,128)(2,1)S(1)} %get-tuple-element.55), channel_id=1, source_target_pairs={{0,4},{2,6},{4,8},{6,10},{8,12},{10,14},{12,16},{14,18},{16,20},{1... | collective-permute-start | bytes 393224 | tf_op jit(solution)/shard_map/ppermute | solution.py:406
  7.6 10.0 %collective-permute-start.3 = (bf16[2,8,32,128]{3,2,1,0:T(8,128)(2,1)S(1)}, bf16[2,8,32,128]{3,2,1,0:T(8,128)(2,1)S(1)}, u32[]{:S(2)}, u32[]{:S(2)}) collective-permute-start(bf16[2,8,32,128]{3,2,1,0:T(8,128)(2,1)S(1)} %get-tuple-element.55), channel_id=1, source_target_pairs={{0,8},{2,10},{4,12},{6,14},{8,16},{10,18},{12,20},{14,22},{16,24},... | collective-permute-start | bytes 393224 | tf_op jit(solution)/shard_map/ppermute | solution.py:406
  12.0 6.7 %collective-permute-start.5 = (bf16[2,8,32,128]{3,2,1,0:T(8,128)(2,1)S(1)}, bf16[2,8,32,128]{3,2,1,0:T(8,128)(2,1)S(1)}, u32[]{:S(2)}, u32[]{:S(2)}) collective-permute-start(bf16[2,8,32,128]{3,2,1,0:T(8,128)(2,1)S(1)} %shard_map.104), channel_id=1, source_target_pairs={{0,6},{2,4},{4,0},{6,2},{8,14},{10,12},{12,8},{14,10},{16,22},{18,... | collective-permute-start | bytes 393224 | tf_op jit(solution)/shard_map/ppermute | solution.py:456
  14.3 1.5 %collective-permute-start.1 = (s32[1,1]{1,0:T(1,128)}, s32[1,1]{1,0:T(1,128)}, u32[]{:S(2)}, u32[]{:S(2)}) collective-permute-start(s32[1,1]{1,0:T(1,128)} %param.11), channel_id=1, source_target_pairs={{0,2},{2,0},{4,6},{6,4},{8,10},{10,8},{12,14},{14,12},{16,18},{18,... | collective-permute-start | bytes 20 | tf_op jit(solution)/shard_map/ppermute | solution.py:421
  20.1 6.4 %collective-permute-start.8 = (bf16[2,8,32,128]{3,2,1,0:T(8,128)(2,1)S(1)}, bf16[2,8,32,128]{3,2,1,0:T(8,128)(2,1)S(1)}, u32[]{:S(2)}, u32[]{:S(2)}) collective-permute-start(bf16[2,8,32,128]{3,2,1,0:T(8,128)(2,1)S(1)} %get-tuple-element.64), channel_id=1, source_target_pairs={{0,4},{2,6},{4,0},{6,2},{8,12},{10,14},{12,8},{14,10},{16,20},{18,... | collective-permute-start | bytes 393224 | tf_op jit(solution)/shard_map/ppermute | solution.py:421
  20.8 10.0 %collective-permute-start.6 = (bf16[2,8,32,128]{3,2,1,0:T(8,128)(2,1)S(1)}, bf16[2,8,32,128]{3,2,1,0:T(8,128)(2,1)S(1)}, u32[]{:S(2)}, u32[]{:S(2)}) collective-permute-start(bf16[2,8,32,128]{3,2,1,0:T(8,128)(2,1)S(1)} %get-tuple-element.62), channel_id=1, source_target_pairs={{8,0},{10,2},{12,4},{14,6},{16,8},{18,10},{20,12},{22,14},{24,16},... | collective-permute-start | bytes 393224 | tf_op jit(solution)/shard_map/ppermute | solution.py:409
  22.1 8.7 %collective-permute-start.7 = (bf16[2,8,32,128]{3,2,1,0:T(8,128)(2,1)S(1)}, bf16[2,8,32,128]{3,2,1,0:T(8,128)(2,1)S(1)}, u32[]{:S(2)}, u32[]{:S(2)}) collective-permute-start(bf16[2,8,32,128]{3,2,1,0:T(8,128)(2,1)S(1)} %get-tuple-element.63), channel_id=1, source_target_pairs={{0,28},{2,30},{4,0},{6,2},{8,4},{10,6},{12,8},{14,10},{16,12},{18,... | collective-permute-start | bytes 393224 | tf_op jit(solution)/shard_map/ppermute | solution.py:406
  26.6 6.9 %collective-permute-start.9 = (bf16[2,8,32,128]{3,2,1,0:T(8,128)(2,1)S(1)}, bf16[2,8,32,128]{3,2,1,0:T(8,128)(2,1)S(1)}, u32[]{:S(2)}, u32[]{:S(2)}) collective-permute-start(bf16[2,8,32,128]{3,2,1,0:T(8,128)(2,1)S(1)} %shard_map.108), channel_id=1, source_target_pairs={{8,0},{10,2},{12,4},{14,6},{16,8},{18,10},{20,12},{22,14},{24,16},... | collective-permute-start | bytes 393224 | tf_op jit(solution)/shard_map/ppermute | solution.py:409
  33.9 1.3 %collective-permute-start.10 = (bf16[8,32,128]{2,1,0:T(8,128)(2,1)S(1)}, bf16[8,32,128]{2,1,0:T(8,128)(2,1)S(1)}, u32[]{:S(2)}, u32[]{:S(2)}) collective-permute-start(bf16[8,32,128]{2,1,0:T(8,128)(2,1)S(1)} %get-tuple-element.73), channel_id=1, source_target_pairs={{0,2},{2,0},{4,6},{6,4},{8,10},{10,8},{12,14},{14,12},{16,18},{18,... | collective-permute-start | bytes 196616 | tf_op jit(solution)/shard_map/ppermute | solution.py:421
  34.1 8.3 %collective-permute-start.15 = (bf16[128,1024]{1,0:T(8,128)(2,1)S(1)}, bf16[128,1024]{1,0:T(8,128)(2,1)S(1)}, u32[]{:S(2)}, u32[]{:S(2)}) collective-permute-start(bf16[128,1024]{1,0:T(8,128)(2,1)S(1)} %get-tuple-element.76), channel_id=1, source_target_pairs={{0,2},{2,0},{4,6},{6,4},{8,10},{10,8},{12,14},{14,12},{16,18},{18,... | collective-permute-start | bytes 786440 | tf_op jit(solution)/shard_map/ppermute | solution.py:421
  34.5 8.5 %collective-permute-start.16 = (bf16[128,1024]{1,0:T(8,128)(2,1)S(1)}, bf16[128,1024]{1,0:T(8,128)(2,1)S(1)}, u32[]{:S(2)}, u32[]{:S(2)}) collective-permute-start(bf16[128,1024]{1,0:T(8,128)(2,1)S(1)} %get-tuple-element.77), channel_id=1, source_target_pairs={{0,2},{2,0},{4,6},{6,4},{8,10},{10,8},{12,14},{14,12},{16,18},{18,... | collective-permute-start | bytes 786440 | tf_op jit(solution)/shard_map/ppermute | solution.py:421
  35.3 4.9 %collective-permute-start.11 = (bf16[2,32,128]{2,1,0:T(8,128)(2,1)S(1)}, bf16[2,32,128]{2,1,0:T(8,128)(2,1)S(1)}, u32[]{:S(2)}, u32[]{:S(2)}) collective-permute-start(bf16[2,32,128]{2,1,0:T(8,128)(2,1)S(1)} %get-tuple-element.93), channel_id=1, source_target_pairs={{0,8},{1,9},{2,10},{3,11},{4,12},{5,13},{6,14},{7,15},{8,0},{9,1},... | collective-permute-start | bytes 49160 | tf_op jit(solution)/shard_map/ppermute | solution.py:616
  35.4 4.8 %collective-permute-start.13 = (bf16[2,32,128]{2,1,0:T(8,128)(2,1)S(1)}, bf16[2,32,128]{2,1,0:T(8,128)(2,1)S(1)}, u32[]{:S(2)}, u32[]{:S(2)}) collective-permute-start(bf16[2,32,128]{2,1,0:T(8,128)(2,1)S(1)} %get-tuple-element.94), channel_id=1, source_target_pairs={{0,12},{1,13},{2,14},{3,15},{4,8},{5,9},{6,10},{7,11},{8,4},{9,5},... | collective-permute-start | bytes 49160 | tf_op jit(solution)/shard_map/ppermute | solution.py:616
  36.4 4.3 %collective-permute-start.12 = (bf16[2,32,128]{2,1,0:T(8,128)(2,1)S(1)}, bf16[2,32,128]{2,1,0:T(8,128)(2,1)S(1)}, u32[]{:S(2)}, u32[]{:S(2)}) collective-permute-start(bf16[2,32,128]{2,1,0:T(8,128)(2,1)S(1)} %get-tuple-element.95), channel_id=1, source_target_pairs={{0,4},{1,5},{2,6},{3,7},{4,0},{5,1},{6,2},{7,3},{8,12},{9,13},{10,... | collective-permute-start | bytes 49160 | tf_op jit(solution)/shard_map/ppermute | solution.py:616
  40.2 5.8 %collective-permute-start.17 = (bf16[128,1024]{1,0:T(8,128)(2,1)S(1)}, bf16[128,1024]{1,0:T(8,128)(2,1)S(1)}, u32[]{:S(2)}, u32[]{:S(2)}) collective-permute-start(bf16[128,1024]{1,0:T(8,128)(2,1)S(1)} %get-tuple-element.84), channel_id=1, source_target_pairs={{0,2},{2,0},{4,6},{6,4},{8,10},{10,8},{12,14},{14,12},{16,18},{18,... | collective-permute-start | bytes 786440 | tf_op jit(solution)/shard_map/ppermute | solution.py:421
  40.2 5.8 %collective-permute-start.18 = (bf16[128,1024]{1,0:T(8,128)(2,1)S(1)}, bf16[128,1024]{1,0:T(8,128)(2,1)S(1)}, u32[]{:S(2)}, u32[]{:S(2)}) collective-permute-start(bf16[128,1024]{1,0:T(8,128)(2,1)S(1)} %get-tuple-element.85), channel_id=1, source_target_pairs={{0,2},{2,0},{4,6},{6,4},{8,10},{10,8},{12,14},{14,12},{16,18},{18,... | collective-permute-start | bytes 786440 | tf_op jit(solution)/shard_map/ppermute | solution.py:421
  40.8 6.1 %collective-permute-start.14 = (bf16[1,32,128]{2,1,0:T(8,128)(2,1)S(1)}, bf16[1,32,128]{2,1,0:T(8,128)(2,1)S(1)}, u32[]{:S(2)}, u32[]{:S(2)}) collective-permute-start(bf16[1,32,128]{2,1,0:T(8,128)(2,1)S(1)} %get-tuple-element.97), channel_id=1, source_target_pairs={{0,1},{1,0},{2,3},{3,2},{4,5},{5,4},{6,7},{7,6},{8,9},{9,8},{10,11... | collective-permute-start | bytes 24584 | tf_op jit(solution)/shard_map/ppermute | solution.py:616
  42.3 5.5 %collective-permute-start.20 = (bf16[1,32,128]{2,1,0:T(8,128)(2,1)S(1)}, bf16[1,32,128]{2,1,0:T(8,128)(2,1)S(1)}, u32[]{:S(2)}, u32[]{:S(2)}) collective-permute-start(bf16[1,32,128]{2,1,0:T(8,128)(2,1)S(1)} %get-tuple-element.96), channel_id=1, source_target_pairs={{0,17},{1,16},{2,19},{3,18},{4,21},{5,20},{6,23},{7,22},{8,25},{9,... | collective-permute-start | bytes 24584 | tf_op jit(solution)/shard_map/ppermute | solution.py:616
  42.9 4.9 %collective-permute-start.19 = (bf16[1,32,128]{2,1,0:T(8,128)(2,1)S(1)}, bf16[1,32,128]{2,1,0:T(8,128)(2,1)S(1)}, u32[]{:S(2)}, u32[]{:S(2)}) collective-permute-start(bf16[1,32,128]{2,1,0:T(8,128)(2,1)S(1)} %get-tuple-element.96), channel_id=1, source_target_pairs={{0,16},{1,17},{2,18},{3,19},{4,20},{5,21},{6,22},{7,23},{8,24},{9,... | collective-permute-start | bytes 24584 | tf_op jit(solution)/shard_map/ppermute | solution.py:616
  (2 other events, 30.2 us)

commit v9 on v8

--- a/solution.py
+++ b/solution.py
@@ -506,8 +506,8 @@
     )(bias, q, got, g, got, own_stats, *slots)
 
     v2 = trade(t2v, 2)
-    k4 = shift_part(t4k, -4)
-    k2 = shift(t2k, -2)
+    k4 = shift(t4k, -4)
+    k2 = shift_part(t2k, -2)
     v4 = shift_part(
         call(relay_kernel, shape(one), [full(one)] * 2, full(one), 0, row_bytes)(t4v, v2), -4
     )

time: 48.7 us -> 48.6 us (level)
  starting transfers between devices: 24.1 us -> 21.6 us
  waiting for transfers between devices: 10.2 us -> 12.6 us
    ppermute x3, starting transfers between devices: 6.74 us -> 4.76 us  [shift(): lax.ppermute(value, 'seq', [(s, (s + steps) % count) for s in range(count)])]
    ppermute x8, waiting for transfers between devices: 2.74 us -> 3.81 us  [trade(): return lax.ppermute(value, 'seq', [(s, s ^ flip) for s in range(count)])]
    ppermute x6, waiting for transfers between devices: 0.98 us -> 1.88 us  [reduce_rest(): arrived.append(lax.ppermute(sent.astype(BF16), ('seq', 'dp'), pairs))]
    ppermute x8, starting transfers between devices: 2.42 us -> 1.91 us  [trade(): return lax.ppermute(value, 'seq', [(s, s ^ flip) for s in range(count)])]
  transfers between devices with their start and end apart: 21 -> 21, of which waited for: 7 -> 8; matrix products, arithmetic and copies ran while one was open for 0% -> 0% of each run, Pallas kernels for 16% -> 16%
where the time goes in v9:
time: 48.6 us; the launch traced here: 48.4 us
  starting transfers between devices  21.6 us (44%)
  waiting for transfers between devices  12.6 us (26%)
  Pallas kernels  11.9 us (24%)
  between operations  1.63 us (3%)
  other arithmetic  0.64 us (1%)
    ppermute x6, starting transfers between devices, reduce_rest(): arrived.append(lax.ppermute(sent.astype(BF16), ('seq', 'dp'), pairs))  8.01 us
    ppermute x3, starting transfers between devices, shift(): lax.ppermute(value, 'seq', [(s, (s + steps) % count) for s in range(count)])  4.76 us
    ppermute x8, waiting for transfers between devices, trade(): return lax.ppermute(value, 'seq', [(s, s ^ flip) for s in range(count)])  3.81 us
    ppermute x2, waiting for transfers between devices, shift_part(): lax.ppermute(value, 'seq', [(s, s + steps) for s in range(count) if 0 <=...  3.04 us
    pallas_call x1, Pallas kernels, local(): call(output_kernel, (shape((seg, width)), shape((seg, width)), shape((seg...  2.86 us
    ppermute x1, waiting for transfers between devices, cross(): lax.ppermute(value, 'seq', [(s, ((s ^ 1) + steps) % count) for s in range...  2.77 us
    ppermute x1, starting transfers between devices, cross(): lax.ppermute(value, 'seq', [(s, ((s ^ 1) + steps) % count) for s in range...  2.68 us
    ppermute x2, starting transfers between devices, shift_part(): lax.ppermute(value, 'seq', [(s, s + steps) for s in range(count) if 0 <=...  2.57 us
  transfers between devices with their start and end apart: 21, of which 8 were waited for; matrix products, arithmetic and copies ran while one was open for 0% of the time, Pallas kernels for 16%

profile of v9, /device:TPU:0, one launch (start us, length us, event | category | flops | bytes accessed | tf_op | source)
XLA Modules:
  0.0 48.4 jit_solution(8892952776806850577)
XLA Ops:
  0.7 2.2 %shard_map.101 = (bf16[2,8,32,128]{3,2,1,0:T(8,128)(2,1)S(1)}, bf16[2,8,32,128]{3,2,1,0:T(8,128)(2,1)S(1)}, bf16[512,1024]{1,0:T(8,128)(2,1)S(1)}) custom-call(bf16[128,2048]{1,0:T(8,128)(2,1)} %bitcast.31, bf16[128,2048]{1,0:T(8,128)(2,1)} %bitcast.33, bf16[128,2048]{1,0:T(8,128)(2,1)} %bitcast.23, bf16[128,2048]{1,0:T(8,128)(2,1)} %bitcast.27, ...), custom_call_target="tpu_custom_call" | custom-call | flops 201326592 | bytes 2621440 | tf_op jit(solution)/shard_map/pallas_call | solution.py:438
  3.4 2.7 %collective-permute-start.4 = (bf16[2,8,32,128]{3,2,1,0:T(8,128)(2,1)S(1)}, bf16[2,8,32,128]{3,2,1,0:T(8,128)(2,1)S(1)}, u32[]{:S(2)}, u32[]{:S(2)}) collective-permute-start(bf16[2,8,32,128]{3,2,1,0:T(8,128)(2,1)S(1)} %get-tuple-element.60.own_ref), channel_id=1, source_target_pairs={{0,10},{2,8},{4,14},{6,12},{8,18},{10,16},{12,22},{14,20},{16,26},... | collective-permute-start | bytes 393224 | tf_op jit(solution)/shard_map/ppermute | solution.py:418
  6.1 1.5 %collective-permute-start.2 = (bf16[2,8,32,128]{3,2,1,0:T(8,128)(2,1)S(1)}, bf16[2,8,32,128]{3,2,1,0:T(8,128)(2,1)S(1)}, u32[]{:S(2)}, u32[]{:S(2)}) collective-permute-start(bf16[2,8,32,128]{3,2,1,0:T(8,128)(2,1)S(1)} %get-tuple-element.55), channel_id=1, source_target_pairs={{0,4},{2,6},{4,8},{6,10},{8,12},{10,14},{12,16},{14,18},{16,20},{1... | collective-permute-start | bytes 393224 | tf_op jit(solution)/shard_map/ppermute | solution.py:406
  7.6 1.6 %collective-permute-start.3 = (bf16[2,8,32,128]{3,2,1,0:T(8,128)(2,1)S(1)}, bf16[2,8,32,128]{3,2,1,0:T(8,128)(2,1)S(1)}, u32[]{:S(2)}, u32[]{:S(2)}) collective-permute-start(bf16[2,8,32,128]{3,2,1,0:T(8,128)(2,1)S(1)} %get-tuple-element.55), channel_id=1, source_target_pairs={{0,8},{2,10},{4,12},{6,14},{8,16},{10,18},{12,20},{14,22},{16,24},... | collective-permute-start | bytes 393224 | tf_op jit(solution)/shard_map/ppermute | solution.py:406
  9.2 2.8 %collective-permute-done.4.got_ref.r4s_ref.refs_8_ = bf16[2,8,32,128]{3,2,1,0:T(8,128)(2,1)S(1)} collective-permute-done((bf16[2,8,32,128]{3,2,1,0:T(8,128)(2,1)S(1)}, bf16[2,8,32,128]{3,2,1,0:T(8,128)(2,1)S(1)}, u32[]{:S(2)}, u32[]{:S(2)}) %collective-permute-start.4) | collective-permute-done | bytes 131104 | tf_op jit(solution)/shard_map/ppermute | solution.py:418
  12.0 1.7 %collective-permute-start.5 = (bf16[2,8,32,128]{3,2,1,0:T(8,128)(2,1)S(1)}, bf16[2,8,32,128]{3,2,1,0:T(8,128)(2,1)S(1)}, u32[]{:S(2)}, u32[]{:S(2)}) collective-permute-start(bf16[2,8,32,128]{3,2,1,0:T(8,128)(2,1)S(1)} %shard_map.104), channel_id=1, source_target_pairs={{0,6},{2,4},{4,0},{6,2},{8,14},{10,12},{12,8},{14,10},{16,22},{18,... | collective-permute-start | bytes 393224 | tf_op jit(solution)/shard_map/ppermute | solution.py:456
  14.4 1.4 %collective-permute-done.1.reach_s_ref = s32[1,1]{1,0:T(1,128)} collective-permute-done((s32[1,1]{1,0:T(1,128)}, s32[1,1]{1,0:T(1,128)}, u32[]{:S(2)}, u32[]{:S(2)}) %collective-permute-start.1) | collective-permute-done | bytes 36 | tf_op jit(solution)/shard_map/ppermute | solution.py:421
  15.8 1.8 %shard_map.102 = (bf16[2,2,128,1024]{3,2,1,0:T(8,128)(2,1)S(1)}, bf16[2,8,32,128]{3,2,1,0:T(8,128)(2,1)S(1)}, f32[3,8,1,256]{3,2,1,0:T(1,128)S(1)}, bf16[512,512...) custom-call(s32[1,1]{1,0:T(1,128)S(6)} %copy.19.reach_ref, ...), custom_call_target="tpu_custom_call" | custom-call | flops 67108864 | bytes 4194304 | tf_op jit(solution)/shard_map/pallas_call | solution.py:465
  17.6 1.1 %collective-permute-done.5.r2s_ref.refs_7_ = bf16[2,8,32,128]{3,2,1,0:T(8,128)(2,1)S(1)} collective-permute-done((bf16[2,8,32,128]{3,2,1,0:T(8,128)(2,1)S(1)}, bf16[2,8,32,128]{3,2,1,0:T(8,128)(2,1)S(1)}, u32[]{:S(2)}, u32[]{:S(2)}) %collective-permute-start.5) | collective-permute-done | bytes 131104 | tf_op jit(solution)/shard_map/ppermute | solution.py:456
  18.7 1.4 %shard_map.105 = (f32[2,8,32,128]{3,2,1,0:T(8,128)S(1)}, bf16[2,8,32,128]{3,2,1,0:T(8,128)(2,1)S(1)}, bf16[2,8,32,128]{3,2,1,0:T(8,128)(2,1)S(1)}, bf16[2,8,32,1...) custom-call(f32[160,256]{1,0:T(8,128)S(1)} %get-tuple-element.54.bia, ...), custom_call_target="tpu_custom_call" | custom-call | flops 268435456 | bytes 4194304 | tf_op jit(solution)/shard_map/pallas_call | solution.py:499
  20.8 1.7 %collective-permute-start.6 = (bf16[2,8,32,128]{3,2,1,0:T(8,128)(2,1)S(1)}, bf16[2,8,32,128]{3,2,1,0:T(8,128)(2,1)S(1)}, u32[]{:S(2)}, u32[]{:S(2)}) collective-permute-start(bf16[2,8,32,128]{3,2,1,0:T(8,128)(2,1)S(1)} %get-tuple-element.62), channel_id=1, source_target_pairs={{0,24},{2,26},{4,28},{6,30},{8,0},{10,2},{12,4},{14,6},{16,8},{18,... | collective-permute-start | bytes 393224 | tf_op jit(solution)/shard_map/ppermute | solution.py:406
  22.5 1.3 %collective-permute-start.7 = (bf16[2,8,32,128]{3,2,1,0:T(8,128)(2,1)S(1)}, bf16[2,8,32,128]{3,2,1,0:T(8,128)(2,1)S(1)}, u32[]{:S(2)}, u32[]{:S(2)}) collective-permute-start(bf16[2,8,32,128]{3,2,1,0:T(8,128)(2,1)S(1)} %get-tuple-element.63), channel_id=1, source_target_pairs={{4,0},{6,2},{8,4},{10,6},{12,8},{14,10},{16,12},{18,14},{20,16},{2... | collective-permute-start | bytes 393224 | tf_op jit(solution)/shard_map/ppermute | solution.py:409
  23.8 1.9 %collective-permute-done.8.v2_ref.passed_ref = bf16[2,8,32,128]{3,2,1,0:T(8,128)(2,1)S(1)} collective-permute-done((bf16[2,8,32,128]{3,2,1,0:T(8,128)(2,1)S(1)}, bf16[2,8,32,128]{3,2,1,0:T(8,128)(2,1)S(1)}, u32[]{:S(2)}, u32[]{:S(2)}) %collective-permute-start.8) | collective-permute-done | bytes 131104 | tf_op jit(solution)/shard_map/ppermute | solution.py:421
  25.7 1.3 %collective-permute-start.9 = (bf16[2,8,32,128]{3,2,1,0:T(8,128)(2,1)S(1)}, bf16[2,8,32,128]{3,2,1,0:T(8,128)(2,1)S(1)}, u32[]{:S(2)}, u32[]{:S(2)}) collective-permute-start(bf16[2,8,32,128]{3,2,1,0:T(8,128)(2,1)S(1)} %shard_map.108), channel_id=1, source_target_pairs={{8,0},{10,2},{12,4},{14,6},{16,8},{18,10},{20,12},{22,14},{24,16},... | collective-permute-start | bytes 393224 | tf_op jit(solution)/shard_map/ppermute | solution.py:409
  27.0 2.9 %shard_map.107 = (bf16[128,2048]{1,0:T(8,128)(2,1)}, bf16[128,2048]{1,0:T(8,128)(2,1)}, bf16[128,1024]{1,0:T(8,128)(2,1)S(1)}, bf16[128,1024]{1,0:T(8,128)(2,1)S(1)}, f32[2,2,128,1024]{3,2,1,0:T(8,128)S(1)}) custom-call(bf16[128,2048]{1,0:T(8,128)(2,1)S(1)} %bitcast.26, bf16[512,1024]{1,0:T(8,128)(2,1)S(1)} %collective-permute-done.got_ref.qs_ref.gs_ref.refs_1_.refs_3_, ...), custom_call_target="tpu_custom_call" | custom-call | flops 536870912 | bytes 6291456 | tf_op jit(solution)/shard_map/pallas_call | solution.py:514
  29.9 3.0 %collective-permute-done.9.v4_ref = bf16[2,8,32,128]{3,2,1,0:T(8,128)(2,1)S(1)} collective-permute-done((bf16[2,8,32,128]{3,2,1,0:T(8,128)(2,1)S(1)}, bf16[2,8,32,128]{3,2,1,0:T(8,128)(2,1)S(1)}, u32[]{:S(2)}, u32[]{:S(2)}) %collective-permute-start.9) | collective-permute-done | bytes 131104 | tf_op jit(solution)/shard_map/ppermute | solution.py:409
  34.8 1.3 %collective-permute-start.11 = (bf16[2,32,128]{2,1,0:T(8,128)(2,1)S(1)}, bf16[2,32,128]{2,1,0:T(8,128)(2,1)S(1)}, u32[]{:S(2)}, u32[]{:S(2)}) collective-permute-start(bf16[2,32,128]{2,1,0:T(8,128)(2,1)S(1)} %get-tuple-element.93), channel_id=1, source_target_pairs={{0,8},{1,9},{2,10},{3,11},{4,12},{5,13},{6,14},{7,15},{8,0},{9,1},... | collective-permute-start | bytes 49160 | tf_op jit(solution)/shard_map/ppermute | solution.py:616
  36.7 1.7 %collective-permute-start.12 = (bf16[2,32,128]{2,1,0:T(8,128)(2,1)S(1)}, bf16[2,32,128]{2,1,0:T(8,128)(2,1)S(1)}, u32[]{:S(2)}, u32[]{:S(2)}) collective-permute-start(bf16[2,32,128]{2,1,0:T(8,128)(2,1)S(1)} %get-tuple-element.95), channel_id=1, source_target_pairs={{0,4},{1,5},{2,6},{3,7},{4,0},{5,1},{6,2},{7,3},{8,12},{9,13},{10,... | collective-permute-start | bytes 49160 | tf_op jit(solution)/shard_map/ppermute | solution.py:616
  38.4 1.4 %shard_map.111 = (bf16[128,2048]{1,0:T(8,128)(2,1)}, bf16[128,2048]{1,0:T(8,128)(2,1)}, bf16[128,1024]{1,0:T(8,128)(2,1)S(1)}, bf16[128,1024]{1,0:T(8,128)(2,1)S(1)}) custom-call(bf16[2,2,8,32,128]{4,3,2,1,0:T(8,128)(2,1)S(1)} %get-tuple-element.80.mg_ref, bf16[512,128]{1,0:T(8,128)(2,1)S(1)} %copy-done.4, f32[2,2,128,1024]{3,2,1,0:T(8,128)S(1)} %get-tuple-element.81.terms_ref), custom_call_target="tpu_custom_call" | custom-call | flops 268435456 | bytes 3670016 | tf_op jit(solution)/shard_map/pallas_call | solution.py:567
  39.7 1.0 %collective-permute-done.13 = bf16[2,32,128]{2,1,0:T(8,128)(2,1)S(1)} collective-permute-done((bf16[2,32,128]{2,1,0:T(8,128)(2,1)S(1)}, bf16[2,32,128]{2,1,0:T(8,128)(2,1)S(1)}, u32[]{:S(2)}, u32[]{:S(2)}) %collective-permute-start.13) | collective-permute-done | bytes 16416 | tf_op jit(solution)/shard_map/ppermute | solution.py:616
  40.8 1.6 %collective-permute-start.14 = (bf16[1,32,128]{2,1,0:T(8,128)(2,1)S(1)}, bf16[1,32,128]{2,1,0:T(8,128)(2,1)S(1)}, u32[]{:S(2)}, u32[]{:S(2)}) collective-permute-start(bf16[1,32,128]{2,1,0:T(8,128)(2,1)S(1)} %get-tuple-element.97), channel_id=1, source_target_pairs={{0,1},{1,0},{2,3},{3,2},{4,5},{5,4},{6,7},{7,6},{8,9},{9,8},{10,11... | collective-permute-start | bytes 24584 | tf_op jit(solution)/shard_map/ppermute | solution.py:616
  42.8 2.4 %collective-permute-start.19 = (bf16[1,32,128]{2,1,0:T(8,128)(2,1)S(1)}, bf16[1,32,128]{2,1,0:T(8,128)(2,1)S(1)}, u32[]{:S(2)}, u32[]{:S(2)}) collective-permute-start(bf16[1,32,128]{2,1,0:T(8,128)(2,1)S(1)} %get-tuple-element.96), channel_id=1, source_target_pairs={{0,16},{1,17},{2,18},{3,19},{4,20},{5,21},{6,22},{7,23},{8,24},{9,... | collective-permute-start | bytes 24584 | tf_op jit(solution)/shard_map/ppermute | solution.py:616
  46.0 0.8 %shard_map.112 = (bf16[128,2048]{1,0:T(8,128)(2,1)}, bf16[128,2048]{1,0:T(8,128)(2,1)}) custom-call(bf16[128,2048]{1,0:T(8,128)(2,1)} %get-tuple-element.82.a_in, bf16[128,2048]{1,0:T(8,128)(2,1)} %get-tuple-element.83.b_in, bf16[128,1024]{1,0:T(8,128)(2,1)S(1)} %collective-permute-done.17.got_a, ...), custom_call_target="tpu_custom_call", output_to_operand_aliasing={{0}: (0, {}), {1}: (1, {})} | custom-call | bytes 1048576 | tf_op jit(solution)/shard_map/pallas_call | solution.py:537
  46.9 0.9 %collective-permute-done.20 = bf16[1,32,128]{2,1,0:T(8,128)(2,1)S(1)} collective-permute-done((bf16[1,32,128]{2,1,0:T(8,128)(2,1)S(1)}, bf16[1,32,128]{2,1,0:T(8,128)(2,1)S(1)}, u32[]{:S(2)}, u32[]{:S(2)}) %collective-permute-start.20) | collective-permute-done | bytes 8224 | tf_op jit(solution)/shard_map/ppermute | solution.py:616
  (45 shorter events, 5.7 us)
Async XLA Ops:
  0.6 15.1 %copy-start.4 = (bf16[512,128]{1,0:T(8,128)(2,1)S(1)}, bf16[512,128]{1,0:T(8,128)(2,1)}, u32[]{:S(2)}) copy-start(bf16[512,128]{1,0:T(8,128)(2,1)} %w_ref.3) | copy-start | bytes 393220
  0.6 15.1 %copy-start.1 = (bf16[1,128,2048]{2,1,0:T(8,128)(2,1)S(1)}, bf16[1,128,2048]{2,1,0:T(8,128)(2,1)}, u32[]{:S(2)}) copy-start(bf16[1,128,2048]{2,1,0:T(8,128)(2,1)} %param.9) | copy-start | bytes 1572868
  0.7 15.1 %copy-start.3 = (bf16[1,128,2048]{2,1,0:T(8,128)(2,1)S(1)}, bf16[1,128,2048]{2,1,0:T(8,128)(2,1)}, u32[]{:S(2)}) copy-start(bf16[1,128,2048]{2,1,0:T(8,128)(2,1)} %param.8) | copy-start | bytes 1572868
  2.9 11.4 %collective-permute-start = (bf16[512,1024]{1,0:T(8,128)(2,1)S(1)}, bf16[512,1024]{1,0:T(8,128)(2,1)S(1)}, u32[]{:S(2)}, u32[]{:S(2)}) collective-permute-start(bf16[512,1024]{1,0:T(8,128)(2,1)S(1)} %get-tuple-element.49), channel_id=1, source_target_pairs={{0,2},{2,0},{4,6},{6,4},{8,10},{10,8},{12,14},{14,12},{16,18},{18,... | collective-permute-start | bytes 3145736 | tf_op jit(solution)/shard_map/ppermute | solution.py:421
  3.4 8.5 %collective-permute-start.4 = (bf16[2,8,32,128]{3,2,1,0:T(8,128)(2,1)S(1)}, bf16[2,8,32,128]{3,2,1,0:T(8,128)(2,1)S(1)}, u32[]{:S(2)}, u32[]{:S(2)}) collective-permute-start(bf16[2,8,32,128]{3,2,1,0:T(8,128)(2,1)S(1)} %get-tuple-element.60.own_ref), channel_id=1, source_target_pairs={{0,10},{2,8},{4,14},{6,12},{8,18},{10,16},{12,22},{14,20},{16,26},... | collective-permute-start | bytes 393224 | tf_op jit(solution)/shard_map/ppermute | solution.py:418
  6.1 11.5 %collective-permute-start.2 = (bf16[2,8,32,128]{3,2,1,0:T(8,128)(2,1)S(1)}, bf16[2,8,32,128]{3,2,1,0:T(8,128)(2,1)S(1)}, u32[]{:S(2)}, u32[]{:S(2)}) collective-permute-start(bf16[2,8,32,128]{3,2,1,0:T(8,128)(2,1)S(1)} %get-tuple-element.55), channel_id=1, source_target_pairs={{0,4},{2,6},{4,8},{6,10},{8,12},{10,14},{12,16},{14,18},{16,20},{1... | collective-permute-start | bytes 393224 | tf_op jit(solution)/shard_map/ppermute | solution.py:406
  7.6 10.0 %collective-permute-start.3 = (bf16[2,8,32,128]{3,2,1,0:T(8,128)(2,1)S(1)}, bf16[2,8,32,128]{3,2,1,0:T(8,128)(2,1)S(1)}, u32[]{:S(2)}, u32[]{:S(2)}) collective-permute-start(bf16[2,8,32,128]{3,2,1,0:T(8,128)(2,1)S(1)} %get-tuple-element.55), channel_id=1, source_target_pairs={{0,8},{2,10},{4,12},{6,14},{8,16},{10,18},{12,20},{14,22},{16,24},... | collective-permute-start | bytes 393224 | tf_op jit(solution)/shard_map/ppermute | solution.py:406
  12.0 6.7 %collective-permute-start.5 = (bf16[2,8,32,128]{3,2,1,0:T(8,128)(2,1)S(1)}, bf16[2,8,32,128]{3,2,1,0:T(8,128)(2,1)S(1)}, u32[]{:S(2)}, u32[]{:S(2)}) collective-permute-start(bf16[2,8,32,128]{3,2,1,0:T(8,128)(2,1)S(1)} %shard_map.104), channel_id=1, source_target_pairs={{0,6},{2,4},{4,0},{6,2},{8,14},{10,12},{12,8},{14,10},{16,22},{18,... | collective-permute-start | bytes 393224 | tf_op jit(solution)/shard_map/ppermute | solution.py:456
  14.3 1.5 %collective-permute-start.1 = (s32[1,1]{1,0:T(1,128)}, s32[1,1]{1,0:T(1,128)}, u32[]{:S(2)}, u32[]{:S(2)}) collective-permute-start(s32[1,1]{1,0:T(1,128)} %param.11), channel_id=1, source_target_pairs={{0,2},{2,0},{4,6},{6,4},{8,10},{10,8},{12,14},{14,12},{16,18},{18,... | collective-permute-start | bytes 20 | tf_op jit(solution)/shard_map/ppermute | solution.py:421
  20.1 5.5 %collective-permute-start.8 = (bf16[2,8,32,128]{3,2,1,0:T(8,128)(2,1)S(1)}, bf16[2,8,32,128]{3,2,1,0:T(8,128)(2,1)S(1)}, u32[]{:S(2)}, u32[]{:S(2)}) collective-permute-start(bf16[2,8,32,128]{3,2,1,0:T(8,128)(2,1)S(1)} %get-tuple-element.64), channel_id=1, source_target_pairs={{0,4},{2,6},{4,0},{6,2},{8,12},{10,14},{12,8},{14,10},{16,20},{18,... | collective-permute-start | bytes 393224 | tf_op jit(solution)/shard_map/ppermute | solution.py:421
  20.8 9.1 %collective-permute-start.6 = (bf16[2,8,32,128]{3,2,1,0:T(8,128)(2,1)S(1)}, bf16[2,8,32,128]{3,2,1,0:T(8,128)(2,1)S(1)}, u32[]{:S(2)}, u32[]{:S(2)}) collective-permute-start(bf16[2,8,32,128]{3,2,1,0:T(8,128)(2,1)S(1)} %get-tuple-element.62), channel_id=1, source_target_pairs={{0,24},{2,26},{4,28},{6,30},{8,0},{10,2},{12,4},{14,6},{16,8},{18,... | collective-permute-start | bytes 393224 | tf_op jit(solution)/shard_map/ppermute | solution.py:406
  22.5 7.4 %collective-permute-start.7 = (bf16[2,8,32,128]{3,2,1,0:T(8,128)(2,1)S(1)}, bf16[2,8,32,128]{3,2,1,0:T(8,128)(2,1)S(1)}, u32[]{:S(2)}, u32[]{:S(2)}) collective-permute-start(bf16[2,8,32,128]{3,2,1,0:T(8,128)(2,1)S(1)} %get-tuple-element.63), channel_id=1, source_target_pairs={{4,0},{6,2},{8,4},{10,6},{12,8},{14,10},{16,12},{18,14},{20,16},{2... | collective-permute-start | bytes 393224 | tf_op jit(solution)/shard_map/ppermute | solution.py:409
  25.7 7.3 %collective-permute-start.9 = (bf16[2,8,32,128]{3,2,1,0:T(8,128)(2,1)S(1)}, bf16[2,8,32,128]{3,2,1,0:T(8,128)(2,1)S(1)}, u32[]{:S(2)}, u32[]{:S(2)}) collective-permute-start(bf16[2,8,32,128]{3,2,1,0:T(8,128)(2,1)S(1)} %shard_map.108), channel_id=1, source_target_pairs={{8,0},{10,2},{12,4},{14,6},{16,8},{18,10},{20,12},{22,14},{24,16},... | collective-permute-start | bytes 393224 | tf_op jit(solution)/shard_map/ppermute | solution.py:409
  33.4 1.3 %collective-permute-start.10 = (bf16[8,32,128]{2,1,0:T(8,128)(2,1)S(1)}, bf16[8,32,128]{2,1,0:T(8,128)(2,1)S(1)}, u32[]{:S(2)}, u32[]{:S(2)}) collective-permute-start(bf16[8,32,128]{2,1,0:T(8,128)(2,1)S(1)} %get-tuple-element.73), channel_id=1, source_target_pairs={{0,2},{2,0},{4,6},{6,4},{8,10},{10,8},{12,14},{14,12},{16,18},{18,... | collective-permute-start | bytes 196616 | tf_op jit(solution)/shard_map/ppermute | solution.py:421
  33.6 8.7 %collective-permute-start.15 = (bf16[128,1024]{1,0:T(8,128)(2,1)S(1)}, bf16[128,1024]{1,0:T(8,128)(2,1)S(1)}, u32[]{:S(2)}, u32[]{:S(2)}) collective-permute-start(bf16[128,1024]{1,0:T(8,128)(2,1)S(1)} %get-tuple-element.76), channel_id=1, source_target_pairs={{0,2},{2,0},{4,6},{6,4},{8,10},{10,8},{12,14},{14,12},{16,18},{18,... | collective-permute-start | bytes 786440 | tf_op jit(solution)/shard_map/ppermute | solution.py:421
  34.0 8.8 %collective-permute-start.16 = (bf16[128,1024]{1,0:T(8,128)(2,1)S(1)}, bf16[128,1024]{1,0:T(8,128)(2,1)S(1)}, u32[]{:S(2)}, u32[]{:S(2)}) collective-permute-start(bf16[128,1024]{1,0:T(8,128)(2,1)S(1)} %get-tuple-element.77), channel_id=1, source_target_pairs={{0,2},{2,0},{4,6},{6,4},{8,10},{10,8},{12,14},{14,12},{16,18},{18,... | collective-permute-start | bytes 786440 | tf_op jit(solution)/shard_map/ppermute | solution.py:421
  34.8 4.9 %collective-permute-start.11 = (bf16[2,32,128]{2,1,0:T(8,128)(2,1)S(1)}, bf16[2,32,128]{2,1,0:T(8,128)(2,1)S(1)}, u32[]{:S(2)}, u32[]{:S(2)}) collective-permute-start(bf16[2,32,128]{2,1,0:T(8,128)(2,1)S(1)} %get-tuple-element.93), channel_id=1, source_target_pairs={{0,8},{1,9},{2,10},{3,11},{4,12},{5,13},{6,14},{7,15},{8,0},{9,1},... | collective-permute-start | bytes 49160 | tf_op jit(solution)/shard_map/ppermute | solution.py:616
  36.1 4.6 %collective-permute-start.13 = (bf16[2,32,128]{2,1,0:T(8,128)(2,1)S(1)}, bf16[2,32,128]{2,1,0:T(8,128)(2,1)S(1)}, u32[]{:S(2)}, u32[]{:S(2)}) collective-permute-start(bf16[2,32,128]{2,1,0:T(8,128)(2,1)S(1)} %get-tuple-element.94), channel_id=1, source_target_pairs={{0,12},{1,13},{2,14},{3,15},{4,8},{5,9},{6,10},{7,11},{8,4},{9,5},... | collective-permute-start | bytes 49160 | tf_op jit(solution)/shard_map/ppermute | solution.py:616
  36.7 4.0 %collective-permute-start.12 = (bf16[2,32,128]{2,1,0:T(8,128)(2,1)S(1)}, bf16[2,32,128]{2,1,0:T(8,128)(2,1)S(1)}, u32[]{:S(2)}, u32[]{:S(2)}) collective-permute-start(bf16[2,32,128]{2,1,0:T(8,128)(2,1)S(1)} %get-tuple-element.95), channel_id=1, source_target_pairs={{0,4},{1,5},{2,6},{3,7},{4,0},{5,1},{6,2},{7,3},{8,12},{9,13},{10,... | collective-permute-start | bytes 49160 | tf_op jit(solution)/shard_map/ppermute | solution.py:616
  39.7 6.3 %collective-permute-start.17 = (bf16[128,1024]{1,0:T(8,128)(2,1)S(1)}, bf16[128,1024]{1,0:T(8,128)(2,1)S(1)}, u32[]{:S(2)}, u32[]{:S(2)}) collective-permute-start(bf16[128,1024]{1,0:T(8,128)(2,1)S(1)} %get-tuple-element.84), channel_id=1, source_target_pairs={{0,2},{2,0},{4,6},{6,4},{8,10},{10,8},{12,14},{14,12},{16,18},{18,... | collective-permute-start | bytes 786440 | tf_op jit(solution)/shard_map/ppermute | solution.py:421
  40.7 5.3 %collective-permute-start.18 = (bf16[128,1024]{1,0:T(8,128)(2,1)S(1)}, bf16[128,1024]{1,0:T(8,128)(2,1)S(1)}, u32[]{:S(2)}, u32[]{:S(2)}) collective-permute-start(bf16[128,1024]{1,0:T(8,128)(2,1)S(1)} %get-tuple-element.85), channel_id=1, source_target_pairs={{0,2},{2,0},{4,6},{6,4},{8,10},{10,8},{12,14},{14,12},{16,18},{18,... | collective-permute-start | bytes 786440 | tf_op jit(solution)/shard_map/ppermute | solution.py:421
  40.8 6.1 %collective-permute-start.14 = (bf16[1,32,128]{2,1,0:T(8,128)(2,1)S(1)}, bf16[1,32,128]{2,1,0:T(8,128)(2,1)S(1)}, u32[]{:S(2)}, u32[]{:S(2)}) collective-permute-start(bf16[1,32,128]{2,1,0:T(8,128)(2,1)S(1)} %get-tuple-element.97), channel_id=1, source_target_pairs={{0,1},{1,0},{2,3},{3,2},{4,5},{5,4},{6,7},{7,6},{8,9},{9,8},{10,11... | collective-permute-start | bytes 24584 | tf_op jit(solution)/shard_map/ppermute | solution.py:616
  42.3 5.4 %collective-permute-start.20 = (bf16[1,32,128]{2,1,0:T(8,128)(2,1)S(1)}, bf16[1,32,128]{2,1,0:T(8,128)(2,1)S(1)}, u32[]{:S(2)}, u32[]{:S(2)}) collective-permute-start(bf16[1,32,128]{2,1,0:T(8,128)(2,1)S(1)} %get-tuple-element.96), channel_id=1, source_target_pairs={{0,17},{1,16},{2,19},{3,18},{4,21},{5,20},{6,23},{7,22},{8,25},{9,... | collective-permute-start | bytes 24584 | tf_op jit(solution)/shard_map/ppermute | solution.py:616
  42.8 5.0 %collective-permute-start.19 = (bf16[1,32,128]{2,1,0:T(8,128)(2,1)S(1)}, bf16[1,32,128]{2,1,0:T(8,128)(2,1)S(1)}, u32[]{:S(2)}, u32[]{:S(2)}) collective-permute-start(bf16[1,32,128]{2,1,0:T(8,128)(2,1)S(1)} %get-tuple-element.96), channel_id=1, source_target_pairs={{0,16},{1,17},{2,18},{3,19},{4,20},{5,21},{6,22},{7,23},{8,24},{9,... | collective-permute-start | bytes 24584 | tf_op jit(solution)/shard_map/ppermute | solution.py:616
  (2 other events, 30.2 us)
